TPU v7x, 32 devices: a whole 2x2x4 slice. The times are simulated.
32 devices in a mesh: batch: 8 (over z, x), tower: 4 (over y, core).
Axes of the slice: x: 2, y: 2, z: 4, core: 2. Of those that a mesh axis runs over, the one named last changes fastest.
Arguments:
- convmaps: bfloat16 [4096, 2, 169, 256], P(('batch', 'tower')), may hold values from -8 to 8
- group: int32 [4096], P(('batch', 'tower')), may hold values from 0 to 1
- alpha1: bfloat16 [2, 2, 256], replicated, may hold values from 0.19921875 to 1
- weight: bfloat16 [9216, 8192], P('batch', 'tower'), may hold values from -0.0625 to 0.0625
- bias: bfloat16 [8192], P('tower'), may hold values from -3 to 3
- alpha2: bfloat16 [2, 8192], P(None, 'tower'), may hold values from 0.19921875 to 1
- cotangent: bfloat16 [4096, 8192], P('batch', 'tower'), may hold values from -6 to 6
Outputs:
- activations: bfloat16 [4096, 8192], P('batch', 'tower')
- input_grad: bfloat16 [4096, 2, 169, 256], P(('batch', 'tower'))
- weight_grad: float32 [9216, 8192], P('batch', 'tower')
- bias_grad: float32 [8192], P('tower')
- alpha1_grad: float32 [2, 2, 256], replicated
- alpha2_grad: float32 [2, 8192], P(None, 'tower')
Inputs may be any that keep to these rules, and one draw needn't show every extreme that they name: `group`: 0 marks an image of a 227 input with a full 6 x 6 pool, 1 an image of a 195 input whose pool is 5 x 5 padded.
All inputs are finite; a program needn't handle non-finite values.
Results may differ from a plain program's by a relative error of at most 0.0055.
Values may be sent and summed in bfloat16 or wider, within the bound.
No kernel may reach another device: no remote copies, remote signals or barrier semaphores. Data moves between devices by JAX's collectives and lax.ppermute only.
A program may use at most 320 MiB of HBM per device.

v0:
```python
import jax
import jax.numpy as jnp
from jax import lax
from jax.sharding import PartitionSpec as P


def swapped(value, axis, apart):
    mask = 2**apart
    pairs = [(source, source ^ mask) for source in range(lax.axis_size(axis))]
    return lax.ppermute(value, axis, pairs)


def pool_table(dtype):
    pooled_pos = jnp.arange(36)[:, None]
    map_pos = jnp.arange(169)[None, :]
    prow = pooled_pos // 6
    pcol = pooled_pos % 6
    qrow = map_pos // 13
    qcol = map_pos % 13
    inside = (
        (qrow >= 2 * prow) & (qrow <= 2 * prow + 2) & (qcol >= 2 * pcol) & (qcol <= 2 * pcol + 2)
    )
    return jnp.where(inside, 1.0, 0.0).astype(dtype)


def keep_mask(group):
    place = jnp.arange(36)
    small = (place // 6 < 5) & (place % 6 < 5)
    return jnp.where((group == 0)[:, None] | small[None, :], 1.0, 0.0).astype(jnp.float32)


def shards(convmaps, group, alpha1, weight, bias, alpha2, cotangent):
    highest = lax.Precision.HIGHEST
    count = convmaps.shape[0]
    channels = convmaps.shape[3]
    table = pool_table(jnp.bfloat16)
    summed = jnp.einsum("pq,nsqc->snpc", table, convmaps, preferred_element_type=jnp.float32)
    keep = keep_mask(group)
    pooled = summed * (1.0 / 9.0) * keep[None, :, :, None]
    first = alpha1.astype(jnp.float32)
    mixed = jnp.einsum("asc,snpc->anpc", first, pooled, precision=highest)
    features = mixed.astype(jnp.bfloat16).reshape(2, count, -1)
    halves = lax.axis_size("tower") // 2
    outgoing = jnp.repeat(features, halves, axis=0)
    arrived = lax.all_to_all(outgoing, "tower", split_axis=0, concat_axis=1, tiled=True)
    rows_in = arrived.reshape(-1, features.shape[2])
    tower_id = lax.axis_index("tower") // halves
    columns = rows_in
    pre = jnp.dot(
        columns,
        lax.all_gather(weight, "batch", axis=0, tiled=True),
        preferred_element_type=jnp.float32,
    )
    pre = pre + bias.astype(jnp.float32)[None, :]
    act_low = jax.nn.gelu(pre).astype(jnp.bfloat16)
    other_act, other_cot, other_second = swapped(
        (act_low, cotangent, alpha2), "tower", halves.bit_length() - 1
    )
    own_first = tower_id == 0
    pair = jnp.where(own_first, jnp.stack([act_low, other_act]), jnp.stack([other_act, act_low]))
    second = alpha2.astype(jnp.float32)
    stitched = second[0][None, :] * pair[0] + second[1][None, :] * pair[1]
    activations = stitched.astype(jnp.bfloat16)
    own_coef = lax.dynamic_index_in_dim(second, tower_id, 0, keepdims=False)
    other_coef = lax.dynamic_index_in_dim(
        other_second.astype(jnp.float32), tower_id, 0, keepdims=False
    )
    dact = own_coef[None, :] * cotangent.astype(jnp.float32) + other_coef[
        None, :
    ] * other_cot.astype(jnp.float32)
    second_local = jnp.einsum("rk,srk->sk", cotangent, pair, preferred_element_type=jnp.float32)
    gelu_out, gelu_back = jax.vjp(jax.nn.gelu, pre)
    dpre_low = gelu_back(dact)[0].astype(jnp.bfloat16)
    bias_local = jnp.sum(dpre_low, axis=0, dtype=jnp.float32)
    alpha2_grad, bias_grad = lax.psum((second_local, bias_local), "batch")
    columns = rows_in
    weight_grad = lax.psum_scatter(
        lax.dot_general(
            columns, dpre_low, (((0,), (0,)), ((), ())), preferred_element_type=jnp.float32
        ),
        "batch",
        scatter_dimension=0,
        tiled=True,
    )
    dfeat = lax.dot_general(
        dpre_low,
        lax.all_gather(weight, "batch", axis=0, tiled=True),
        (((1,), (1,)), ((), ())),
        preferred_element_type=jnp.float32,
    )
    returning = dfeat.reshape(lax.axis_size("tower"), count, -1)
    returned = lax.all_to_all(returning, "tower", split_axis=0, concat_axis=0, tiled=True)
    dmixed = returned.reshape(2, halves, count, -1).sum(axis=1).reshape(2, count, 36, channels)
    first_local = jnp.einsum("anpc,snpc->asc", dmixed, pooled, precision=highest)
    dpooled = (
        jnp.einsum("asc,anpc->snpc", first, dmixed, precision=highest)
        * (1.0 / 9.0)
        * keep[None, :, :, None]
    )
    input_grad = jnp.einsum(
        "pq,snpc->nsqc", table.astype(jnp.float32), dpooled, precision=highest
    ).astype(jnp.bfloat16)
    alpha1_grad = lax.psum(first_local, ("batch", "tower"))
    return (activations, input_grad, weight_grad, bias_grad, alpha1_grad, alpha2_grad)


def solution(mesh):
    in_specs = (
        P(("batch", "tower"), None, None, None),
        P(("batch", "tower")),
        P(),
        P("batch", "tower"),
        P("tower"),
        P(None, "tower"),
        P("batch", "tower"),
    )
    out_specs = (
        P("batch", "tower"),
        P(("batch", "tower"), None, None, None),
        P("batch", "tower"),
        P("tower"),
        P(),
        P(None, "tower"),
    )
    return jax.shard_map(shards, mesh=mesh, in_specs=in_specs, out_specs=out_specs, check_vma=False)
```

profile of v0, /device:TPU:0, one launch (start us, length us, event | category | flops | bytes accessed | tf_op | source)
XLA Modules:
  0.0 1982.3 jit_solution(3323926294600063746)
XLA Ops:
  7.2 0.7 all-gather.2.cloned.1.call-update
  8.3 11.5 fusion
  19.9 7.9 bitcast_multiply_fusion
  27.8 14.9 copy.44
  42.8 22.8 %fusion.6 = bf16[2,128,36,256]{1,0,2,3:T(2,128)(2,1)S(1)} fusion(f32[2,128,36,256]{1,0,2,3:T(2,128)} %copy.44, bf16[2,2,256,1]{0,1,3,2:T(2,128)(2,1)S(1)} %copy.58), kind=kOutput, calls=%fused_computation.14 | convolution fusion | flops 58982400 | bytes 14157824 | tf_op jit(solution)/shard_map/asc,snpc->anpc/dot_general | solution.py:41
  65.5 3.4 copy.46
  68.9 6.6 copy.47
  75.6 7.2 broadcast_in_dim.32
  82.8 6.0 all-to-all-start
  88.8 3.0 collective-permute-start.2
  92.0 146.9 %collective-permute-done.1 = bf16[2,2048]{1,0:T(2,128)(2,1)S(1)} collective-permute-done((bf16[2,2048]{1,0:T(2,128)(2,1)S(1)}, bf16[2,2048]{1,0:T(2,128)(2,1)S(1)}, u32[]{:S(2)}, u32[]{:S(2)}) %collective-permute-start.1) | collective-permute-done | bytes 8224 | tf_op jit(solution)/shard_map/ppermute | solution.py:10
  238.9 489.7 %all-gather.2.cloned.1.call-done = bf16[9216,2048]{1,0:T(8,128)(2,1)} async-done(((bf16[1152,2048]{1,0:T(8,128)(2,1)}), bf16[9216,2048]{1,0:T(8,128)(2,1)}) %all-gather.2.cloned.1.call-update) | async-done | bytes 37748752 | tf_op jit(solution)/shard_map/all_gather | solution.py:51
  728.7 31.3 %convert_reduce_fusion = (f32[2048]{0:T(1024)S(1)}, bf16[512,2048]{1,0:T(8,128)(2,1)}, bf16[512,2048]{1,0:T(8,128)(2,1)}) fusion(f32[2048]{0:T(1024)S(1)} %convert_element_type.62, bf16[512,2048]{1,0:T(8,128)(2,1)} %collective-permute-done.2, f32[2048]{0:T(1024)S(1)} %bitcast.70, bf16[512,2048]{1,0:T(8,128)(2,1)S(1)} %copy-done, f32[2048]{0:T(1024)S(1)} %bitcast.69, ...), kind=kOutput, calls=%fused_computation.27 | convolution fusion | flops 19358808064 | bytes 55607296 | tf_op jit(solution)/shard_map/dot_general | solution.py:49
  760.0 34.6 %fusion.33 = f32[9216,2048]{1,0:T(8,128)} fusion(bf16[512,9216]{1,0:T(8,128)(2,1)} %bitcast.10, bf16[512,2048]{1,0:T(8,128)(2,1)} %get-tuple-element.35), kind=kOutput, calls=%fused_computation.62 | convolution fusion | flops 19327352832 | bytes 87031808 | tf_op jit(solution)/shard_map/dot_general | solution.py:78
  794.6 27.7 %fusion.32 = f32[512,9216]{1,0:T(8,128)} fusion(bf16[512,2048]{1,0:T(8,128)(2,1)} %get-tuple-element.35, bf16[9216,2048]{1,0:T(8,128)(2,1)} %all-gather.2.cloned.1.call-done), kind=kOutput, calls=%fused_computation.61 | convolution fusion | flops 19327352832 | bytes 58720256 | tf_op jit(solution)/shard_map/dot_general | solution.py:85
  822.4 7.7 all-to-all-start.1
  830.1 2.0 collective-permute-start
  832.1 0.5 bitcast_convert_fusion
  832.6 247.9 %collective-permute-done = bf16[512,2048]{1,0:T(8,128)(2,1)} collective-permute-done((bf16[512,2048]{1,0:T(8,128)(2,1)}, bf16[512,2048]{1,0:T(8,128)(2,1)}, u32[]{:S(2)}, u32[]{:S(2)}) %collective-permute-start) | collective-permute-done | bytes 2097184 | tf_op jit(solution)/shard_map/ppermute | solution.py:10
  1080.6 5.0 multiply_reduce_fusion
  1085.5 38.6 %all-reduce = (f32[2048]{0:T(1024)}, f32[2,2048]{1,0:T(2,128)}) all-reduce(f32[2048]{0:T(1024)S(1)} %get-tuple-element.34, f32[2,2048]{1,0:T(2,128)S(1)} %bitcast.66), channel_id=1, replica_groups=mesh['batch'=8,'tower'=4] {'batch'}, use_global_device_ids=true, to_apply=%region_3.4 | all-reduce | flops 6144 | bytes 49152 | tf_op jit(solution)/shard_map/psum | solution.py:75
  1124.1 4.6 fusion.17
  1128.7 11.7 bitcast_reduce_fusion
  1140.4 9.7 copy.48
  1150.1 87.1 %fusion.18 = f32[2,2,256]{0,1,2:T(2,128)S(1)} fusion(f32[2,128,36,256]{1,0,2,3:T(2,128)} %copy.44, f32[2,128,36,256]{1,3,2,0:T(8,128)} %bitcast.63), kind=kOutput, calls=%fused_computation.32 | convolution fusion | flops 56623104 | bytes 18878464 | tf_op jit(solution)/shard_map/anpc,snpc->asc/dot_general | solution.py:94
  1237.2 43.3 %psum.22 = f32[2,2,256]{0,1,2:T(2,128)S(1)} all-reduce(f32[2,2,256]{0,1,2:T(2,128)S(1)} %fusion.18), channel_id=1, replica_groups=mesh['batch'=8,'tower'=4] {'batch','tower'}, use_global_device_ids=true, to_apply=%region_4.5 | all-reduce | flops 1024 | bytes 8192 | tf_op jit(solution)/shard_map/psum | solution.py:103
  1280.4 0.7 copy.55
  1281.1 30.7 %multiply_bitcast_fusion = f32[2,128,36,256]{1,0,2,3:T(2,128)} fusion(f32[128,36]{0,1:T(8,128)S(1)} %copy-done.5, bf16[2,2,256,1]{0,1,3,2:T(2,128)(2,1)S(1)} %copy-done.3, f32[2,128,36,256]{1,3,2,0:T(8,128)} %bitcast.64), kind=kOutput, calls=%fused_computation.5 | convolution fusion | flops 58982400 | bytes 18894848 | tf_op jit(solution)/shard_map/asc,anpc->snpc/dot_general | solution.py:96
  1311.9 12.5 copy.51
  1324.5 25.3 %convert_bitcast_fusion = bf16[128,2,169,256]{3,2,0,1:T(8,128)(2,1)} fusion(f32[2,128,36,256]{3,2,1,0:T(8,128)} %copy.51, s32[169]{0:T(256)S(1)} %copy-done.9, s32[169]{0:T(256)S(1)} %copy-done.11, s32[36]{0:T(128)S(1)} %copy-done.19, s32[36]{0:T(128)S(1)} %copy-done.21, s32[36]{0:T(128)S(1)} %copy-done.15, s32[36]{0:T(128)S(1)} %copy-done.17), kind=kOutput, calls=%fused_computation.2 | convolution fusion | flops 4795782656 | bytes 31590280 | tf_op jit(solution)/shard_map/pq,snpc->nsqc/dot_general | solution.py:100
  1349.8 32.5 %copy.54 = bf16[128,2,169,256]{3,1,2,0:T(2,128)(2,1)} copy(bf16[128,2,169,256]{3,2,0,1:T(8,128)(2,1)} %convert_bitcast_fusion) | data formatting | bytes 44302336
  1382.2 592.7 %reduce-scatter.2.cloned.1.call-done = f32[1152,2048]{1,0:T(8,128)} async-done(((f32[9216,2048]{1,0:T(8,128)}), f32[1152,2048]{1,0:T(8,128)}) %reduce-scatter.2.cloned.1.call-update) | async-done | bytes 9437200 | tf_op jit(solution)/shard_map/reduce_scatter | solution.py:77
  (65 shorter events, 0.6 us)
Async XLA Ops:
  7.2 0.8 copy-start.13
  7.2 1.1 copy-start.22
  7.2 721.5 %all-gather.2.cloned.1.call-start = ((), (), s32[]{:S(2)}) async-start(), calls=%async_computation.3 | async-start | bytes 42467328 | tf_op jit(solution)/shard_map/all_gather | solution.py:51
  8.1 34.7 %copy-start.2 = (bf16[2,2,256,1]{0,1,3,2:T(2,128)(2,1)}, bf16[2,2,256,1]{0,1,3,2:T(2,128)(2,1)S(1)}, u32[]{:S(2)}) copy-start(bf16[2,2,256,1]{0,1,3,2:T(2,128)(2,1)S(1)} %copy.58) | copy-start | bytes 6148
  8.2 11.7 copy-start.14
  8.2 11.7 copy-start.16
  8.2 11.6 copy-start.18
  8.2 11.6 copy-start.20
  8.2 11.6 copy-start.8
  8.2 11.6 copy-start.10
  8.3 11.5 copy-start.4
  82.8 6.0 copy-start
  82.8 9.1 copy-start.6
  82.8 9.2 copy-start.12
  82.8 156.1 %all-to-all-start = ((bf16[4,128,9216]{2,1,0:T(8,128)(2,1)}), bf16[4,128,9216]{2,1,0:T(8,128)(2,1)}, u32[]{:S(2)}, u32[]{:S(2)}) async-start(bf16[4,128,9216]{2,1,0:T(8,128)(2,1)} %bitcast.60), calls=%async_computation | async-start | bytes 18874368 | tf_op jit(solution)/shard_map/all_to_all | solution.py:45
  88.8 1886.2 %reduce-scatter.2.cloned.1.call-start = ((), (), s32[]{:S(2)}) async-start(), calls=%async_computation.4 | async-start | bytes 84934656 | tf_op jit(solution)/shard_map/reduce_scatter | solution.py:77
  88.8 150.1 %collective-permute-start.2 = (bf16[512,2048]{1,0:T(8,128)(2,1)S(1)}, bf16[512,2048]{1,0:T(8,128)(2,1)}, u32[]{:S(2)}, u32[]{:S(2)}) collective-permute-start(bf16[512,2048]{1,0:T(8,128)(2,1)S(1)} %copy-done), channel_id=1, source_target_pairs={{0,2},{1,3},{2,0},{3,1},{4,6},{5,7},{6,4},{7,5},{8,10},{9,11},{10,... | collective-permute-start | bytes 6291464 | tf_op jit(solution)/shard_map/ppermute | solution.py:10
  91.8 147.0 %collective-permute-start.1 = (bf16[2,2048]{1,0:T(2,128)(2,1)S(1)}, bf16[2,2048]{1,0:T(2,128)(2,1)S(1)}, u32[]{:S(2)}, u32[]{:S(2)}) collective-permute-start(bf16[2,2048]{1,0:T(2,128)(2,1)S(1)} %copy-done.6), channel_id=1, source_target_pairs={{0,2},{1,3},{2,0},{3,1},{4,6},{5,7},{6,4},{7,5},{8,10},{9,11},{10,... | collective-permute-start | bytes 24584 | tf_op jit(solution)/shard_map/ppermute | solution.py:10
  822.3 9.7 copy-start.7
  822.4 306.3 %all-to-all-start.1 = ((f32[4,128,9216]{2,1,0:T(8,128)}), f32[4,128,9216]{2,1,0:T(8,128)}, u32[]{:S(2)}, u32[]{:S(2)}) async-start(f32[4,128,9216]{2,1,0:T(8,128)} %bitcast.61), calls=%async_computation.1 | async-start | bytes 37748736 | tf_op jit(solution)/shard_map/all_to_all | solution.py:92
  830.1 250.5 %collective-permute-start = (bf16[512,2048]{1,0:T(8,128)(2,1)}, bf16[512,2048]{1,0:T(8,128)(2,1)}, u32[]{:S(2)}, u32[]{:S(2)}) collective-permute-start(bf16[512,2048]{1,0:T(8,128)(2,1)} %get-tuple-element.36), channel_id=1, source_target_pairs={{0,2},{1,3},{2,0},{3,1},{4,6},{5,7},{6,4},{7,5},{8,10},{9,11},{10,... | collective-permute-start | bytes 6291464 | tf_op jit(solution)/shard_map/ppermute | solution.py:10
  832.1 248.5 %copy-start.1 = (bf16[512,2048]{1,0:T(8,128)(2,1)S(1)}, bf16[512,2048]{1,0:T(8,128)(2,1)}, u32[]{:S(2)}) copy-start(bf16[512,2048]{1,0:T(8,128)(2,1)} %get-tuple-element.36) | copy-start | bytes 6291460
  1150.1 131.0 %copy-start.3 = (bf16[2,2,256,1]{0,1,3,2:T(2,128)(2,1)S(1)}, bf16[2,2,256,1]{0,1,3,2:T(2,128)(2,1)}, u32[]{:S(2)}) copy-start(bf16[2,2,256,1]{0,1,3,2:T(2,128)(2,1)} %copy-done.2) | copy-start | bytes 6148
  1150.1 131.0 %copy-start.5 = (f32[128,36]{0,1:T(8,128)S(1)}, f32[128,36]{0,1:T(8,128)}, u32[]{:S(2)}) copy-start(f32[128,36]{0,1:T(8,128)} %copy-done.4) | copy-start | bytes 55300
  1311.9 12.6 copy-start.9
  1311.9 12.6 copy-start.11
  1311.9 12.6 copy-start.15
  1311.9 12.6 copy-start.17
  1311.9 12.6 copy-start.19
  1311.9 12.6 copy-start.21
Sparse Core Ops, SparseCore 0:
  9.6 719.0 all-gather.1
  794.8 1180.1 reduce-scatter.1
where the time goes:
time: 1990 us; the launch traced here: 1980 us
  waiting for transfers between devices  1480 us (74%)
  matrix products  271 us (14%)
  local copies, waits for them, and re-layouts  87.9 us (4%)
  blocking collectives  81.8 us (4%)
  other arithmetic  29.8 us (1%)
    reduce_scatter x1, waiting for transfers between devices, shards(): lax.psum_scatter(lax.dot_general(columns, dpre_low, (((0,), (0,)), ((), (...  593 us
    all_gather x1, waiting for transfers between devices, shards(): lax.all_gather(weight, 'batch', axis=0, tiled=True)  490 us
    ppermute x3, waiting for transfers between devices, swapped(): return lax.ppermute(value, axis, pairs)  395 us
    dot_general x1, matrix products, shards(): jnp.einsum('anpc,snpc->asc', dmixed, pooled, precision=highest)  87.1 us
    psum x1, blocking collectives, shards(): alpha1_grad = lax.psum(first_local, ('batch', 'tower'))  43.3 us
  transfers between devices with their start and end apart: 7, of which 4 were waited for; matrix products, arithmetic and copies ran while one was open for 16% of the time, Pallas kernels for 0%

commit v1 on v0

v1 whole, which is shorter than its diff:
```python
import functools

import jax
import jax.numpy as jnp
from jax import lax
from jax.experimental import pallas as pl
from jax.experimental.pallas import tpu as pltpu
from jax.sharding import PartitionSpec as P

F32 = jnp.float32
BF16 = jnp.bfloat16
POOLED = 36
PITCH = 48
LANES = 128
VMEM_LIMIT = 56 * 1024 * 1024
CHUNKS = 4


def params():
    return pltpu.CompilerParams(vmem_limit_bytes=VMEM_LIMIT)


def flipped(value, axis, bit):
    pairs = [(source, source ^ bit) for source in range(lax.axis_size(axis))]
    return lax.ppermute(value, axis, pairs)


def x_swap(value):
    return flipped(value, "batch", 1)


def y_swap(value):
    return flipped(value, "tower", 2)


def c_swap(value):
    return flipped(value, "tower", 1)


def line(value, kind):
    steps = {
        "near": ((0, 1), (1, 0), (2, 3), (3, 2)),
        "middle": ((1, 2), (2, 1)),
        "outward": ((1, 0), (2, 3)),
        "inward": ((0, 1), (3, 2)),
    }[kind]
    pairs = [(2 * a + x, 2 * b + x) for a, b in steps for x in range(2)]
    return lax.ppermute(value, "batch", pairs)


def slab_groups():
    size = lax.axis_size("batch")
    return [list(range(x, size, 2)) for x in range(2)]


def is_line():
    return lax.axis_size("batch") == 8


def line_order(z):
    rows = jnp.array([[0, 1, 2, 3], [1, 0, 2, 3], [2, 3, 1, 0], [3, 2, 1, 0]])
    return rows[z]


def gather_rows(block):
    if not is_line():
        return [(lax.all_gather(block, "batch", axis=0, tiled=True, axis_index_groups=slab_groups()),)]
    near = line(block, "near")
    inner = line(block, "middle")
    passed = line(inner, "outward")
    outer = line(near, "middle")
    last = line(outer, "outward")
    return [(block,), (near,), (inner, passed), (outer, last)]


def scatter_rows(total):
    if not is_line():
        return lax.psum_scatter(total, "batch", scatter_dimension=0, tiled=True, axis_index_groups=slab_groups())
    own, near, inner, outer = jnp.split(total, 4, axis=0)
    from_end = line(outer.astype(BF16), "inward").astype(F32)
    crossed = line((outer + from_end).astype(BF16), "middle").astype(F32)
    from_end2 = line(inner.astype(BF16), "inward").astype(F32)
    mine = line((inner + from_end2).astype(BF16), "middle").astype(F32)
    last = line((near + crossed).astype(BF16), "near").astype(F32)
    return own + mine + last


def sum_slabs(value):
    if not is_line():
        return lax.psum(value, "batch", axis_index_groups=slab_groups())
    value = value + flipped(value, "batch", 2)
    return value + flipped(value, "batch", 4)


def sum_all(value):
    if not is_line():
        return lax.psum(value, ("batch", "tower"))
    value = value + c_swap(value)
    value = value + y_swap(value)
    value = value + x_swap(value)
    return sum_slabs(value)


def pool_table(order):
    map_pos = jnp.arange(169)[None, :]
    prow = (order // 6)[:, None]
    pcol = (order % 6)[:, None]
    qrow = map_pos // 13
    qcol = map_pos % 13
    inside = (
        (qrow >= 2 * prow) & (qrow <= 2 * prow + 2) & (qcol >= 2 * pcol) & (qcol <= 2 * pcol + 2)
    )
    small = (prow < 5) & (pcol < 5)
    table = jnp.stack([inside, inside & small]).astype(BF16)
    return jnp.pad(table, ((0, 0), (0, PITCH - POOLED), (0, 0)))


def pool_kernel(group, table, first, maps, own_out, other_out, pooled_out, own, other, pool0, pool1):
    count = maps.shape[0]
    base = pl.program_id(0) * count
    ch = maps.shape[3]

    def image(n, carry):
        window = table[group[base + n]]
        p0 = jnp.dot(window, maps[n, 0], preferred_element_type=F32) * (1.0 / 9.0)
        p1 = jnp.dot(window, maps[n, 1], preferred_element_type=F32) * (1.0 / 9.0)
        rows = pl.ds(pl.multiple_of(n * PITCH, PITCH), PITCH)
        mixed0 = first[0:1, :] * p0 + first[1:2, :] * p1
        mixed1 = first[2:3, :] * p0 + first[3:4, :] * p1
        for hold, value in ((pool0, p0), (pool1, p1), (own, mixed0), (other, mixed1)):
            for h in range(ch // LANES):
                hold[h, rows, :] = value[:, h * LANES : (h + 1) * LANES]
        return carry

    lax.fori_loop(0, count, image, 0, unroll=2)
    for p in range(POOLED):
        rows = pl.ds(p, count, stride=PITCH)
        for h in range(ch // LANES):
            lanes = slice(p * ch + h * LANES, p * ch + (h + 1) * LANES)
            own_out[:, lanes] = own[h, rows, :].astype(BF16)
            other_out[:, lanes] = other[h, rows, :].astype(BF16)
            pooled_out[0, :, lanes] = pool0[h, rows, :]
            pooled_out[1, :, lanes] = pool1[h, rows, :]


def pool(convmaps, group, table, first):
    count, _, places, ch = convmaps.shape
    nb = 16
    feats = POOLED * ch
    return pl.pallas_call(
        pool_kernel,
        grid_spec=pltpu.PrefetchScalarGridSpec(
            num_scalar_prefetch=1,
            grid=(count // nb,),
            in_specs=[
                pl.BlockSpec((2, PITCH, places), lambda i, g: (0, 0, 0)),
                pl.BlockSpec((4, ch), lambda i, g: (0, 0)),
                pl.BlockSpec((nb, 2, places, ch), lambda i, g: (i, 0, 0, 0)),
            ],
            out_specs=[
                pl.BlockSpec((nb, feats), lambda i, g: (i, 0)),
                pl.BlockSpec((nb, feats), lambda i, g: (i, 0)),
                pl.BlockSpec((2, nb, feats), lambda i, g: (0, i, 0)),
            ],
            scratch_shapes=[pltpu.VMEM((ch // LANES, nb * PITCH, LANES), F32)] * 4,
        ),
        out_shape=[
            jax.ShapeDtypeStruct((count, feats), BF16),
            jax.ShapeDtypeStruct((count, feats), BF16),
            jax.ShapeDtypeStruct((2, count, feats), F32),
        ],
        compiler_params=params(),
        cost_estimate=pl.CostEstimate(
            flops=2 * count * 2 * PITCH * places * ch, bytes_accessed=count * ch * 600, transcendentals=0
        ),
        name="pool",
    )(group, table, first, convmaps)


def first_grad_kernel(pooled, *refs):
    pieces = (len(refs) - 1) // 2
    out = refs[-1]
    ch = out.shape[2]

    @pl.when(pl.program_id(0) == 0)
    def _():
        out[...] = jnp.zeros_like(out)

    for a in range(2):
        sums = [0.0, 0.0]
        start = 0
        for ref in refs[a * pieces : (a + 1) * pieces]:
            for p in range(ref.shape[1] // ch):
                grad = ref[:, p * ch : (p + 1) * ch].astype(F32)
                lanes = slice(start + p * ch, start + (p + 1) * ch)
                for s in range(2):
                    sums[s] = sums[s] + grad * pooled[s, :, lanes]
            start += ref.shape[1]
        for s in range(2):
            out[2 * a + s] += sums[s]


def first_grad(pooled, own, other):
    count, feats = pooled.shape[1:]
    ch = feats // POOLED
    nb = 16
    specs = [pl.BlockSpec((nb, piece.shape[1]), lambda i: (i, 0)) for piece in own + other]
    sums = pl.pallas_call(
        first_grad_kernel,
        grid=(count // nb,),
        in_specs=[pl.BlockSpec((2, nb, feats), lambda i: (0, i, 0))] + specs,
        out_specs=pl.BlockSpec((4, nb, ch), lambda i: (0, 0, 0)),
        out_shape=jax.ShapeDtypeStruct((4, nb, ch), F32),
        compiler_params=params(),
        cost_estimate=pl.CostEstimate(
            flops=8 * count * feats, bytes_accessed=count * feats * 14, transcendentals=0
        ),
        name="first_grad",
    )(pooled, *own, *other)
    return jnp.sum(sums, axis=1)


def unpool_kernel(group, table, first, *refs):
    pieces = (len(refs) - 3) // 2
    out, own, other = refs[-3:]
    count = out.shape[0]
    base = pl.program_id(0) * count
    ch = out.shape[3]
    places = out.shape[2]

    @pl.when(pl.program_id(0) == 0)
    def _():
        own[...] = jnp.zeros_like(own)
        other[...] = jnp.zeros_like(other)

    for hold, parts in ((own, refs[:pieces]), (other, refs[pieces : 2 * pieces])):
        start = 0
        for ref in parts:
            for p in range(ref.shape[1] // ch):
                for h in range(ch // LANES):
                    lanes = slice(p * ch + h * LANES, p * ch + (h + 1) * LANES)
                    hold[h, pl.ds(start + p, count, stride=PITCH), :] = ref[:, lanes].astype(F32)
            start += ref.shape[1] // ch

    def image(n, carry):
        window = table[group[base + n]]
        rows = pl.ds(pl.multiple_of(n * PITCH, PITCH), PITCH)
        g0, g1 = (
            jnp.concatenate([hold[h, rows, :] for h in range(ch // LANES)], axis=1) for hold in (own, other)
        )
        for s in range(2):
            grad = (first[s : s + 1, :] * g0 + first[2 + s : 3 + s, :] * g1) * (1.0 / 9.0)
            high = grad.astype(BF16)
            low = (grad - high.astype(F32)).astype(BF16)
            both = jnp.concatenate([high, low], axis=0)
            spread = jnp.dot(window, both, preferred_element_type=F32)
            out[n, s] = spread[:places].astype(BF16)
        return carry

    lax.fori_loop(0, count, image, 0, unroll=2)


def unpool(own, other, group, table, first, places):
    count = own[0].shape[0]
    ch = first.shape[1]
    nb = 16
    specs = [pl.BlockSpec((nb, piece.shape[1]), lambda i, g: (i, 0)) for piece in own + other]
    spread = jnp.swapaxes(table, 1, 2)
    spread = jnp.pad(jnp.concatenate([spread, spread], axis=2), ((0, 0), (0, 176 - places), (0, 0)))
    return pl.pallas_call(
        unpool_kernel,
        grid_spec=pltpu.PrefetchScalarGridSpec(
            num_scalar_prefetch=1,
            grid=(count // nb,),
            in_specs=[
                pl.BlockSpec(spread.shape, lambda i, g: (0, 0, 0)),
                pl.BlockSpec((4, ch), lambda i, g: (0, 0)),
            ]
            + specs,
            out_specs=pl.BlockSpec((nb, 2, places, ch), lambda i, g: (i, 0, 0, 0)),
            scratch_shapes=[pltpu.VMEM((ch // LANES, nb * PITCH, LANES), F32)] * 2,
        ),
        out_shape=jax.ShapeDtypeStruct((count, 2, places, ch), BF16),
        compiler_params=params(),
        cost_estimate=pl.CostEstimate(
            flops=2 * count * 2 * 2 * PITCH * places * ch, bytes_accessed=count * ch * 700, transcendentals=0
        ),
        name="unpool",
    )(group, spread, first, *own, *other)


def tile_of(rows):
    return next(t for t in (1152, 768, 576, 512, 384, 256, 128) if rows % t == 0)


def forward_kernel(layout, tile, feats, vectors, cot_own, cot_other, *refs):
    terms = sum(layout)
    pieces = refs[:terms]
    act_out, dpre_out, sums_out, total, weight = refs[terms:]
    step = pl.program_id(0)
    per = pl.num_programs(0) // len(layout)
    at = 0
    for s, many in enumerate(layout):
        group = pieces[at : at + many]
        at += many

        @pl.when(step // per == s)
        def _(group=group):
            value = group[0][...]
            for extra in group[1:]:
                value = value + extra[...]
            weight[...] = value

    @pl.when(step == 0)
    def _():
        total[...] = jnp.zeros_like(total)

    total[...] += jnp.dot(feats[...], weight[...], preferred_element_type=F32)

    @pl.when(step == pl.num_programs(0) - 1)
    def _():
        bias, own_coef, other_coef = (vectors[i : i + 1, :] for i in range(3))
        c = 0.7978845608028654
        block = 64

        def rows_of(i, sums):
            rows = pl.ds(pl.multiple_of(i * block, block), block)
            x = total[rows, :] + bias
            x2 = x * x
            t = jnp.tanh(c * (x + 0.044715 * (x2 * x)))
            half = 0.5 * (1.0 + t)
            act = (x * half).astype(BF16)
            slope = half + (0.5 * c) * x * (1.0 - t * t) * (1.0 + (3.0 * 0.044715) * x2)
            k0 = cot_own[rows, :].astype(F32)
            k1 = cot_other[rows, :].astype(F32)
            dpre = ((own_coef * k0 + other_coef * k1) * slope).astype(BF16)
            act_out[rows, :] = act
            dpre_out[rows, :] = dpre
            actf = act.astype(F32)

            def fold(v):
                return jnp.sum(v.reshape(block // 8, 8, v.shape[1]), axis=0)

            return (
                sums[0] + fold(dpre.astype(F32)),
                sums[1] + fold(k0 * actf),
                sums[2] + fold(k1 * actf),
            )

        zero = jnp.zeros((8, total.shape[1]), F32)
        sums = lax.fori_loop(0, total.shape[0] // block, rows_of, (zero, zero, zero))
        for i in range(3):
            sums_out[i] = sums[i]


def forward(feats, pieces, vectors, cot_own, cot_other):
    rows, depth = feats.shape
    units = cot_own.shape[1]
    tile = tile_of(pieces[0][0].shape[0])
    per = pieces[0][0].shape[0] // tile
    steps = per * len(pieces)
    specs, terms = [], []
    for s, piece in enumerate(pieces):
        for term in piece:
            terms.append(term)
            specs.append(
                pl.BlockSpec((tile, units), lambda k, s=s: (jnp.clip(k - s * per, 0, per - 1), 0))
            )
    whole = pl.BlockSpec((rows, units), lambda k: (0, 0))
    return pl.pallas_call(
        functools.partial(forward_kernel, [len(p) for p in pieces], tile),
        grid=(steps,),
        in_specs=[
            pl.BlockSpec((rows, tile), lambda k: (0, k)),
            pl.BlockSpec((8, units), lambda k: (0, 0)),
            whole,
            whole,
        ]
        + specs,
        out_specs=[whole, whole, pl.BlockSpec((3, 8, units), lambda k: (0, 0, 0))],
        out_shape=[
            jax.ShapeDtypeStruct((rows, units), BF16),
            jax.ShapeDtypeStruct((rows, units), BF16),
            jax.ShapeDtypeStruct((3, 8, units), F32),
        ],
        scratch_shapes=[pltpu.VMEM((rows, units), F32), pltpu.VMEM((tile, units), BF16)],
        compiler_params=params(),
        cost_estimate=pl.CostEstimate(
            flops=2 * rows * depth * units, bytes_accessed=rows * depth * 2, transcendentals=rows * units
        ),
        name="forward",
    )(feats, vectors, cot_own, cot_other, *terms)


def back_kernel(layout, *refs):
    grads = refs[: len(layout)]
    keep_out, send_out, grad, weight = refs[-4:]
    units = grads[0].shape[1]
    at = len(layout)
    for j, many in enumerate(layout):
        value = refs[at][...]
        for extra in refs[at + 1 : at + many]:
            value = value + extra[...]
        weight[:, j * units : (j + 1) * units] = value
        at += many

    @pl.when(pl.program_id(0) == 0)
    def _():
        for j, ref in enumerate(grads):
            grad[:, j * units : (j + 1) * units] = ref[...]

    half = keep_out.shape[0]
    block = 256
    contract = (((1,), (1,)), ((), ()))

    def rows_of(i, carry):
        rows = pl.ds(pl.multiple_of(i * block, block), block)
        lower = pl.ds(pl.multiple_of(half + i * block, block), block)
        keep_out[rows, :] = lax.dot_general(grad[rows, :], weight[...], contract, preferred_element_type=F32)
        send_out[rows, :] = lax.dot_general(
            grad[lower, :], weight[...], contract, preferred_element_type=F32
        ).astype(BF16)
        return carry

    lax.fori_loop(0, half // block, rows_of, 0)


def back(grads, piece):
    rows, units = grads[0].shape
    depth = piece[0][0].shape[0]
    tile = tile_of(depth) if depth < 1152 else 384
    specs = [pl.BlockSpec((rows, units), lambda k: (0, 0)) for _ in grads]
    terms = [term for chunk in piece for term in chunk]
    specs += [pl.BlockSpec((tile, units), lambda k: (k, 0)) for _ in terms]
    half = pl.BlockSpec((rows // 2, tile), lambda k: (0, k))
    total = units * len(grads)
    return pl.pallas_call(
        functools.partial(back_kernel, [len(c) for c in piece]),
        grid=(depth // tile,),
        in_specs=specs,
        out_specs=[half, half],
        out_shape=[
            jax.ShapeDtypeStruct((rows // 2, depth), F32),
            jax.ShapeDtypeStruct((rows // 2, depth), BF16),
        ],
        scratch_shapes=[pltpu.VMEM((rows, total), BF16), pltpu.VMEM((tile, total), BF16)],
        compiler_params=params(),
        cost_estimate=pl.CostEstimate(
            flops=2 * rows * depth * total, bytes_accessed=rows * depth * 4, transcendentals=0
        ),
        name="back",
    )(*grads, *terms)


def either(flag, value, axis):
    return jnp.where(flag, jnp.flip(value, axis), value)


def shards(convmaps, group, alpha1, weight, bias, alpha2, cotangent):
    count, _, places, channels = convmaps.shape
    batch_id = lax.axis_index("batch")
    tower_id = lax.axis_index("tower")
    x = batch_id % 2
    z = batch_id // 2
    y = tower_id // 2
    core = tower_id % 2
    depth, width = weight.shape
    units = width // 2
    n = units // CHUNKS
    images = 8 * count
    mine, theirs = x * units, (1 - x) * units

    own_cols = lax.dynamic_slice_in_dim(weight, mine, units, 1)
    other_cols = lax.dynamic_slice_in_dim(weight, theirs, units, 1)
    chunks = []
    for j in range(CHUNKS):
        cols = slice(j * n, (j + 1) * n)
        a, b = own_cols[:, cols], x_swap(other_cols[:, cols])
        slab = jnp.where(x == 0, jnp.concatenate([a, b]), jnp.concatenate([b, a]))
        chunks.append(gather_rows(slab))

    cot = cotangent.reshape(2, 2, count, width)
    cot = either(core == 1, either(y == 1, cot, 0), 1).swapaxes(0, 1)
    cot_mine = lax.dynamic_slice_in_dim(cot, mine, units, 3)
    cot_theirs = lax.dynamic_slice_in_dim(cot, theirs, units, 3)
    cot_own = jnp.stack([cot_mine, x_swap(cot_theirs)], axis=1)
    cot_other = jnp.flip(y_swap(cot_own), 2).reshape(images, units)
    cot_own = cot_own.reshape(images, units)
    second = lax.dynamic_slice_in_dim(alpha2, mine, units, 1)
    own_coef = lax.dynamic_index_in_dim(second, y, 0, keepdims=True).astype(F32)
    cross = lax.dynamic_index_in_dim(second, 1 - y, 0, keepdims=True)
    cross_back = y_swap(cross).astype(F32)
    cross = cross.astype(F32)
    own_bias = lax.dynamic_slice_in_dim(bias, mine, units, 0)[None, :].astype(F32)
    vectors = jnp.concatenate([own_bias, own_coef, cross_back, jnp.zeros((5, units), F32)])

    order = jnp.arange(POOLED)
    if is_line():
        order = order.reshape(4, -1)[line_order(z)].reshape(-1)
    table = pool_table(order)
    first = alpha1.astype(F32)
    first = either(y == 1, first, 0).reshape(4, channels)
    kept, sent, pooled = pool(convmaps, group, table, first)
    arrived = y_swap(sent)
    blocks = [kept, arrived, x_swap(kept), x_swap(arrived)]
    blocks += [c_swap(block) for block in blocks]
    feats = jnp.concatenate(blocks)

    acts, grads, sums, stitched, crossed, owned = [], [], [], [], [], []
    weight_grad = jnp.zeros((depth, width), F32)
    for j in range(CHUNKS):
        cols = slice(j * n, (j + 1) * n)
        act, dpre, sums_j = forward(feats, chunks[j], vectors[:, cols], cot_own[:, cols], cot_other[:, cols])
        grads.append(dpre)
        sums.append(jnp.sum(sums_j, axis=1))
        total = lax.dot_general(feats, dpre, (((0,), (0,)), ((), ())), preferred_element_type=F32)
        slab = scatter_rows(total)
        stay = lax.dynamic_slice_in_dim(slab, x * depth, depth, 0)
        leave = lax.dynamic_slice_in_dim(slab, (1 - x) * depth, depth, 0)
        came = x_swap(leave.astype(BF16)).astype(F32)
        weight_grad = lax.dynamic_update_slice(weight_grad, stay, (0, mine + j * n))
        weight_grad = lax.dynamic_update_slice(weight_grad, came, (0, theirs + j * n))
        other_act = jnp.flip(y_swap(act).reshape(4, 2, count, n), 1).reshape(images, n)
        mix = (own_coef[:, cols] * act.astype(F32) + cross[:, cols] * other_act.astype(F32)).astype(BF16)
        mix = mix.reshape(2, 2, 2, count, n)
        stitched.append(mix[:, 0])
        crossed.append(x_swap(mix[:, 1]))

    left = jnp.concatenate(stitched, axis=3)
    right = jnp.concatenate(crossed, axis=3)
    rows = jnp.where(x == 0, jnp.concatenate([left, right], 3), jnp.concatenate([right, left], 3))
    rows = either(y == 1, either(core == 1, rows, 0), 1).swapaxes(0, 1)
    activations = rows.reshape(4 * count, width)

    sums = sum_slabs(jnp.concatenate(sums, axis=1))
    far = x_swap(sums)
    sums = jnp.where(x == 0, jnp.concatenate([sums, far], 1), jnp.concatenate([far, sums], 1))
    bias_grad = sums[0]
    other_second = y_swap(sums[2])
    alpha2_grad = either(y == 1, jnp.stack([sums[1], other_second]), 0)

    own_parts, other_parts = [], []
    for s in range(len(chunks[0])):
        keep, send = back(grads, [chunk[s] for chunk in chunks])
        part = keep + c_swap(send).astype(F32)
        keep, send = part[: 2 * count], part[2 * count :]
        part = keep + x_swap(send.astype(BF16)).astype(F32)
        own_parts.append(part[:count])
        other_parts.append(y_swap(part[count:].astype(BF16)))
    partial = first_grad(pooled, own_parts, other_parts)
    partial = either(y == 1, partial.reshape(2, 2, channels), 0)
    alpha1_grad = sum_all(partial)
    input_grad = unpool(own_parts, other_parts, group, table, first, places)
    return (activations, input_grad, weight_grad, bias_grad, alpha1_grad, alpha2_grad)


def solution(mesh):
    in_specs = (
        P(("batch", "tower"), None, None, None),
        P(("batch", "tower")),
        P(),
        P("batch", "tower"),
        P("tower"),
        P(None, "tower"),
        P("batch", "tower"),
    )
    out_specs = (
        P("batch", "tower"),
        P(("batch", "tower"), None, None, None),
        P("batch", "tower"),
        P("tower"),
        P(),
        P(None, "tower"),
    )
    return jax.shard_map(shards, mesh=mesh, in_specs=in_specs, out_specs=out_specs, check_vma=False)
```

time: 1990 us -> 1190 us (0.60)
  waiting for transfers between devices: 1480 us -> 512 us
  matrix products: 271 us -> 36.3 us
  starting transfers between devices: 18.9 us -> 218 us
  Pallas kernels: 0 us -> 175 us
  blocking collectives: 81.8 us -> 0 us
  local copies, waits for them, and re-layouts: 87.9 us -> 153 us
  other arithmetic: 29.8 us -> 85.4 us
    reduce_scatter x1 -> x0, waiting for transfers between devices: 593 us -> none  [shards(): lax.psum_scatter(lax.dot_general(columns, dpre_low, (((0,), (0,)), ((), (...]
    all_gather x1 -> x0, waiting for transfers between devices: 490 us -> none  [shards(): lax.all_gather(weight, 'batch', axis=0, tiled=True)]
    dot_general x8 -> x4, matrix products: 271 us -> 36.3 us  [shards(): lax.dot_general(feats, dpre, (((0,), (0,)), ((), ())), preferred_element_...]
    ppermute x3 -> x87, starting transfers between devices: 5.09 us -> 218 us  [the longest x40 178 us: line(): return lax.ppermute(value, 'batch', pairs)]
    pallas_call x0 -> x11, Pallas kernels: none -> 175 us  [the longest x4 65.9 us: forward(): pl.pallas_call(functools.partial(forward_kernel, [len(p) for p in pieces]...]
    ppermute x3 -> x87, waiting for transfers between devices: 395 us -> 512 us  [the longest x40 320 us: line(): return lax.ppermute(value, 'batch', pairs)]
    psum x2 -> x0, blocking collectives: 81.8 us -> none  [the longest x1 43.3 us: shards(): alpha1_grad = lax.psum(first_local, ('batch', 'tower'))]
    unnamed x49 -> x163, local copies, waits for them, and re-layouts: 33.4 us -> 85.9 us
  transfers between devices with their start and end apart: 7 -> 87, of which waited for: 4 -> 40; matrix products, arithmetic and copies ran while one was open for 16% -> 20% of each run, Pallas kernels for 0% -> 12%
where the time goes in v1:
time: 1190 us; the launch traced here: 1180 us
  waiting for transfers between devices  512 us (43%)
  starting transfers between devices  218 us (18%)
  Pallas kernels  175 us (15%)
  local copies, waits for them, and re-layouts  153 us (13%)
  other arithmetic  85.4 us (7%)
  matrix products  36.3 us (3%)
    ppermute x40, waiting for transfers between devices, line(): return lax.ppermute(value, 'batch', pairs)  320 us
    ppermute x47, waiting for transfers between devices, flipped(): return lax.ppermute(value, axis, pairs)  193 us
    ppermute x40, starting transfers between devices, line(): return lax.ppermute(value, 'batch', pairs)  178 us
    unnamed x163, local copies, waits for them, and re-layouts  85.9 us
    pallas_call x4, Pallas kernels, forward(): pl.pallas_call(functools.partial(forward_kernel, [len(p) for p in pieces]...  65.9 us
    pallas_call x4, Pallas kernels, back(): pl.pallas_call(functools.partial(back_kernel, [len(c) for c in piece]), g...  53.5 us
    ppermute x47, starting transfers between devices, flipped(): return lax.ppermute(value, axis, pairs)  40 us
    dot_general x4, matrix products, shards(): lax.dot_general(feats, dpre, (((0,), (0,)), ((), ())), preferred_element_...  36.3 us
  transfers between devices with their start and end apart: 87, of which 40 were waited for; matrix products, arithmetic and copies ran while one was open for 20% of the time, Pallas kernels for 12%

profile of v1, /device:TPU:0, one launch (start us, length us, event | category | flops | bytes accessed | tf_op | source)
XLA Modules:
  0.0 1181.9 jit_solution(7363382059431296679)
XLA Ops:
  4.6 23.1 %copy.30.maps = bf16[128,2,169,256]{3,2,1,0:T(8,128)(2,1)} copy(bf16[128,2,169,256]{3,1,2,0:T(2,128)(2,1)} %param.8) | data formatting | bytes 44302336 | tf_op args[0]
  27.7 22.5 %pool.1 = (bf16[128,9216]{1,0:T(8,128)(2,1)}, bf16[128,9216]{1,0:T(8,128)(2,1)}, f32[2,128,9216]{2,1,0:T(8,128)}) custom-call(s32[128]{0:T(128)} %group.3, bf16[2,48,169]{2,1,0:T(8,128)(2,1)} %copy.29.table, f32[4,256]{1,0:T(4,128)} %reshape.568.first, bf16[128,2,169,256]{3,2,1,0:T(8,128)(2,1)} %copy.30.maps), custom_call_target="tpu_custom_call" | custom-call | flops 1063256064 | bytes 19660800 | tf_op jit(solution)/shard_map/pool/pallas_call | solution.py:150
  88.0 16.8 %collective-permute-done.7 = bf16[1,1024]{1,0:T(2,128)(2,1)S(1)} collective-permute-done((bf16[1,1024]{1,0:T(2,128)(2,1)S(1)}, bf16[1,1024]{1,0:T(2,128)(2,1)S(1)}, u32[]{:S(2)}, u32[]{:S(2)}) %collective-permute-start.7) | collective-permute-done | bytes 2080 | tf_op jit(solution)/shard_map/ppermute | solution.py:25
  106.6 14.6 %collective-permute-done.17 = bf16[1152,256]{1,0:T(8,128)(2,1)} collective-permute-done((bf16[1152,256]{1,0:T(8,128)(2,1)}, bf16[1152,256]{1,0:T(8,128)(2,1)}, u32[]{:S(2)}, u32[]{:S(2)}) %collective-permute-start.17) | collective-permute-done | bytes 589856 | tf_op jit(solution)/shard_map/ppermute | solution.py:25
  167.0 17.2 %collective-permute-done.18.refs_1_.refs_5_ = bf16[2304,256]{1,0:T(8,128)(2,1)} collective-permute-done((bf16[2304,256]{1,0:T(8,128)(2,1)}, bf16[2304,256]{1,0:T(8,128)(2,1)}, u32[]{:S(2)}, u32[]{:S(2)}) %collective-permute-start.18) | collective-permute-done | bytes 1179680 | tf_op jit(solution)/shard_map/ppermute | solution.py:48
  213.0 28.0 %collective-permute-done.2 = bf16[128,9216]{1,0:T(8,128)(2,1)} collective-permute-done((bf16[128,9216]{1,0:T(8,128)(2,1)}, bf16[128,9216]{1,0:T(8,128)(2,1)}, u32[]{:S(2)}, u32[]{:S(2)}) %collective-permute-start.2) | collective-permute-done | bytes 2359328 | tf_op jit(solution)/shard_map/ppermute | solution.py:25
  261.5 29.8 %collective-permute-done.27.refs_3_.refs_9_ = bf16[2304,256]{1,0:T(8,128)(2,1)S(1)} collective-permute-done((bf16[2304,256]{1,0:T(8,128)(2,1)S(1)}, bf16[2304,256]{1,0:T(8,128)(2,1)S(1)}, u32[]{:S(2)}, u32[]{:S(2)}) %collective-permute-start.27) | collective-permute-done | bytes 1179680 | tf_op jit(solution)/shard_map/ppermute | solution.py:48
  298.1 18.5 %collective-permute-done.36.refs_5_.refs_11_ = bf16[2304,256]{1,0:T(8,128)(2,1)S(1)} collective-permute-done((bf16[2304,256]{1,0:T(8,128)(2,1)S(1)}, bf16[2304,256]{1,0:T(8,128)(2,1)S(1)}, u32[]{:S(2)}, u32[]{:S(2)}) %collective-permute-start.36) | collective-permute-done | bytes 1179680 | tf_op jit(solution)/shard_map/ppermute | solution.py:48
  318.3 16.5 %forward.7 = (bf16[1024,256]{1,0:T(8,128)(2,1)}, bf16[1024,256]{1,0:T(8,128)(2,1)}, f32[3,8,256]{2,1,0:T(8,128)}) custom-call(bf16[1024,9216]{1,0:T(8,128)(2,1)} %constant_dynamic-update-slice_fusion.feats, f32[8,256]{1,0:T(8,128)} %get-tuple-element.124.vectors, bf16[1024,256]{1,0:T(8,128)(2,1)} %get-tuple-element.97.cot_own, ...), custom_call_target="tpu_custom_call" | custom-call | flops 4831838208 | bytes 18874368 | tf_op jit(solution)/shard_map/forward/pallas_call | solution.py:370
  335.6 31.7 %collective-permute-done.29.refs_5_.refs_9_ = bf16[2304,256]{1,0:T(8,128)(2,1)} collective-permute-done((bf16[2304,256]{1,0:T(8,128)(2,1)S(1)}, bf16[2304,256]{1,0:T(8,128)(2,1)}, u32[]{:S(2)}, u32[]{:S(2)}) %collective-permute-start.29) | collective-permute-done | bytes 1179680 | tf_op jit(solution)/shard_map/ppermute | solution.py:48
  367.2 16.5 %forward.6 = (bf16[1024,256]{1,0:T(8,128)(2,1)}, bf16[1024,256]{1,0:T(8,128)(2,1)}, f32[3,8,256]{2,1,0:T(8,128)}) custom-call(bf16[1024,9216]{1,0:T(8,128)(2,1)} %constant_dynamic-update-slice_fusion.feats, f32[8,256]{1,0:T(8,128)} %get-tuple-element.125.vectors, bf16[1024,256]{1,0:T(8,128)(2,1)} %get-tuple-element.98.cot_own, ...), custom_call_target="tpu_custom_call" | custom-call | flops 4831838208 | bytes 18874368 | tf_op jit(solution)/shard_map/forward/pallas_call | solution.py:370
  392.5 16.4 %forward.5 = (bf16[1024,256]{1,0:T(8,128)(2,1)}, bf16[1024,256]{1,0:T(8,128)(2,1)}, f32[3,8,256]{2,1,0:T(8,128)}) custom-call(bf16[1024,9216]{1,0:T(8,128)(2,1)} %constant_dynamic-update-slice_fusion.feats, f32[8,256]{1,0:T(8,128)} %get-tuple-element.126.vectors, bf16[1024,256]{1,0:T(8,128)(2,1)} %get-tuple-element.99.cot_own, ...), custom_call_target="tpu_custom_call" | custom-call | flops 4831838208 | bytes 18874368 | tf_op jit(solution)/shard_map/forward/pallas_call | solution.py:370
  417.7 24.8 %collective-permute-done.15.refs_5_ = bf16[2304,256]{1,0:T(8,128)(2,1)} collective-permute-done((bf16[2304,256]{1,0:T(8,128)(2,1)}, bf16[2304,256]{1,0:T(8,128)(2,1)}, u32[]{:S(2)}, u32[]{:S(2)}) %collective-permute-start.15) | collective-permute-done | bytes 1179680 | tf_op jit(solution)/shard_map/ppermute | solution.py:48
  442.5 16.5 %forward.4 = (bf16[1024,256]{1,0:T(8,128)(2,1)}, bf16[1024,256]{1,0:T(8,128)(2,1)}, f32[3,8,256]{2,1,0:T(8,128)}) custom-call(bf16[1024,9216]{1,0:T(8,128)(2,1)} %constant_dynamic-update-slice_fusion.feats, f32[8,256]{1,0:T(8,128)} %get-tuple-element.127.vectors, bf16[1024,256]{1,0:T(8,128)(2,1)} %get-tuple-element.100.cot_own, ...), custom_call_target="tpu_custom_call" | custom-call | flops 4831838208 | bytes 18874368 | tf_op jit(solution)/shard_map/forward/pallas_call | solution.py:370
  519.8 12.8 %back.4 = (f32[512,2304]{1,0:T(8,128)}, bf16[512,2304]{1,0:T(8,128)(2,1)}) custom-call(bf16[1024,256]{1,0:T(8,128)(2,1)} %get-tuple-element.35.refs_0_, bf16[1024,256]{1,0:T(8,128)(2,1)} %get-tuple-element.36.refs_1_, bf16[1024,256]{1,0:T(8,128)(2,1)} %get-tuple-element.37.refs_2_, bf16[1024,256]{1,0:T(8,128)(2,1)} %get-tuple-element.38.refs_3_, ...), custom_call_target="tpu_custom_call" | custom-call | flops 4831838208 | bytes 9437184 | tf_op jit(solution)/shard_map/back/pallas_call | solution.py:437
  532.7 13.9 %back.7 = (f32[512,2304]{1,0:T(8,128)}, bf16[512,2304]{1,0:T(8,128)(2,1)}) custom-call(bf16[1024,256]{1,0:T(8,128)(2,1)} %get-tuple-element.35.refs_0_, bf16[1024,256]{1,0:T(8,128)(2,1)} %get-tuple-element.36.refs_1_, bf16[1024,256]{1,0:T(8,128)(2,1)} %get-tuple-element.37.refs_2_, bf16[1024,256]{1,0:T(8,128)(2,1)} %get-tuple-element.38.refs_3_, ...), custom_call_target="tpu_custom_call" | custom-call | flops 4831838208 | bytes 9437184 | tf_op jit(solution)/shard_map/back/pallas_call | solution.py:437
  550.3 14.0 %back.6 = (f32[512,2304]{1,0:T(8,128)}, bf16[512,2304]{1,0:T(8,128)(2,1)}) custom-call(bf16[1024,256]{1,0:T(8,128)(2,1)} %get-tuple-element.35.refs_0_, bf16[1024,256]{1,0:T(8,128)(2,1)} %get-tuple-element.36.refs_1_, bf16[1024,256]{1,0:T(8,128)(2,1)} %get-tuple-element.37.refs_2_, bf16[1024,256]{1,0:T(8,128)(2,1)} %get-tuple-element.38.refs_3_, ...), custom_call_target="tpu_custom_call" | custom-call | flops 4831838208 | bytes 9437184 | tf_op jit(solution)/shard_map/back/pallas_call | solution.py:437
  565.5 12.8 %back.5 = (f32[512,2304]{1,0:T(8,128)}, bf16[512,2304]{1,0:T(8,128)(2,1)}) custom-call(bf16[1024,256]{1,0:T(8,128)(2,1)} %get-tuple-element.35.refs_0_, bf16[1024,256]{1,0:T(8,128)(2,1)} %get-tuple-element.36.refs_1_, bf16[1024,256]{1,0:T(8,128)(2,1)} %get-tuple-element.37.refs_2_, bf16[1024,256]{1,0:T(8,128)(2,1)} %get-tuple-element.38.refs_3_, ...), custom_call_target="tpu_custom_call" | custom-call | flops 4831838208 | bytes 9437184 | tf_op jit(solution)/shard_map/back/pallas_call | solution.py:437
  653.3 16.0 %collective-permute-done.66 = bf16[2304,256]{1,0:T(8,128)(2,1)S(1)} collective-permute-done((bf16[2304,256]{1,0:T(8,128)(2,1)}, bf16[2304,256]{1,0:T(8,128)(2,1)S(1)}, u32[]{:S(2)}, u32[]{:S(2)}) %collective-permute-start.66) | collective-permute-done | bytes 1179680 | tf_op jit(solution)/shard_map/ppermute | solution.py:48
  674.6 20.0 %collective-permute-done.68 = bf16[2304,256]{1,0:T(8,128)(2,1)S(1)} collective-permute-done((bf16[2304,256]{1,0:T(8,128)(2,1)}, bf16[2304,256]{1,0:T(8,128)(2,1)S(1)}, u32[]{:S(2)}, u32[]{:S(2)}) %collective-permute-start.68) | collective-permute-done | bytes 1179680 | tf_op jit(solution)/shard_map/ppermute | solution.py:48
  702.4 17.5 %collective-permute-done.60 = bf16[2304,256]{1,0:T(8,128)(2,1)} collective-permute-done((bf16[2304,256]{1,0:T(8,128)(2,1)}, bf16[2304,256]{1,0:T(8,128)(2,1)}, u32[]{:S(2)}, u32[]{:S(2)}) %collective-permute-start.60) | collective-permute-done | bytes 1179680 | tf_op jit(solution)/shard_map/ppermute | solution.py:48
  719.9 25.3 %collective-permute-done.62 = bf16[2304,256]{1,0:T(8,128)(2,1)} collective-permute-done((bf16[2304,256]{1,0:T(8,128)(2,1)}, bf16[2304,256]{1,0:T(8,128)(2,1)}, u32[]{:S(2)}, u32[]{:S(2)}) %collective-permute-start.62) | collective-permute-done | bytes 1179680 | tf_op jit(solution)/shard_map/ppermute | solution.py:48
  750.6 19.9 %collective-permute-done.54 = bf16[2304,256]{1,0:T(8,128)(2,1)} collective-permute-done((bf16[2304,256]{1,0:T(8,128)(2,1)}, bf16[2304,256]{1,0:T(8,128)(2,1)}, u32[]{:S(2)}, u32[]{:S(2)}) %collective-permute-start.54) | collective-permute-done | bytes 1179680 | tf_op jit(solution)/shard_map/ppermute | solution.py:48
  770.5 21.4 %collective-permute-done.56 = bf16[2304,256]{1,0:T(8,128)(2,1)} collective-permute-done((bf16[2304,256]{1,0:T(8,128)(2,1)}, bf16[2304,256]{1,0:T(8,128)(2,1)}, u32[]{:S(2)}, u32[]{:S(2)}) %collective-permute-start.56) | collective-permute-done | bytes 1179680 | tf_op jit(solution)/shard_map/ppermute | solution.py:48
  824.6 67.4 %collective-permute-start.58 = (bf16[2304,256]{1,0:T(8,128)(2,1)}, bf16[2304,256]{1,0:T(8,128)(2,1)}, u32[]{:S(2)}, u32[]{:S(2)}) collective-permute-start(bf16[2304,256]{1,0:T(8,128)(2,1)} %fusion.6), channel_id=1, source_target_pairs={{0,8},{4,12},{8,0},{12,4},{16,24},{20,28},{24,16},{28,20},{1,9},{5... | collective-permute-start | bytes 3538952 | tf_op jit(solution)/shard_map/ppermute | solution.py:48
  919.2 31.3 %collective-permute-start.70 = (bf16[2304,256]{1,0:T(8,128)(2,1)S(1)}, bf16[2304,256]{1,0:T(8,128)(2,1)S(1)}, u32[]{:S(2)}, u32[]{:S(2)}) collective-permute-start(bf16[2304,256]{1,0:T(8,128)(2,1)S(1)} %copy-done.33), channel_id=1, source_target_pairs={{0,8},{4,12},{8,0},{12,4},{16,24},{20,28},{24,16},{28,20},{1,9},{5... | collective-permute-start | bytes 3538952 | tf_op jit(solution)/shard_map/ppermute | solution.py:48
  958.9 18.5 %collective-permute-done.70 = bf16[2304,256]{1,0:T(8,128)(2,1)S(1)} collective-permute-done((bf16[2304,256]{1,0:T(8,128)(2,1)S(1)}, bf16[2304,256]{1,0:T(8,128)(2,1)S(1)}, u32[]{:S(2)}, u32[]{:S(2)}) %collective-permute-start.70) | collective-permute-done | bytes 1179680 | tf_op jit(solution)/shard_map/ppermute | solution.py:48
  980.7 14.6 %collective-permute-done.76 = bf16[2304,256]{1,0:T(8,128)(2,1)S(1)} collective-permute-done((bf16[2304,256]{1,0:T(8,128)(2,1)S(1)}, bf16[2304,256]{1,0:T(8,128)(2,1)S(1)}, u32[]{:S(2)}, u32[]{:S(2)}) %collective-permute-start.76) | collective-permute-done | bytes 1179680 | tf_op jit(solution)/shard_map/ppermute | solution.py:48
  1011.8 22.7 %collective-permute-done.45 = bf16[256,2304]{1,0:T(8,128)(2,1)S(1)} collective-permute-done((bf16[256,2304]{1,0:T(8,128)(2,1)}, bf16[256,2304]{1,0:T(8,128)(2,1)S(1)}, u32[]{:S(2)}, u32[]{:S(2)}) %collective-permute-start.45) | collective-permute-done | bytes 1179680 | tf_op jit(solution)/shard_map/ppermute | solution.py:25
  1035.9 23.9 %collective-permute-done.43 = bf16[256,2304]{1,0:T(8,128)(2,1)S(1)} collective-permute-done((bf16[256,2304]{1,0:T(8,128)(2,1)}, bf16[256,2304]{1,0:T(8,128)(2,1)S(1)}, u32[]{:S(2)}, u32[]{:S(2)}) %collective-permute-start.43) | collective-permute-done | bytes 1179680 | tf_op jit(solution)/shard_map/ppermute | solution.py:25
  1124.1 24.4 %unpool.1 = bf16[128,2,169,256]{3,2,1,0:T(8,128)(2,1)} custom-call(s32[128]{0:T(128)} %group.3, bf16[2,176,96]{2,1,0:T(8,128)(2,1)} %fusion.26.table, f32[4,256]{1,0:T(4,128)} %reshape.568.first, f32[128,2304]{1,0:T(8,128)} %slice.260.refs_0_, f32[128,2304]{1,0:T(8,128)} %slice.263.refs_1_, f32[128,2304]{1,0:T(8,128)} %slice.266.refs_2_, ...), custom_call_target="tpu_custom_call" | custom-call | flops 2126512128 | bytes 22937600 | tf_op jit(solution)/shard_map/unpool/pallas_call | solution.py:270
  1148.6 32.3 %copy.42 = bf16[128,2,169,256]{3,1,2,0:T(2,128)(2,1)} copy(bf16[128,2,169,256]{3,2,1,0:T(8,128)(2,1)} %unpool.1) | data formatting | bytes 44302336
  (456 shorter events, 477.9 us)
Async XLA Ops:
  50.2 135.6 %collective-permute-start = (bf16[128,9216]{1,0:T(8,128)(2,1)}, bf16[128,9216]{1,0:T(8,128)(2,1)}, u32[]{:S(2)}, u32[]{:S(2)}) collective-permute-start(bf16[128,9216]{1,0:T(8,128)(2,1)} %get-tuple-element.30), channel_id=1, source_target_pairs={{0,2},{1,3},{2,0},{3,1},{4,6},{5,7},{6,4},{7,5},{8,10},{9,11},{10,... | collective-permute-start | bytes 7077896 | tf_op jit(solution)/shard_map/ppermute | solution.py:25
  63.5 75.1 %collective-permute-start.8 = (bf16[2,2,128,1024]{3,2,1,0:T(8,128)(2,1)}, bf16[2,2,128,1024]{3,2,1,0:T(8,128)(2,1)}, u32[]{:S(2)}, u32[]{:S(2)}) collective-permute-start(bf16[2,2,128,1024]{3,2,1,0:T(8,128)(2,1)} %get-tuple-element.102), channel_id=1, source_target_pairs={{0,4},{4,0},{8,12},{12,8},{16,20},{20,16},{24,28},{28,24},{1,5},{5... | collective-permute-start | bytes 3145736 | tf_op jit(solution)/shard_map/ppermute | solution.py:25
  65.0 56.2 %collective-permute-start.17 = (bf16[1152,256]{1,0:T(8,128)(2,1)}, bf16[1152,256]{1,0:T(8,128)(2,1)}, u32[]{:S(2)}, u32[]{:S(2)}) collective-permute-start(bf16[1152,256]{1,0:T(8,128)(2,1)} %get-tuple-element.88), channel_id=1, source_target_pairs={{0,4},{4,0},{8,12},{12,8},{16,20},{20,16},{24,28},{28,24},{1,5},{5... | collective-permute-start | bytes 1769480 | tf_op jit(solution)/shard_map/ppermute | solution.py:25
  73.3 59.0 %collective-permute-start.10 = (bf16[1152,256]{1,0:T(8,128)(2,1)}, bf16[1152,256]{1,0:T(8,128)(2,1)}, u32[]{:S(2)}, u32[]{:S(2)}) collective-permute-start(bf16[1152,256]{1,0:T(8,128)(2,1)} %get-tuple-element.90), channel_id=1, source_target_pairs={{0,4},{4,0},{8,12},{12,8},{16,20},{20,16},{24,28},{28,24},{1,5},{5... | collective-permute-start | bytes 1769480 | tf_op jit(solution)/shard_map/ppermute | solution.py:25
  185.8 55.3 %collective-permute-start.2 = (bf16[128,9216]{1,0:T(8,128)(2,1)}, bf16[128,9216]{1,0:T(8,128)(2,1)}, u32[]{:S(2)}, u32[]{:S(2)}) collective-permute-start(bf16[128,9216]{1,0:T(8,128)(2,1)} %collective-permute-done), channel_id=1, source_target_pairs={{0,4},{4,0},{8,12},{12,8},{16,20},{20,16},{24,28},{28,24},{1,5},{5... | collective-permute-start | bytes 7077896 | tf_op jit(solution)/shard_map/ppermute | solution.py:25
  258.7 57.9 %collective-permute-start.36 = (bf16[2304,256]{1,0:T(8,128)(2,1)S(1)}, bf16[2304,256]{1,0:T(8,128)(2,1)S(1)}, u32[]{:S(2)}, u32[]{:S(2)}) collective-permute-start(bf16[2304,256]{1,0:T(8,128)(2,1)S(1)} %collective-permute-done.35.refs_4_.refs_10_), channel_id=1, source_target_pairs={{8,0},{12,4},{16,24},{20,28},{9,1},{13,5},{17,25},{21,29},{10,2},{... | collective-permute-start | bytes 3538952 | tf_op jit(solution)/shard_map/ppermute | solution.py:48
  291.3 93.2 %collective-permute-start.20 = (bf16[2304,256]{1,0:T(8,128)(2,1)}, bf16[2304,256]{1,0:T(8,128)(2,1)S(1)}, u32[]{:S(2)}, u32[]{:S(2)}) collective-permute-start(bf16[2304,256]{1,0:T(8,128)(2,1)} %collective-permute-done.19.refs_2_.refs_6_), channel_id=1, source_target_pairs={{8,0},{12,4},{16,24},{20,28},{9,1},{13,5},{17,25},{21,29},{10,2},{... | collective-permute-start | bytes 3538952 | tf_op jit(solution)/shard_map/ppermute | solution.py:48
  292.6 74.6 %collective-permute-start.29 = (bf16[2304,256]{1,0:T(8,128)(2,1)S(1)}, bf16[2304,256]{1,0:T(8,128)(2,1)}, u32[]{:S(2)}, u32[]{:S(2)}) collective-permute-start(bf16[2304,256]{1,0:T(8,128)(2,1)S(1)} %collective-permute-done.28.refs_4_.refs_8_), channel_id=1, source_target_pairs={{8,0},{12,4},{16,24},{20,28},{9,1},{13,5},{17,25},{21,29},{10,2},{... | collective-permute-start | bytes 3538952 | tf_op jit(solution)/shard_map/ppermute | solution.py:48
  293.9 98.6 %collective-permute-start.22 = (bf16[2304,256]{1,0:T(8,128)(2,1)}, bf16[2304,256]{1,0:T(8,128)(2,1)}, u32[]{:S(2)}, u32[]{:S(2)}) collective-permute-start(bf16[2304,256]{1,0:T(8,128)(2,1)} %collective-permute-done.21.refs_4_.refs_6_), channel_id=1, source_target_pairs={{8,0},{12,4},{16,24},{20,28},{9,1},{13,5},{17,25},{21,29},{10,2},{... | collective-permute-start | bytes 3538952 | tf_op jit(solution)/shard_map/ppermute | solution.py:48
  296.8 120.9 %collective-permute-start.13 = (bf16[2304,256]{1,0:T(8,128)(2,1)}, bf16[2304,256]{1,0:T(8,128)(2,1)S(1)}, u32[]{:S(2)}, u32[]{:S(2)}) collective-permute-start(bf16[2304,256]{1,0:T(8,128)(2,1)} %collective-permute-done.12.refs_2_.refs_4_), channel_id=1, source_target_pairs={{8,0},{12,4},{16,24},{20,28},{9,1},{13,5},{17,25},{21,29},{10,2},{... | collective-permute-start | bytes 3538952 | tf_op jit(solution)/shard_map/ppermute | solution.py:48
  316.6 125.9 %collective-permute-start.15 = (bf16[2304,256]{1,0:T(8,128)(2,1)}, bf16[2304,256]{1,0:T(8,128)(2,1)}, u32[]{:S(2)}, u32[]{:S(2)}) collective-permute-start(bf16[2304,256]{1,0:T(8,128)(2,1)} %collective-permute-done.14.refs_4_), channel_id=1, source_target_pairs={{8,0},{12,4},{16,24},{20,28},{9,1},{13,5},{17,25},{21,29},{10,2},{... | collective-permute-start | bytes 3538952 | tf_op jit(solution)/shard_map/ppermute | solution.py:48
  459.8 72.8 %collective-permute-start.78 = (f32[3,1024]{1,0:T(4,128)S(1)}, f32[3,1024]{1,0:T(4,128)S(1)}, u32[]{:S(2)}, u32[]{:S(2)}) collective-permute-start(f32[3,1024]{1,0:T(4,128)S(1)} %pad_maximum_fusion.1), channel_id=1, source_target_pairs={{0,8},{4,12},{8,0},{12,4},{16,24},{20,28},{24,16},{28,20},{1,9},{5... | collective-permute-start | bytes 36872 | tf_op jit(solution)/shard_map/ppermute | solution.py:25
  474.1 154.6 %collective-permute-start.72 = (bf16[2304,256]{1,0:T(8,128)(2,1)}, bf16[2304,256]{1,0:T(8,128)(2,1)}, u32[]{:S(2)}, u32[]{:S(2)}) collective-permute-start(bf16[2304,256]{1,0:T(8,128)(2,1)} %get-tuple-element.71), channel_id=1, source_target_pairs={{0,8},{4,12},{24,16},{28,20},{1,9},{5,13},{25,17},{29,21},{2,10},{... | collective-permute-start | bytes 3538952 | tf_op jit(solution)/shard_map/ppermute | solution.py:48
  546.6 265.1 %collective-permute-start.48 = (bf16[512,2304]{1,0:T(8,128)(2,1)}, bf16[512,2304]{1,0:T(8,128)(2,1)S(1)}, u32[]{:S(2)}, u32[]{:S(2)}) collective-permute-start(bf16[512,2304]{1,0:T(8,128)(2,1)} %get-tuple-element.46), channel_id=1, source_target_pairs={{0,1},{1,0},{2,3},{3,2},{4,5},{5,4},{6,7},{7,6},{8,9},{9,8},{10,11... | collective-permute-start | bytes 7077896 | tf_op jit(solution)/shard_map/ppermute | solution.py:25
  622.0 72.6 %collective-permute-start.68 = (bf16[2304,256]{1,0:T(8,128)(2,1)}, bf16[2304,256]{1,0:T(8,128)(2,1)S(1)}, u32[]{:S(2)}, u32[]{:S(2)}) collective-permute-start(bf16[2304,256]{1,0:T(8,128)(2,1)} %get-tuple-element.76), channel_id=1, source_target_pairs={{0,8},{4,12},{24,16},{28,20},{1,9},{5,13},{25,17},{29,21},{2,10},{... | collective-permute-start | bytes 3538952 | tf_op jit(solution)/shard_map/ppermute | solution.py:48
  628.8 91.1 %collective-permute-start.60 = (bf16[2304,256]{1,0:T(8,128)(2,1)}, bf16[2304,256]{1,0:T(8,128)(2,1)}, u32[]{:S(2)}, u32[]{:S(2)}) collective-permute-start(bf16[2304,256]{1,0:T(8,128)(2,1)} %get-tuple-element.79), channel_id=1, source_target_pairs={{0,8},{4,12},{24,16},{28,20},{1,9},{5,13},{25,17},{29,21},{2,10},{... | collective-permute-start | bytes 3538952 | tf_op jit(solution)/shard_map/ppermute | solution.py:48
  644.0 101.2 %collective-permute-start.62 = (bf16[2304,256]{1,0:T(8,128)(2,1)}, bf16[2304,256]{1,0:T(8,128)(2,1)}, u32[]{:S(2)}, u32[]{:S(2)}) collective-permute-start(bf16[2304,256]{1,0:T(8,128)(2,1)} %get-tuple-element.80), channel_id=1, source_target_pairs={{0,8},{4,12},{24,16},{28,20},{1,9},{5,13},{25,17},{29,21},{2,10},{... | collective-permute-start | bytes 3538952 | tf_op jit(solution)/shard_map/ppermute | solution.py:48
  669.3 101.1 %collective-permute-start.54 = (bf16[2304,256]{1,0:T(8,128)(2,1)}, bf16[2304,256]{1,0:T(8,128)(2,1)}, u32[]{:S(2)}, u32[]{:S(2)}) collective-permute-start(bf16[2304,256]{1,0:T(8,128)(2,1)} %get-tuple-element.83), channel_id=1, source_target_pairs={{0,8},{4,12},{24,16},{28,20},{1,9},{5,13},{25,17},{29,21},{2,10},{... | collective-permute-start | bytes 3538952 | tf_op jit(solution)/shard_map/ppermute | solution.py:48
  694.6 97.3 %collective-permute-start.56 = (bf16[2304,256]{1,0:T(8,128)(2,1)}, bf16[2304,256]{1,0:T(8,128)(2,1)}, u32[]{:S(2)}, u32[]{:S(2)}) collective-permute-start(bf16[2304,256]{1,0:T(8,128)(2,1)} %get-tuple-element.84), channel_id=1, source_target_pairs={{0,8},{4,12},{24,16},{28,20},{1,9},{5,13},{25,17},{29,21},{2,10},{... | collective-permute-start | bytes 3538952 | tf_op jit(solution)/shard_map/ppermute | solution.py:48
  719.9 97.1 %collective-permute-start.46 = (bf16[512,2304]{1,0:T(8,128)(2,1)}, bf16[512,2304]{1,0:T(8,128)(2,1)}, u32[]{:S(2)}, u32[]{:S(2)}) collective-permute-start(bf16[512,2304]{1,0:T(8,128)(2,1)} %get-tuple-element.44), channel_id=1, source_target_pairs={{0,1},{1,0},{2,3},{3,2},{4,5},{5,4},{6,7},{7,6},{8,9},{9,8},{10,11... | collective-permute-start | bytes 7077896 | tf_op jit(solution)/shard_map/ppermute | solution.py:25
  805.5 92.1 %collective-permute-start.42 = (bf16[512,2304]{1,0:T(8,128)(2,1)}, bf16[512,2304]{1,0:T(8,128)(2,1)}, u32[]{:S(2)}, u32[]{:S(2)}) collective-permute-start(bf16[512,2304]{1,0:T(8,128)(2,1)} %get-tuple-element.40), channel_id=1, source_target_pairs={{0,1},{1,0},{2,3},{3,2},{4,5},{5,4},{6,7},{7,6},{8,9},{9,8},{10,11... | collective-permute-start | bytes 7077896 | tf_op jit(solution)/shard_map/ppermute | solution.py:25
  806.9 173.2 %collective-permute-start.73 = (bf16[2304,256]{1,0:T(8,128)(2,1)}, bf16[2304,256]{1,0:T(8,128)(2,1)}, u32[]{:S(2)}, u32[]{:S(2)}) collective-permute-start(bf16[2304,256]{1,0:T(8,128)(2,1)} %get-tuple-element.69), channel_id=1, source_target_pairs={{8,16},{12,20},{16,8},{20,12},{9,17},{13,21},{17,9},{21,13},{10,18... | collective-permute-start | bytes 3538952 | tf_op jit(solution)/shard_map/ppermute | solution.py:48
  811.7 142.5 %collective-permute-start.61 = (bf16[2304,256]{1,0:T(8,128)(2,1)}, bf16[2304,256]{1,0:T(8,128)(2,1)}, u32[]{:S(2)}, u32[]{:S(2)}) collective-permute-start(bf16[2304,256]{1,0:T(8,128)(2,1)} %get-tuple-element.77), channel_id=1, source_target_pairs={{8,16},{12,20},{16,8},{20,12},{9,17},{13,21},{17,9},{21,13},{10,18... | collective-permute-start | bytes 3538952 | tf_op jit(solution)/shard_map/ppermute | solution.py:48
  817.0 96.2 %collective-permute-start.55 = (bf16[2304,256]{1,0:T(8,128)(2,1)}, bf16[2304,256]{1,0:T(8,128)(2,1)}, u32[]{:S(2)}, u32[]{:S(2)}) collective-permute-start(bf16[2304,256]{1,0:T(8,128)(2,1)} %get-tuple-element.81), channel_id=1, source_target_pairs={{8,16},{12,20},{16,8},{20,12},{9,17},{13,21},{17,9},{21,13},{10,18... | collective-permute-start | bytes 3538952 | tf_op jit(solution)/shard_map/ppermute | solution.py:48
  824.6 94.6 %collective-permute-start.58 = (bf16[2304,256]{1,0:T(8,128)(2,1)}, bf16[2304,256]{1,0:T(8,128)(2,1)}, u32[]{:S(2)}, u32[]{:S(2)}) collective-permute-start(bf16[2304,256]{1,0:T(8,128)(2,1)} %fusion.6), channel_id=1, source_target_pairs={{0,8},{4,12},{8,0},{12,4},{16,24},{20,28},{24,16},{28,20},{1,9},{5... | collective-permute-start | bytes 3538952 | tf_op jit(solution)/shard_map/ppermute | solution.py:48
  897.6 56.6 %collective-permute-start.64 = (bf16[2304,256]{1,0:T(8,128)(2,1)}, bf16[2304,256]{1,0:T(8,128)(2,1)}, u32[]{:S(2)}, u32[]{:S(2)}) collective-permute-start(bf16[2304,256]{1,0:T(8,128)(2,1)} %fusion.4), channel_id=1, source_target_pairs={{0,8},{4,12},{8,0},{12,4},{16,24},{20,28},{24,16},{28,20},{1,9},{5... | collective-permute-start | bytes 3538952 | tf_op jit(solution)/shard_map/ppermute | solution.py:48
  919.2 58.2 %collective-permute-start.70 = (bf16[2304,256]{1,0:T(8,128)(2,1)S(1)}, bf16[2304,256]{1,0:T(8,128)(2,1)S(1)}, u32[]{:S(2)}, u32[]{:S(2)}) collective-permute-start(bf16[2304,256]{1,0:T(8,128)(2,1)S(1)} %copy-done.33), channel_id=1, source_target_pairs={{0,8},{4,12},{8,0},{12,4},{16,24},{20,28},{24,16},{28,20},{1,9},{5... | collective-permute-start | bytes 3538952 | tf_op jit(solution)/shard_map/ppermute | solution.py:48
  977.4 57.0 %collective-permute-start.45 = (bf16[256,2304]{1,0:T(8,128)(2,1)}, bf16[256,2304]{1,0:T(8,128)(2,1)S(1)}, u32[]{:S(2)}, u32[]{:S(2)}) collective-permute-start(bf16[256,2304]{1,0:T(8,128)(2,1)} %slice.291), channel_id=1, source_target_pairs={{0,4},{4,0},{8,12},{12,8},{16,20},{20,16},{24,28},{28,24},{1,5},{5... | collective-permute-start | bytes 3538952 | tf_op jit(solution)/shard_map/ppermute | solution.py:25
  980.1 79.6 %collective-permute-start.43 = (bf16[256,2304]{1,0:T(8,128)(2,1)}, bf16[256,2304]{1,0:T(8,128)(2,1)S(1)}, u32[]{:S(2)}, u32[]{:S(2)}) collective-permute-start(bf16[256,2304]{1,0:T(8,128)(2,1)} %slice.292), channel_id=1, source_target_pairs={{0,4},{4,0},{8,12},{12,8},{16,20},{20,16},{24,28},{28,24},{1,5},{5... | collective-permute-start | bytes 3538952 | tf_op jit(solution)/shard_map/ppermute | solution.py:25
  995.3 75.4 %collective-permute-start.59 = (bf16[1152,256]{1,0:T(8,128)(2,1)}, bf16[1152,256]{1,0:T(8,128)(2,1)S(1)}, u32[]{:S(2)}, u32[]{:S(2)}) collective-permute-start(bf16[1152,256]{1,0:T(8,128)(2,1)} %dynamic-slice_convert_fusion.3), channel_id=1, source_target_pairs={{0,4},{4,0},{8,12},{12,8},{16,20},{20,16},{24,28},{28,24},{1,5},{5... | collective-permute-start | bytes 1769480 | tf_op jit(solution)/shard_map/ppermute | solution.py:25
  1006.6 75.4 %collective-permute-start.65 = (bf16[1152,256]{1,0:T(8,128)(2,1)S(1)}, bf16[1152,256]{1,0:T(8,128)(2,1)S(1)}, u32[]{:S(2)}, u32[]{:S(2)}) collective-permute-start(bf16[1152,256]{1,0:T(8,128)(2,1)S(1)} %dynamic-slice_convert_fusion.2), channel_id=1, source_target_pairs={{0,4},{4,0},{8,12},{12,8},{16,20},{20,16},{24,28},{28,24},{1,5},{5... | collective-permute-start | bytes 1769480 | tf_op jit(solution)/shard_map/ppermute | solution.py:25
  1122.5 58.4 %collective-permute-start.85 = (f32[2,2,256]{2,1,0:T(2,128)S(1)}, f32[2,2,256]{2,1,0:T(2,128)S(1)}, u32[]{:S(2)}, u32[]{:S(2)}) collective-permute-start(f32[2,2,256]{2,1,0:T(2,128)S(1)} %add.351), channel_id=1, source_target_pairs={{0,16},{4,20},{8,24},{12,28},{16,0},{20,4},{24,8},{28,12},{1,17},{... | collective-permute-start | bytes 12296 | tf_op jit(solution)/shard_map/ppermute | solution.py:25
  (125 other events, 3049.7 us)

commit v2 on v0

v2 whole, which is shorter than its diff:
```python
import functools

import jax
import jax.numpy as jnp
from jax import lax
from jax.experimental import pallas as pl
from jax.experimental.pallas import tpu as pltpu
from jax.sharding import PartitionSpec as P

F32 = jnp.float32
BF16 = jnp.bfloat16
POOLED = 36
PITCH = 48
LANES = 128
VMEM_LIMIT = 56 * 1024 * 1024
SMALL = pl.CostEstimate(flops=1000, bytes_accessed=1000, transcendentals=0)
AHEAD = 3
IMAGE_BLOCK = 16
HALVES = 2
GROUPS = 2


def params():
    return pltpu.CompilerParams(vmem_limit_bytes=VMEM_LIMIT)


def flipped(value, axis, bit):
    pairs = [(source, source ^ bit) for source in range(lax.axis_size(axis))]
    return lax.ppermute(value, axis, pairs)


def x_swap(value):
    return flipped(value, "batch", 1)


def y_swap(value):
    return flipped(value, "tower", 2)


def c_swap(value):
    return flipped(value, "tower", 1)


def line(value, kind):
    steps = {
        "near": ((0, 1), (1, 0), (2, 3), (3, 2)),
        "middle": ((1, 2), (2, 1)),
        "outward": ((1, 0), (2, 3)),
        "inward": ((0, 1), (3, 2)),
    }[kind]
    pairs = [(2 * a + x, 2 * b + x) for a, b in steps for x in range(2)]
    return lax.ppermute(value, "batch", pairs)


def slab_groups():
    size = lax.axis_size("batch")
    return [list(range(x, size, 2)) for x in range(2)]


def after(value, *others):
    return lax.optimization_barrier((value, *others))[0]


class Order:
    def __init__(self):
        self.last = None

    def then(self, value):
        return value if self.last is None else after(value, self.last)

    def did(self, value):
        self.last = value
        return value


def is_line():
    return lax.axis_size("batch") == 8


def line_order(z):
    rows = jnp.array([[0, 1, 2, 3], [1, 0, 2, 3], [2, 3, 1, 0], [3, 2, 1, 0]])
    return rows[z]


def both_cores(value):
    size = lax.axis_size("tower")
    groups = [[t, t + 1] for t in range(0, size, 2)]
    return lax.all_gather(value, "tower", axis=0, tiled=True, axis_index_groups=groups)


def pool_table(order):
    map_pos = jnp.arange(169)[None, :]
    prow = (order // 6)[:, None]
    pcol = (order % 6)[:, None]
    qrow = map_pos // 13
    qcol = map_pos % 13
    inside = (
        (qrow >= 2 * prow) & (qrow <= 2 * prow + 2) & (qcol >= 2 * pcol) & (qcol <= 2 * pcol + 2)
    )
    small = (prow < 5) & (pcol < 5)
    table = jnp.stack([inside, inside & small]).astype(BF16)
    table = jnp.pad(table, ((0, 0), (0, PITCH - POOLED), (0, 0)))
    both = table[:, None, :, :, None] * jnp.eye(2, dtype=BF16)[None, :, None, None, :]
    return both.reshape(2, 2 * PITCH, 338)


def pool_kernel(start, group, table, first, maps, *refs):
    *feature_outs, pooled_out, own, other, pool0, pool1 = refs[-(2 * HALVES + 5) :]
    count, places, _, ch = maps.shape
    base = (start + pl.program_id(0)) * count

    def image(n, carry):
        window = table[group[base + n]]
        rows_in = maps[n].reshape(2 * places, ch)
        both = jnp.dot(window, rows_in, preferred_element_type=F32) * (1.0 / 9.0)
        p0, p1 = both[:PITCH], both[PITCH:]
        rows = pl.ds(pl.multiple_of(n * PITCH, PITCH), PITCH)
        mixed0 = first[0:1, :] * p0 + first[1:2, :] * p1
        mixed1 = first[2:3, :] * p0 + first[3:4, :] * p1
        for hold, value in ((pool0, p0), (pool1, p1), (own, mixed0), (other, mixed1)):
            for h in range(ch // LANES):
                hold[h, rows, :] = value[:, h * LANES : (h + 1) * LANES]
        return carry

    lax.fori_loop(0, count, image, 0, unroll=2)
    per = POOLED // HALVES
    for p in range(POOLED):
        rows = pl.ds(p, count, stride=PITCH)
        for h in range(ch // LANES):
            lanes = slice(p * ch + h * LANES, p * ch + (h + 1) * LANES)
            part = slice((p % per) * ch + h * LANES, (p % per) * ch + (h + 1) * LANES)
            feature_outs[p // per][:, part] = own[h, rows, :].astype(BF16)
            feature_outs[HALVES + p // per][:, part] = other[h, rows, :].astype(BF16)
            pooled_out[0, :, lanes] = pool0[h, rows, :]
            pooled_out[1, :, lanes] = pool1[h, rows, :]


def pool(convmaps, group, table, first, at, steps, before=()):
    count, _, places, ch = convmaps.shape
    nb = IMAGE_BLOCK
    feats = POOLED * ch
    features = [((count, feats // HALVES), BF16)] * (2 * HALVES)
    return pl.pallas_call(
        functools.partial(pool_kernel, at),
        grid_spec=pltpu.PrefetchScalarGridSpec(
            num_scalar_prefetch=1,
            grid=(steps,),
            in_specs=[
                pl.BlockSpec(table.shape, lambda i, g: (0, 0, 0)),
                pl.BlockSpec((4, ch), lambda i, g: (0, 0)),
                pl.BlockSpec((nb, places, 2, ch), lambda i, g: (at + i, 0, 0, 0)),
            ]
            + [pl.BlockSpec(memory_space=pl.ANY)] * len(before),
            out_specs=[pl.BlockSpec((nb, feats // HALVES), lambda i, g: (at + i, 0))] * (2 * HALVES)
            + [pl.BlockSpec((2, nb, feats), lambda i, g: (0, at + i, 0))],
            scratch_shapes=[pltpu.VMEM((ch // LANES, nb * PITCH, LANES), F32)] * 4,
        ),
        out_shape=[jax.ShapeDtypeStruct(*f) for f in features]
        + [jax.ShapeDtypeStruct((2, count, feats), F32)],
        input_output_aliases={4 + i: i for i in range(len(before))},
        compiler_params=params(),
        cost_estimate=SMALL,
        name="pool",
    )(group, table, first, jnp.swapaxes(convmaps, 1, 2), *before)


def first_grad_kernel(begin, pooled, *refs):
    pieces = (len(refs) - 1) // 2
    out = refs[-1]
    ch = out.shape[2]

    @pl.when(pl.program_id(0) == 0)
    def _():
        out[...] = jnp.zeros_like(out)

    for a in range(2):
        sums = [0.0, 0.0]
        start = begin
        for ref in refs[a * pieces : (a + 1) * pieces]:
            for p in range(ref.shape[1] // ch):
                grad = ref[:, p * ch : (p + 1) * ch].astype(F32)
                lanes = slice(start + p * ch, start + (p + 1) * ch)
                for s in range(2):
                    sums[s] = sums[s] + grad * pooled[s, :, lanes]
            start += ref.shape[1]
        for s in range(2):
            out[2 * a + s] += sums[s]


def first_grad(pooled, own, other, begin):
    count, feats = pooled.shape[1:]
    ch = feats // POOLED
    nb = 16
    specs = [pl.BlockSpec((nb, piece.shape[1]), lambda i: (i, 0)) for piece in own + other]
    sums = pl.pallas_call(
        functools.partial(first_grad_kernel, begin),
        grid=(count // nb,),
        in_specs=[pl.BlockSpec((2, nb, feats), lambda i: (0, i, 0))] + specs,
        out_specs=pl.BlockSpec((4, nb, ch), lambda i: (0, 0, 0)),
        out_shape=jax.ShapeDtypeStruct((4, nb, ch), F32),
        compiler_params=params(),
        cost_estimate=SMALL,
        name="first_grad",
    )(pooled, *own, *other)
    return jnp.sum(sums, axis=1)


def unpool_kernel(start, pieces, group, table, first, *refs):
    out, own, other = refs[-3:]
    count = out.shape[0]
    base = (start + pl.program_id(0)) * count
    ch = out.shape[3]
    places = out.shape[1]

    @pl.when(pl.program_id(0) == 0)
    def _():
        own[...] = jnp.zeros_like(own)
        other[...] = jnp.zeros_like(other)

    for hold, parts in ((own, refs[:pieces]), (other, refs[pieces : 2 * pieces])):
        start = 0
        for ref in parts:
            for p in range(ref.shape[1] // ch):
                for h in range(ch // LANES):
                    lanes = slice(p * ch + h * LANES, p * ch + (h + 1) * LANES)
                    hold[h, pl.ds(start + p, count, stride=PITCH), :] = ref[:, lanes].astype(F32)
            start += ref.shape[1] // ch

    def image(n, carry):
        window = table[group[base + n]]
        rows = pl.ds(pl.multiple_of(n * PITCH, PITCH), PITCH)
        g0, g1 = (
            jnp.concatenate([hold[h, rows, :] for h in range(ch // LANES)], axis=1) for hold in (own, other)
        )
        highs, lows = [], []
        for s in range(2):
            grad = (first[s : s + 1, :] * g0 + first[2 + s : 3 + s, :] * g1) * (1.0 / 9.0)
            highs.append(grad.astype(BF16))
            lows.append((grad - highs[s].astype(F32)).astype(BF16))
        parts = jnp.concatenate(highs + lows, axis=0)
        spread = jnp.dot(window, parts, preferred_element_type=F32).astype(BF16)
        out[n] = spread[: 2 * places].reshape(places, 2, ch)
        return carry

    lax.fori_loop(0, count, image, 0, unroll=2)


def unpool(own, other, group, table, first, places, at, steps, before=()):
    count = own[0].shape[0]
    ch = first.shape[1]
    nb = IMAGE_BLOCK
    specs = [pl.BlockSpec((nb, piece.shape[1]), lambda i, g: (at + i, 0)) for piece in own + other]
    specs += [pl.BlockSpec(memory_space=pl.ANY)] * len(before)
    spread = jnp.swapaxes(table, 1, 2)
    spread = jnp.pad(jnp.concatenate([spread, spread], axis=2), ((0, 0), (0, 352 - 2 * places), (0, 0)))
    return pl.pallas_call(
        functools.partial(unpool_kernel, at, len(own)),
        grid_spec=pltpu.PrefetchScalarGridSpec(
            num_scalar_prefetch=1,
            grid=(steps,),
            in_specs=[
                pl.BlockSpec(spread.shape, lambda i, g: (0, 0, 0)),
                pl.BlockSpec((4, ch), lambda i, g: (0, 0)),
            ]
            + specs,
            out_specs=pl.BlockSpec((nb, places, 2, ch), lambda i, g: (at + i, 0, 0, 0)),
            scratch_shapes=[pltpu.VMEM((ch // LANES, nb * PITCH, LANES), F32)] * 2,
        ),
        out_shape=jax.ShapeDtypeStruct((count, places, 2, ch), BF16),
        input_output_aliases={3 + 2 * len(own): 0} if before else {},
        compiler_params=params(),
        cost_estimate=SMALL,
        name="unpool",
    )(group, spread, first, *own, *other, *before)


def tile_of(rows):
    return next(t for t in (1152, 768, 576, 512, 384, 256, 128) if rows % t == 0)


def fetch(outer, terms, rows, target, sem):
    def copy(term):
        return pltpu.make_async_copy(term.at[rows, :], target, sem)

    if len(terms) == 1:
        copy(terms[0]).start()
    else:
        pl.when(outer == 1)(lambda: copy(terms[0]).start())
        pl.when(outer == 0)(lambda: copy(terms[1]).start())


def chunk_kernel(layout, blocks, roles, vectors, cot_own, cot_other, *refs):
    chunks, count = len(layout), len(layout[0])
    feats, refs = refs[: blocks * HALVES], refs[blocks * HALVES :]
    at = 0
    pieces = []
    for counts in layout:
        pieces.append([])
        for many in counts:
            pieces[-1].append(refs[at : at + many])
            at += many
    act_out, dpre_out, sums_out = refs[at : at + 3]
    outs = [refs[at + 3 + i * count : at + 3 + (i + 1) * count] for i in range(chunks)]
    held, weight, total, k_own, k_other, high, low, in_sems, w_sems, cot_sems, out_sems = refs[-11:]
    steps, images, tile = held.shape
    per = steps // count
    units = total.shape[1] // chunks
    half, height = steps // HALVES, images // blocks

    def columns(i):
        return slice(i * units, (i + 1) * units)

    def begin(k):
        for s in range(count):

            @pl.when(k // per == s)
            def _(s=s):
                rows = pl.ds(pl.multiple_of((k - s * per) * tile, tile), tile)
                for i in range(chunks):
                    fetch(roles[0], pieces[i][s], rows, weight.at[k, :, columns(i)], w_sems.at[k])

        for h in range(HALVES):

            @pl.when(k // half == h)
            def _(h=h):
                cols = pl.ds(pl.multiple_of((k - h * half) * tile, tile), tile)
                for r in range(blocks):
                    part = feats[r * HALVES + h]
                    start = 0 if part.shape[0] == height else pl.multiple_of(roles[1] * height, height)
                    part = part.at[pl.ds(start, height), cols]
                    rows = pl.ds(r * height, height)
                    pltpu.make_async_copy(part, held.at[k, rows, :], in_sems.at[k]).start()

    def arrive(target, sem):
        pltpu.make_async_copy(target, target, sem).wait()

    ahead = min(AHEAD, steps)
    for k in range(ahead):
        begin(jnp.int32(k))
    cot_copies = [
        pltpu.make_async_copy(cot_own, k_own, cot_sems.at[0]),
        pltpu.make_async_copy(cot_other, k_other, cot_sems.at[1]),
    ]
    for copy in cot_copies:
        copy.start()
    total[...] = jnp.zeros_like(total)

    def forward_step(k, carry):
        pl.when(k + ahead < steps)(lambda: begin(k + ahead))
        arrive(held.at[k], in_sems.at[k])
        arrive(weight.at[k], w_sems.at[k])
        total[...] += jnp.dot(held[k], weight[k], preferred_element_type=F32)
        return carry

    lax.fori_loop(0, steps, forward_step, 0)
    for copy in cot_copies:
        copy.wait()

    bias, own_coef, other_coef = (vectors[i : i + 1, :] for i in range(3))
    c = 0.7978845608028654
    block = 32

    def rows_of(i, sums):
        rows = pl.ds(pl.multiple_of(i * block, block), block)
        x = total[rows, :] + bias
        x2 = x * x
        t = jnp.tanh(c * (x + 0.044715 * (x2 * x)))
        half = 0.5 * (1.0 + t)
        act = (x * half).astype(BF16)
        slope = half + (0.5 * c) * x * (1.0 - t * t) * (1.0 + (3.0 * 0.044715) * x2)
        k0 = k_own[rows, :].astype(F32)
        k1 = k_other[rows, :].astype(F32)
        dpre = ((own_coef * k0 + other_coef * k1) * slope).astype(BF16)
        act_out[rows, :] = act
        dpre_out[rows, :] = dpre
        actf = act.astype(F32)

        def fold(v):
            return jnp.sum(v.reshape(block // 8, 8, v.shape[1]), axis=0)

        return (
            sums[0] + fold(dpre.astype(F32)),
            sums[1] + fold(k0 * actf),
            sums[2] + fold(k1 * actf),
        )

    zero = jnp.zeros((8, total.shape[1]), F32)
    sums = lax.fori_loop(0, images // block, rows_of, (zero, zero, zero))
    for i in range(3):
        sums_out[i] = sums[i]

    def product(k):
        return lax.dot_general(
            held[k], dpre_out[...], (((0,), (0,)), ((), ())), preferred_element_type=F32
        )

    def last_steps(k, carry):
        made = product(k).astype(BF16)
        for i in range(chunks):
            low[k - per, i] = made[:, columns(i)]
        for s in range(1, count):

            @pl.when(k // per == s)
            def _(s=s):
                rows = pl.ds(pl.multiple_of((k - s * per) * tile, tile), tile)
                for i in range(chunks):
                    pltpu.make_async_copy(low.at[k - per, i], outs[i][s].at[rows, :], out_sems.at[k]).start()

        return carry

    def first_steps(k, carry):
        made = product(k)
        rows = pl.ds(pl.multiple_of(k * tile, tile), tile)
        for i in range(chunks):
            high[k, i] = made[:, columns(i)]
            pltpu.make_async_copy(high.at[k, i], outs[i][0].at[rows, :], out_sems.at[k]).start()
        return carry

    if count > 1:
        lax.fori_loop(per, steps, last_steps, 0)
    lax.fori_loop(0, per, first_steps, 0)
    for k in range(steps):
        arrive(high.at[k] if k < per else low.at[k - per], out_sems.at[k])


def chunk(roles, feats, pieces, vectors, cot_own, cot_other):
    images, width = cot_own.shape
    units = width // len(pieces)
    depth = sum(part.shape[1] for part in feats[0])
    count = len(pieces[0])
    height = pieces[0][0][0].shape[0]
    tile = tile_of(height)
    steps, per = depth // tile, height // tile
    terms = [term for chunk in pieces for piece in chunk for term in piece]
    anywhere = pl.BlockSpec(memory_space=pl.ANY)
    vmem = pl.BlockSpec(memory_space=pltpu.VMEM)
    kinds = ([F32] + [BF16] * (count - 1)) * len(pieces)
    return pl.pallas_call(
        functools.partial(chunk_kernel, [[len(p) for p in chunk] for chunk in pieces], len(feats)),
        in_specs=[pl.BlockSpec(memory_space=pltpu.SMEM), vmem]
        + [anywhere] * (2 + len(feats) * HALVES + len(terms)),
        out_specs=[vmem] * 3 + [anywhere] * len(kinds),
        out_shape=[
            jax.ShapeDtypeStruct((images, width), BF16),
            jax.ShapeDtypeStruct((images, width), BF16),
            jax.ShapeDtypeStruct((3, 8, width), F32),
        ]
        + [jax.ShapeDtypeStruct((height, units), kind) for kind in kinds],
        scratch_shapes=[
            pltpu.VMEM((steps, images, tile), BF16),
            pltpu.VMEM((steps, tile, width), BF16),
            pltpu.VMEM((images, width), F32),
            pltpu.VMEM((images, width), BF16),
            pltpu.VMEM((images, width), BF16),
            pltpu.VMEM((per, len(pieces), tile, units), F32),
            pltpu.VMEM((max(steps - per, 1), len(pieces), tile, units), BF16),
            pltpu.SemaphoreType.DMA((steps,)),
            pltpu.SemaphoreType.DMA((steps,)),
            pltpu.SemaphoreType.DMA((2,)),
            pltpu.SemaphoreType.DMA((steps,)),
        ],
        compiler_params=params(),
        cost_estimate=SMALL,
        name="chunk",
    )(roles, vectors, cot_own, cot_other, *[part for block in feats for part in block], *terms)


def back_kernel(layout, groups, roles, *refs):
    count = len(layout)
    grads = refs[:groups]
    at = groups
    pieces = []
    for many in layout:
        pieces.append(refs[at : at + many])
        at += many
    keep_out, send_out, grad, weight, keep, send, grad_sems, w_sems, out_sems = refs[at:]
    steps, tile, total = weight.shape
    units, width = total // count, total // groups
    half = keep.shape[1]
    grad_copies = []
    for j in range(groups):
        cols = pl.ds(j * width, width)
        grad_copies.append(pltpu.make_async_copy(grads[j], grad.at[:, cols], grad_sems.at[j]))
        grad_copies[j].start()
    for k in range(steps):
        for j in range(count):
            rows, cols = pl.ds(k * tile, tile), pl.ds(j * units, units)
            fetch(roles[0], pieces[j], rows, weight.at[k, :, cols], w_sems.at[k])
    for copy in grad_copies:
        copy.wait()
    contract = (((1,), (1,)), ((), ()))

    def step(k, carry):
        pltpu.make_async_copy(weight.at[k], weight.at[k], w_sems.at[k]).wait()
        cols = pl.ds(pl.multiple_of(k * tile, tile), tile)
        send[k] = lax.dot_general(grad[half:, :], weight[k], contract, preferred_element_type=F32).astype(BF16)
        pltpu.make_async_copy(send.at[k], send_out.at[:, cols], out_sems.at[k, 0]).start()
        keep[k] = lax.dot_general(grad[:half, :], weight[k], contract, preferred_element_type=F32)
        pltpu.make_async_copy(keep.at[k], keep_out.at[:, cols], out_sems.at[k, 1]).start()
        return carry

    lax.fori_loop(0, steps, step, 0)
    for k in range(steps):
        pltpu.make_async_copy(send.at[k], send.at[k], out_sems.at[k, 0]).wait()
        pltpu.make_async_copy(keep.at[k], keep.at[k], out_sems.at[k, 1]).wait()


def back(roles, grads, piece):
    rows, width = grads[0].shape
    depth = piece[0][0].shape[0]
    tile = next(t for t in (768, 512, 384, 256, 128) if depth % t == 0)
    steps = depth // tile
    terms = [term for part in piece for term in part]
    anywhere = pl.BlockSpec(memory_space=pl.ANY)
    half, total, groups = rows // 2, width * len(grads), len(grads)
    return pl.pallas_call(
        functools.partial(back_kernel, [len(c) for c in piece], groups),
        in_specs=[pl.BlockSpec(memory_space=pltpu.SMEM)] + [anywhere] * (groups + len(terms)),
        out_specs=[anywhere, anywhere],
        out_shape=[
            jax.ShapeDtypeStruct((half, depth), F32),
            jax.ShapeDtypeStruct((half, depth), BF16),
        ],
        scratch_shapes=[
            pltpu.VMEM((rows, total), BF16),
            pltpu.VMEM((steps, tile, total), BF16),
            pltpu.VMEM((steps, half, tile), F32),
            pltpu.VMEM((steps, half, tile), BF16),
            pltpu.SemaphoreType.DMA((groups,)),
            pltpu.SemaphoreType.DMA((steps,)),
            pltpu.SemaphoreType.DMA((steps, 2)),
        ],
        compiler_params=params(),
        cost_estimate=SMALL,
        name="back",
    )(roles, *grads, *terms)


def tile_of(rows):
    return next(t for t in (1152, 768, 576, 512, 384, 256, 128) if rows % t == 0)


def either(flag, value, axis):
    return jnp.where(flag, jnp.flip(value, axis), value)


class Program:
    def __init__(self, convmaps, group, alpha1, weight, bias, alpha2, cotangent):
        self.order = Order()
        self.convmaps, self.group, self.weight = convmaps, group, weight
        self.count, _, self.places, self.channels = convmaps.shape
        batch_id = lax.axis_index("batch")
        tower_id = lax.axis_index("tower")
        self.x, self.z = batch_id % 2, batch_id // 2
        self.y, self.core = tower_id // 2, tower_id % 2
        self.depth, self.width = weight.shape
        self.units = self.width // 2
        self.m = self.units // GROUPS
        self.n = self.m // 2 if is_line() else self.m
        self.images = 8 * self.count
        self.mine, self.theirs = self.x * self.units, (1 - self.x) * self.units
        units = self.units
        second = lax.dynamic_slice_in_dim(alpha2, self.mine, units, 1)
        self.own_coef = lax.dynamic_index_in_dim(second, self.y, 0, keepdims=True).astype(F32)
        self.cross = lax.dynamic_index_in_dim(second, 1 - self.y, 0, keepdims=True)
        own_bias = lax.dynamic_slice_in_dim(bias, self.mine, units, 0)[None, :].astype(F32)
        self.own_bias = own_bias
        cot = cotangent.reshape(2, 2, self.count, self.width)
        cot = either(self.core == 1, either(self.y == 1, cot, 0), 1).swapaxes(0, 1)
        self.cot_mine = lax.dynamic_slice_in_dim(cot, self.mine, units, 3)
        self.cot_theirs = lax.dynamic_slice_in_dim(cot, self.theirs, units, 3)
        places = jnp.arange(POOLED)
        if is_line():
            places = places.reshape(4, -1)[line_order(self.z)].reshape(-1)
        self.table = pool_table(places)
        self.first = either(self.y == 1, alpha1.astype(F32), 0).reshape(4, self.channels)
        self.weight_grad = jnp.zeros((self.depth, self.width), F32)
        self.is_outer = (self.z == 0) | (self.z == 3)
        self.roles = jnp.stack([self.is_outer.astype(jnp.int32), 1 - self.core])
        self.cot_own, self.cot_other = {}, {}
        self.acts, self.grads, self.sums = {}, {}, {}
        self.stitched, self.crossed = {}, {}

    def then(self, value):
        return self.order.then(value)

    def did(self, value):
        return self.order.did(value)

    def send_cross(self):
        return self.send(y_swap, self.cross)

    def keep_cross(self, came):
        cross_back = self.then(came).astype(F32)
        zeros = jnp.zeros((5, self.units), F32)
        self.vectors = jnp.concatenate([self.own_bias, self.own_coef, cross_back, zeros])
        self.cross = self.cross.astype(F32)

    def group_cols(self, g):
        return slice(g * self.m, (g + 1) * self.m)

    def weight_part(self, start, j, many=1):
        return lax.dynamic_slice(self.weight, (0, start + j * self.n), (self.depth, many * self.n))

    def swap_weight(self, j, many=1):
        return self.send(x_swap, self.weight_part(self.theirs, j, many))

    def slab_weight(self, j, came):
        a, b = self.weight_part(self.mine, j), self.then(came)
        return self.did(jnp.where(self.x == 0, jnp.concatenate([a, b]), jnp.concatenate([b, a])))

    def swap_cotangents(self, g):
        return self.send(x_swap, self.cot_theirs[..., self.group_cols(g)])

    def pass_cotangents(self, g, came):
        cot = self.did(jnp.stack([self.cot_mine[..., self.group_cols(g)], self.then(came)], axis=1))
        self.cot_own[g] = cot.reshape(self.images, self.m)
        return self.send(y_swap, cot)

    def keep_cotangents(self, g, came):
        self.cot_other[g] = self.did(jnp.flip(self.then(came), 2).reshape(self.images, self.m))

    def send(self, move, value, *args):
        return move(self.did(self.then(value)), *args)

    def chunk(self, g, feats, pieces):
        act, dpre, sums, *products = chunk(
            self.roles,
            feats,
            pieces,
            self.then(self.vectors[:, self.group_cols(g)]),
            self.cot_own[g],
            self.cot_other[g],
        )
        self.did(dpre)
        self.acts[g], self.grads[g], self.sums[g] = act, dpre, sums
        count = len(pieces[0])
        return [products[i * count : (i + 1) * count] for i in range(len(pieces))]

    def swap_act(self, g):
        return self.send(y_swap, self.acts[g])

    def stitch(self, g, came):
        cols = self.group_cols(g)
        other_act = jnp.flip(self.then(came).reshape(4, 2, self.count, self.m), 1).reshape(self.images, self.m)
        mix = self.own_coef[:, cols] * self.acts[g].astype(F32) + self.cross[:, cols] * other_act.astype(F32)
        mix = self.did(mix.astype(BF16)).reshape(2, 2, 2, self.count, self.m)
        self.stitched[g] = mix[:, 0]
        return mix[:, 1]

    def swap_grad(self, j, slab):
        leave = lax.dynamic_slice_in_dim(slab, (1 - self.x) * self.depth, self.depth, 0)
        came = self.send(x_swap, leave.astype(BF16))
        stay = lax.dynamic_slice_in_dim(slab, self.x * self.depth, self.depth, 0)
        self.weight_grad = self.did(
            lax.dynamic_update_slice(self.weight_grad, stay, (0, self.mine + j * self.n))
        )
        return came

    def store_grad(self, j, came):
        self.weight_grad = self.did(
            lax.dynamic_update_slice(
                self.weight_grad, self.then(came).astype(F32), (0, self.theirs + j * self.n)
            )
        )

    def activations(self):
        left = jnp.concatenate([self.stitched[g] for g in range(GROUPS)], axis=3)
        right = jnp.concatenate([self.crossed[g] for g in range(GROUPS)], axis=3)
        rows = jnp.where(
            self.x == 0, jnp.concatenate([left, right], 3), jnp.concatenate([right, left], 3)
        )
        rows = either(self.y == 1, either(self.core == 1, rows, 0), 1).swapaxes(0, 1)
        return rows.reshape(4 * self.count, self.width)

    def unit_sums(self):
        return self.did(
            jnp.concatenate([jnp.sum(self.then(self.sums[g]), axis=1) for g in range(GROUPS)], axis=1)
        )

    def small_grads(self, sums, far, other_second):
        sums, other_second = (
            jnp.where(self.x == 0, jnp.concatenate([a, b], -1), jnp.concatenate([b, a], -1))
            for a, b in ((sums, far), other_second)
        )
        return sums[0], either(self.y == 1, jnp.stack([sums[1], other_second]), 0)

    def back(self, s, chunks):
        grads = [self.grads[g] for g in range(GROUPS)]
        keep, send = back(self.roles, [self.then(grads[0])] + grads[1:], [chunk[s] for chunk in chunks])
        return keep, self.did(send)

    def back_x(self, keep, came):
        part = keep + self.then(came).astype(F32)
        return part[: 2 * self.count], self.did(part[2 * self.count :].astype(BF16))

    def back_y(self, keep, came):
        part = keep + self.then(came).astype(F32)
        return part[: self.count], self.did(part[self.count :].astype(BF16))

    def first_grad(self, own, other, pooled, begin=0):
        return self.did(first_grad(pooled, [self.then(own[0])] + own[1:], other, begin))

    def by_tower(self, partial):
        return either(self.y == 1, partial.reshape(2, 2, self.channels), 0)

    def unpool(self, own, other, at, steps, before=()):
        return unpool(
            [self.then(own[0])] + own[1:],
            other,
            self.group,
            self.table,
            self.first,
            self.places,
            at,
            steps,
            before,
        )


def line_program(p):
    then, did = p.then, p.did
    came, blocks, near, inner, outer, first_out, last_out = {}, {}, {}, {}, {}, {}, {}
    total, into, crossed, middle, final, slab_came = {}, {}, {}, {}, {}, {}
    from_own, swapped = {}, {}

    def send(kind, value):
        return p.send(line, value, kind)

    def arrive(value):
        return did(then(value))

    def block(j):
        blocks[j] = p.slab_weight(j, came[j])

    def pieces(j):
        beside = (near[j],) if j < 2 else (from_own[j], swapped[j])
        return [(blocks[j],), beside, (first_out[j], inner[j]), (last_out[j], outer[j])]

    def part(j, s):
        return total[j][s]

    def payload(inward, outward):
        return did(jnp.where(p.is_outer, then(inward), outward))

    def ends(value):
        return send("near", value)

    def inward(j, s):
        return send("inward", then(part(j, s)))

    def plus(j, s, value):
        return (part(j, s).astype(F32) + then(value).astype(F32)).astype(BF16)

    def slab(j):
        ends = jnp.where(
            p.is_outer,
            then(final[j]).astype(F32),
            into[j, 1].astype(F32) + then(middle[j]).astype(F32),
        )
        slab_came[j] = p.swap_grad(j, did(part(j, 0) + ends))

    image_blocks = p.count // IMAGE_BLOCK
    early = image_blocks // 8
    came[0] = p.swap_weight(0)
    made = pool(p.convmaps, p.group, then(p.table), p.first, 0, early)
    did(made[0])
    came[0] = arrive(came[0])
    block(0)
    near[0] = ends(blocks[0])
    inner[0] = send("middle", blocks[0])
    came[1] = p.swap_weight(1)
    cot_came = p.swap_cotangents(0)
    cross_came = p.send_cross()
    kept_a, kept_b, sent_a, sent_b, pooled = pool(
        p.convmaps, p.group, then(p.table), p.first, early, image_blocks - early, made
    )
    did(kept_a)
    came[1] = arrive(came[1])
    block(1)
    near[0] = arrive(near[0])
    near[1] = ends(blocks[1])
    inner[0] = arrive(inner[0])
    inner[1] = send("middle", blocks[1])
    cot_came = arrive(cot_came)
    p.keep_cross(cross_came)
    x_a = p.send(x_swap, kept_a)
    y_a = p.send(y_swap, sent_a)
    near[1] = arrive(near[1])
    first_out[0] = send("outward", inner[0])
    inner[1] = arrive(inner[1])
    outer[0] = send("middle", near[0])
    x_a = arrive(x_a)
    came_pair = p.swap_weight(2, 2)
    y_a = arrive(y_a)
    y_b = p.send(y_swap, sent_b)
    c_kept = [both_cores(arrive(kept_a)), both_cores(arrive(kept_b))]
    c_x_a, c_y_a = both_cores(x_a), both_cores(y_a)
    first_out[0] = arrive(first_out[0])
    first_out[1] = send("outward", inner[1])
    outer[0] = arrive(outer[0])
    outer[1] = send("middle", near[1])
    came_pair = arrive(came_pair)
    x_b = p.send(x_swap, kept_b)
    y_b = arrive(y_b)
    cot_passed = p.pass_cotangents(0, cot_came)
    c_y_b = both_cores(y_b)
    came[2], came[3] = came_pair[:, : p.n], came_pair[:, p.n :]
    block(2)
    block(3)
    value = payload(blocks[2], outer[0])
    first_out[1] = arrive(first_out[1])
    swapped[2] = last_out[0] = ends(value)
    outer[1] = arrive(outer[1])
    inner[2] = send("middle", blocks[2])
    x_b = arrive(x_b)
    x_y_a = p.send(x_swap, y_a)
    c_x_b = both_cores(x_b)
    value = payload(blocks[3], outer[1])
    cot_passed = arrive(cot_passed)
    p.keep_cotangents(0, cot_passed)
    swapped[2] = last_out[0] = arrive(swapped[2])
    swapped[3] = last_out[1] = ends(value)
    inner[2] = arrive(inner[2])
    inner[3] = send("middle", blocks[3])
    x_y_a = arrive(x_y_a)
    x_y_b = p.send(x_swap, y_b)
    c_x_y_a = p.send(c_swap, x_y_a)
    swapped[3] = last_out[1] = arrive(swapped[3])
    from_own[2] = send("outward", blocks[2])
    inner[3] = arrive(inner[3])
    outer[2] = send("middle", swapped[2])
    c_x_y_a = arrive(c_x_y_a)
    x_y_b = arrive(x_y_b)
    c_x_y_b = p.send(c_swap, x_y_b)
    cot_came = p.swap_cotangents(1)
    c_x_y_b = arrive(c_x_y_b)
    feats = [
        [kept_a, kept_b],
        [y_a, y_b],
        [x_a, x_b],
        [x_y_a, x_y_b],
        c_kept,
        [c_y_a, c_y_b],
        [c_x_a, c_x_b],
        [c_x_y_a, c_x_y_b],
    ]
    total[0], total[1] = p.chunk(0, feats, [pieces(0), pieces(1)])
    value = payload(part(0, 3), blocks[3])
    from_own[2] = arrive(from_own[2])
    into[0, 3] = from_own[3] = ends(value)
    outer[2] = arrive(outer[2])
    outer[3] = send("middle", swapped[3])
    cot_came = arrive(cot_came)
    act_came = p.swap_act(0)
    value = payload(part(0, 2), inner[2])
    into[0, 3] = from_own[3] = arrive(into[0, 3])
    into[0, 2] = first_out[2] = ends(value)
    outer[3] = arrive(outer[3])
    crossed[0] = send("middle", plus(0, 3, into[0, 3]))
    act_came = arrive(act_came)
    cot_passed = p.pass_cotangents(1, cot_came)
    value = payload(part(0, 1), inner[3])
    mix = p.stitch(0, act_came)
    into[0, 2] = first_out[2] = arrive(into[0, 2])
    into[0, 1] = first_out[3] = ends(value)
    crossed[0] = arrive(crossed[0])
    middle[0] = send("middle", plus(0, 2, into[0, 2]))
    p.crossed[0] = p.send(x_swap, mix)
    value = payload(part(1, 3), outer[2])
    cot_passed = arrive(cot_passed)
    p.keep_cotangents(1, cot_passed)
    into[0, 1] = first_out[3] = arrive(into[0, 1])
    into[1, 3] = last_out[2] = ends(value)
    middle[0] = arrive(middle[0])
    p.crossed[0] = arrive(p.crossed[0])
    value = payload(part(1, 2), outer[3])
    into[1, 3] = last_out[2] = arrive(into[1, 3])
    into[1, 2] = last_out[3] = ends(value)
    crossed[1] = send("middle", plus(1, 3, into[1, 3]))
    value = payload(part(1, 1), plus(0, 1, crossed[0]))
    into[1, 2] = last_out[3] = arrive(into[1, 2])
    into[1, 1] = final[0] = ends(value)
    crossed[1] = arrive(crossed[1])
    middle[1] = send("middle", plus(1, 2, into[1, 2]))
    total[2], total[3] = p.chunk(1, feats, [pieces(2), pieces(3)])
    value = payload(part(2, 3), plus(1, 1, crossed[1]))
    chunks = [pieces(j) for j in range(4)]
    kept_c, send_c, came_c, kept_x, send_x, came_x = {}, {}, {}, {}, {}, {}
    own, send_y, other = {}, {}, {}
    into[1, 1] = final[0] = arrive(into[1, 1])
    into[2, 3] = final[1] = ends(value)
    middle[1] = arrive(middle[1])
    kept_c[0], send_c[0] = p.back(0, chunks)
    came_c[0] = p.send(c_swap, send_c[0])
    slab(0)
    sums = p.unit_sums()
    sums_came = p.send(flipped, sums, "batch", 2)
    act_came = p.swap_act(1)
    came_c[0] = arrive(came_c[0])
    kept_x[0], send_x[0] = p.back_x(kept_c[0], came_c[0])
    came_x[0] = p.send(x_swap, send_x[0])
    kept_c[1], send_c[1] = p.back(1, chunks)
    into[2, 3] = final[1] = arrive(into[2, 3])
    into[3, 3] = inward(3, 3)
    crossed[2] = send("middle", plus(2, 3, into[2, 3]))
    came_c[1] = p.send(c_swap, send_c[1])
    act_came = arrive(act_came)
    sums = did(sums + then(sums_came))
    slab_came[0] = arrive(slab_came[0])
    kept_c[2], send_c[2] = p.back(2, chunks)
    came_c[1] = arrive(came_c[1])
    kept_x[1], send_x[1] = p.back_x(kept_c[1], came_c[1])
    mix = p.stitch(1, act_came)
    came_x[0] = arrive(came_x[0])
    came_x[1] = p.send(x_swap, send_x[1])
    own[0], send_y[0] = p.back_y(kept_x[0], came_x[0])
    into[3, 3] = arrive(into[3, 3])
    into[2, 2] = inward(2, 2)
    crossed[2] = arrive(crossed[2])
    crossed[3] = send("middle", plus(3, 3, into[3, 3]))
    came_c[2] = p.send(c_swap, send_c[2])
    other[0] = p.send(y_swap, send_y[0])
    kept_c[3], send_c[3] = p.back(3, chunks)
    came_c[2] = arrive(came_c[2])
    kept_x[2], send_x[2] = p.back_x(kept_c[2], came_c[2])
    came_x[1] = arrive(came_x[1])
    came_x[2] = p.send(x_swap, send_x[2])
    own[1], send_y[1] = p.back_y(kept_x[1], came_x[1])
    into[2, 2] = arrive(into[2, 2])
    into[3, 2] = inward(3, 2)
    crossed[3] = arrive(crossed[3])
    middle[2] = send("middle", plus(2, 2, into[2, 2]))
    other[0] = arrive(other[0])
    came_c[3] = p.send(c_swap, send_c[3])
    other[1] = p.send(y_swap, send_y[1])
    value = payload(part(2, 1), plus(2, 1, crossed[2]))
    p.store_grad(0, slab_came[0])
    came_c[3] = arrive(came_c[3])
    kept_x[3], send_x[3] = p.back_x(kept_c[3], came_c[3])
    came_x[2] = arrive(came_x[2])
    came_x[3] = p.send(x_swap, send_x[3])
    own[2], send_y[2] = p.back_y(kept_x[2], came_x[2])
    into[3, 2] = arrive(into[3, 2])
    into[2, 1] = final[2] = ends(value)
    middle[2] = arrive(middle[2])
    middle[3] = send("middle", plus(3, 2, into[3, 2]))
    other[1] = arrive(other[1])
    other[2] = p.send(y_swap, send_y[2])
    sums_came = p.send(flipped, sums, "batch", 4)
    value = payload(part(3, 1), plus(3, 1, crossed[3]))
    quarter = p.channels * POOLED // 4
    partial = p.first_grad([own[0], own[1]], [other[0], other[1]], pooled)
    came_x[3] = arrive(came_x[3])
    own[3], send_y[3] = p.back_y(kept_x[3], came_x[3])
    slab(1)
    into[2, 1] = final[2] = arrive(into[2, 1])
    into[3, 1] = final[3] = ends(value)
    middle[3] = arrive(middle[3])
    other[2] = arrive(other[2])
    other[3] = p.send(y_swap, send_y[3])
    sums = did(sums + then(sums_came))
    far = p.send(x_swap, sums)
    slab(2)
    p.crossed[1] = p.send(x_swap, mix)
    other[3] = arrive(other[3])
    owns, others = ([parts[s] for s in range(4)] for parts in (own, other))
    partial = partial + p.first_grad(owns[2:], others[2:], pooled, 2 * quarter)
    partial = did(p.by_tower(partial))
    partial_came = p.send(c_swap, partial)
    grad = did(p.unpool(owns, others, 0, image_blocks // 2))
    into[3, 1] = final[3] = arrive(into[3, 1])
    slab(3)
    partial = did(partial + then(partial_came))
    partial_came = p.send(y_swap, partial)
    far = arrive(far)
    other_second = p.send(y_swap, jnp.stack([sums[2], far[2]]))
    slab_came[1] = arrive(slab_came[1])
    slab_came[2] = arrive(slab_came[2])
    p.crossed[1] = arrive(p.crossed[1])
    grad = did(p.unpool(owns, others, image_blocks // 2, image_blocks - image_blocks // 2, (grad,)))
    partial = did(partial + then(partial_came))
    partial_came = p.send(x_swap, partial)
    p.store_grad(1, slab_came[1])
    partial = did(partial + then(partial_came))
    partial_came = p.send(flipped, partial, "batch", 2)
    p.store_grad(2, slab_came[2])
    partial = did(partial + then(partial_came))
    partial_came = p.send(flipped, partial, "batch", 4)
    p.store_grad(3, slab_came[3])
    alpha1_grad = partial + then(partial_came)
    bias_grad, alpha2_grad = p.small_grads(sums, far, other_second)
    input_grad = jnp.swapaxes(grad, 1, 2)
    return (p.activations(), input_grad, p.weight_grad, bias_grad, alpha1_grad, alpha2_grad)


def plain_program(p):
    groups = slab_groups()
    p.keep_cross(p.send_cross())
    *features, pooled = pool(p.convmaps, p.group, p.table, p.first, 0, p.count // IMAGE_BLOCK)
    feats = [features[:HALVES], [y_swap(part) for part in features[HALVES:]]]
    feats += [[x_swap(part) for part in block] for block in feats]
    feats += [[c_swap(part) for part in block] for block in feats]
    chunks = []
    for g in range(GROUPS):
        p.keep_cotangents(g, p.pass_cotangents(g, p.swap_cotangents(g)))
        block = p.slab_weight(g, p.swap_weight(g))
        rows = lax.all_gather(block, "batch", axis=0, tiled=True, axis_index_groups=groups)
        chunks.append([(rows,)])
        [[total]] = p.chunk(g, feats, [chunks[g]])
        slab = lax.psum_scatter(total, "batch", scatter_dimension=0, tiled=True, axis_index_groups=groups)
        p.store_grad(g, p.swap_grad(g, slab))
        p.crossed[g] = p.send(x_swap, p.stitch(g, p.swap_act(g)))
    sums = lax.psum(p.unit_sums(), "batch", axis_index_groups=groups)
    far = x_swap(sums)
    bias_grad, alpha2_grad = p.small_grads(sums, far, y_swap(jnp.stack([sums[2], far[2]])))
    keep, send = p.back(0, chunks)
    keep, send = p.back_x(keep, c_swap(send))
    own, send = p.back_y(keep, x_swap(send))
    other = y_swap(send)
    alpha1_grad = lax.psum(p.by_tower(p.first_grad([own], [other], pooled)), ("batch", "tower"))
    grad = p.unpool([own], [other], 0, p.count // IMAGE_BLOCK)
    input_grad = jnp.swapaxes(grad, 1, 2)
    return (p.activations(), input_grad, p.weight_grad, bias_grad, alpha1_grad, alpha2_grad)


def shards(*args):
    return (line_program if is_line() else plain_program)(Program(*args))


def solution(mesh):
    in_specs = (
        P(("batch", "tower"), None, None, None),
        P(("batch", "tower")),
        P(),
        P("batch", "tower"),
        P("tower"),
        P(None, "tower"),
        P("batch", "tower"),
    )
    out_specs = (
        P("batch", "tower"),
        P(("batch", "tower"), None, None, None),
        P("batch", "tower"),
        P("tower"),
        P(),
        P(None, "tower"),
    )
    return jax.shard_map(shards, mesh=mesh, in_specs=in_specs, out_specs=out_specs, check_vma=False)
```

time: 1990 us -> 741 us (0.37)
  waiting for transfers between devices: 1480 us -> 258 us
  matrix products: 271 us -> 0 us
  Pallas kernels: 0 us -> 185 us
  starting transfers between devices: 18.9 us -> 120 us
  blocking collectives: 81.8 us -> 0 us
  other arithmetic: 29.8 us -> 90.8 us
  local copies, waits for them, and re-layouts: 87.9 us -> 63.2 us
    reduce_scatter x1 -> x0, waiting for transfers between devices: 593 us -> none  [shards(): lax.psum_scatter(lax.dot_general(columns, dpre_low, (((0,), (0,)), ((), (...]
    all_gather x1 -> x6, waiting for transfers between devices: 490 us -> 0.07 us  [both_cores(): lax.all_gather(value, 'tower', axis=0, tiled=True, axis_index_groups=groups)]
    dot_general x8 -> x0, matrix products: 271 us -> none  [the longest x1 87.1 us: shards(): jnp.einsum('anpc,snpc->asc', dmixed, pooled, precision=highest)]
    pallas_call x0 -> x12, Pallas kernels: none -> 185 us  [the longest x2 66.2 us: chunk(): pl.pallas_call(functools.partial(chunk_kernel, [[len(p) for p in chunk] f...]
    ppermute x3 -> x80, waiting for transfers between devices: 395 us -> 256 us  [the longest x35 164 us: line(): return lax.ppermute(value, 'batch', pairs)]
    ppermute x3 -> x80, starting transfers between devices: 5.09 us -> 120 us  [the longest x35 70.9 us: line(): return lax.ppermute(value, 'batch', pairs)]
    psum x2 -> x0, blocking collectives: 81.8 us -> none  [the longest x1 43.3 us: shards(): alpha1_grad = lax.psum(first_local, ('batch', 'tower'))]
    select_n x0 -> x26, other arithmetic: none -> 32.3 us  [the longest x11 20 us: payload(): return did(jnp.where(p.is_outer, then(inward), outward))]
  transfers between devices with their start and end apart: 7 -> 86, of which waited for: 4 -> 27; matrix products, arithmetic and copies ran while one was open for 16% -> 19% of each run, Pallas kernels for 0% -> 24%
where the time goes in v2:
time: 741 us; the launch traced here: 732 us
  waiting for transfers between devices  258 us (35%)
  Pallas kernels  185 us (25%)
  starting transfers between devices  120 us (16%)
  other arithmetic  90.8 us (12%)
  local copies, waits for them, and re-layouts  63.2 us (9%)
  between operations  15.8 us (2%)
    ppermute x35, waiting for transfers between devices, line(): return lax.ppermute(value, 'batch', pairs)  164 us
    ppermute x45, waiting for transfers between devices, flipped(): return lax.ppermute(value, axis, pairs)  91.7 us
    ppermute x35, starting transfers between devices, line(): return lax.ppermute(value, 'batch', pairs)  70.9 us
    pallas_call x2, Pallas kernels, chunk(): pl.pallas_call(functools.partial(chunk_kernel, [[len(p) for p in chunk] f...  66.2 us
    ppermute x45, starting transfers between devices, flipped(): return lax.ppermute(value, axis, pairs)  48.9 us
    pallas_call x4, Pallas kernels, back(): pl.pallas_call(functools.partial(back_kernel, [len(c) for c in piece], gr...  42.5 us
    pallas_call x2, Pallas kernels, pool(): pl.pallas_call(functools.partial(pool_kernel, at), grid_spec=pltpu.Prefet...  31 us
    pallas_call x2, Pallas kernels, unpool(): pl.pallas_call(functools.partial(unpool_kernel, at, len(own)), grid_spec=...  30.4 us
  transfers between devices with their start and end apart: 86, of which 27 were waited for; matrix products, arithmetic and copies ran while one was open for 19% of the time, Pallas kernels for 24%

profile of v2, /device:TPU:0, one launch (start us, length us, event | category | flops | bytes accessed | tf_op | source)
XLA Modules:
  0.0 732.0 jit_solution(8372837576914484700)
XLA Ops:
  18.0 6.5 pool.2
  36.8 24.4 %pool.3 = (bf16[128,4608]{1,0:T(8,128)(2,1)}, bf16[128,4608]{1,0:T(8,128)(2,1)}, bf16[128,4608]{1,0:T(8,128)(2,1)}, bf16[128,4608]{1,0:T(8,128)(2,1)}, f32[2,128,9216]{2,1,0:T(8,128)}) custom-call(s32[128]{0:T(128)} %group.7, bf16[2,96,338]{2,1,0:T(8,128)(2,1)} %copy.46.table, ...), custom_call_target="tpu_custom_call", output_to_operand_aliasing={{0}: (4, {}), {1}: (5, {}), {2}: (6, {}), {3}: (7, {}), {4}... | custom-call | flops 1000 | bytes 1000 | tf_op jit(solution)/shard_map/pool/pallas_call | solution.py:143
  74.9 17.2 %collective-permute-done.9.refs_23_.refs_3_ = bf16[2304,256]{1,0:T(8,128)(2,1)} collective-permute-done((bf16[2304,256]{1,0:T(8,128)(2,1)}, bf16[2304,256]{1,0:T(8,128)(2,1)}, u32[]{:S(2)}, u32[]{:S(2)}) %collective-permute-start.9) | collective-permute-done | bytes 1179680 | tf_op jit(solution)/shard_map/ppermute | solution.py:52
  104.9 19.9 %collective-permute-done.13.refs_18_.refs_2_ = bf16[2304,256]{1,0:T(8,128)(2,1)S(1)} collective-permute-done((bf16[2304,256]{1,0:T(8,128)(2,1)}, bf16[2304,256]{1,0:T(8,128)(2,1)S(1)}, u32[]{:S(2)}, u32[]{:S(2)}) %collective-permute-start.13) | collective-permute-done | bytes 1179680 | tf_op jit(solution)/shard_map/ppermute | solution.py:52
  137.1 15.7 %collective-permute-done.16.refs_24_.refs_4_ = bf16[2304,256]{1,0:T(8,128)(2,1)} collective-permute-done((bf16[2304,256]{1,0:T(8,128)(2,1)}, bf16[2304,256]{1,0:T(8,128)(2,1)}, u32[]{:S(2)}, u32[]{:S(2)}) %collective-permute-start.16) | collective-permute-done | bytes 1179680 | tf_op jit(solution)/shard_map/ppermute | solution.py:52
  157.9 14.9 %collective-permute-done.20 = bf16[2,2,2,128,512]{4,3,2,0,1:T(8,128)(2,1)} collective-permute-done((bf16[2,2,2,128,512]{4,3,2,0,1:T(8,128)(2,1)}, bf16[2,2,2,128,512]{4,3,2,0,1:T(8,128)(2,1)}, u32[]{:S(2)}, u32[]{:S(2)}) %collective-permute-start.20) | collective-permute-done | bytes 1048608 | tf_op jit(solution)/shard_map/ppermute | solution.py:29
  177.4 5.4 collective-permute-start.24
  185.6 16.2 %collective-permute-done.24.refs_26_.refs_25_.refs_7_.refs_4_ = bf16[2304,256]{1,0:T(8,128)(2,1)} collective-permute-done((bf16[2304,256]{1,0:T(8,128)(2,1)}, bf16[2304,256]{1,0:T(8,128)(2,1)}, u32[]{:S(2)}, u32[]{:S(2)}) %collective-permute-start.24) | collective-permute-done | bytes 1179680 | tf_op jit(solution)/shard_map/ppermute | solution.py:52
  201.9 11.4 %collective-permute-done.21.refs_7_ = bf16[128,4608]{1,0:T(8,128)(2,1)} collective-permute-done((bf16[128,4608]{1,0:T(8,128)(2,1)}, bf16[128,4608]{1,0:T(8,128)(2,1)}, u32[]{:S(2)}, u32[]{:S(2)}) %collective-permute-start.21) | collective-permute-done | bytes 1179680 | tf_op jit(solution)/shard_map/ppermute | solution.py:29
  224.4 33.1 %chunk.2 = (bf16[1024,512]{1,0:T(8,128)(2,1)}, bf16[1024,512]{1,0:T(8,128)(2,1)}, f32[3,8,512]{2,1,0:T(8,128)}, f32[2304,256]{1,0:T(8,128)}, bf16[2304,256]{1,0:...) custom-call(s32[2]{0:T(128)} %pad_add_fusion.1.roles, ...), custom_call_target="tpu_custom_call" | custom-call | flops 1000 | bytes 1000 | tf_op jit(solution)/shard_map/chunk/pallas_call | solution.py:438
  266.7 20.5 %collective-permute-done.30.refs_24_.refs_6_ = bf16[2304,256]{1,0:T(8,128)(2,1)S(1)} collective-permute-done((bf16[2304,256]{1,0:T(8,128)(2,1)S(1)}, bf16[2304,256]{1,0:T(8,128)(2,1)S(1)}, u32[]{:S(2)}, u32[]{:S(2)}) %collective-permute-start.30) | collective-permute-done | bytes 1179680 | tf_op jit(solution)/shard_map/ppermute | solution.py:52
  302.0 11.2 %collective-permute-done.32.refs_19_.refs_6_ = bf16[2304,256]{1,0:T(8,128)(2,1)S(1)} collective-permute-done((bf16[2304,256]{1,0:T(8,128)(2,1)}, bf16[2304,256]{1,0:T(8,128)(2,1)S(1)}, u32[]{:S(2)}, u32[]{:S(2)}) %collective-permute-start.32) | collective-permute-done | bytes 1179680 | tf_op jit(solution)/shard_map/ppermute | solution.py:52
  322.5 16.8 %collective-permute-done.36.refs_26_.refs_8_ = bf16[2304,256]{1,0:T(8,128)(2,1)S(1)} collective-permute-done((bf16[2304,256]{1,0:T(8,128)(2,1)}, bf16[2304,256]{1,0:T(8,128)(2,1)S(1)}, u32[]{:S(2)}, u32[]{:S(2)}) %collective-permute-start.36) | collective-permute-done | bytes 1179680 | tf_op jit(solution)/shard_map/ppermute | solution.py:52
  342.4 23.3 %collective-permute-done.38.refs_21_.refs_6_ = bf16[2304,256]{1,0:T(8,128)(2,1)S(1)} collective-permute-done((bf16[2304,256]{1,0:T(8,128)(2,1)}, bf16[2304,256]{1,0:T(8,128)(2,1)S(1)}, u32[]{:S(2)}, u32[]{:S(2)}) %collective-permute-start.38) | collective-permute-done | bytes 1179680 | tf_op jit(solution)/shard_map/ppermute | solution.py:52
  371.2 20.4 %collective-permute-done.39.refs_28_.refs_8_ = bf16[2304,256]{1,0:T(8,128)(2,1)S(1)} collective-permute-done((bf16[2304,256]{1,0:T(8,128)(2,1)S(1)}, bf16[2304,256]{1,0:T(8,128)(2,1)S(1)}, u32[]{:S(2)}, u32[]{:S(2)}) %collective-permute-start.39) | collective-permute-done | bytes 1179680 | tf_op jit(solution)/shard_map/ppermute | solution.py:52
  394.7 33.0 %chunk.3 = (bf16[1024,512]{1,0:T(8,128)(2,1)}, bf16[1024,512]{1,0:T(8,128)(2,1)}, f32[3,8,512]{2,1,0:T(8,128)}, f32[2304,256]{1,0:T(8,128)}, bf16[2304,256]{1,0:...) custom-call(s32[2]{0:T(128)} %pad_add_fusion.1.roles, ...), custom_call_target="tpu_custom_call" | custom-call | flops 1000 | bytes 1000 | tf_op jit(solution)/shard_map/chunk/pallas_call | solution.py:438
  430.6 10.8 %back.4 = (f32[512,2304]{1,0:T(8,128)}, bf16[512,2304]{1,0:T(8,128)(2,1)}) custom-call(s32[2]{0:T(128)} %pad_add_fusion.1.roles, bf16[1024,512]{1,0:T(8,128)(2,1)} %get-tuple-element.441.refs_0_, bf16[1024,512]{1,0:T(8,128)(2,1)} %get-tuple-element.392.refs_1_, bf16[2304,256]{1,0:T(8,128)(2,1)} %copy-done.18, ...), custom_call_target="tpu_custom_call" | custom-call | flops 1000 | bytes 1000 | tf_op jit(solution)/shard_map/back/pallas_call | solution.py:516
  445.7 4.9 broadcast_in_dim.5
  459.2 10.6 %back.5 = (f32[512,2304]{1,0:T(8,128)}, bf16[512,2304]{1,0:T(8,128)(2,1)}) custom-call(s32[2]{0:T(128)} %pad_add_fusion.1.roles, bf16[1024,512]{1,0:T(8,128)(2,1)} %get-tuple-element.441.refs_0_, bf16[1024,512]{1,0:T(8,128)(2,1)} %get-tuple-element.392.refs_1_, bf16[2304,256]{1,0:T(8,128)(2,1)} %copy-done.37, ...), custom_call_target="tpu_custom_call" | custom-call | flops 1000 | bytes 1000 | tf_op jit(solution)/shard_map/back/pallas_call | solution.py:516
  477.9 20.8 %collective-permute-done.43 = bf16[1024,512]{1,0:T(8,128)(2,1)} collective-permute-done((bf16[1024,512]{1,0:T(8,128)(2,1)}, bf16[1024,512]{1,0:T(8,128)(2,1)}, u32[]{:S(2)}, u32[]{:S(2)}) %collective-permute-start.43) | collective-permute-done | bytes 1048608 | tf_op jit(solution)/shard_map/ppermute | solution.py:29
  498.7 4.4 collective-permute-start.51
  505.6 10.7 %back.6 = (f32[512,2304]{1,0:T(8,128)}, bf16[512,2304]{1,0:T(8,128)(2,1)}) custom-call(s32[2]{0:T(128)} %pad_add_fusion.1.roles, bf16[1024,512]{1,0:T(8,128)(2,1)} %get-tuple-element.441.refs_0_, bf16[1024,512]{1,0:T(8,128)(2,1)} %get-tuple-element.392.refs_1_, bf16[2304,256]{1,0:T(8,128)(2,1)} %copy-done.38, ...), custom_call_target="tpu_custom_call" | custom-call | flops 1000 | bytes 1000 | tf_op jit(solution)/shard_map/back/pallas_call | solution.py:516
  531.6 6.1 collective-permute-start.55
  540.9 10.5 %back.7 = (f32[512,2304]{1,0:T(8,128)}, bf16[512,2304]{1,0:T(8,128)(2,1)}) custom-call(s32[2]{0:T(128)} %pad_add_fusion.1.roles, bf16[1024,512]{1,0:T(8,128)(2,1)} %get-tuple-element.441.refs_0_, bf16[1024,512]{1,0:T(8,128)(2,1)} %get-tuple-element.392.refs_1_, bf16[2304,256]{1,0:T(8,128)(2,1)} %copy-done.2, bf16[2304,256]{1,0:T(8,128)(2,1)} %copy-done.17, ...), custom_call_target="tpu_custom_call" | custom-call | flops 1000 | bytes 1000 | tf_op jit(solution)/shard_map/back/pallas_call | solution.py:516
  570.7 6.1 collective-permute-start.61
  589.5 8.5 %collective-permute-done.58 = bf16[256,2304]{1,0:T(8,128)(2,1)S(1)} collective-permute-done((bf16[256,2304]{1,0:T(8,128)(2,1)S(1)}, bf16[256,2304]{1,0:T(8,128)(2,1)S(1)}, u32[]{:S(2)}, u32[]{:S(2)}) %collective-permute-start.58) | collective-permute-done | bytes 1179680 | tf_op jit(solution)/shard_map/ppermute | solution.py:29
  615.3 7.3 first_grad.2
  631.0 5.9 collective-permute-done.64
  651.2 7.3 first_grad.3
  659.5 15.3 %unpool.2.refs_8_ = bf16[128,169,2,256]{3,2,1,0:T(2,128)(2,1)} custom-call(s32[128]{0:T(128)} %group.7, bf16[2,352,192]{2,1,0:T(8,128)(2,1)} %fusion.10.table, f32[4,256]{1,0:T(4,128)} %reshape.617.first, f32[128,2304]{1,0:T(8,128)} %slice.177.refs_0_, f32[128,2304]{1,0:T(8,128)} %slice.180.refs_1_, f32[128,2304]{1,0:T(8,128)} %slice.183.refs_0_.refs_2_, ...), custom_call_target="tpu_custom_call" | custom-call | flops 1000 | bytes 1000 | tf_op jit(solution)/shard_map/unpool/pallas_call | solution.py:256
  685.8 15.2 %unpool.3 = bf16[128,169,2,256]{3,2,1,0:T(2,128)(2,1)} custom-call(s32[128]{0:T(128)} %group.7, bf16[2,352,192]{2,1,0:T(8,128)(2,1)} %fusion.10.table, f32[4,256]{1,0:T(4,128)} %reshape.617.first, f32[128,2304]{1,0:T(8,128)} %slice.177.refs_0_, f32[128,2304]{1,0:T(8,128)} %slice.180.refs_1_, ...), custom_call_target="tpu_custom_call", output_to_operand_aliasing={{}: (11, {})} | custom-call | flops 1000 | bytes 1000 | tf_op jit(solution)/shard_map/unpool/pallas_call | solution.py:256
  704.1 12.1 %collective-permute-done.75 = f32[2,2,256]{2,1,0:T(2,128)S(1)} collective-permute-done((f32[2,2,256]{2,1,0:T(2,128)S(1)}, f32[2,2,256]{2,1,0:T(2,128)S(1)}, u32[]{:S(2)}, u32[]{:S(2)}) %collective-permute-start.75) | collective-permute-done | bytes 4128 | tf_op jit(solution)/shard_map/ppermute | solution.py:29
  (470 shorter events, 270.0 us)
Async XLA Ops:
  7.2 217.1 %all-gather.9.cloned.1.call-start = ((), (), s32[]{:S(2)}) async-start(), calls=%async_computation.1 | async-start | bytes 3538944 | tf_op jit(solution)/shard_map/all_gather | solution.py:88
  27.4 36.9 %collective-permute-start.5 = (bf16[2304,256]{1,0:T(8,128)(2,1)S(1)}, bf16[2304,256]{1,0:T(8,128)(2,1)S(1)}, u32[]{:S(2)}, u32[]{:S(2)}) collective-permute-start(bf16[2304,256]{1,0:T(8,128)(2,1)S(1)} %maximum_select_fusion.1.refs_16_.refs_2_), channel_id=1, source_target_pairs={{0,8},{4,12},{8,0},{12,4},{16,24},{20,28},{24,16},{28,20},{1,9},{5... | collective-permute-start | bytes 3538952 | tf_op jit(solution)/shard_map/ppermute | solution.py:52
  29.3 38.4 %collective-permute-start.4 = (bf16[2304,256]{1,0:T(8,128)(2,1)S(1)}, bf16[2304,256]{1,0:T(8,128)(2,1)}, u32[]{:S(2)}, u32[]{:S(2)}) collective-permute-start(bf16[2304,256]{1,0:T(8,128)(2,1)S(1)} %maximum_select_fusion.1.refs_16_.refs_2_), channel_id=1, source_target_pairs={{8,16},{12,20},{16,8},{20,12},{9,17},{13,21},{17,9},{21,13},{10,18... | collective-permute-start | bytes 3538952 | tf_op jit(solution)/shard_map/ppermute | solution.py:52
  31.0 30.2 %collective-permute-start.3 = (bf16[1152,256]{1,0:T(8,128)(2,1)}, bf16[1152,256]{1,0:T(8,128)(2,1)}, u32[]{:S(2)}, u32[]{:S(2)}) collective-permute-start(bf16[1152,256]{1,0:T(8,128)(2,1)} %get-tuple-element.269), channel_id=1, source_target_pairs={{0,4},{4,0},{8,12},{12,8},{16,20},{20,16},{24,28},{28,24},{1,5},{5... | collective-permute-start | bytes 1769480 | tf_op jit(solution)/shard_map/ppermute | solution.py:29
  35.4 34.1 %collective-permute-start.2 = (bf16[2,2,128,512]{3,2,1,0:T(8,128)(2,1)}, bf16[2,2,128,512]{3,2,1,0:T(8,128)(2,1)}, u32[]{:S(2)}, u32[]{:S(2)}) collective-permute-start(bf16[2,2,128,512]{3,2,1,0:T(8,128)(2,1)} %get-tuple-element.270), channel_id=1, source_target_pairs={{0,4},{4,0},{8,12},{12,8},{16,20},{20,16},{24,28},{28,24},{1,5},{5... | collective-permute-start | bytes 1572872 | tf_op jit(solution)/shard_map/ppermute | solution.py:29
  96.3 128.0 %all-gather.7.cloned.1.call-start = ((), (), s32[]{:S(2)}) async-start(), calls=%async_computation | async-start | bytes 3538944 | tf_op jit(solution)/shard_map/all_gather | solution.py:88
  97.1 127.2 %all-gather.11.cloned.1.call-start = ((), (), s32[]{:S(2)}) async-start(), calls=%async_computation.2 | async-start | bytes 3538944 | tf_op jit(solution)/shard_map/all_gather | solution.py:88
  97.8 126.5 %all-gather.15.cloned.1.call-start = ((), (), s32[]{:S(2)}) async-start(), calls=%async_computation.4 | async-start | bytes 3538944 | tf_op jit(solution)/shard_map/all_gather | solution.py:88
  98.4 126.0 %all-gather.13.cloned.1.call-start = ((), (), s32[]{:S(2)}) async-start(), calls=%async_computation.3 | async-start | bytes 3538944 | tf_op jit(solution)/shard_map/all_gather | solution.py:88
  133.1 91.3 %all-gather.17.cloned.1.call-start = ((), (), s32[]{:S(2)}) async-start(), calls=%async_computation.5 | async-start | bytes 3538944 | tf_op jit(solution)/shard_map/all_gather | solution.py:88
  152.8 30.1 %collective-permute-start.18 = (bf16[2304,256]{1,0:T(8,128)(2,1)S(1)}, bf16[2304,256]{1,0:T(8,128)(2,1)}, u32[]{:S(2)}, u32[]{:S(2)}) collective-permute-start(bf16[2304,256]{1,0:T(8,128)(2,1)S(1)} %maximum_select_fusion.3.refs_16_.refs_4_), channel_id=1, source_target_pairs={{8,16},{12,20},{16,8},{20,12},{9,17},{13,21},{17,9},{21,13},{10,18... | collective-permute-start | bytes 3538952 | tf_op jit(solution)/shard_map/ppermute | solution.py:52
  154.5 30.1 %collective-permute-start.17 = (bf16[128,4608]{1,0:T(8,128)(2,1)}, bf16[128,4608]{1,0:T(8,128)(2,1)}, u32[]{:S(2)}, u32[]{:S(2)}) collective-permute-start(bf16[128,4608]{1,0:T(8,128)(2,1)} %copy-done.16), channel_id=1, source_target_pairs={{0,4},{4,0},{8,12},{12,8},{16,20},{20,16},{24,28},{28,24},{1,5},{5... | collective-permute-start | bytes 3538952 | tf_op jit(solution)/shard_map/ppermute | solution.py:29
  184.6 28.7 %collective-permute-start.21 = (bf16[128,4608]{1,0:T(8,128)(2,1)}, bf16[128,4608]{1,0:T(8,128)(2,1)}, u32[]{:S(2)}, u32[]{:S(2)}) collective-permute-start(bf16[128,4608]{1,0:T(8,128)(2,1)} %collective-permute-done.10.refs_3_), channel_id=1, source_target_pairs={{0,4},{4,0},{8,12},{12,8},{16,20},{20,16},{24,28},{28,24},{1,5},{5... | collective-permute-start | bytes 3538952 | tf_op jit(solution)/shard_map/ppermute | solution.py:29
  216.9 42.2 %collective-permute-start.28 = (bf16[2304,256]{1,0:T(8,128)(2,1)S(1)}, bf16[2304,256]{1,0:T(8,128)(2,1)}, u32[]{:S(2)}, u32[]{:S(2)}) collective-permute-start(bf16[2304,256]{1,0:T(8,128)(2,1)S(1)} %maximum_select_fusion.3.refs_16_.refs_4_), channel_id=1, source_target_pairs={{8,0},{12,4},{16,24},{20,28},{9,1},{13,5},{17,25},{21,29},{10,2},{... | collective-permute-start | bytes 3538952 | tf_op jit(solution)/shard_map/ppermute | solution.py:52
  218.2 44.3 %collective-permute-start.27 = (bf16[2304,256]{1,0:T(8,128)(2,1)S(1)}, bf16[2304,256]{1,0:T(8,128)(2,1)}, u32[]{:S(2)}, u32[]{:S(2)}) collective-permute-start(bf16[2304,256]{1,0:T(8,128)(2,1)S(1)} %collective-permute-done.19.refs_20_.refs_18_.refs_5_.refs_2_), channel_id=1, source_target_pairs={{8,16},{12,20},{16,8},{20,12},{9,17},{13,21},{17,9},{21,13},{10,18... | collective-permute-start | bytes 3538952 | tf_op jit(solution)/shard_map/ppermute | solution.py:52
  223.2 40.7 %collective-permute-start.26 = (bf16[2,2,128,512]{3,2,1,0:T(8,128)(2,1)}, bf16[2,2,128,512]{3,2,1,0:T(8,128)(2,1)}, u32[]{:S(2)}, u32[]{:S(2)}) collective-permute-start(bf16[2,2,128,512]{3,2,1,0:T(8,128)(2,1)} %get-tuple-element.334), channel_id=1, source_target_pairs={{0,4},{4,0},{8,12},{12,8},{16,20},{20,16},{24,28},{28,24},{1,5},{5... | collective-permute-start | bytes 1572872 | tf_op jit(solution)/shard_map/ppermute | solution.py:29
  391.6 39.0 %collective-permute-start.41 = (bf16[2304,256]{1,0:T(8,128)(2,1)}, bf16[2304,256]{1,0:T(8,128)(2,1)S(1)}, u32[]{:S(2)}, u32[]{:S(2)}) collective-permute-start(bf16[2304,256]{1,0:T(8,128)(2,1)} %fusion.4), channel_id=1, source_target_pairs={{0,8},{4,12},{8,0},{12,4},{16,24},{20,28},{24,16},{28,20},{1,9},{5... | collective-permute-start | bytes 3538952 | tf_op jit(solution)/shard_map/ppermute | solution.py:52
  393.5 37.0 %collective-permute-start.42 = (bf16[2304,256]{1,0:T(8,128)(2,1)S(1)}, bf16[2304,256]{1,0:T(8,128)(2,1)S(1)}, u32[]{:S(2)}, u32[]{:S(2)}) collective-permute-start(bf16[2304,256]{1,0:T(8,128)(2,1)S(1)} %add_convert_fusion.7), channel_id=1, source_target_pairs={{8,16},{12,20},{16,8},{20,12},{9,17},{13,21},{17,9},{21,13},{10,18... | collective-permute-start | bytes 3538952 | tf_op jit(solution)/shard_map/ppermute | solution.py:52
  472.8 43.5 %collective-permute-start.46 = (bf16[512,2304]{1,0:T(8,128)(2,1)}, bf16[512,2304]{1,0:T(8,128)(2,1)}, u32[]{:S(2)}, u32[]{:S(2)}) collective-permute-start(bf16[512,2304]{1,0:T(8,128)(2,1)} %get-tuple-element.417), channel_id=1, source_target_pairs={{0,1},{1,0},{2,3},{3,2},{4,5},{5,4},{6,7},{7,6},{8,9},{9,8},{10,11... | collective-permute-start | bytes 7077896 | tf_op jit(solution)/shard_map/ppermute | solution.py:29
  474.5 31.1 %collective-permute-start.47 = (bf16[1152,256]{1,0:T(8,128)(2,1)S(1)}, bf16[1152,256]{1,0:T(8,128)(2,1)S(1)}, u32[]{:S(2)}, u32[]{:S(2)}) collective-permute-start(bf16[1152,256]{1,0:T(8,128)(2,1)S(1)} %dynamic-slice_convert_fusion.3), channel_id=1, source_target_pairs={{0,4},{4,0},{8,12},{12,8},{16,20},{20,16},{24,28},{28,24},{1,5},{5... | collective-permute-start | bytes 1769480 | tf_op jit(solution)/shard_map/ppermute | solution.py:29
  476.8 48.8 %collective-permute-start.49 = (bf16[256,2304]{1,0:T(8,128)(2,1)}, bf16[256,2304]{1,0:T(8,128)(2,1)}, u32[]{:S(2)}, u32[]{:S(2)}) collective-permute-start(bf16[256,2304]{1,0:T(8,128)(2,1)} %slice.204), channel_id=1, source_target_pairs={{0,4},{4,0},{8,12},{12,8},{16,20},{20,16},{24,28},{28,24},{1,5},{5... | collective-permute-start | bytes 3538952 | tf_op jit(solution)/shard_map/ppermute | solution.py:29
  498.7 29.2 %collective-permute-start.51 = (bf16[2304,256]{1,0:T(8,128)(2,1)S(1)}, bf16[2304,256]{1,0:T(8,128)(2,1)}, u32[]{:S(2)}, u32[]{:S(2)}) collective-permute-start(bf16[2304,256]{1,0:T(8,128)(2,1)S(1)} %copy-done.50), channel_id=1, source_target_pairs={{0,8},{4,12},{24,16},{28,20},{1,9},{5,13},{25,17},{29,21},{2,10},{... | collective-permute-start | bytes 3538952 | tf_op jit(solution)/shard_map/ppermute | solution.py:52
  531.6 30.7 %collective-permute-start.55 = (bf16[2304,256]{1,0:T(8,128)(2,1)S(1)}, bf16[2304,256]{1,0:T(8,128)(2,1)}, u32[]{:S(2)}, u32[]{:S(2)}) collective-permute-start(bf16[2304,256]{1,0:T(8,128)(2,1)S(1)} %copy-done.49), channel_id=1, source_target_pairs={{0,8},{4,12},{24,16},{28,20},{1,9},{5,13},{25,17},{29,21},{2,10},{... | collective-permute-start | bytes 3538952 | tf_op jit(solution)/shard_map/ppermute | solution.py:52
  570.7 31.6 %collective-permute-start.61 = (bf16[2304,256]{1,0:T(8,128)(2,1)S(1)}, bf16[2304,256]{1,0:T(8,128)(2,1)S(1)}, u32[]{:S(2)}, u32[]{:S(2)}) collective-permute-start(bf16[2304,256]{1,0:T(8,128)(2,1)S(1)} %copy-done.48), channel_id=1, source_target_pairs={{0,8},{4,12},{24,16},{28,20},{1,9},{5,13},{25,17},{29,21},{2,10},{... | collective-permute-start | bytes 3538952 | tf_op jit(solution)/shard_map/ppermute | solution.py:52
  577.5 30.6 %collective-permute-start.60 = (bf16[128,2304]{1,0:T(8,128)(2,1)S(1)}, bf16[128,2304]{1,0:T(8,128)(2,1)S(1)}, u32[]{:S(2)}, u32[]{:S(2)}) collective-permute-start(bf16[128,2304]{1,0:T(8,128)(2,1)S(1)} %copy-done.61), channel_id=1, source_target_pairs={{0,2},{1,3},{2,0},{3,1},{4,6},{5,7},{6,4},{7,5},{8,10},{9,11},{10,... | collective-permute-start | bytes 1769480 | tf_op jit(solution)/shard_map/ppermute | solution.py:29
  602.2 28.7 %collective-permute-start.63 = (bf16[2304,256]{1,0:T(8,128)(2,1)}, bf16[2304,256]{1,0:T(8,128)(2,1)}, u32[]{:S(2)}, u32[]{:S(2)}) collective-permute-start(bf16[2304,256]{1,0:T(8,128)(2,1)} %fusion.6), channel_id=1, source_target_pairs={{0,8},{4,12},{8,0},{12,4},{16,24},{20,28},{24,16},{28,20},{1,9},{5... | collective-permute-start | bytes 3538952 | tf_op jit(solution)/shard_map/ppermute | solution.py:52
  639.5 35.2 %collective-permute-start.73 = (bf16[2304,256]{1,0:T(8,128)(2,1)}, bf16[2304,256]{1,0:T(8,128)(2,1)}, u32[]{:S(2)}, u32[]{:S(2)}) collective-permute-start(bf16[2304,256]{1,0:T(8,128)(2,1)} %fusion.7), channel_id=1, source_target_pairs={{0,8},{4,12},{8,0},{12,4},{16,24},{20,28},{24,16},{28,20},{1,9},{5... | collective-permute-start | bytes 3538952 | tf_op jit(solution)/shard_map/ppermute | solution.py:52
  640.1 39.9 %collective-permute-start.70 = (f32[3,1024]{1,0:T(4,128)S(1)}, f32[3,1024]{1,0:T(4,128)S(1)}, u32[]{:S(2)}, u32[]{:S(2)}) collective-permute-start(f32[3,1024]{1,0:T(4,128)S(1)} %add.350), channel_id=1, source_target_pairs={{0,4},{4,0},{8,12},{12,8},{16,20},{20,16},{24,28},{28,24},{1,5},{5... | collective-permute-start | bytes 36872 | tf_op jit(solution)/shard_map/ppermute | solution.py:29
  644.4 36.2 %collective-permute-start.69 = (bf16[1152,256]{1,0:T(8,128)(2,1)S(1)}, bf16[1152,256]{1,0:T(8,128)(2,1)S(1)}, u32[]{:S(2)}, u32[]{:S(2)}) collective-permute-start(bf16[1152,256]{1,0:T(8,128)(2,1)S(1)} %dynamic-slice_convert_fusion.1), channel_id=1, source_target_pairs={{0,4},{4,0},{8,12},{12,8},{16,20},{20,16},{24,28},{28,24},{1,5},{5... | collective-permute-start | bytes 1769480 | tf_op jit(solution)/shard_map/ppermute | solution.py:29
  645.6 35.0 %collective-permute-start.68 = (bf16[1152,256]{1,0:T(8,128)(2,1)S(1)}, bf16[1152,256]{1,0:T(8,128)(2,1)S(1)}, u32[]{:S(2)}, u32[]{:S(2)}) collective-permute-start(bf16[1152,256]{1,0:T(8,128)(2,1)S(1)} %dynamic-slice_convert_fusion.2), channel_id=1, source_target_pairs={{0,4},{4,0},{8,12},{12,8},{16,20},{20,16},{24,28},{28,24},{1,5},{5... | collective-permute-start | bytes 1769480 | tf_op jit(solution)/shard_map/ppermute | solution.py:29
  650.3 30.9 %collective-permute-start.67 = (bf16[2,2,128,512]{3,2,0,1:T(8,128)(2,1)}, bf16[2,2,128,512]{3,2,0,1:T(8,128)(2,1)}, u32[]{:S(2)}, u32[]{:S(2)}) collective-permute-start(bf16[2,2,128,512]{3,2,0,1:T(8,128)(2,1)} %bitcast.60), channel_id=1, source_target_pairs={{0,4},{4,0},{8,12},{12,8},{16,20},{20,16},{24,28},{28,24},{1,5},{5... | collective-permute-start | bytes 1572872 | tf_op jit(solution)/shard_map/ppermute | solution.py:29
  680.0 38.0 %collective-permute-start.79 = (f32[2,1024]{1,0:T(2,128)S(1)}, f32[2,1024]{1,0:T(2,128)S(1)}, u32[]{:S(2)}, u32[]{:S(2)}) collective-permute-start(f32[2,1024]{1,0:T(2,128)S(1)} %pad_maximum_fusion.4), channel_id=1, source_target_pairs={{0,2},{1,3},{2,0},{3,1},{4,6},{5,7},{6,4},{7,5},{8,10},{9,11},{10,... | collective-permute-start | bytes 24584 | tf_op jit(solution)/shard_map/ppermute | solution.py:29
  (133 other events, 2265.8 us)
Sparse Core Ops, SparseCore 0:
  96.4 9.5 all-gather.8
  108.1 12.1 all-gather.6
  121.8 12.1 all-gather.10
  135.4 12.1 all-gather.14
  149.0 12.1 all-gather.12
  185.8 10.0 all-gather.16

commit v3 on v2

v3 whole, which is shorter than its diff:
```python
import functools

import jax
import jax.numpy as jnp
from jax import lax
from jax.experimental import pallas as pl
from jax.experimental.pallas import tpu as pltpu
from jax.sharding import PartitionSpec as P

F32 = jnp.float32
BF16 = jnp.bfloat16
POOLED = 36
PITCH = 48
LANES = 128
VMEM_LIMIT = 56 * 1024 * 1024
SMALL = pl.CostEstimate(flops=1000, bytes_accessed=1000, transcendentals=0)
AHEAD = 2
IMAGE_BLOCK = 16
HALVES = 2


def params():
    return pltpu.CompilerParams(vmem_limit_bytes=VMEM_LIMIT)


def flipped(value, axis, bit):
    pairs = [(source, source ^ bit) for source in range(lax.axis_size(axis))]
    return lax.ppermute(value, axis, pairs)


def x_swap(value):
    return flipped(value, "batch", 1)


def y_swap(value):
    return flipped(value, "tower", 2)


def c_swap(value):
    return flipped(value, "tower", 1)


def line(value, kind):
    steps = {
        "near": ((0, 1), (1, 0), (2, 3), (3, 2)),
        "middle": ((1, 2), (2, 1)),
        "outward": ((1, 0), (2, 3)),
        "inward": ((0, 1), (3, 2)),
    }[kind]
    pairs = [(2 * a + x, 2 * b + x) for a, b in steps for x in range(2)]
    return lax.ppermute(value, "batch", pairs)


def slab_groups():
    size = lax.axis_size("batch")
    return [list(range(x, size, 2)) for x in range(2)]


def after(value, *others):
    return lax.optimization_barrier((value, *others))[0]


class Order:
    def __init__(self):
        self.last = None

    def then(self, value):
        return value if self.last is None else after(value, self.last)

    def did(self, value):
        self.last = value
        return value


def is_line():
    return lax.axis_size("batch") == 8


def line_order(z):
    rows = jnp.array([[0, 1, 2, 3], [1, 0, 2, 3], [2, 3, 1, 0], [3, 2, 1, 0]])
    return rows[z]


def core_groups():
    return [[t, t + 1] for t in range(0, lax.axis_size("tower"), 2)]


def both_cores(value):
    return lax.all_gather(value, "tower", axis=0, tiled=True, axis_index_groups=core_groups())


def pool_table(order):
    map_pos = jnp.arange(169)[None, :]
    prow = (order // 6)[:, None]
    pcol = (order % 6)[:, None]
    qrow = map_pos // 13
    qcol = map_pos % 13
    inside = (
        (qrow >= 2 * prow) & (qrow <= 2 * prow + 2) & (qcol >= 2 * pcol) & (qcol <= 2 * pcol + 2)
    )
    small = (prow < 5) & (pcol < 5)
    table = jnp.stack([inside, inside & small]).astype(BF16)
    table = jnp.pad(table, ((0, 0), (0, PITCH - POOLED), (0, 0)))
    both = table[:, None, :, :, None] * jnp.eye(2, dtype=BF16)[None, :, None, None, :]
    return both.reshape(2, 2 * PITCH, 338)


def pool_kernel(start, group, table, first, maps, *refs):
    *feature_outs, pooled_out, own, other, pool0, pool1 = refs[-(2 * HALVES + 5) :]
    count, places, _, ch = maps.shape
    base = (start + pl.program_id(0)) * count

    def image(n, carry):
        window = table[group[base + n]]
        rows_in = maps[n].reshape(2 * places, ch)
        both = jnp.dot(window, rows_in, preferred_element_type=F32) * (1.0 / 9.0)
        p0, p1 = both[:PITCH], both[PITCH:]
        rows = pl.ds(pl.multiple_of(n * PITCH, PITCH), PITCH)
        mixed0 = first[0:1, :] * p0 + first[1:2, :] * p1
        mixed1 = first[2:3, :] * p0 + first[3:4, :] * p1
        for hold, value in ((pool0, p0), (pool1, p1), (own, mixed0), (other, mixed1)):
            for h in range(ch // LANES):
                hold[h, rows, :] = value[:, h * LANES : (h + 1) * LANES]
        return carry

    lax.fori_loop(0, count, image, 0, unroll=2)
    per = POOLED // HALVES
    for p in range(POOLED):
        rows = pl.ds(p, count, stride=PITCH)
        for h in range(ch // LANES):
            lanes = slice(p * ch + h * LANES, p * ch + (h + 1) * LANES)
            part = slice((p % per) * ch + h * LANES, (p % per) * ch + (h + 1) * LANES)
            feature_outs[p // per][:, part] = own[h, rows, :].astype(BF16)
            feature_outs[HALVES + p // per][:, part] = other[h, rows, :].astype(BF16)
            pooled_out[0, :, lanes] = pool0[h, rows, :]
            pooled_out[1, :, lanes] = pool1[h, rows, :]


def pool(convmaps, group, table, first, at, steps, before=()):
    count, _, places, ch = convmaps.shape
    nb = IMAGE_BLOCK
    feats = POOLED * ch
    features = [((count, feats // HALVES), BF16)] * (2 * HALVES)
    return pl.pallas_call(
        functools.partial(pool_kernel, at),
        grid_spec=pltpu.PrefetchScalarGridSpec(
            num_scalar_prefetch=1,
            grid=(steps,),
            in_specs=[
                pl.BlockSpec(table.shape, lambda i, g: (0, 0, 0)),
                pl.BlockSpec((4, ch), lambda i, g: (0, 0)),
                pl.BlockSpec((nb, places, 2, ch), lambda i, g: (at + i, 0, 0, 0)),
            ]
            + [pl.BlockSpec(memory_space=pl.ANY)] * len(before),
            out_specs=[pl.BlockSpec((nb, feats // HALVES), lambda i, g: (at + i, 0))] * (2 * HALVES)
            + [pl.BlockSpec((2, nb, feats), lambda i, g: (0, at + i, 0))],
            scratch_shapes=[pltpu.VMEM((ch // LANES, nb * PITCH, LANES), F32)] * 4,
        ),
        out_shape=[jax.ShapeDtypeStruct(*f) for f in features]
        + [jax.ShapeDtypeStruct((2, count, feats), F32)],
        input_output_aliases={4 + i: i for i in range(len(before))},
        compiler_params=params(),
        cost_estimate=SMALL,
        name="pool",
    )(group, table, first, jnp.swapaxes(convmaps, 1, 2), *before)


def first_grad_kernel(pooled, keep, came, other, out):
    ch = out.shape[2]

    @pl.when(pl.program_id(0) == 0)
    def _():
        out[...] = jnp.zeros_like(out)

    for a in range(2):
        sums = [0.0, 0.0]
        for p in range(POOLED):
            lanes = slice(p * ch, (p + 1) * ch)
            if a == 0:
                grad = keep[:, lanes].astype(F32) + came[:, lanes].astype(F32)
            else:
                grad = other[:, lanes].astype(F32)
            for s in range(2):
                sums[s] = sums[s] + grad * pooled[s, :, lanes]
        for s in range(2):
            out[2 * a + s] += sums[s]


def first_grad(pooled, keep, came, other, at):
    images, feats = keep.shape
    ch = feats // POOLED
    nb = IMAGE_BLOCK
    rows = pl.BlockSpec((nb, feats), lambda i: (i, 0))
    sums = pl.pallas_call(
        first_grad_kernel,
        grid=(images // nb,),
        in_specs=[pl.BlockSpec((2, nb, feats), lambda i: (0, at // nb + i, 0)), rows, rows, rows],
        out_specs=pl.BlockSpec((4, nb, ch), lambda i: (0, 0, 0)),
        out_shape=jax.ShapeDtypeStruct((4, nb, ch), F32),
        compiler_params=params(),
        cost_estimate=SMALL,
        name="first_grad",
    )(pooled, keep, came, other)
    return jnp.sum(sums, axis=1)


def unpool_kernel(start, group, table, first, keep_in, came_in, other_in, *refs):
    out, own, other = refs[-3:]
    count = out.shape[0]
    base = start + pl.program_id(0) * count
    ch = out.shape[3]
    places = out.shape[1]

    @pl.when(pl.program_id(0) == 0)
    def _():
        own[...] = jnp.zeros_like(own)
        other[...] = jnp.zeros_like(other)

    for p in range(POOLED):
        for h in range(ch // LANES):
            lanes = slice(p * ch + h * LANES, p * ch + (h + 1) * LANES)
            rows = pl.ds(p, count, stride=PITCH)
            own[h, rows, :] = keep_in[:, lanes].astype(F32) + came_in[:, lanes].astype(F32)
            other[h, rows, :] = other_in[:, lanes].astype(F32)

    def image(n, carry):
        window = table[group[base + n]]
        rows = pl.ds(pl.multiple_of(n * PITCH, PITCH), PITCH)
        g0, g1 = (
            jnp.concatenate([hold[h, rows, :] for h in range(ch // LANES)], axis=1) for hold in (own, other)
        )
        highs, lows = [], []
        for s in range(2):
            grad = (first[s : s + 1, :] * g0 + first[2 + s : 3 + s, :] * g1) * (1.0 / 9.0)
            highs.append(grad.astype(BF16))
            lows.append((grad - highs[s].astype(F32)).astype(BF16))
        parts = jnp.concatenate(highs + lows, axis=0)
        spread = jnp.dot(window, parts, preferred_element_type=F32).astype(BF16)
        out[n] = spread[: 2 * places].reshape(places, 2, ch)
        return carry

    lax.fori_loop(0, count, image, 0, unroll=2)


def unpool(keep, came, other, group, table, first, places, at, count, before=()):
    images, feats = keep.shape
    ch = first.shape[1]
    nb = IMAGE_BLOCK
    rows = pl.BlockSpec((nb, feats), lambda i, g: (i, 0))
    spread = jnp.swapaxes(table, 1, 2)
    spread = jnp.pad(jnp.concatenate([spread, spread], axis=2), ((0, 0), (0, 352 - 2 * places), (0, 0)))
    return pl.pallas_call(
        functools.partial(unpool_kernel, at),
        grid_spec=pltpu.PrefetchScalarGridSpec(
            num_scalar_prefetch=1,
            grid=(images // nb,),
            in_specs=[
                pl.BlockSpec(spread.shape, lambda i, g: (0, 0, 0)),
                pl.BlockSpec((4, ch), lambda i, g: (0, 0)),
                rows,
                rows,
                rows,
            ]
            + [pl.BlockSpec(memory_space=pl.ANY)] * len(before),
            out_specs=pl.BlockSpec((nb, places, 2, ch), lambda i, g: (at // nb + i, 0, 0, 0)),
            scratch_shapes=[pltpu.VMEM((ch // LANES, nb * PITCH, LANES), F32)] * 2,
        ),
        out_shape=jax.ShapeDtypeStruct((count, places, 2, ch), BF16),
        input_output_aliases={6: 0} if before else {},
        compiler_params=params(),
        cost_estimate=SMALL,
        name="unpool",
    )(group, spread, first, keep, came, other, *before)


def store_kernel(chunk, chunks, x, own, came, *refs):
    out, stay, go, sems = refs[-4:]
    rows, width = came.shape

    def columns(at):
        return out.at[:, pl.ds(pl.multiple_of(at * width, width), width)]

    source = own.at[pl.ds(pl.multiple_of(x[0] * rows, rows), rows), :]
    read = pltpu.make_async_copy(source, stay, sems.at[0])
    read.start()
    go[...] = came[...].astype(F32)
    write = pltpu.make_async_copy(go, columns((1 - x[0]) * chunks + chunk), sems.at[1])
    write.start()
    read.wait()
    write_own = pltpu.make_async_copy(stay, columns(x[0] * chunks + chunk), sems.at[2])
    write_own.start()
    write.wait()
    write_own.wait()


def store(own, came, x, chunk, chunks, shape, before=()):
    anywhere = pl.BlockSpec(memory_space=pl.ANY)
    return pl.pallas_call(
        functools.partial(store_kernel, chunk, chunks),
        in_specs=[pl.BlockSpec(memory_space=pltpu.SMEM), anywhere, pl.BlockSpec(memory_space=pltpu.VMEM)]
        + [anywhere] * len(before),
        out_specs=anywhere,
        out_shape=jax.ShapeDtypeStruct(shape, F32),
        scratch_shapes=[pltpu.VMEM(came.shape, F32)] * 2 + [pltpu.SemaphoreType.DMA((3,))],
        input_output_aliases={3: 0} if before else {},
        compiler_params=params(),
        cost_estimate=SMALL,
        name="store",
    )(x, own, came, *before)


def place_rows_kernel(places, *refs):
    *parts, out, sem = refs
    height, width = parts[0].shape[0] // 4, parts[0].shape[1]
    chunks = len(parts) // 2
    x, y, core = places[0], places[1], places[2]
    copies = []
    for i, part in enumerate(parts):
        side, j = i // chunks, i % chunks
        col = (jnp.where(x == side, 0, chunks) + j) * width
        cols = pl.ds(pl.multiple_of(col, width), width)
        for b in range(4):
            row = (2 * ((b % 2) ^ y) + ((b // 2) ^ core)) * height
            target = out.at[pl.ds(pl.multiple_of(row, height), height), cols]
            copies.append(pltpu.make_async_copy(part.at[pl.ds(b * height, height), :], target, sem.at[i, b]))
            copies[-1].start()
    for copy in copies:
        copy.wait()


def place_rows(places, own, other):
    parts = own + other
    rows, width = parts[0].shape
    return pl.pallas_call(
        place_rows_kernel,
        in_specs=[pl.BlockSpec(memory_space=pltpu.SMEM)] + [pl.BlockSpec(memory_space=pltpu.VMEM)] * len(parts),
        out_specs=pl.BlockSpec(memory_space=pl.ANY),
        out_shape=jax.ShapeDtypeStruct((rows, width * len(parts)), BF16),
        scratch_shapes=[pltpu.SemaphoreType.DMA((len(parts), 4))],
        compiler_params=params(),
        cost_estimate=SMALL,
        name="place_rows",
    )(places, *parts)


def tile_of(rows):
    return next(t for t in (1152, 768, 576, 512, 384, 256, 128) if rows % t == 0)


def fetch(outer, terms, rows, target, sem):
    def copy(term):
        return pltpu.make_async_copy(term.at[rows, :], target, sem)

    if len(terms) == 1:
        copy(terms[0]).start()
    else:
        pl.when(outer == 1)(lambda: copy(terms[0]).start())
        pl.when(outer == 0)(lambda: copy(terms[1]).start())


def chunk_kernel(layout, starts, cot_cols, roles, vectors, *refs):
    chunks, count = len(layout), len(layout[0])
    cots, refs = refs[:4], refs[4:]
    blocks = len(starts) // HALVES
    feats, refs = refs[: blocks * HALVES], refs[blocks * HALVES :]
    at = 0
    pieces = []
    for counts in layout:
        pieces.append([])
        for many in counts:
            pieces[-1].append(refs[at : at + many])
            at += many
    act_out, keep_out, send_out, sums_out = refs[at : at + 4]
    outs = [refs[at + 4 + i * count : at + 4 + (i + 1) * count] for i in range(chunks)]
    held, weight, total, dpre_out, k_own, k_other, high, low, in_sems, w_sems, cot_sems, out_sems = refs[-12:]
    steps, images, tile = held.shape
    per = steps // count
    units = total.shape[1] // chunks
    half, height = steps // HALVES, images // blocks

    def columns(i):
        return slice(i * units, (i + 1) * units)

    def begin(k):
        for s in range(count):

            @pl.when(k // per == s)
            def _(s=s):
                rows = pl.ds(pl.multiple_of((k - s * per) * tile, tile), tile)
                for i in range(chunks):
                    fetch(roles[0], pieces[i][s], rows, weight.at[k, :, columns(i)], w_sems.at[k])

        for h in range(HALVES):

            @pl.when(k // half == h)
            def _(h=h):
                cols = pl.ds(pl.multiple_of((k - h * half) * tile, tile), tile)
                for r in range(blocks):
                    at = r * HALVES + h
                    start = starts[at]
                    if start is None:
                        start = pl.multiple_of(roles[1] * height, height)
                    part = feats[at].at[pl.ds(start, height), cols]
                    rows = pl.ds(r * height, height)
                    pltpu.make_async_copy(part, held.at[k, rows, :], in_sems.at[k]).start()

    def arrive(target, sem):
        pltpu.make_async_copy(target, target, sem).wait()

    ahead = min(AHEAD, steps)
    for k in range(ahead):
        begin(jnp.int32(k))
    for tower, target in enumerate((k_own, k_other)):
        for r in range(blocks):
            core, x, y = r // 4, r // 2 % 2, r % 2
            source, col = cots[2 * tower + x], cot_cols[2 * tower + x]
            rows = pl.ds((2 * core + (y ^ tower)) * height, height)
            source = source.at[rows, pl.ds(col, total.shape[1])]
            target_rows = target.at[pl.ds(r * height, height), :]
            pltpu.make_async_copy(source, target_rows, cot_sems.at[tower]).start()
    total[...] = jnp.zeros_like(total)

    def forward_step(k, carry):
        pl.when(k + ahead < steps)(lambda: begin(k + ahead))
        arrive(held.at[k], in_sems.at[k])
        arrive(weight.at[k], w_sems.at[k])
        total[...] += jnp.dot(held[k], weight[k], preferred_element_type=F32)
        return carry

    lax.fori_loop(0, steps, forward_step, 0)
    arrive(k_own, cot_sems.at[0])
    arrive(k_other, cot_sems.at[1])

    bias, own_coef, other_coef = (vectors[i : i + 1, :] for i in range(3))
    c = 0.7978845608028654
    block = 32

    def rows_of(i, sums):
        rows = pl.ds(pl.multiple_of(i * block, block), block)
        x = total[rows, :] + bias
        x2 = x * x
        t = jnp.tanh(c * (x + 0.044715 * (x2 * x)))
        half = 0.5 * (1.0 + t)
        act = (x * half).astype(BF16)
        slope = half + (0.5 * c) * x * (1.0 - t * t) * (1.0 + (3.0 * 0.044715) * x2)
        k0 = k_own[rows, :].astype(F32)
        k1 = k_other[rows, :].astype(F32)
        dpre = ((own_coef * k0 + other_coef * k1) * slope).astype(BF16)
        act_out[rows, :] = act
        dpre_out[rows, :] = dpre
        actf = act.astype(F32)

        def fold(v):
            return jnp.sum(v.reshape(block // 8, 8, v.shape[1]), axis=0)

        return (
            sums[0] + fold(dpre.astype(F32)),
            sums[1] + fold(k0 * actf),
            sums[2] + fold(k1 * actf),
        )

    zero = jnp.zeros((8, total.shape[1]), F32)
    sums = lax.fori_loop(0, images // block, rows_of, (zero, zero, zero))
    for i in range(3):
        sums_out[i : i + 1, :] = jnp.sum(sums[i], axis=0, keepdims=True)
    keep_out[...] = dpre_out[: images // 2]
    send_out[...] = dpre_out[images // 2 :]

    def product(k):
        return lax.dot_general(
            held[k], dpre_out[...], (((0,), (0,)), ((), ())), preferred_element_type=F32
        )

    def last_steps(k, carry):
        made = product(k).astype(BF16)
        for i in range(chunks):
            low[k - per, i] = made[:, columns(i)]
        for s in range(1, count):

            @pl.when(k // per == s)
            def _(s=s):
                rows = pl.ds(pl.multiple_of((k - s * per) * tile, tile), tile)
                for i in range(chunks):
                    pltpu.make_async_copy(low.at[k - per, i], outs[i][s].at[rows, :], out_sems.at[k]).start()

        return carry

    def first_steps(k, carry):
        made = product(k)
        rows = pl.ds(pl.multiple_of(k * tile, tile), tile)
        for i in range(chunks):
            high[k, i] = made[:, columns(i)]
            pltpu.make_async_copy(high.at[k, i], outs[i][0].at[rows, :], out_sems.at[k]).start()
        return carry

    if count > 1:
        lax.fori_loop(per, steps, last_steps, 0)
    lax.fori_loop(0, per, first_steps, 0)
    for k in range(steps):
        arrive(high.at[k] if k < per else low.at[k - per], out_sems.at[k])


def chunk(roles, feats, pieces, vectors, cots):
    images = len(feats) * feats[-1][-1][0].shape[0]
    units = pieces[0][0][0].shape[1]
    width = units * len(pieces)
    depth = sum(part.shape[1] for part, _ in feats[0])
    starts = [start for block in feats for _, start in block]
    count = len(pieces[0])
    height = pieces[0][0][0].shape[0]
    tile = tile_of(height)
    steps, per = depth // tile, height // tile
    terms = [term for chunk in pieces for piece in chunk for term in piece]
    anywhere = pl.BlockSpec(memory_space=pl.ANY)
    vmem = pl.BlockSpec(memory_space=pltpu.VMEM)
    kinds = ([F32] + [BF16] * (count - 1)) * len(pieces)
    return pl.pallas_call(
        functools.partial(chunk_kernel, [[len(p) for p in chunk] for chunk in pieces], starts, [c for _, c in cots]),
        in_specs=[pl.BlockSpec(memory_space=pltpu.SMEM), vmem]
        + [anywhere] * (len(cots) + len(feats) * HALVES + len(terms)),
        out_specs=[vmem] * 4 + [anywhere] * len(kinds),
        out_shape=[
            jax.ShapeDtypeStruct((images, width), BF16),
            jax.ShapeDtypeStruct((images // 2, width), BF16),
            jax.ShapeDtypeStruct((images // 2, width), BF16),
            jax.ShapeDtypeStruct((8, width), F32),
        ]
        + [jax.ShapeDtypeStruct((height, units), kind) for kind in kinds],
        scratch_shapes=[
            pltpu.VMEM((steps, images, tile), BF16),
            pltpu.VMEM((steps, tile, width), BF16),
            pltpu.VMEM((images, width), F32),
            pltpu.VMEM((images, width), BF16),
            pltpu.VMEM((images, width), BF16),
            pltpu.VMEM((images, width), BF16),
            pltpu.VMEM((per, len(pieces), tile, units), F32),
            pltpu.VMEM((max(steps - per, 1), len(pieces), tile, units), BF16),
            pltpu.SemaphoreType.DMA((steps,)),
            pltpu.SemaphoreType.DMA((steps,)),
            pltpu.SemaphoreType.DMA((2,)),
            pltpu.SemaphoreType.DMA((steps,)),
        ],
        compiler_params=params(),
        cost_estimate=SMALL,
        name="chunk",
    )(roles, vectors, *[cot for cot, _ in cots], *[part for block in feats for part, _ in block], *terms)


def back_kernel(count, *refs):
    outs = refs[-14:-6]
    grad, weight, made, grad_sems, w_sems, out_sems = refs[-6:]
    sources = (len(refs) - 14) // (1 + count)
    grads, pieces = refs[:sources], refs[sources:-14]
    slots, tile, total = weight.shape
    units = total // sources
    steps = made.shape[0]
    per = steps // count
    share = made.shape[1] // len(outs)

    def columns(j):
        return slice(j * units, (j + 1) * units)

    def begin(k):
        slot = lax.rem(k, slots)
        for s in range(count):

            @pl.when(k // per == s)
            def _(s=s):
                rows = pl.ds(pl.multiple_of((k - s * per) * tile, tile), tile)
                for j in range(sources):
                    piece = pieces[j * count + s].at[rows, :]
                    pltpu.make_async_copy(piece, weight.at[slot, :, columns(j)], w_sems.at[slot]).start()

    def arrive(target, sem):
        pltpu.make_async_copy(target, target, sem).wait()

    copies = []
    for j in range(sources):
        copies.append(pltpu.make_async_copy(grads[j], grad.at[:, columns(j)], grad_sems.at[j]))
        copies[-1].start()
    ahead = min(slots - 1, steps)
    for k in range(ahead):
        begin(jnp.int32(k))
    for copy in copies:
        copy.wait()

    def step(k, carry):
        pl.when(k + ahead < steps)(lambda: begin(k + ahead))
        slot = lax.rem(k, slots)
        arrive(weight.at[slot], w_sems.at[slot])
        made[k] = lax.dot_general(
            grad[...], weight[slot], (((1,), (1,)), ((), ())), preferred_element_type=F32
        ).astype(BF16)
        cols = pl.ds(pl.multiple_of(k * tile, tile), tile)
        for i, out in enumerate(outs):
            source = made.at[k, pl.ds(i * share, share), :]
            pltpu.make_async_copy(source, out.at[:, cols], out_sems.at[k]).start()
        return carry

    lax.fori_loop(0, steps, step, 0)
    for k in range(steps):
        arrive(made.at[k], out_sems.at[k])


def back(grads, pieces):
    images, units = grads[0].shape
    count = len(pieces[0])
    height = pieces[0][0].shape[0]
    depth = height * count
    tile = next(t for t in (768, 512, 384, 256, 128) if height % t == 0)
    steps = depth // tile
    total = units * len(grads)
    terms = [piece for chunk in pieces for piece in chunk]
    anywhere = pl.BlockSpec(memory_space=pl.ANY)
    return pl.pallas_call(
        functools.partial(back_kernel, count),
        in_specs=[anywhere] * (len(grads) + len(terms)),
        out_specs=[anywhere] * 8,
        out_shape=[jax.ShapeDtypeStruct((images // 8, depth), BF16)] * 8,
        scratch_shapes=[
            pltpu.VMEM((images, total), BF16),
            pltpu.VMEM((AHEAD + 1, tile, total), BF16),
            pltpu.VMEM((steps, images, tile), BF16),
            pltpu.SemaphoreType.DMA((len(grads),)),
            pltpu.SemaphoreType.DMA((AHEAD + 1,)),
            pltpu.SemaphoreType.DMA((steps,)),
        ],
        compiler_params=params(),
        cost_estimate=SMALL,
        name="back",
    )(*grads, *terms)


def either(flag, value, axis):
    return jnp.where(flag, jnp.flip(value, axis), value)


class Program:
    def __init__(self, convmaps, group, alpha1, weight, bias, alpha2, cotangent):
        self.order = Order()
        self.convmaps, self.group, self.weight = convmaps, group, weight
        self.count, _, self.places, self.channels = convmaps.shape
        batch_id = lax.axis_index("batch")
        tower_id = lax.axis_index("tower")
        self.x, self.z = batch_id % 2, batch_id // 2
        self.y, self.core = tower_id // 2, tower_id % 2
        self.depth, self.width = weight.shape
        self.units = self.width // 2
        self.n = self.units // (4 if is_line() else 2)
        self.chunks = self.units // self.n
        self.images = 8 * self.count
        self.mine, self.theirs = self.x * self.units, (1 - self.x) * self.units
        units = self.units
        second = lax.dynamic_slice_in_dim(alpha2, self.mine, units, 1)
        self.own_coef = lax.dynamic_index_in_dim(second, self.y, 0, keepdims=True).astype(F32)
        self.cross = lax.dynamic_index_in_dim(second, 1 - self.y, 0, keepdims=True)
        own_bias = lax.dynamic_slice_in_dim(bias, self.mine, units, 0)[None, :].astype(F32)
        self.own_bias = own_bias
        cot = cotangent.reshape(2, 2, self.count, self.width)
        cot = either(self.core == 1, either(self.y == 1, cot, 0), 1).swapaxes(0, 1)
        cot = cot.reshape(-1, self.width)
        self.cot_mine = lax.dynamic_slice_in_dim(cot, self.mine, units, 1)
        self.cot_theirs = lax.dynamic_slice_in_dim(cot, self.theirs, units, 1)
        places = jnp.arange(POOLED)
        if is_line():
            places = places.reshape(4, -1)[line_order(self.z)].reshape(-1)
        self.table = pool_table(places)
        self.first = either(self.y == 1, alpha1.astype(F32), 0).reshape(4, self.channels)
        self.is_outer = (self.z == 0) | (self.z == 3)
        self.roles = jnp.stack([self.is_outer.astype(jnp.int32), 1 - self.core])
        self.cots = {}
        self.places_of = jnp.stack([self.x, self.y, self.core]).astype(jnp.int32)
        self.weight_grad = ()
        self.acts, self.grads, self.far_grads, self.sums = {}, {}, {}, {}
        self.stitched, self.crossed = {}, {}

    def then(self, value):
        return self.order.then(value)

    def did(self, value):
        return self.order.did(value)

    def keep_cross(self, came):
        cross_back = self.did(self.then(came)).astype(F32)
        zeros = jnp.zeros((5, self.units), F32)
        self.vectors = jnp.concatenate([self.own_bias, self.own_coef, cross_back, zeros])
        self.cross = self.cross.astype(F32)

    def cols(self, j):
        return slice(j * self.n, (j + 1) * self.n)

    def span(self, js):
        return slice(js[0] * self.n, (js[-1] + 1) * self.n)

    def weight_part(self, start, j, many=1):
        return lax.dynamic_slice(self.weight, (0, start + j * self.n), (self.depth, many * self.n))

    def swap_weight(self, j, many=1):
        return self.send(x_swap, self.weight_part(self.theirs, j, many))

    def slab_weight(self, j, came):
        a, b = self.weight_part(self.mine, j), self.then(came)
        return self.did(jnp.where(self.x == 0, jnp.concatenate([a, b]), jnp.concatenate([b, a])))

    def swap_cotangents(self, js):
        return self.send(x_swap, self.cot_theirs[:, self.span(js)])

    def cots_of(self, j):
        here, there = self.cots[j]
        first = (j - min(i for i in self.cots if self.cots[i][0] is here)) * self.n
        return [(self.cot_mine, j * self.n), (here, first), (self.cot_across, j * self.n), (there, first)]

    def send(self, move, value, *args):
        return move(self.did(self.then(value)), *args)

    def chunk(self, j, feats, pieces):
        act, keep, send, sums, *products = chunk(
            self.roles,
            feats,
            [pieces],
            self.then(self.vectors[:, self.cols(j)]),
            self.cots_of(j),
        )
        self.did(act)
        self.acts[j], self.grads[j], self.far_grads[j], self.sums[j] = act, keep, send, sums
        return products

    def stitch(self, j, came):
        cols = self.cols(j)
        other_act = jnp.flip(self.then(came).reshape(4, 2, self.count, self.n), 1).reshape(self.images, self.n)
        mix = self.own_coef[:, cols] * self.acts[j].astype(F32) + self.cross[:, cols] * other_act.astype(F32)
        mix = self.did(mix.astype(BF16)).reshape(2, 2, 2 * self.count, self.n)
        self.stitched[j] = mix[:, 0].reshape(-1, self.n)
        return mix[:, 1].reshape(-1, self.n)

    def leaving(self, slab):
        return lax.dynamic_slice_in_dim(slab, (1 - self.x) * self.depth, self.depth, 0).astype(BF16)

    def store(self, j, rows, came):
        shape = (self.depth, self.width)
        made = store(self.then(rows), came, self.places_of, j, self.chunks, shape, self.weight_grad)
        self.weight_grad = (self.did(made),)

    def activations(self):
        own, other = ([parts[j] for j in range(self.chunks)] for parts in (self.stitched, self.crossed))
        return place_rows(self.places_of, [self.then(own[0])] + own[1:], other)

    def unit_sums(self):
        return jnp.concatenate([self.sums[j][:3] for j in range(self.chunks)], axis=1)

    def small_grads(self, sums):
        mine, far = sums[:3], sums[3:6]
        wide = jnp.where(
            self.x == 0, jnp.concatenate([mine, far], -1), jnp.concatenate([far, mine], -1)
        )
        return wide[0], either(self.y == 1, wide[1:3], 0)

    def back(self, came_grads, pieces, came_pieces):
        chunks = range(self.chunks)
        grads = [self.grads[j] for j in chunks] + [came_grads[j] for j in chunks]
        parts = back(
            [self.then(grads[0])] + grads[1:],
            [pieces[j] for j in chunks] + [came_pieces[j] for j in chunks],
        )
        self.did(parts[0])
        return parts[:4], parts[4:]

    def add(self, keep, came):
        return self.did((keep.astype(F32) + self.then(came).astype(F32)).astype(BF16))

    def first_grad(self, i, keep, came, other, pooled):
        return self.did(first_grad(pooled, self.then(keep), came, other, i * keep.shape[0]))

    def by_tower(self, partial):
        return either(self.y == 1, partial.reshape(2, 2, self.channels), 0)

    def unpool(self, i, keep, came, other, before=()):
        at = i * keep.shape[0]
        return self.did(
            unpool(
                self.then(keep),
                came,
                other,
                self.group,
                self.table,
                self.first,
                self.places,
                at,
                self.count,
                before,
            )
        )


def line_program(p):
    then, did = p.then, p.did
    came, blocks, near, inner, outer, first_out, last_out = {}, {}, {}, {}, {}, {}, {}
    total, into, crossed, middle, final, slab_came = {}, {}, {}, {}, {}, {}
    from_own, swapped = {}, {}

    def send(kind, value):
        return p.send(line, value, kind)

    def arrive(value):
        return did(then(value))

    def block(j):
        blocks[j] = p.slab_weight(j, came[j])

    def pieces(j):
        beside = (near[j],) if j < 2 else (from_own[j], swapped[j])
        return [(blocks[j],), beside, (first_out[j], inner[j]), (last_out[j], outer[j])]

    def part(j, s):
        return total[j][s]

    def payload(inward, outward):
        return did(jnp.where(p.is_outer, then(inward), outward))

    def ends(value):
        return send("near", value)

    def inward(j, s):
        return send("inward", then(part(j, s)))

    def plus(j, s, value):
        return (part(j, s).astype(F32) + then(value).astype(F32)).astype(BF16)

    def edge(j):
        return jnp.where(
            p.is_outer, then(final[j]).astype(F32), into[j, 1].astype(F32) + middle[j].astype(F32)
        )

    def pick(a, b):
        return did(jnp.where(p.is_outer, then(a), b))

    def core_swap(j, s):
        came_pieces[j, s] = p.send(c_swap, picked[j, s])

    def core_came(j, s):
        came_pieces[j, s] = arrive(came_pieces[j, s])

    picked, came_pieces, came_grads = {}, {}, {}

    def far_end(j):
        return plus(j, 3, into[j, 3])

    image_blocks = p.count // IMAGE_BLOCK
    cuts = [0, image_blocks // 4, image_blocks]

    def pool_part(i, before=()):
        made = pool(
            p.convmaps, p.group, then(p.table), p.first, cuts[i], cuts[i + 1] - cuts[i], before
        )
        did(made[0])
        return made

    came[0] = p.swap_weight(0)
    came[1] = p.swap_weight(1)
    cross_came = p.send(y_swap, p.cross)
    made = pool_part(0)
    came[0] = arrive(came[0])
    block(0)
    near[0] = ends(blocks[0])
    inner[0] = send("middle", blocks[0])
    p.keep_cross(cross_came)
    came[1] = arrive(came[1])
    came_pair = p.swap_weight(2, 2)
    p.cot_across = p.send(y_swap, p.cot_mine)
    cot_came = p.swap_cotangents([0, 1])
    block(1)
    kept_a, kept_b, sent_a, sent_b, pooled = pool_part(1, made)
    near[0] = arrive(near[0])
    near[1] = ends(blocks[1])
    inner[0] = arrive(inner[0])
    inner[1] = send("middle", blocks[1])
    came_pair = arrive(came_pair)
    p.cot_across = arrive(p.cot_across)
    cot_came = arrive(cot_came)
    x_a = p.send(x_swap, kept_a)
    y_a = p.send(y_swap, sent_a)
    came[2], came[3] = came_pair[:, : p.n], came_pair[:, p.n :]
    block(2)
    block(3)
    near[1] = arrive(near[1])
    first_out[0] = send("outward", inner[0])
    inner[1] = arrive(inner[1])
    outer[0] = send("middle", near[0])
    x_a = arrive(x_a)
    x_b = p.send(x_swap, kept_b)
    y_a = arrive(y_a)
    y_b = p.send(y_swap, sent_b)
    c_kept = [both_cores(arrive(kept_a)), both_cores(arrive(kept_b))]
    c_x_a, c_y_a = both_cores(x_a), both_cores(y_a)
    first_out[0] = arrive(first_out[0])
    first_out[1] = send("outward", inner[1])
    outer[0] = arrive(outer[0])
    outer[1] = send("middle", near[1])
    x_b = arrive(x_b)
    x_y_a = p.send(x_swap, y_a)
    y_b = arrive(y_b)
    cot_crossed = p.send(y_swap, cot_came)
    c_x_b, c_y_b = both_cores(x_b), both_cores(y_b)
    value = payload(blocks[2], outer[0])
    first_out[1] = arrive(first_out[1])
    swapped[2] = last_out[0] = ends(value)
    outer[1] = arrive(outer[1])
    inner[2] = send("middle", blocks[2])
    x_y_a = arrive(x_y_a)
    x_y_b = p.send(x_swap, y_b)
    p.cots[0] = p.cots[1] = (cot_came, arrive(cot_crossed))
    for j in range(4):
        picked[j, 0] = blocks[j]
    picked[0, 1], picked[1, 1] = near[0], near[1]
    core_swap(0, 0)
    value = payload(blocks[3], outer[1])
    picked[0, 2] = pick(first_out[0], inner[0])
    picked[1, 2] = pick(first_out[1], inner[1])
    swapped[2] = last_out[0] = arrive(swapped[2])
    swapped[3] = last_out[1] = ends(value)
    inner[2] = arrive(inner[2])
    inner[3] = send("middle", blocks[3])
    x_y_b = arrive(x_y_b)
    core_came(0, 0)
    c_x_y_a = p.send(c_swap, x_y_a)
    core_swap(0, 1)
    core_swap(1, 0)
    picked[0, 3] = pick(last_out[0], outer[0])
    swapped[3] = last_out[1] = arrive(swapped[3])
    from_own[2] = send("outward", blocks[2])
    inner[3] = arrive(inner[3])
    outer[2] = send("middle", swapped[2])
    c_x_y_a = arrive(c_x_y_a)
    c_x_y_b = p.send(c_swap, x_y_b)
    core_came(0, 1)
    core_came(1, 0)
    c_x_y_b = arrive(c_x_y_b)
    feats = [
        [(kept_a, 0), (kept_b, 0)],
        [(y_a, 0), (y_b, 0)],
        [(x_a, 0), (x_b, 0)],
        [(x_y_a, 0), (x_y_b, 0)],
        [(c_kept[0], None), (c_kept[1], None)],
        [(c_y_a, None), (c_y_b, None)],
        [(c_x_a, None), (c_x_b, None)],
        [(c_x_y_a, 0), (c_x_y_b, 0)],
    ]
    total[0] = p.chunk(0, feats, pieces(0))
    value = payload(part(0, 3), inner[2])
    from_own[2] = arrive(from_own[2])
    into[0, 3] = first_out[2] = ends(value)
    outer[2] = arrive(outer[2])
    outer[3] = send("middle", swapped[3])
    cot_came = p.swap_cotangents([2, 3])
    act_came = p.send(y_swap, p.acts[0])
    core_swap(1, 1)
    total[1] = p.chunk(1, feats, pieces(1))
    value = payload(part(0, 2), outer[2])
    into[0, 3] = first_out[2] = arrive(into[0, 3])
    into[0, 2] = last_out[2] = ends(value)
    outer[3] = arrive(outer[3])
    crossed[0] = send("middle", far_end(0))
    cot_came = arrive(cot_came)
    act_came = arrive(act_came)
    cot_crossed = p.send(y_swap, cot_came)
    core_came(1, 1)
    core_swap(0, 2)
    core_swap(1, 2)
    value = payload(part(0, 1), blocks[3])
    mix = p.stitch(0, act_came)
    picked[1, 3] = pick(last_out[1], outer[1])
    picked[2, 1] = pick(from_own[2], swapped[2])
    into[0, 2] = last_out[2] = arrive(into[0, 2])
    into[0, 1] = from_own[3] = ends(value)
    crossed[0] = arrive(crossed[0])
    middle[0] = send("middle", plus(0, 2, into[0, 2]))
    p.cots[2] = p.cots[3] = (cot_came, arrive(cot_crossed))
    core_came(0, 2)
    core_came(1, 2)
    p.crossed[0] = p.send(x_swap, mix)
    act_came = p.send(y_swap, p.acts[1])
    core_swap(0, 3)
    total[2] = p.chunk(2, feats, pieces(2))
    value = payload(part(1, 3), inner[3])
    into[0, 1] = from_own[3] = arrive(into[0, 1])
    into[1, 3] = first_out[3] = ends(value)
    middle[0] = arrive(middle[0])
    p.crossed[0] = arrive(p.crossed[0])
    act_came = arrive(act_came)
    core_came(0, 3)
    act_came2 = p.send(y_swap, p.acts[2])
    core_swap(1, 3)
    core_swap(2, 0)
    core_swap(3, 0)
    value = payload(part(1, 2), outer[3])
    mix = p.stitch(1, act_came)
    picked[2, 2] = pick(first_out[2], inner[2])
    picked[2, 3] = pick(last_out[2], outer[2])
    picked[3, 1] = pick(from_own[3], swapped[3])
    into[1, 3] = first_out[3] = arrive(into[1, 3])
    into[1, 2] = last_out[3] = ends(value)
    for at in ((1, 3), (2, 0), (3, 0)):
        core_came(*at)
    crossed[1] = send("middle", far_end(1))
    act_came = arrive(act_came2)
    p.crossed[1] = p.send(x_swap, mix)
    core_swap(2, 1)
    core_swap(2, 2)
    value = payload(part(1, 1), plus(0, 1, crossed[0]))
    picked[3, 2] = pick(first_out[3], inner[3])
    mix = p.stitch(2, act_came)
    for j in range(3):
        came_grads[j] = arrive(p.send(c_swap, p.far_grads[j]))
    into[1, 2] = last_out[3] = arrive(into[1, 2])
    into[1, 1] = final[0] = ends(value)
    crossed[1] = arrive(crossed[1])
    middle[1] = send("middle", plus(1, 2, into[1, 2]))
    p.crossed[1] = arrive(p.crossed[1])
    core_came(2, 1)
    core_came(2, 2)
    p.crossed[2] = p.send(x_swap, mix)
    core_swap(2, 3)
    core_swap(3, 1)
    picked[3, 3] = pick(last_out[3], outer[3])
    total[3] = p.chunk(3, feats, pieces(3))
    value = payload(part(2, 3), plus(1, 1, crossed[1]))
    into[1, 1] = final[0] = arrive(into[1, 1])
    into[2, 3] = final[1] = ends(value)
    middle[1] = arrive(middle[1])
    p.crossed[2] = arrive(p.crossed[2])
    core_came(2, 3)
    core_came(3, 1)
    core_swap(3, 2)
    core_swap(3, 3)
    came_grads[3] = p.send(c_swap, p.far_grads[3])
    rows = {0: did(part(0, 0) + edge(0))}
    core_came(3, 2)
    core_came(3, 3)
    came_grads[3] = arrive(came_grads[3])
    slab_came[0] = p.send(x_swap, p.leaving(rows[0]))
    act_came = p.send(y_swap, p.acts[3])
    keep, leave = p.back(
        came_grads,
        [[picked[j, s] for s in range(4)] for j in range(4)],
        [[came_pieces[j, s] for s in range(4)] for j in range(4)],
    )
    came_x, own_y = {}, {}
    into[2, 3] = final[1] = arrive(into[2, 3])
    into[3, 3] = inward(3, 3)
    slab_came[0] = arrive(slab_came[0])
    crossed[2] = send("middle", far_end(2))
    came_x[0] = p.send(x_swap, leave[2])
    act_came = arrive(act_came)
    p.store(0, rows[0], slab_came[0])
    rows[1] = did(part(1, 0) + edge(1))
    mix = p.stitch(3, act_came)
    into[3, 3] = arrive(into[3, 3])
    into[2, 2] = inward(2, 2)
    crossed[2] = arrive(crossed[2])
    crossed[3] = send("middle", far_end(3))
    came_x[0] = arrive(came_x[0])
    came_x[1] = p.send(x_swap, leave[3])
    own_y[0] = p.send(y_swap, p.add(keep[2], came_x[0]))
    sums = did(then(p.unit_sums()))
    into[2, 2] = arrive(into[2, 2])
    into[3, 2] = inward(3, 2)
    crossed[3] = arrive(crossed[3])
    middle[2] = send("middle", plus(2, 2, into[2, 2]))
    came_x[1] = arrive(came_x[1])
    came_x[2] = p.send(x_swap, leave[0])
    own_y[0] = arrive(own_y[0])
    own_y[1] = p.send(y_swap, p.add(keep[3], came_x[1]))
    value = payload(part(2, 1), plus(2, 1, crossed[2]))
    into[3, 2] = arrive(into[3, 2])
    into[2, 1] = final[2] = ends(value)
    middle[2] = arrive(middle[2])
    middle[3] = send("middle", plus(3, 2, into[3, 2]))
    came_x[2] = arrive(came_x[2])
    came_x[3] = p.send(x_swap, leave[1])
    own_y[1] = arrive(own_y[1])
    value = payload(part(3, 1), plus(3, 1, crossed[3]))
    partial = p.first_grad(0, keep[0], came_x[2], own_y[0], pooled)
    grad = (p.unpool(0, keep[0], came_x[2], own_y[0]),)
    into[2, 1] = final[2] = arrive(into[2, 1])
    into[3, 1] = final[3] = ends(value)
    middle[3] = arrive(middle[3])
    came_x[3] = arrive(came_x[3])
    slab_came[1] = p.send(x_swap, p.leaving(rows[1]))
    rows[2] = did(part(2, 0) + edge(2))
    slab_came[2] = p.send(x_swap, p.leaving(rows[2]))
    p.crossed[3] = p.send(x_swap, mix)
    partial = partial + p.first_grad(1, keep[1], came_x[3], own_y[1], pooled)
    partial = did(p.by_tower(partial).reshape(1, -1))
    partial_came = p.send(c_swap, partial)
    grad = p.unpool(1, keep[1], came_x[3], own_y[1], grad)
    partial = did(partial + then(partial_came))
    second_came = p.send(y_swap, jnp.concatenate([sums[2:], partial]))
    into[3, 1] = final[3] = arrive(into[3, 1])
    rows[3] = did(part(3, 0) + edge(3))
    slab_came[1] = arrive(slab_came[1])
    slab_came[3] = p.send(x_swap, p.leaving(rows[3]))
    second_came = arrive(second_came)
    sums = did(jnp.concatenate([sums[:2], second_came[:1], partial + second_came[1:]]))
    sums_came = p.send(flipped, sums, "batch", 2)
    p.store(1, rows[1], slab_came[1])
    sums = did(sums + then(sums_came))
    sums_came = p.send(flipped, sums, "batch", 4)
    slab_came[2] = arrive(slab_came[2])
    p.store(2, rows[2], slab_came[2])
    p.crossed[3] = arrive(p.crossed[3])
    activations = did(p.activations())
    sums = did(sums + then(sums_came))
    slab_came[3] = arrive(slab_came[3])
    sums_came = p.send(x_swap, sums)
    p.store(3, rows[3], slab_came[3])
    sums_came = then(sums_came)
    bias_grad, alpha2_grad = p.small_grads(jnp.concatenate([sums[:3], sums_came[:3]]))
    alpha1_grad = (sums[3] + sums_came[3]).reshape(2, 2, p.channels)
    input_grad = jnp.swapaxes(grad, 1, 2)
    return (activations, input_grad, p.weight_grad[0], bias_grad, alpha1_grad, alpha2_grad)


def plain_program(p):
    groups = slab_groups()
    p.keep_cross(p.send(y_swap, p.cross))
    p.cot_across = p.send(y_swap, p.cot_mine)
    *features, pooled = pool(p.convmaps, p.group, p.table, p.first, 0, p.count // IMAGE_BLOCK)
    feats = [features[:HALVES], [y_swap(part) for part in features[HALVES:]]]
    feats += [[x_swap(part) for part in block] for block in feats]
    feats += [[c_swap(part) for part in block] for block in feats]
    feats = [[(part, 0) for part in block] for block in feats]
    chunks = []
    for j in range(p.chunks):
        came = p.swap_cotangents([j])
        p.cots[j] = (came, p.send(y_swap, came))
        block = p.slab_weight(j, p.swap_weight(j))
        rows = lax.all_gather(block, "batch", axis=0, tiled=True, axis_index_groups=groups)
        chunks.append([(rows,)])
        [total] = p.chunk(j, feats, chunks[j])
        slab = lax.psum_scatter(total, "batch", scatter_dimension=0, tiled=True, axis_index_groups=groups)
        p.store(j, slab, p.send(x_swap, p.leaving(slab)))
        p.crossed[j] = p.send(x_swap, p.stitch(j, p.send(y_swap, p.acts[j])))
    sums = lax.psum(p.unit_sums(), "batch", axis_index_groups=groups)
    far = x_swap(sums)
    second = y_swap(jnp.concatenate([sums[2:], far[2:]]))
    bias_grad, alpha2_grad = p.small_grads(
        jnp.concatenate([sums[:2], second[:1], far[:2], second[1:]])
    )
    own_pieces = [[term for [term] in chunk] for chunk in chunks]
    keep, leave = p.back(
        [c_swap(p.far_grads[j]) for j in range(p.chunks)],
        own_pieces,
        [[c_swap(term) for term in chunk] for chunk in own_pieces],
    )
    partial, grad = 0.0, ()
    for i in range(2):
        other = y_swap(p.add(keep[2 + i], x_swap(leave[2 + i])))
        came = x_swap(leave[i])
        partial = partial + p.first_grad(i, keep[i], came, other, pooled)
        grad = (p.unpool(i, keep[i], came, other, grad),)
    alpha1_grad = lax.psum(p.by_tower(partial), ("batch", "tower"))
    input_grad = jnp.swapaxes(grad[0], 1, 2)
    return (p.activations(), input_grad, p.weight_grad[0], bias_grad, alpha1_grad, alpha2_grad)


def shards(*args):
    return (line_program if is_line() else plain_program)(Program(*args))


def solution(mesh):
    in_specs = (
        P(("batch", "tower"), None, None, None),
        P(("batch", "tower")),
        P(),
        P("batch", "tower"),
        P("tower"),
        P(None, "tower"),
        P("batch", "tower"),
    )
    out_specs = (
        P("batch", "tower"),
        P(("batch", "tower"), None, None, None),
        P("batch", "tower"),
        P("tower"),
        P(),
        P(None, "tower"),
    )
    return jax.shard_map(shards, mesh=mesh, in_specs=in_specs, out_specs=out_specs, check_vma=False)
```

time: 741 us -> 682 us (0.920)
  waiting for transfers between devices: 258 us -> 214 us
  local copies, waits for them, and re-layouts: 63.2 us -> 40.4 us
  Pallas kernels: 185 us -> 203 us
  other arithmetic: 90.8 us -> 80.9 us
    ppermute x45 -> x60, waiting for transfers between devices: 91.7 us -> 31.5 us  [flipped(): return lax.ppermute(value, axis, pairs)]
    add x14 -> x6, other arithmetic: 28.3 us -> 8.37 us  [the longest x1 2.1 us: line_program(): rows[2] = did(part(2, 0) + edge(2))]
    pallas_call x2 -> x4, Pallas kernels: 66.2 us -> 85.3 us  [chunk(): pl.pallas_call(functools.partial(chunk_kernel, [[len(p) for p in chunk] f...]
    ppermute x35, waiting for transfers between devices: 164 us -> 180 us  [line(): return lax.ppermute(value, 'batch', pairs)]
    select_n x3 -> x11, other arithmetic: 2.11 us -> 17.5 us  [the longest x10 17.5 us: pick(): return did(jnp.where(p.is_outer, then(a), b))]
    slice x20 -> x15, local copies, waits for them, and re-layouts: 15.2 us -> 7.48 us  [the longest x3 2.47 us: stitch(): self.stitched[j] = mix[:, 0].reshape(-1, self.n)]
    pallas_call x8 -> x10, Pallas kernels: 87.6 us -> 86.4 us  [the longest x2 30.8 us: unpool(): pl.pallas_call(functools.partial(unpool_kernel, at), grid_spec=pltpu.Pref...]
    ppermute x45 -> x60, starting transfers between devices: 48.9 us -> 48.1 us  [flipped(): return lax.ppermute(value, axis, pairs)]
  transfers between devices with their start and end apart: 86 -> 101, of which waited for: 27 -> 23; matrix products, arithmetic and copies ran while one was open for 19% -> 15% of each run, Pallas kernels for 24% -> 30%
where the time goes in v3:
time: 682 us; the launch traced here: 672 us
  waiting for transfers between devices  214 us (31%)
  Pallas kernels  203 us (30%)
  starting transfers between devices  118 us (17%)
  other arithmetic  80.9 us (12%)
  local copies, waits for them, and re-layouts  40.4 us (6%)
  between operations  16.3 us (2%)
    ppermute x35, waiting for transfers between devices, line(): return lax.ppermute(value, 'batch', pairs)  180 us
    pallas_call x4, Pallas kernels, chunk(): pl.pallas_call(functools.partial(chunk_kernel, [[len(p) for p in chunk] f...  85.3 us
    ppermute x35, starting transfers between devices, line(): return lax.ppermute(value, 'batch', pairs)  69.6 us
    ppermute x60, starting transfers between devices, flipped(): return lax.ppermute(value, axis, pairs)  48.1 us
    ppermute x60, waiting for transfers between devices, flipped(): return lax.ppermute(value, axis, pairs)  31.5 us
    pallas_call x2, Pallas kernels, pool(): pl.pallas_call(functools.partial(pool_kernel, at), grid_spec=pltpu.Prefet...  31.1 us
    pallas_call x2, Pallas kernels, unpool(): pl.pallas_call(functools.partial(unpool_kernel, at), grid_spec=pltpu.Pref...  30.8 us
    pallas_call x1, Pallas kernels, back(): pl.pallas_call(functools.partial(back_kernel, count), in_specs=[anywhere]...  27.1 us
  transfers between devices with their start and end apart: 101, of which 23 were waited for; matrix products, arithmetic and copies ran while one was open for 15% of the time, Pallas kernels for 30%

profile of v3, /device:TPU:0, one launch (start us, length us, event | category | flops | bytes accessed | tf_op | source)
XLA Modules:
  0.0 672.0 jit_solution(17080456406803302716)
XLA Ops:
  7.3 3.9 constant_dynamic-slice_fusion.2
  21.2 9.6 %pool.2 = (bf16[128,4608]{1,0:T(8,128)(2,1)}, bf16[128,4608]{1,0:T(8,128)(2,1)}, bf16[128,4608]{1,0:T(8,128)(2,1)}, bf16[128,4608]{1,0:T(8,128)(2,1)}, f32[2,128,9216]{2,1,0:T(8,128)}) custom-call(s32[128]{0:T(128)} %group.7, bf16[2,96,338]{2,1,0:T(8,128)(2,1)} %copy.48.table, f32[4,256]{1,0:T(4,128)} %reshape.582.first, bf16[128,169,2,256]{3,2,1,0:T(2,128)(2,1)} %bitcast.79), custom_call_target="tpu_custom_call" | custom-call | flops 1000 | bytes 1000 | tf_op jit(solution)/shard_map/pool/pallas_call | solution.py:144
  50.2 21.5 %pool.3 = (bf16[128,4608]{1,0:T(8,128)(2,1)}, bf16[128,4608]{1,0:T(8,128)(2,1)}, bf16[128,4608]{1,0:T(8,128)(2,1)}, bf16[128,4608]{1,0:T(8,128)(2,1)}, f32[2,128,9216]{2,1,0:T(8,128)}) custom-call(s32[128]{0:T(128)} %group.7, bf16[2,96,338]{2,1,0:T(8,128)(2,1)} %copy.51.table, ...), custom_call_target="tpu_custom_call", output_to_operand_aliasing={{0}: (4, {}), {1}: (5, {}), {2}: (6, {}), {3}: (7, {}), {4}... | custom-call | flops 1000 | bytes 1000 | tf_op jit(solution)/shard_map/pool/pallas_call | solution.py:144
  86.1 11.8 %collective-permute-done.11.refs_21_.refs_13_ = bf16[2304,256]{1,0:T(8,128)(2,1)S(1)} collective-permute-done((bf16[2304,256]{1,0:T(8,128)(2,1)}, bf16[2304,256]{1,0:T(8,128)(2,1)S(1)}, u32[]{:S(2)}, u32[]{:S(2)}) %collective-permute-start.11) | collective-permute-done | bytes 1179680 | tf_op jit(solution)/shard_map/ppermute | solution.py:51
  100.1 5.5 collective-permute-done.9.refs_8_
  113.9 21.8 %collective-permute-done.15.refs_22_ = bf16[2304,256]{1,0:T(8,128)(2,1)S(1)} collective-permute-done((bf16[2304,256]{1,0:T(8,128)(2,1)}, bf16[2304,256]{1,0:T(8,128)(2,1)S(1)}, u32[]{:S(2)}, u32[]{:S(2)}) %collective-permute-start.15) | collective-permute-done | bytes 1179680 | tf_op jit(solution)/shard_map/ppermute | solution.py:51
  142.9 21.1 %collective-permute-done.18.refs_22_ = bf16[2304,256]{1,0:T(8,128)(2,1)} collective-permute-done((bf16[2304,256]{1,0:T(8,128)(2,1)}, bf16[2304,256]{1,0:T(8,128)(2,1)}, u32[]{:S(2)}, u32[]{:S(2)}) %collective-permute-start.18) | collective-permute-done | bytes 1179680 | tf_op jit(solution)/shard_map/ppermute | solution.py:51
  171.4 18.5 %collective-permute-done.22.refs_24_.refs_22_ = bf16[2304,256]{1,0:T(8,128)(2,1)} collective-permute-done((bf16[2304,256]{1,0:T(8,128)(2,1)S(1)}, bf16[2304,256]{1,0:T(8,128)(2,1)}, u32[]{:S(2)}, u32[]{:S(2)}) %collective-permute-start.22) | collective-permute-done | bytes 1179680 | tf_op jit(solution)/shard_map/ppermute | solution.py:51
  195.8 16.7 %collective-permute-done.26.refs_24_.refs_22_ = bf16[2304,256]{1,0:T(8,128)(2,1)} collective-permute-done((bf16[2304,256]{1,0:T(8,128)(2,1)}, bf16[2304,256]{1,0:T(8,128)(2,1)}, u32[]{:S(2)}, u32[]{:S(2)}) %collective-permute-start.26) | collective-permute-done | bytes 1179680 | tf_op jit(solution)/shard_map/ppermute | solution.py:51
  217.5 21.2 %chunk.4 = (bf16[1024,256]{1,0:T(8,128)(2,1)}, bf16[512,256]{1,0:T(8,128)(2,1)}, bf16[512,256]{1,0:T(8,128)(2,1)}, f32[8,256]{1,0:T(8,128)}, f32[2304,256]{1,0:T...) custom-call(s32[2]{0:T(128)} %pad_add_fusion.2.roles, ...), custom_call_target="tpu_custom_call" | custom-call | flops 1000 | bytes 1000 | tf_op jit(solution)/shard_map/chunk/pallas_call | solution.py:517
  241.3 9.0 %collective-permute-done.31.refs_21_ = bf16[2304,256]{1,0:T(8,128)(2,1)} collective-permute-done((bf16[2304,256]{1,0:T(8,128)(2,1)}, bf16[2304,256]{1,0:T(8,128)(2,1)}, u32[]{:S(2)}, u32[]{:S(2)}) %collective-permute-start.31) | collective-permute-done | bytes 1179680 | tf_op jit(solution)/shard_map/ppermute | solution.py:51
  254.4 21.3 %chunk.5 = (bf16[1024,256]{1,0:T(8,128)(2,1)}, bf16[512,256]{1,0:T(8,128)(2,1)}, bf16[512,256]{1,0:T(8,128)(2,1)}, f32[8,256]{1,0:T(8,128)}, f32[2304,256]{1,0:T...) custom-call(s32[2]{0:T(128)} %pad_add_fusion.2.roles, ...), custom_call_target="tpu_custom_call" | custom-call | flops 1000 | bytes 1000 | tf_op jit(solution)/shard_map/chunk/pallas_call | solution.py:517
  296.8 14.4 %collective-permute-done.40.refs_25_ = bf16[2304,256]{1,0:T(8,128)(2,1)S(1)} collective-permute-done((bf16[2304,256]{1,0:T(8,128)(2,1)}, bf16[2304,256]{1,0:T(8,128)(2,1)S(1)}, u32[]{:S(2)}, u32[]{:S(2)}) %collective-permute-start.40) | collective-permute-done | bytes 1179680 | tf_op jit(solution)/shard_map/ppermute | solution.py:51
  318.5 21.2 %chunk.6 = (bf16[1024,256]{1,0:T(8,128)(2,1)}, bf16[512,256]{1,0:T(8,128)(2,1)}, bf16[512,256]{1,0:T(8,128)(2,1)}, f32[8,256]{1,0:T(8,128)}, f32[2304,256]{1,0:T...) custom-call(s32[2]{0:T(128)} %pad_add_fusion.2.roles, ...), custom_call_target="tpu_custom_call" | custom-call | flops 1000 | bytes 1000 | tf_op jit(solution)/shard_map/chunk/pallas_call | solution.py:517
  340.9 5.4 collective-permute-start.47
  357.0 15.5 %collective-permute-done.47.refs_23_ = bf16[2304,256]{1,0:T(8,128)(2,1)S(1)} collective-permute-done((bf16[2304,256]{1,0:T(8,128)(2,1)}, bf16[2304,256]{1,0:T(8,128)(2,1)S(1)}, u32[]{:S(2)}, u32[]{:S(2)}) %collective-permute-start.47) | collective-permute-done | bytes 1179680 | tf_op jit(solution)/shard_map/ppermute | solution.py:51
  392.5 7.7 %collective-permute-done.48.refs_25_ = bf16[2304,256]{1,0:T(8,128)(2,1)} collective-permute-done((bf16[2304,256]{1,0:T(8,128)(2,1)}, bf16[2304,256]{1,0:T(8,128)(2,1)}, u32[]{:S(2)}, u32[]{:S(2)}) %collective-permute-start.48) | collective-permute-done | bytes 1179680 | tf_op jit(solution)/shard_map/ppermute | solution.py:51
  409.9 21.6 %chunk.7 = (bf16[1024,256]{1,0:T(8,128)(2,1)}, bf16[512,256]{1,0:T(8,128)(2,1)}, bf16[512,256]{1,0:T(8,128)(2,1)}, f32[8,256]{1,0:T(8,128)}, f32[2304,256]{1,0:T...) custom-call(s32[2]{0:T(128)} %pad_add_fusion.2.roles, ...), custom_call_target="tpu_custom_call" | custom-call | flops 1000 | bytes 1000 | tf_op jit(solution)/shard_map/chunk/pallas_call | solution.py:517
  435.1 5.5 collective-permute-start.69
  446.6 27.1 %back.1 = (bf16[64,9216]{1,0:T(8,128)(2,1)}, bf16[64,9216]{1,0:T(8,128)(2,1)}, bf16[64,9216]{1,0:T(8,128)(2,1)}, bf16[64,9216]{1,0:T(8,128)(2,1)}, bf16[64,9216]...) custom-call(bf16[512,256]{1,0:T(8,128)(2,1)} %get-tuple-element.515.refs_0_, ...), custom_call_target="tpu_custom_call" | custom-call | flops 1000 | bytes 1000 | tf_op jit(solution)/shard_map/back/pallas_call | solution.py:615
  473.8 4.2 collective-permute-start.72
  482.2 4.1 store.4.refs_0_
  489.9 12.5 %collective-permute-done.72 = bf16[2304,256]{1,0:T(8,128)(2,1)} collective-permute-done((bf16[2304,256]{1,0:T(8,128)(2,1)}, bf16[2304,256]{1,0:T(8,128)(2,1)}, u32[]{:S(2)}, u32[]{:S(2)}) %collective-permute-start.72) | collective-permute-done | bytes 1179680 | tf_op jit(solution)/shard_map/ppermute | solution.py:51
  502.4 4.6 collective-permute-start.75
  515.1 16.1 %collective-permute-done.75 = bf16[2304,256]{1,0:T(8,128)(2,1)S(1)} collective-permute-done((bf16[2304,256]{1,0:T(8,128)(2,1)S(1)}, bf16[2304,256]{1,0:T(8,128)(2,1)S(1)}, u32[]{:S(2)}, u32[]{:S(2)}) %collective-permute-start.75) | collective-permute-done | bytes 1179680 | tf_op jit(solution)/shard_map/ppermute | solution.py:51
  531.2 4.6 collective-permute-start.78
  545.1 14.0 %collective-permute-done.78 = bf16[2304,256]{1,0:T(8,128)(2,1)S(1)} collective-permute-done((bf16[2304,256]{1,0:T(8,128)(2,1)S(1)}, bf16[2304,256]{1,0:T(8,128)(2,1)S(1)}, u32[]{:S(2)}, u32[]{:S(2)}) %collective-permute-start.78) | collective-permute-done | bytes 1179680 | tf_op jit(solution)/shard_map/ppermute | solution.py:51
  571.5 5.0 first_grad.2
  577.9 15.5 %unpool.2.refs_0_ = bf16[128,169,2,256]{3,2,1,0:T(2,128)(2,1)} custom-call(s32[128]{0:T(128)} %group.7, bf16[2,352,192]{2,1,0:T(8,128)(2,1)} %fusion.14.table, f32[4,256]{1,0:T(4,128)} %reshape.582.first, bf16[64,9216]{1,0:T(8,128)(2,1)} %get-tuple-element.582.keep.keep_in, bf16[64,9216]{1,0:T(8,128)(2,1)} %copy-done.36, bf16[64,9216]{1,0:T(8,128)(2,1)} %copy-done.35), custom_call_target="tpu_custom_call" | custom-call | flops 1000 | bytes 1000 | tf_op jit(solution)/shard_map/unpool/pallas_call | solution.py:252
  600.2 4.9 first_grad.3
  610.0 15.3 %unpool.3 = bf16[128,169,2,256]{3,2,1,0:T(2,128)(2,1)} custom-call(s32[128]{0:T(128)} %group.7, bf16[2,352,192]{2,1,0:T(8,128)(2,1)} %fusion.14.table, f32[4,256]{1,0:T(4,128)} %reshape.582.first, bf16[64,9216]{1,0:T(8,128)(2,1)} %get-tuple-element.594.keep.keep_in, ...), custom_call_target="tpu_custom_call", output_to_operand_aliasing={{}: (6, {})} | custom-call | flops 1000 | bytes 1000 | tf_op jit(solution)/shard_map/unpool/pallas_call | solution.py:252
  628.7 13.0 %collective-permute-done.90.came = bf16[1152,256]{1,0:T(8,128)(2,1)S(1)} collective-permute-done((bf16[1152,256]{1,0:T(8,128)(2,1)}, bf16[1152,256]{1,0:T(8,128)(2,1)S(1)}, u32[]{:S(2)}, u32[]{:S(2)}) %collective-permute-start.90) | collective-permute-done | bytes 589856 | tf_op jit(solution)/shard_map/ppermute | solution.py:28
  (548 shorter events, 241.8 us)
Async XLA Ops:
  7.2 210.2 %all-gather.7.cloned.1.call-start = ((), (), s32[]{:S(2)}) async-start(), calls=%async_computation | async-start | bytes 3538944 | tf_op jit(solution)/shard_map/all_gather | solution.py:89
  36.9 34.7 %collective-permute-start.7 = (bf16[2304,256]{1,0:T(8,128)(2,1)S(1)}, bf16[2304,256]{1,0:T(8,128)(2,1)}, u32[]{:S(2)}, u32[]{:S(2)}) collective-permute-start(bf16[2304,256]{1,0:T(8,128)(2,1)S(1)} %maximum_select_fusion.refs_20_.refs_8_), channel_id=1, source_target_pairs={{0,8},{4,12},{8,0},{12,4},{16,24},{20,28},{24,16},{28,20},{1,9},{5... | collective-permute-start | bytes 3538952 | tf_op jit(solution)/shard_map/ppermute | solution.py:51
  38.6 35.2 %collective-permute-start.6 = (bf16[2304,256]{1,0:T(8,128)(2,1)S(1)}, bf16[2304,256]{1,0:T(8,128)(2,1)}, u32[]{:S(2)}, u32[]{:S(2)}) collective-permute-start(bf16[2304,256]{1,0:T(8,128)(2,1)S(1)} %maximum_select_fusion.refs_20_.refs_8_), channel_id=1, source_target_pairs={{8,16},{12,20},{16,8},{20,12},{9,17},{13,21},{17,9},{21,13},{10,18... | collective-permute-start | bytes 3538952 | tf_op jit(solution)/shard_map/ppermute | solution.py:51
  40.4 34.1 %collective-permute-start.5 = (bf16[1152,512]{1,0:T(8,128)(2,1)}, bf16[1152,512]{1,0:T(8,128)(2,1)}, u32[]{:S(2)}, u32[]{:S(2)}) collective-permute-start(bf16[1152,512]{1,0:T(8,128)(2,1)} %constant_dynamic-slice_fusion.3), channel_id=1, source_target_pairs={{0,4},{4,0},{8,12},{12,8},{16,20},{20,16},{24,28},{28,24},{1,5},{5... | collective-permute-start | bytes 3538952 | tf_op jit(solution)/shard_map/ppermute | solution.py:28
  42.2 32.3 %collective-permute-start.4 = (bf16[512,1024]{1,0:T(8,128)(2,1)S(1)}, bf16[512,1024]{1,0:T(8,128)(2,1)S(1)}, u32[]{:S(2)}, u32[]{:S(2)}) collective-permute-start(bf16[512,1024]{1,0:T(8,128)(2,1)S(1)} %constant_dynamic-slice_fusion.4.refs_0_), channel_id=1, source_target_pairs={{0,2},{1,3},{2,0},{3,1},{4,6},{5,7},{6,4},{7,5},{8,10},{9,11},{10,... | collective-permute-start | bytes 3145736 | tf_op jit(solution)/shard_map/ppermute | solution.py:28
  46.1 33.0 %collective-permute-start.3 = (bf16[512,512]{1,0:T(8,128)(2,1)}, bf16[512,512]{1,0:T(8,128)(2,1)}, u32[]{:S(2)}, u32[]{:S(2)}) collective-permute-start(bf16[512,512]{1,0:T(8,128)(2,1)} %get-tuple-element.322), channel_id=1, source_target_pairs={{0,4},{4,0},{8,12},{12,8},{16,20},{20,16},{24,28},{28,24},{1,5},{5... | collective-permute-start | bytes 1572872 | tf_op jit(solution)/shard_map/ppermute | solution.py:28
  106.4 111.0 %all-gather.9.cloned.1.call-start = ((), (), s32[]{:S(2)}) async-start(), calls=%async_computation.1 | async-start | bytes 3538944 | tf_op jit(solution)/shard_map/all_gather | solution.py:89
  107.4 110.0 %all-gather.11.cloned.1.call-start = ((), (), s32[]{:S(2)}) async-start(), calls=%async_computation.2 | async-start | bytes 3538944 | tf_op jit(solution)/shard_map/all_gather | solution.py:89
  108.1 109.3 %all-gather.15.cloned.1.call-start = ((), (), s32[]{:S(2)}) async-start(), calls=%async_computation.4 | async-start | bytes 3538944 | tf_op jit(solution)/shard_map/all_gather | solution.py:89
  108.7 108.8 %all-gather.13.cloned.1.call-start = ((), (), s32[]{:S(2)}) async-start(), calls=%async_computation.3 | async-start | bytes 3538944 | tf_op jit(solution)/shard_map/all_gather | solution.py:89
  141.1 76.4 %all-gather.17.cloned.1.call-start = ((), (), s32[]{:S(2)}) async-start(), calls=%async_computation.5 | async-start | bytes 3538944 | tf_op jit(solution)/shard_map/all_gather | solution.py:89
  213.5 36.8 %collective-permute-start.30 = (bf16[2304,256]{1,0:T(8,128)(2,1)}, bf16[2304,256]{1,0:T(8,128)(2,1)}, u32[]{:S(2)}, u32[]{:S(2)}) collective-permute-start(bf16[2304,256]{1,0:T(8,128)(2,1)} %collective-permute-done.22.refs_24_.refs_22_), channel_id=1, source_target_pairs={{8,16},{12,20},{16,8},{20,12},{9,17},{13,21},{17,9},{21,13},{10,18... | collective-permute-start | bytes 3538952 | tf_op jit(solution)/shard_map/ppermute | solution.py:51
  215.2 35.1 %collective-permute-start.31 = (bf16[2304,256]{1,0:T(8,128)(2,1)}, bf16[2304,256]{1,0:T(8,128)(2,1)}, u32[]{:S(2)}, u32[]{:S(2)}) collective-permute-start(bf16[2304,256]{1,0:T(8,128)(2,1)} %maximum_select_fusion.2.refs_20_.refs_16_), channel_id=1, source_target_pairs={{8,0},{12,4},{16,24},{20,28},{9,1},{13,5},{17,25},{21,29},{10,2},{... | collective-permute-start | bytes 3538952 | tf_op jit(solution)/shard_map/ppermute | solution.py:51
  279.8 36.5 %collective-permute-start.38 = (bf16[2304,256]{1,0:T(8,128)(2,1)S(1)}, bf16[2304,256]{1,0:T(8,128)(2,1)}, u32[]{:S(2)}, u32[]{:S(2)}) collective-permute-start(bf16[2304,256]{1,0:T(8,128)(2,1)S(1)} %copy-done.37), channel_id=1, source_target_pairs={{0,1},{1,0},{2,3},{3,2},{4,5},{5,4},{6,7},{7,6},{8,9},{9,8},{10,11... | collective-permute-start | bytes 3538952 | tf_op jit(solution)/shard_map/ppermute | solution.py:28
  279.8 36.4 %collective-permute-start.39 = (bf16[512,512]{1,0:T(8,128)(2,1)}, bf16[512,512]{1,0:T(8,128)(2,1)}, u32[]{:S(2)}, u32[]{:S(2)}) collective-permute-start(bf16[512,512]{1,0:T(8,128)(2,1)} %collective-permute-done.33.refs_1_), channel_id=1, source_target_pairs={{0,2},{1,3},{2,0},{3,1},{4,6},{5,7},{6,4},{7,5},{8,10},{9,11},{10,... | collective-permute-start | bytes 1572872 | tf_op jit(solution)/shard_map/ppermute | solution.py:28
  314.3 31.9 %collective-permute-start.45 = (bf16[2304,256]{1,0:T(8,128)(2,1)}, bf16[2304,256]{1,0:T(8,128)(2,1)}, u32[]{:S(2)}, u32[]{:S(2)}) collective-permute-start(bf16[2304,256]{1,0:T(8,128)(2,1)} %add_convert_fusion.12), channel_id=1, source_target_pairs={{8,16},{12,20},{16,8},{20,12},{9,17},{13,21},{17,9},{21,13},{10,18... | collective-permute-start | bytes 3538952 | tf_op jit(solution)/shard_map/ppermute | solution.py:51
  316.3 30.0 %collective-permute-start.42 = (bf16[2304,256]{1,0:T(8,128)(2,1)S(1)}, bf16[2304,256]{1,0:T(8,128)(2,1)}, u32[]{:S(2)}, u32[]{:S(2)}) collective-permute-start(bf16[2304,256]{1,0:T(8,128)(2,1)S(1)} %copy-done.38), channel_id=1, source_target_pairs={{0,1},{1,0},{2,3},{3,2},{4,5},{5,4},{6,7},{7,6},{8,9},{9,8},{10,11... | collective-permute-start | bytes 3538952 | tf_op jit(solution)/shard_map/ppermute | solution.py:28
  316.3 29.9 %collective-permute-start.43 = (bf16[1024,256]{1,0:T(8,128)(2,1)}, bf16[1024,256]{1,0:T(8,128)(2,1)}, u32[]{:S(2)}, u32[]{:S(2)}) collective-permute-start(bf16[1024,256]{1,0:T(8,128)(2,1)} %get-tuple-element.434), channel_id=1, source_target_pairs={{0,2},{1,3},{2,0},{3,1},{4,6},{5,7},{6,4},{7,5},{8,10},{9,11},{10,... | collective-permute-start | bytes 1572872 | tf_op jit(solution)/shard_map/ppermute | solution.py:28
  340.9 31.7 %collective-permute-start.47 = (bf16[2304,256]{1,0:T(8,128)(2,1)}, bf16[2304,256]{1,0:T(8,128)(2,1)S(1)}, u32[]{:S(2)}, u32[]{:S(2)}) collective-permute-start(bf16[2304,256]{1,0:T(8,128)(2,1)} %broadcast_select_fusion.6), channel_id=1, source_target_pairs={{0,8},{4,12},{8,0},{12,4},{16,24},{20,28},{24,16},{28,20},{1,9},{5... | collective-permute-start | bytes 3538952 | tf_op jit(solution)/shard_map/ppermute | solution.py:51
  346.3 31.2 %collective-permute-start.49 = (bf16[1024,256]{1,0:T(8,128)(2,1)}, bf16[1024,256]{1,0:T(8,128)(2,1)}, u32[]{:S(2)}, u32[]{:S(2)}) collective-permute-start(bf16[1024,256]{1,0:T(8,128)(2,1)} %get-tuple-element.446), channel_id=1, source_target_pairs={{0,2},{1,3},{2,0},{3,1},{4,6},{5,7},{6,4},{7,5},{8,10},{9,11},{10,... | collective-permute-start | bytes 1572872 | tf_op jit(solution)/shard_map/ppermute | solution.py:28
  400.2 34.2 %collective-permute-start.60 = (bf16[2304,256]{1,0:T(8,128)(2,1)}, bf16[2304,256]{1,0:T(8,128)(2,1)S(1)}, u32[]{:S(2)}, u32[]{:S(2)}) collective-permute-start(bf16[2304,256]{1,0:T(8,128)(2,1)} %fusion), channel_id=1, source_target_pairs={{0,8},{4,12},{8,0},{12,4},{16,24},{20,28},{24,16},{28,20},{1,9},{5... | collective-permute-start | bytes 3538952 | tf_op jit(solution)/shard_map/ppermute | solution.py:51
  435.1 38.7 %collective-permute-start.69 = (bf16[2304,256]{1,0:T(8,128)(2,1)}, bf16[2304,256]{1,0:T(8,128)(2,1)S(1)}, u32[]{:S(2)}, u32[]{:S(2)}) collective-permute-start(bf16[2304,256]{1,0:T(8,128)(2,1)} %fusion.1), channel_id=1, source_target_pairs={{0,8},{4,12},{8,0},{12,4},{16,24},{20,28},{24,16},{28,20},{1,9},{5... | collective-permute-start | bytes 3538952 | tf_op jit(solution)/shard_map/ppermute | solution.py:51
  444.7 33.2 %collective-permute-start.70 = (bf16[1152,256]{1,0:T(8,128)(2,1)}, bf16[1152,256]{1,0:T(8,128)(2,1)S(1)}, u32[]{:S(2)}, u32[]{:S(2)}) collective-permute-start(bf16[1152,256]{1,0:T(8,128)(2,1)} %dynamic-slice_convert_fusion.3), channel_id=1, source_target_pairs={{0,4},{4,0},{8,12},{12,8},{16,20},{20,16},{24,28},{28,24},{1,5},{5... | collective-permute-start | bytes 1769480 | tf_op jit(solution)/shard_map/ppermute | solution.py:28
  446.1 36.0 %collective-permute-start.68 = (bf16[1024,256]{1,0:T(8,128)(2,1)}, bf16[1024,256]{1,0:T(8,128)(2,1)S(1)}, u32[]{:S(2)}, u32[]{:S(2)}) collective-permute-start(bf16[1024,256]{1,0:T(8,128)(2,1)} %get-tuple-element.513), channel_id=1, source_target_pairs={{0,2},{1,3},{2,0},{3,1},{4,6},{5,7},{6,4},{7,5},{8,10},{9,11},{10,... | collective-permute-start | bytes 1572872 | tf_op jit(solution)/shard_map/ppermute | solution.py:28
  539.5 30.5 %collective-permute-start.80 = (bf16[64,9216]{1,0:T(8,128)(2,1)S(1)}, bf16[64,9216]{1,0:T(8,128)(2,1)S(1)}, u32[]{:S(2)}, u32[]{:S(2)}) collective-permute-start(bf16[64,9216]{1,0:T(8,128)(2,1)S(1)} %add_convert_fusion.3), channel_id=1, source_target_pairs={{0,2},{1,3},{2,0},{3,1},{4,6},{5,7},{6,4},{7,5},{8,10},{9,11},{10,... | collective-permute-start | bytes 3538952 | tf_op jit(solution)/shard_map/ppermute | solution.py:28
  559.1 34.3 %collective-permute-start.79 = (bf16[2304,256]{1,0:T(8,128)(2,1)}, bf16[2304,256]{1,0:T(8,128)(2,1)}, u32[]{:S(2)}, u32[]{:S(2)}) collective-permute-start(bf16[2304,256]{1,0:T(8,128)(2,1)} %fusion.2), channel_id=1, source_target_pairs={{0,8},{4,12},{8,0},{12,4},{16,24},{20,28},{24,16},{28,20},{1,9},{5... | collective-permute-start | bytes 3538952 | tf_op jit(solution)/shard_map/ppermute | solution.py:51
  563.1 34.0 %collective-permute-start.84 = (bf16[2304,256]{1,0:T(8,128)(2,1)}, bf16[2304,256]{1,0:T(8,128)(2,1)}, u32[]{:S(2)}, u32[]{:S(2)}) collective-permute-start(bf16[2304,256]{1,0:T(8,128)(2,1)} %add_convert_fusion.1), channel_id=1, source_target_pairs={{8,16},{12,20},{16,8},{20,12},{9,17},{13,21},{17,9},{21,13},{10,18... | collective-permute-start | bytes 3538952 | tf_op jit(solution)/shard_map/ppermute | solution.py:51
  567.0 30.1 %collective-permute-start.83 = (bf16[64,9216]{1,0:T(8,128)(2,1)}, bf16[64,9216]{1,0:T(8,128)(2,1)}, u32[]{:S(2)}, u32[]{:S(2)}) collective-permute-start(bf16[64,9216]{1,0:T(8,128)(2,1)} %get-tuple-element.577), channel_id=1, source_target_pairs={{0,4},{4,0},{8,12},{12,8},{16,20},{20,16},{24,28},{28,24},{1,5},{5... | collective-permute-start | bytes 3538952 | tf_op jit(solution)/shard_map/ppermute | solution.py:28
  593.4 33.5 %collective-permute-start.89 = (bf16[2304,256]{1,0:T(8,128)(2,1)}, bf16[2304,256]{1,0:T(8,128)(2,1)S(1)}, u32[]{:S(2)}, u32[]{:S(2)}) collective-permute-start(bf16[2304,256]{1,0:T(8,128)(2,1)} %fusion.3), channel_id=1, source_target_pairs={{0,8},{4,12},{8,0},{12,4},{16,24},{20,28},{24,16},{28,20},{1,9},{5... | collective-permute-start | bytes 3538952 | tf_op jit(solution)/shard_map/ppermute | solution.py:51
  607.4 46.5 %collective-permute-start.85 = (bf16[512,256]{1,0:T(8,128)(2,1)}, bf16[512,256]{1,0:T(8,128)(2,1)S(1)}, u32[]{:S(2)}, u32[]{:S(2)}) collective-permute-start(bf16[512,256]{1,0:T(8,128)(2,1)} %bitcast.94), channel_id=1, source_target_pairs={{0,4},{4,0},{8,12},{12,8},{16,20},{20,16},{24,28},{28,24},{1,5},{5... | collective-permute-start | bytes 786440 | tf_op jit(solution)/shard_map/ppermute | solution.py:28
  608.0 41.3 %collective-permute-start.86 = (bf16[1152,256]{1,0:T(8,128)(2,1)}, bf16[1152,256]{1,0:T(8,128)(2,1)S(1)}, u32[]{:S(2)}, u32[]{:S(2)}) collective-permute-start(bf16[1152,256]{1,0:T(8,128)(2,1)} %dynamic-slice_convert_fusion.1), channel_id=1, source_target_pairs={{0,4},{4,0},{8,12},{12,8},{16,20},{20,16},{24,28},{28,24},{1,5},{5... | collective-permute-start | bytes 1769480 | tf_op jit(solution)/shard_map/ppermute | solution.py:28
  609.5 32.1 %collective-permute-start.90 = (bf16[1152,256]{1,0:T(8,128)(2,1)}, bf16[1152,256]{1,0:T(8,128)(2,1)S(1)}, u32[]{:S(2)}, u32[]{:S(2)}) collective-permute-start(bf16[1152,256]{1,0:T(8,128)(2,1)} %dynamic-slice_convert_fusion.2), channel_id=1, source_target_pairs={{0,4},{4,0},{8,12},{12,8},{16,20},{20,16},{24,28},{28,24},{1,5},{5... | collective-permute-start | bytes 1769480 | tf_op jit(solution)/shard_map/ppermute | solution.py:28
  (183 other events, 2570.0 us)
Sparse Core Ops, SparseCore 0:
  106.5 11.2 all-gather.6
  119.4 12.1 all-gather.8
  133.7 12.1 all-gather.10
  147.2 12.1 all-gather.14
  160.8 12.1 all-gather.12
  192.8 14.2 all-gather.16

commit v4 on v3

--- a/solution.py
+++ b/solution.py
@@ -89,7 +89,7 @@
     return lax.all_gather(value, "tower", axis=0, tiled=True, axis_index_groups=core_groups())
 
 
-def pool_table(order):
+def windows(order):
     map_pos = jnp.arange(169)[None, :]
     prow = (order // 6)[:, None]
     pcol = (order % 6)[:, None]
@@ -98,24 +98,28 @@
     inside = (
         (qrow >= 2 * prow) & (qrow <= 2 * prow + 2) & (qcol >= 2 * pcol) & (qcol <= 2 * pcol + 2)
     )
-    small = (prow < 5) & (pcol < 5)
+    return inside, (prow < 5) & (pcol < 5)
+
+
+def spread_table(order):
+    inside, small = windows(order)
     table = jnp.stack([inside, inside & small]).astype(BF16)
     table = jnp.pad(table, ((0, 0), (0, PITCH - POOLED), (0, 0)))
     both = table[:, None, :, :, None] * jnp.eye(2, dtype=BF16)[None, :, None, None, :]
-    return both.reshape(2, 2 * PITCH, 338)
-
-
-def pool_kernel(start, group, table, first, maps, *refs):
-    *feature_outs, pooled_out, own, other, pool0, pool1 = refs[-(2 * HALVES + 5) :]
-    count, places, _, ch = maps.shape
-    base = (start + pl.program_id(0)) * count
+    spread = jnp.swapaxes(both.reshape(2, 2 * PITCH, 338), 1, 2)
+    return jnp.pad(jnp.concatenate([spread, spread], axis=2), ((0, 0), (0, 352 - 338), (0, 0)))
+
+
+def mix_kernel(group, keep, first, summed, *refs):
+    *feature_outs, pooled_out, own, other, pool0, pool1 = refs
+    count, _, places, ch = summed.shape
+    base = pl.program_id(0) * count
 
     def image(n, carry):
-        window = table[group[base + n]]
-        rows_in = maps[n].reshape(2 * places, ch)
-        both = jnp.dot(window, rows_in, preferred_element_type=F32) * (1.0 / 9.0)
-        p0, p1 = both[:PITCH], both[PITCH:]
-        rows = pl.ds(pl.multiple_of(n * PITCH, PITCH), PITCH)
+        scale = keep[group[base + n]]
+        p0 = summed[n, 0] * scale
+        p1 = summed[n, 1] * scale
+        rows = pl.ds(pl.multiple_of(n * PITCH, PITCH), places)
         mixed0 = first[0:1, :] * p0 + first[1:2, :] * p1
         mixed1 = first[2:3, :] * p0 + first[3:4, :] * p1
         for hold, value in ((pool0, p0), (pool1, p1), (own, mixed0), (other, mixed1)):
@@ -136,33 +140,31 @@
             pooled_out[1, :, lanes] = pool1[h, rows, :]
 
 
-def pool(convmaps, group, table, first, at, steps, before=()):
-    count, _, places, ch = convmaps.shape
+def mix(summed, group, keep, first):
+    count, _, places, ch = summed.shape
     nb = IMAGE_BLOCK
-    feats = POOLED * ch
+    feats = places * ch
     features = [((count, feats // HALVES), BF16)] * (2 * HALVES)
     return pl.pallas_call(
-        functools.partial(pool_kernel, at),
+        mix_kernel,
         grid_spec=pltpu.PrefetchScalarGridSpec(
             num_scalar_prefetch=1,
-            grid=(steps,),
+            grid=(count // nb,),
             in_specs=[
-                pl.BlockSpec(table.shape, lambda i, g: (0, 0, 0)),
+                pl.BlockSpec(keep.shape, lambda i, g: (0, 0, 0)),
                 pl.BlockSpec((4, ch), lambda i, g: (0, 0)),
-                pl.BlockSpec((nb, places, 2, ch), lambda i, g: (at + i, 0, 0, 0)),
-            ]
-            + [pl.BlockSpec(memory_space=pl.ANY)] * len(before),
-            out_specs=[pl.BlockSpec((nb, feats // HALVES), lambda i, g: (at + i, 0))] * (2 * HALVES)
-            + [pl.BlockSpec((2, nb, feats), lambda i, g: (0, at + i, 0))],
+                pl.BlockSpec((nb, 2, places, ch), lambda i, g: (i, 0, 0, 0)),
+            ],
+            out_specs=[pl.BlockSpec((nb, feats // HALVES), lambda i, g: (i, 0))] * (2 * HALVES)
+            + [pl.BlockSpec((2, nb, feats), lambda i, g: (0, i, 0))],
             scratch_shapes=[pltpu.VMEM((ch // LANES, nb * PITCH, LANES), F32)] * 4,
         ),
         out_shape=[jax.ShapeDtypeStruct(*f) for f in features]
         + [jax.ShapeDtypeStruct((2, count, feats), F32)],
-        input_output_aliases={4 + i: i for i in range(len(before))},
         compiler_params=params(),
         cost_estimate=SMALL,
-        name="pool",
-    )(group, table, first, jnp.swapaxes(convmaps, 1, 2), *before)
+        name="mix",
+    )(group, keep, first, summed)
 
 
 def first_grad_kernel(pooled, keep, came, other, out):
@@ -247,15 +249,13 @@
     ch = first.shape[1]
     nb = IMAGE_BLOCK
     rows = pl.BlockSpec((nb, feats), lambda i, g: (i, 0))
-    spread = jnp.swapaxes(table, 1, 2)
-    spread = jnp.pad(jnp.concatenate([spread, spread], axis=2), ((0, 0), (0, 352 - 2 * places), (0, 0)))
     return pl.pallas_call(
         functools.partial(unpool_kernel, at),
         grid_spec=pltpu.PrefetchScalarGridSpec(
             num_scalar_prefetch=1,
             grid=(images // nb,),
             in_specs=[
-                pl.BlockSpec(spread.shape, lambda i, g: (0, 0, 0)),
+                pl.BlockSpec(table.shape, lambda i, g: (0, 0, 0)),
                 pl.BlockSpec((4, ch), lambda i, g: (0, 0)),
                 rows,
                 rows,
@@ -270,7 +270,7 @@
         compiler_params=params(),
         cost_estimate=SMALL,
         name="unpool",
-    )(group, spread, first, keep, came, other, *before)
+    )(group, table, first, keep, came, other, *before)
 
 
 def store_kernel(chunk, chunks, x, own, came, *refs):
@@ -546,11 +546,18 @@
     )(roles, vectors, *[cot for cot, _ in cots], *[part for block in feats for part, _ in block], *terms)
 
 
-def back_kernel(count, *refs):
-    outs = refs[-14:-6]
+def back_kernel(layout, firsts, blocks, roles, *refs):
+    outs = refs[-10:-6]
     grad, weight, made, grad_sems, w_sems, out_sems = refs[-6:]
-    sources = (len(refs) - 14) // (1 + count)
-    grads, pieces = refs[:sources], refs[sources:-14]
+    sources, count = len(layout), len(layout[0])
+    grads = refs[:sources]
+    at = sources
+    pieces = []
+    for counts in layout:
+        pieces.append([])
+        for many in counts:
+            pieces[-1].append(refs[at : at + many])
+            at += many
     slots, tile, total = weight.shape
     units = total // sources
     steps = made.shape[0]
@@ -568,16 +575,19 @@
             def _(s=s):
                 rows = pl.ds(pl.multiple_of((k - s * per) * tile, tile), tile)
                 for j in range(sources):
-                    piece = pieces[j * count + s].at[rows, :]
-                    pltpu.make_async_copy(piece, weight.at[slot, :, columns(j)], w_sems.at[slot]).start()
+                    fetch(roles[0], pieces[j][s], rows, weight.at[slot, :, columns(j)], w_sems.at[slot])
 
     def arrive(target, sem):
         pltpu.make_async_copy(target, target, sem).wait()
 
     copies = []
     for j in range(sources):
-        copies.append(pltpu.make_async_copy(grads[j], grad.at[:, columns(j)], grad_sems.at[j]))
-        copies[-1].start()
+        for i, block in enumerate(blocks):
+            rows = grad.shape[0] // len(blocks)
+            source = grads[j].at[pl.ds(firsts[j] + block * rows, rows), :]
+            target = grad.at[pl.ds(i * rows, rows), columns(j)]
+            copies.append(pltpu.make_async_copy(source, target, grad_sems.at[j, i]))
+            copies[-1].start()
     ahead = min(slots - 1, steps)
     for k in range(ahead):
         begin(jnp.int32(k))
@@ -602,33 +612,35 @@
         arrive(made.at[k], out_sems.at[k])
 
 
-def back(grads, pieces):
-    images, units = grads[0].shape
+def back(roles, grads, pieces, blocks):
+    units = grads[0][0].shape[1]
+    images = min(grad.shape[0] for grad, _ in grads) // 4 * len(blocks)
     count = len(pieces[0])
-    height = pieces[0][0].shape[0]
+    height = pieces[0][0][0].shape[0]
     depth = height * count
     tile = next(t for t in (768, 512, 384, 256, 128) if height % t == 0)
     steps = depth // tile
     total = units * len(grads)
-    terms = [piece for chunk in pieces for piece in chunk]
+    terms = [term for chunk in pieces for piece in chunk for term in piece]
+    layout = [[len(piece) for piece in chunk] for chunk in pieces]
     anywhere = pl.BlockSpec(memory_space=pl.ANY)
     return pl.pallas_call(
-        functools.partial(back_kernel, count),
-        in_specs=[anywhere] * (len(grads) + len(terms)),
-        out_specs=[anywhere] * 8,
-        out_shape=[jax.ShapeDtypeStruct((images // 8, depth), BF16)] * 8,
+        functools.partial(back_kernel, layout, [row for _, row in grads], blocks),
+        in_specs=[pl.BlockSpec(memory_space=pltpu.SMEM)] + [anywhere] * (len(grads) + len(terms)),
+        out_specs=[anywhere] * 4,
+        out_shape=[jax.ShapeDtypeStruct((images // 4, depth), BF16)] * 4,
         scratch_shapes=[
             pltpu.VMEM((images, total), BF16),
             pltpu.VMEM((AHEAD + 1, tile, total), BF16),
             pltpu.VMEM((steps, images, tile), BF16),
-            pltpu.SemaphoreType.DMA((len(grads),)),
+            pltpu.SemaphoreType.DMA((len(grads), len(blocks))),
             pltpu.SemaphoreType.DMA((AHEAD + 1,)),
             pltpu.SemaphoreType.DMA((steps,)),
         ],
         compiler_params=params(),
         cost_estimate=SMALL,
         name="back",
-    )(*grads, *terms)
+    )(roles, *[grad for grad, _ in grads], *terms)
 
 
 def either(flag, value, axis):
@@ -656,15 +668,15 @@
         self.cross = lax.dynamic_index_in_dim(second, 1 - self.y, 0, keepdims=True)
         own_bias = lax.dynamic_slice_in_dim(bias, self.mine, units, 0)[None, :].astype(F32)
         self.own_bias = own_bias
-        cot = cotangent.reshape(2, 2, self.count, self.width)
-        cot = either(self.core == 1, either(self.y == 1, cot, 0), 1).swapaxes(0, 1)
-        cot = cot.reshape(-1, self.width)
-        self.cot_mine = lax.dynamic_slice_in_dim(cot, self.mine, units, 1)
-        self.cot_theirs = lax.dynamic_slice_in_dim(cot, self.theirs, units, 1)
+        self.cotangent = cotangent
         places = jnp.arange(POOLED)
         if is_line():
             places = places.reshape(4, -1)[line_order(self.z)].reshape(-1)
-        self.table = pool_table(places)
+        self.table = spread_table(places)
+        inside, small = windows(places)
+        self.pool_table = inside.astype(BF16)
+        keep = jnp.stack([jnp.ones_like(small), small]).astype(F32) * (1.0 / 9.0)
+        self.keep = jnp.broadcast_to(keep, (2, POOLED, self.channels))
         self.first = either(self.y == 1, alpha1.astype(F32), 0).reshape(4, self.channels)
         self.is_outer = (self.z == 0) | (self.z == 3)
         self.roles = jnp.stack([self.is_outer.astype(jnp.int32), 1 - self.core])
@@ -686,6 +698,18 @@
         self.vectors = jnp.concatenate([self.own_bias, self.own_coef, cross_back, zeros])
         self.cross = self.cross.astype(F32)
 
+    def load_cotangents(self):
+        cot = self.then(self.cotangent).reshape(2, 2, self.count, self.width)
+        cot = either(self.core == 1, either(self.y == 1, cot, 0), 1).swapaxes(0, 1).reshape(-1, self.width)
+        self.cot_mine = self.did(lax.dynamic_slice_in_dim(cot, self.mine, self.units, 1))
+        self.cot_theirs = lax.dynamic_slice_in_dim(cot, self.theirs, self.units, 1)
+
+    def pool(self):
+        return jnp.einsum("pq,nsqc->nspc", self.pool_table, self.convmaps, preferred_element_type=F32)
+
+    def mix(self, summed):
+        return mix(summed, self.group, self.keep, self.first)
+
     def cols(self, j):
         return slice(j * self.n, (j + 1) * self.n)
 
@@ -693,7 +717,7 @@
         return slice(js[0] * self.n, (js[-1] + 1) * self.n)
 
     def weight_part(self, start, j, many=1):
-        return lax.dynamic_slice(self.weight, (0, start + j * self.n), (self.depth, many * self.n))
+        return lax.dynamic_slice(self.then(self.weight), (0, start + j * self.n), (self.depth, many * self.n))
 
     def swap_weight(self, j, many=1):
         return self.send(x_swap, self.weight_part(self.theirs, j, many))
@@ -755,15 +779,18 @@
         )
         return wide[0], either(self.y == 1, wide[1:3], 0)
 
-    def back(self, came_grads, pieces, came_pieces):
+    def back(self, y, came_grads, pieces, came_pieces):
         chunks = range(self.chunks)
-        grads = [self.grads[j] for j in chunks] + [came_grads[j] for j in chunks]
+        grads = [(self.grads[j], 0) for j in chunks] + list(came_grads)
+        grads[0] = (self.then(grads[0][0]), 0)
         parts = back(
-            [self.then(grads[0])] + grads[1:],
+            self.roles,
+            grads,
             [pieces[j] for j in chunks] + [came_pieces[j] for j in chunks],
+            [y, 2 + y],
         )
         self.did(parts[0])
-        return parts[:4], parts[4:]
+        return parts[:2], parts[2:]
 
     def add(self, keep, came):
         return self.did((keep.astype(F32) + self.then(came).astype(F32)).astype(BF16))
@@ -840,45 +867,39 @@
     def core_came(j, s):
         came_pieces[j, s] = arrive(came_pieces[j, s])
 
-    picked, came_pieces, came_grads = {}, {}, {}
+    picked, came_pieces = {}, {}
 
     def far_end(j):
         return plus(j, 3, into[j, 3])
-
-    image_blocks = p.count // IMAGE_BLOCK
-    cuts = [0, image_blocks // 4, image_blocks]
-
-    def pool_part(i, before=()):
-        made = pool(
-            p.convmaps, p.group, then(p.table), p.first, cuts[i], cuts[i + 1] - cuts[i], before
-        )
-        did(made[0])
-        return made
 
     came[0] = p.swap_weight(0)
     came[1] = p.swap_weight(1)
     cross_came = p.send(y_swap, p.cross)
-    made = pool_part(0)
+    came_pair = p.swap_weight(2, 2)
+    p.load_cotangents()
+    p.keep_cross(cross_came)
     came[0] = arrive(came[0])
     block(0)
     near[0] = ends(blocks[0])
     inner[0] = send("middle", blocks[0])
-    p.keep_cross(cross_came)
+    p.cot_across = p.send(y_swap, p.cot_mine)
+    p.pool_table = then(p.pool_table)
+    summed = did(p.pool())
     came[1] = arrive(came[1])
-    came_pair = p.swap_weight(2, 2)
-    p.cot_across = p.send(y_swap, p.cot_mine)
     cot_came = p.swap_cotangents([0, 1])
     block(1)
-    kept_a, kept_b, sent_a, sent_b, pooled = pool_part(1, made)
     near[0] = arrive(near[0])
     near[1] = ends(blocks[1])
     inner[0] = arrive(inner[0])
     inner[1] = send("middle", blocks[1])
+    kept_a, kept_b, sent_a, sent_b, pooled = p.mix(then(summed))
+    did(kept_a)
     came_pair = arrive(came_pair)
     p.cot_across = arrive(p.cot_across)
     cot_came = arrive(cot_came)
     x_a = p.send(x_swap, kept_a)
     y_a = p.send(y_swap, sent_a)
+    c_kept_a = p.send(c_swap, kept_a)
     came[2], came[3] = came_pair[:, : p.n], came_pair[:, p.n :]
     block(2)
     block(3)
@@ -890,8 +911,8 @@
     x_b = p.send(x_swap, kept_b)
     y_a = arrive(y_a)
     y_b = p.send(y_swap, sent_b)
-    c_kept = [both_cores(arrive(kept_a)), both_cores(arrive(kept_b))]
-    c_x_a, c_y_a = both_cores(x_a), both_cores(y_a)
+    c_kept_a = arrive(c_kept_a)
+    c_kept_b = p.send(c_swap, kept_b)
     first_out[0] = arrive(first_out[0])
     first_out[1] = send("outward", inner[1])
     outer[0] = arrive(outer[0])
@@ -900,7 +921,8 @@
     x_y_a = p.send(x_swap, y_a)
     y_b = arrive(y_b)
     cot_crossed = p.send(y_swap, cot_came)
-    c_x_b, c_y_b = both_cores(x_b), both_cores(y_b)
+    c_kept_b = arrive(c_kept_b)
+    c_x_a = p.send(c_swap, x_a)
     value = payload(blocks[2], outer[0])
     first_out[1] = arrive(first_out[1])
     swapped[2] = last_out[0] = ends(value)
@@ -909,48 +931,51 @@
     x_y_a = arrive(x_y_a)
     x_y_b = p.send(x_swap, y_b)
     p.cots[0] = p.cots[1] = (cot_came, arrive(cot_crossed))
+    c_x_a = arrive(c_x_a)
+    c_y_a = p.send(c_swap, y_a)
+    c_x_b = p.send(c_swap, x_b)
+    value = payload(blocks[3], outer[1])
     for j in range(4):
         picked[j, 0] = blocks[j]
     picked[0, 1], picked[1, 1] = near[0], near[1]
-    core_swap(0, 0)
-    value = payload(blocks[3], outer[1])
     picked[0, 2] = pick(first_out[0], inner[0])
-    picked[1, 2] = pick(first_out[1], inner[1])
     swapped[2] = last_out[0] = arrive(swapped[2])
     swapped[3] = last_out[1] = ends(value)
     inner[2] = arrive(inner[2])
-    inner[3] = send("middle", blocks[3])
+    outer[2] = send("middle", swapped[2])
     x_y_b = arrive(x_y_b)
-    core_came(0, 0)
+    c_y_a = arrive(c_y_a)
+    c_x_b = arrive(c_x_b)
+    c_y_b = p.send(c_swap, y_b)
     c_x_y_a = p.send(c_swap, x_y_a)
+    c_x_y_b = p.send(c_swap, x_y_b)
+    picked[1, 2] = pick(first_out[1], inner[1])
+    swapped[3] = last_out[1] = arrive(swapped[3])
+    from_own[2] = send("outward", blocks[2])
+    c_y_b = arrive(c_y_b)
+    c_x_y_a = arrive(c_x_y_a)
+    c_x_y_b = arrive(c_x_y_b)
+    core_swap(0, 0)
     core_swap(0, 1)
     core_swap(1, 0)
-    picked[0, 3] = pick(last_out[0], outer[0])
-    swapped[3] = last_out[1] = arrive(swapped[3])
-    from_own[2] = send("outward", blocks[2])
-    inner[3] = arrive(inner[3])
-    outer[2] = send("middle", swapped[2])
-    c_x_y_a = arrive(c_x_y_a)
-    c_x_y_b = p.send(c_swap, x_y_b)
-    core_came(0, 1)
-    core_came(1, 0)
-    c_x_y_b = arrive(c_x_y_b)
     feats = [
         [(kept_a, 0), (kept_b, 0)],
         [(y_a, 0), (y_b, 0)],
         [(x_a, 0), (x_b, 0)],
         [(x_y_a, 0), (x_y_b, 0)],
-        [(c_kept[0], None), (c_kept[1], None)],
-        [(c_y_a, None), (c_y_b, None)],
-        [(c_x_a, None), (c_x_b, None)],
+        [(c_kept_a, 0), (c_kept_b, 0)],
+        [(c_y_a, 0), (c_y_b, 0)],
+        [(c_x_a, 0), (c_x_b, 0)],
         [(c_x_y_a, 0), (c_x_y_b, 0)],
     ]
     total[0] = p.chunk(0, feats, pieces(0))
     value = payload(part(0, 3), inner[2])
     from_own[2] = arrive(from_own[2])
     into[0, 3] = first_out[2] = ends(value)
+    for at in ((0, 0), (0, 1), (1, 0)):
+        core_came(*at)
     outer[2] = arrive(outer[2])
-    outer[3] = send("middle", swapped[3])
+    inner[3] = send("middle", blocks[3])
     cot_came = p.swap_cotangents([2, 3])
     act_came = p.send(y_swap, p.acts[0])
     core_swap(1, 1)
@@ -958,161 +983,178 @@
     value = payload(part(0, 2), outer[2])
     into[0, 3] = first_out[2] = arrive(into[0, 3])
     into[0, 2] = last_out[2] = ends(value)
-    outer[3] = arrive(outer[3])
-    crossed[0] = send("middle", far_end(0))
+    inner[3] = arrive(inner[3])
+    outer[3] = send("middle", swapped[3])
+    value = payload(part(0, 1), blocks[3])
     cot_came = arrive(cot_came)
     act_came = arrive(act_came)
+    core_came(1, 1)
     cot_crossed = p.send(y_swap, cot_came)
-    core_came(1, 1)
     core_swap(0, 2)
     core_swap(1, 2)
-    value = payload(part(0, 1), blocks[3])
-    mix = p.stitch(0, act_came)
-    picked[1, 3] = pick(last_out[1], outer[1])
-    picked[2, 1] = pick(from_own[2], swapped[2])
+    act_mix = p.stitch(0, act_came)
+    picked[0, 3] = pick(last_out[0], outer[0])
     into[0, 2] = last_out[2] = arrive(into[0, 2])
     into[0, 1] = from_own[3] = ends(value)
-    crossed[0] = arrive(crossed[0])
-    middle[0] = send("middle", plus(0, 2, into[0, 2]))
+    rest = did(far_end(0))
+    outer[3] = arrive(outer[3])
+    crossed[0] = send("middle", rest)
     p.cots[2] = p.cots[3] = (cot_came, arrive(cot_crossed))
     core_came(0, 2)
     core_came(1, 2)
-    p.crossed[0] = p.send(x_swap, mix)
+    p.crossed[0] = p.send(x_swap, act_mix)
     act_came = p.send(y_swap, p.acts[1])
     core_swap(0, 3)
     total[2] = p.chunk(2, feats, pieces(2))
     value = payload(part(1, 3), inner[3])
     into[0, 1] = from_own[3] = arrive(into[0, 1])
     into[1, 3] = first_out[3] = ends(value)
-    middle[0] = arrive(middle[0])
+    rest = did(plus(0, 2, into[0, 2]))
+    picked[1, 3] = pick(last_out[1], outer[1])
+    crossed[0] = arrive(crossed[0])
+    middle[0] = send("middle", rest)
     p.crossed[0] = arrive(p.crossed[0])
     act_came = arrive(act_came)
     core_came(0, 3)
     act_came2 = p.send(y_swap, p.acts[2])
     core_swap(1, 3)
     core_swap(2, 0)
-    core_swap(3, 0)
     value = payload(part(1, 2), outer[3])
-    mix = p.stitch(1, act_came)
+    act_mix = p.stitch(1, act_came)
+    picked[2, 1] = pick(from_own[2], swapped[2])
     picked[2, 2] = pick(first_out[2], inner[2])
-    picked[2, 3] = pick(last_out[2], outer[2])
     picked[3, 1] = pick(from_own[3], swapped[3])
     into[1, 3] = first_out[3] = arrive(into[1, 3])
     into[1, 2] = last_out[3] = ends(value)
-    for at in ((1, 3), (2, 0), (3, 0)):
-        core_came(*at)
-    crossed[1] = send("middle", far_end(1))
+    rest = did(far_end(1))
+    value = payload(part(1, 1), plus(0, 1, crossed[0]))
+    picked[2, 3] = pick(last_out[2], outer[2])
+    middle[0] = arrive(middle[0])
+    crossed[1] = send("middle", rest)
     act_came = arrive(act_came2)
-    p.crossed[1] = p.send(x_swap, mix)
+    core_came(1, 3)
+    core_came(2, 0)
+    p.crossed[1] = p.send(x_swap, act_mix)
+    core_swap(3, 0)
+    core_swap(3, 1)
+    act_mix = p.stitch(2, act_came)
+    picked[3, 2] = pick(first_out[3], inner[3])
+    far = did(jnp.concatenate([then(p.far_grads[0]), p.far_grads[1], p.far_grads[2]]))
+    into[1, 2] = last_out[3] = arrive(into[1, 2])
+    into[1, 1] = final[0] = ends(value)
+    p.crossed[1] = arrive(p.crossed[1])
+    core_came(3, 0)
+    core_came(3, 1)
+    p.crossed[2] = p.send(x_swap, act_mix)
     core_swap(2, 1)
     core_swap(2, 2)
-    value = payload(part(1, 1), plus(0, 1, crossed[0]))
-    picked[3, 2] = pick(first_out[3], inner[3])
-    mix = p.stitch(2, act_came)
-    for j in range(3):
-        came_grads[j] = arrive(p.send(c_swap, p.far_grads[j]))
-    into[1, 2] = last_out[3] = arrive(into[1, 2])
-    into[1, 1] = final[0] = ends(value)
+    total[3] = p.chunk(3, feats, pieces(3))
     crossed[1] = arrive(crossed[1])
-    middle[1] = send("middle", plus(1, 2, into[1, 2]))
-    p.crossed[1] = arrive(p.crossed[1])
-    core_came(2, 1)
-    core_came(2, 2)
-    p.crossed[2] = p.send(x_swap, mix)
-    core_swap(2, 3)
-    core_swap(3, 1)
-    picked[3, 3] = pick(last_out[3], outer[3])
-    total[3] = p.chunk(3, feats, pieces(3))
     value = payload(part(2, 3), plus(1, 1, crossed[1]))
     into[1, 1] = final[0] = arrive(into[1, 1])
     into[2, 3] = final[1] = ends(value)
-    middle[1] = arrive(middle[1])
     p.crossed[2] = arrive(p.crossed[2])
+    core_came(2, 1)
+    core_came(2, 2)
+    core_swap(2, 3)
+    core_swap(3, 2)
+    far = p.send(c_swap, far)
+    came_last = p.send(c_swap, last_out[3])
+    middle[1] = send("middle", did(plus(1, 2, into[1, 2])))
     core_came(2, 3)
-    core_came(3, 1)
-    core_swap(3, 2)
-    core_swap(3, 3)
-    came_grads[3] = p.send(c_swap, p.far_grads[3])
+    came_outer = p.send(c_swap, outer[3])
+    core_came(3, 2)
+    far = arrive(far)
+    far3 = p.send(c_swap, p.far_grads[3])
     rows = {0: did(part(0, 0) + edge(0))}
-    core_came(3, 2)
-    core_came(3, 3)
-    came_grads[3] = arrive(came_grads[3])
+    came_last = arrive(came_last)
     slab_came[0] = p.send(x_swap, p.leaving(rows[0]))
+    came_outer = arrive(came_outer)
+    far3 = arrive(far3)
     act_came = p.send(y_swap, p.acts[3])
-    keep, leave = p.back(
-        came_grads,
-        [[picked[j, s] for s in range(4)] for j in range(4)],
-        [[came_pieces[j, s] for s in range(4)] for j in range(4)],
+    third = far.shape[0] // 3
+    came_grads = [(far, 0), (far, third), (far, 2 * third), (far3, 0)]
+    picked[3, 3], came_pieces[3, 3] = (last_out[3], outer[3]), (came_last, came_outer)
+    own_pieces, far_pieces = (
+        [[terms if isinstance(terms := kind[j, s], tuple) else (terms,) for s in range(4)] for j in range(4)]
+        for kind in (picked, came_pieces)
     )
-    came_x, own_y = {}, {}
+    keep_far, leave_far = p.back(1, came_grads, own_pieces, far_pieces)
+    came_far, came_x, own_y = {}, {}, {}
     into[2, 3] = final[1] = arrive(into[2, 3])
     into[3, 3] = inward(3, 3)
     slab_came[0] = arrive(slab_came[0])
-    crossed[2] = send("middle", far_end(2))
-    came_x[0] = p.send(x_swap, leave[2])
+    came_far[0] = p.send(x_swap, leave_far[0])
     act_came = arrive(act_came)
-    p.store(0, rows[0], slab_came[0])
-    rows[1] = did(part(1, 0) + edge(1))
-    mix = p.stitch(3, act_came)
+    rest = did(far_end(2))
+    middle[1] = arrive(middle[1])
+    crossed[2] = send("middle", rest)
+    keep, leave = p.back(0, came_grads, own_pieces, far_pieces)
     into[3, 3] = arrive(into[3, 3])
     into[2, 2] = inward(2, 2)
+    rest = did(far_end(3))
+    came_far[0] = arrive(came_far[0])
+    came_far[1] = p.send(x_swap, leave_far[1])
     crossed[2] = arrive(crossed[2])
-    crossed[3] = send("middle", far_end(3))
-    came_x[0] = arrive(came_x[0])
-    came_x[1] = p.send(x_swap, leave[3])
-    own_y[0] = p.send(y_swap, p.add(keep[2], came_x[0]))
+    crossed[3] = send("middle", rest)
+    own_y[0] = p.send(y_swap, p.add(keep_far[0], came_far[0]))
     sums = did(then(p.unit_sums()))
+    act_mix = p.stitch(3, act_came)
+    p.store(0, rows[0], slab_came[0])
     into[2, 2] = arrive(into[2, 2])
     into[3, 2] = inward(3, 2)
+    rest = did(plus(2, 2, into[2, 2]))
+    came_far[1] = arrive(came_far[1])
+    came_x[0] = p.send(x_swap, leave[0])
     crossed[3] = arrive(crossed[3])
-    middle[2] = send("middle", plus(2, 2, into[2, 2]))
-    came_x[1] = arrive(came_x[1])
-    came_x[2] = p.send(x_swap, leave[0])
+    middle[2] = send("middle", rest)
     own_y[0] = arrive(own_y[0])
-    own_y[1] = p.send(y_swap, p.add(keep[3], came_x[1]))
+    own_y[1] = p.send(y_swap, p.add(keep_far[1], came_far[1]))
     value = payload(part(2, 1), plus(2, 1, crossed[2]))
+    rows[1] = did(part(1, 0) + edge(1))
     into[3, 2] = arrive(into[3, 2])
     into[2, 1] = final[2] = ends(value)
+    rest = did(plus(3, 2, into[3, 2]))
+    came_x[0] = arrive(came_x[0])
+    came_x[1] = p.send(x_swap, leave[1])
     middle[2] = arrive(middle[2])
-    middle[3] = send("middle", plus(3, 2, into[3, 2]))
-    came_x[2] = arrive(came_x[2])
-    came_x[3] = p.send(x_swap, leave[1])
+    middle[3] = send("middle", rest)
     own_y[1] = arrive(own_y[1])
     value = payload(part(3, 1), plus(3, 1, crossed[3]))
-    partial = p.first_grad(0, keep[0], came_x[2], own_y[0], pooled)
-    grad = (p.unpool(0, keep[0], came_x[2], own_y[0]),)
+    partial = p.first_grad(0, keep[0], came_x[0], own_y[0], pooled)
     into[2, 1] = final[2] = arrive(into[2, 1])
     into[3, 1] = final[3] = ends(value)
+    came_x[1] = arrive(came_x[1])
+    slab_came[1] = p.send(x_swap, p.leaving(rows[1]))
     middle[3] = arrive(middle[3])
-    came_x[3] = arrive(came_x[3])
-    slab_came[1] = p.send(x_swap, p.leaving(rows[1]))
     rows[2] = did(part(2, 0) + edge(2))
     slab_came[2] = p.send(x_swap, p.leaving(rows[2]))
-    p.crossed[3] = p.send(x_swap, mix)
-    partial = partial + p.first_grad(1, keep[1], came_x[3], own_y[1], pooled)
+    p.crossed[3] = p.send(x_swap, act_mix)
+    partial = partial + p.first_grad(1, keep[1], came_x[1], own_y[1], pooled)
     partial = did(p.by_tower(partial).reshape(1, -1))
+    grad = (p.unpool(0, keep[0], came_x[0], own_y[0]),)
+    into[3, 1] = final[3] = arrive(into[3, 1])
+    rows[3] = did(part(3, 0) + edge(3))
+    slab_came[3] = p.send(x_swap, p.leaving(rows[3]))
     partial_came = p.send(c_swap, partial)
-    grad = p.unpool(1, keep[1], came_x[3], own_y[1], grad)
+    slab_came[1] = arrive(slab_came[1])
+    p.store(1, rows[1], slab_came[1])
     partial = did(partial + then(partial_came))
     second_came = p.send(y_swap, jnp.concatenate([sums[2:], partial]))
-    into[3, 1] = final[3] = arrive(into[3, 1])
-    rows[3] = did(part(3, 0) + edge(3))
-    slab_came[1] = arrive(slab_came[1])
-    slab_came[3] = p.send(x_swap, p.leaving(rows[3]))
+    slab_came[2] = arrive(slab_came[2])
+    p.store(2, rows[2], slab_came[2])
     second_came = arrive(second_came)
     sums = did(jnp.concatenate([sums[:2], second_came[:1], partial + second_came[1:]]))
     sums_came = p.send(flipped, sums, "batch", 2)
-    p.store(1, rows[1], slab_came[1])
+    grad = p.unpool(1, keep[1], came_x[1], own_y[1], grad)
     sums = did(sums + then(sums_came))
     sums_came = p.send(flipped, sums, "batch", 4)
-    slab_came[2] = arrive(slab_came[2])
-    p.store(2, rows[2], slab_came[2])
+    slab_came[3] = arrive(slab_came[3])
+    p.store(3, rows[3], slab_came[3])
+    sums = did(sums + then(sums_came))
+    sums_came = p.send(x_swap, sums)
     p.crossed[3] = arrive(p.crossed[3])
     activations = did(p.activations())
-    sums = did(sums + then(sums_came))
-    slab_came[3] = arrive(slab_came[3])
-    sums_came = p.send(x_swap, sums)
-    p.store(3, rows[3], slab_came[3])
     sums_came = then(sums_came)
     bias_grad, alpha2_grad = p.small_grads(jnp.concatenate([sums[:3], sums_came[:3]]))
     alpha1_grad = (sums[3] + sums_came[3]).reshape(2, 2, p.channels)
@@ -1123,8 +1165,9 @@
 def plain_program(p):
     groups = slab_groups()
     p.keep_cross(p.send(y_swap, p.cross))
+    p.load_cotangents()
     p.cot_across = p.send(y_swap, p.cot_mine)
-    *features, pooled = pool(p.convmaps, p.group, p.table, p.first, 0, p.count // IMAGE_BLOCK)
+    *features, pooled = p.mix(p.pool())
     feats = [features[:HALVES], [y_swap(part) for part in features[HALVES:]]]
     feats += [[x_swap(part) for part in block] for block in feats]
     feats += [[c_swap(part) for part in block] for block in feats]
@@ -1146,15 +1189,14 @@
     bias_grad, alpha2_grad = p.small_grads(
         jnp.concatenate([sums[:2], second[:1], far[:2], second[1:]])
     )
-    own_pieces = [[term for [term] in chunk] for chunk in chunks]
-    keep, leave = p.back(
-        [c_swap(p.far_grads[j]) for j in range(p.chunks)],
-        own_pieces,
-        [[c_swap(term) for term in chunk] for chunk in own_pieces],
-    )
+    own_pieces = chunks
+    far = [(c_swap(p.far_grads[j]), 0) for j in range(p.chunks)]
+    far_pieces = [[(c_swap(term),) for [term] in chunk] for chunk in own_pieces]
+    keep, leave = p.back(0, far, own_pieces, far_pieces)
+    keep_far, leave_far = p.back(1, far, own_pieces, far_pieces)
     partial, grad = 0.0, ()
     for i in range(2):
-        other = y_swap(p.add(keep[2 + i], x_swap(leave[2 + i])))
+        other = y_swap(p.add(keep_far[i], x_swap(leave_far[i])))
         came = x_swap(leave[i])
         partial = partial + p.first_grad(i, keep[i], came, other, pooled)
         grad = (p.unpool(i, keep[i], came, other, grad),)

time: 682 us -> 654 us (0.959)
  waiting for transfers between devices: 214 us -> 185 us
  matrix products: 0 us -> 13.9 us
  between operations: 16.3 us -> 2.95 us
  Pallas kernels: 203 us -> 194 us
    ppermute x35, waiting for transfers between devices: 180 us -> 128 us  [line(): return lax.ppermute(value, 'batch', pairs)]
    ppermute x60 -> x65, waiting for transfers between devices: 31.5 us -> 56.9 us  [flipped(): return lax.ppermute(value, axis, pairs)]
    dot_general x0 -> x1, matrix products: none -> 13.9 us  [pool(): jnp.einsum('pq,nsqc->nspc', self.pool_table, self.convmaps, preferred_ele...]
    pallas_call x3, Pallas kernels: 58.2 us -> 49.5 us  [the longest x2 35.3 us: back(): pl.pallas_call(functools.partial(back_kernel, layout, [row for _, row in...]
    select_n x10 -> x9, other arithmetic: 17.5 us -> 16.1 us  [pick(): return did(jnp.where(p.is_outer, then(a), b))]
    ppermute x60 -> x65, starting transfers between devices: 48.1 us -> 47 us  [flipped(): return lax.ppermute(value, axis, pairs)]
  transfers between devices with their start and end apart: 101 -> 100, of which waited for: 23 -> 25; matrix products, arithmetic and copies ran while one was open for 15% -> 20% of each run, Pallas kernels for 30% -> 30%
where the time goes in v4:
time: 654 us; the launch traced here: 642 us
  Pallas kernels  194 us (30%)
  waiting for transfers between devices  185 us (28%)
  starting transfers between devices  115 us (18%)
  other arithmetic  87.4 us (13%)
  local copies, waits for them, and re-layouts  44.8 us (7%)
  matrix products  13.9 us (2%)
    ppermute x35, waiting for transfers between devices, line(): return lax.ppermute(value, 'batch', pairs)  128 us
    pallas_call x4, Pallas kernels, chunk(): pl.pallas_call(functools.partial(chunk_kernel, [[len(p) for p in chunk] f...  84.9 us
    ppermute x35, starting transfers between devices, line(): return lax.ppermute(value, 'batch', pairs)  67.8 us
    ppermute x65, waiting for transfers between devices, flipped(): return lax.ppermute(value, axis, pairs)  56.9 us
    ppermute x65, starting transfers between devices, flipped(): return lax.ppermute(value, axis, pairs)  47 us
    pallas_call x2, Pallas kernels, back(): pl.pallas_call(functools.partial(back_kernel, layout, [row for _, row in...  35.3 us
    pallas_call x2, Pallas kernels, unpool(): pl.pallas_call(functools.partial(unpool_kernel, at), grid_spec=pltpu.Pref...  30.4 us
    select_n x11, other arithmetic, payload(): return did(jnp.where(p.is_outer, then(inward), outward))  20.7 us
  transfers between devices with their start and end apart: 100, of which 25 were waited for; matrix products, arithmetic and copies ran while one was open for 20% of the time, Pallas kernels for 30%

profile of v4, /device:TPU:0, one launch (start us, length us, event | category | flops | bytes accessed | tf_op | source)
XLA Modules:
  0.0 642.5 jit_solution(4377447798540679324)
XLA Ops:
  27.4 13.9 %fusion.2.summed = f32[128,2,36,256]{3,2,1,0:T(8,128)} fusion(bf16[128,2,169,256]{3,1,2,0:T(2,128)(2,1)} %param.8, bf16[36,169]{1,0:T(8,128)(2,1)S(1)} %and_convert_fusion), kind=kOutput, calls=%fused_computation.3 | convolution fusion | flops 797442048 | bytes 31600520 | tf_op jit(solution)/shard_map/pq,nsqc->nspc/dot_general | solution.py:708
  45.5 4.8 collective-permute-done.3.refs_21_.refs_9_
  53.0 6.5 %collective-permute-start.11 = (bf16[2304,256]{1,0:T(8,128)(2,1)S(1)}, bf16[2304,256]{1,0:T(8,128)(2,1)S(1)}, u32[]{:S(2)}, u32[]{:S(2)}) collective-permute-start(bf16[2304,256]{1,0:T(8,128)(2,1)S(1)} %maximum_select_fusion.1.refs_20_.refs_12_), channel_id=1, source_target_pairs={{0,8},{4,12},{8,0},{12,4},{16,24},{20,28},{24,16},{28,20},{1,9},{5... | collective-permute-start | bytes 3538952 | tf_op jit(solution)/shard_map/ppermute | solution.py:51
  60.3 14.2 %mix.1 = (bf16[128,4608]{1,0:T(8,128)(2,1)}, bf16[128,4608]{1,0:T(8,128)(2,1)}, bf16[128,4608]{1,0:T(8,128)(2,1)}, bf16[128,4608]{1,0:T(8,128)(2,1)}, f32[2,128,9216]{2,1,0:T(8,128)}) custom-call(s32[128]{0:T(128)} %group.5, f32[2,36,256]{2,1,0:T(8,128)} %broadcast_in_dim.8.keep, f32[4,256]{1,0:T(4,128)} %reshape.655.first, f32[128,2,36,256]{3,2,1,0:T(8,128)} %fusion.2.summed), custom_call_target="tpu_custom_call" | custom-call | flops 1000 | bytes 1000 | tf_op jit(solution)/shard_map/mix/pallas_call | solution.py:148
  85.1 17.5 %collective-permute-done.9.refs_8_ = bf16[128,4608]{1,0:T(8,128)(2,1)} collective-permute-done((bf16[128,4608]{1,0:T(8,128)(2,1)S(1)}, bf16[128,4608]{1,0:T(8,128)(2,1)}, u32[]{:S(2)}, u32[]{:S(2)}) %collective-permute-start.9) | collective-permute-done | bytes 1179680 | tf_op jit(solution)/shard_map/ppermute | solution.py:28
  104.6 8.4 %collective-permute-done.15.refs_22_ = bf16[2304,256]{1,0:T(8,128)(2,1)S(1)} collective-permute-done((bf16[2304,256]{1,0:T(8,128)(2,1)S(1)}, bf16[2304,256]{1,0:T(8,128)(2,1)S(1)}, u32[]{:S(2)}, u32[]{:S(2)}) %collective-permute-start.15) | collective-permute-done | bytes 1179680 | tf_op jit(solution)/shard_map/ppermute | solution.py:51
  115.9 12.5 %collective-permute-done.13.refs_9_ = bf16[128,4608]{1,0:T(8,128)(2,1)S(1)} collective-permute-done((bf16[128,4608]{1,0:T(8,128)(2,1)S(1)}, bf16[128,4608]{1,0:T(8,128)(2,1)S(1)}, u32[]{:S(2)}, u32[]{:S(2)}) %collective-permute-start.13) | collective-permute-done | bytes 1179680 | tf_op jit(solution)/shard_map/ppermute | solution.py:28
  131.6 10.9 %collective-permute-done.20.refs_22_ = bf16[2304,256]{1,0:T(8,128)(2,1)} collective-permute-done((bf16[2304,256]{1,0:T(8,128)(2,1)}, bf16[2304,256]{1,0:T(8,128)(2,1)}, u32[]{:S(2)}, u32[]{:S(2)}) %collective-permute-start.20) | collective-permute-done | bytes 1179680 | tf_op jit(solution)/shard_map/ppermute | solution.py:51
  143.2 11.4 %collective-permute-done.17.refs_10_ = bf16[128,4608]{1,0:T(8,128)(2,1)} collective-permute-done((bf16[128,4608]{1,0:T(8,128)(2,1)}, bf16[128,4608]{1,0:T(8,128)(2,1)}, u32[]{:S(2)}, u32[]{:S(2)}) %collective-permute-start.17) | collective-permute-done | bytes 1179680 | tf_op jit(solution)/shard_map/ppermute | solution.py:28
  158.5 10.4 %collective-permute-done.22.refs_24_.refs_22_ = bf16[2304,256]{1,0:T(8,128)(2,1)S(1)} collective-permute-done((bf16[2304,256]{1,0:T(8,128)(2,1)S(1)}, bf16[2304,256]{1,0:T(8,128)(2,1)S(1)}, u32[]{:S(2)}, u32[]{:S(2)}) %collective-permute-start.22) | collective-permute-done | bytes 1179680 | tf_op jit(solution)/shard_map/ppermute | solution.py:51
  169.2 8.2 %collective-permute-done.21.refs_11_ = bf16[128,4608]{1,0:T(8,128)(2,1)} collective-permute-done((bf16[128,4608]{1,0:T(8,128)(2,1)}, bf16[128,4608]{1,0:T(8,128)(2,1)}, u32[]{:S(2)}, u32[]{:S(2)}) %collective-permute-start.21) | collective-permute-done | bytes 1179680 | tf_op jit(solution)/shard_map/ppermute | solution.py:28
  185.8 9.0 %collective-permute-done.31.refs_24_.refs_22_ = bf16[2304,256]{1,0:T(8,128)(2,1)} collective-permute-done((bf16[2304,256]{1,0:T(8,128)(2,1)}, bf16[2304,256]{1,0:T(8,128)(2,1)}, u32[]{:S(2)}, u32[]{:S(2)}) %collective-permute-start.31) | collective-permute-done | bytes 1179680 | tf_op jit(solution)/shard_map/ppermute | solution.py:51
  197.7 21.1 %chunk.4 = (bf16[1024,256]{1,0:T(8,128)(2,1)}, bf16[512,256]{1,0:T(8,128)(2,1)}, bf16[512,256]{1,0:T(8,128)(2,1)}, f32[8,256]{1,0:T(8,128)}, f32[2304,256]{1,0:T...) custom-call(s32[2]{0:T(128)} %pad_add_fusion.2.roles, ...), custom_call_target="tpu_custom_call" | custom-call | flops 1000 | bytes 1000 | tf_op jit(solution)/shard_map/chunk/pallas_call | solution.py:517
  230.1 21.3 %chunk.5 = (bf16[1024,256]{1,0:T(8,128)(2,1)}, bf16[512,256]{1,0:T(8,128)(2,1)}, bf16[512,256]{1,0:T(8,128)(2,1)}, f32[8,256]{1,0:T(8,128)}, f32[2304,256]{1,0:T...) custom-call(s32[2]{0:T(128)} %pad_add_fusion.2.roles, ...), custom_call_target="tpu_custom_call" | custom-call | flops 1000 | bytes 1000 | tf_op jit(solution)/shard_map/chunk/pallas_call | solution.py:517
  265.6 21.3 %collective-permute-done.45.refs_25_ = bf16[2304,256]{1,0:T(8,128)(2,1)} collective-permute-done((bf16[2304,256]{1,0:T(8,128)(2,1)}, bf16[2304,256]{1,0:T(8,128)(2,1)}, u32[]{:S(2)}, u32[]{:S(2)}) %collective-permute-start.45) | collective-permute-done | bytes 1179680 | tf_op jit(solution)/shard_map/ppermute | solution.py:51
  293.9 21.3 %chunk.6 = (bf16[1024,256]{1,0:T(8,128)(2,1)}, bf16[512,256]{1,0:T(8,128)(2,1)}, bf16[512,256]{1,0:T(8,128)(2,1)}, f32[8,256]{1,0:T(8,128)}, f32[2304,256]{1,0:T...) custom-call(s32[2]{0:T(128)} %pad_add_fusion.2.roles, ...), custom_call_target="tpu_custom_call" | custom-call | flops 1000 | bytes 1000 | tf_op jit(solution)/shard_map/chunk/pallas_call | solution.py:517
  338.4 13.8 %collective-permute-done.53.refs_23_ = bf16[2304,256]{1,0:T(8,128)(2,1)} collective-permute-done((bf16[2304,256]{1,0:T(8,128)(2,1)}, bf16[2304,256]{1,0:T(8,128)(2,1)}, u32[]{:S(2)}, u32[]{:S(2)}) %collective-permute-start.53) | collective-permute-done | bytes 1179680 | tf_op jit(solution)/shard_map/ppermute | solution.py:51
  373.5 16.7 %collective-permute-done.60.refs_25_.refs_23_ = bf16[2304,256]{1,0:T(8,128)(2,1)S(1)} collective-permute-done((bf16[2304,256]{1,0:T(8,128)(2,1)}, bf16[2304,256]{1,0:T(8,128)(2,1)S(1)}, u32[]{:S(2)}, u32[]{:S(2)}) %collective-permute-start.60) | collective-permute-done | bytes 1179680 | tf_op jit(solution)/shard_map/ppermute | solution.py:51
  392.9 21.2 %chunk.7 = (bf16[1024,256]{1,0:T(8,128)(2,1)}, bf16[512,256]{1,0:T(8,128)(2,1)}, bf16[512,256]{1,0:T(8,128)(2,1)}, f32[8,256]{1,0:T(8,128)}, f32[2304,256]{1,0:T...) custom-call(s32[2]{0:T(128)} %pad_add_fusion.2.roles, ...), custom_call_target="tpu_custom_call" | custom-call | flops 1000 | bytes 1000 | tf_op jit(solution)/shard_map/chunk/pallas_call | solution.py:517
  433.7 17.6 %back.2 = (bf16[64,9216]{1,0:T(8,128)(2,1)}, bf16[64,9216]{1,0:T(8,128)(2,1)}, bf16[64,9216]{1,0:T(8,128)(2,1)}, bf16[64,9216]{1,0:T(8,128)(2,1)}) custom-call(s32[2]{0:T(128)} %pad_add_fusion.2.roles, bf16[512,256]{1,0:T(8,128)(2,1)} %get-tuple-element.555.refs_0_, bf16[512,256]{1,0:T(8,128)(2,1)} %get-tuple-element.536.refs_1_, ...), custom_call_target="tpu_custom_call" | custom-call | flops 1000 | bytes 1000 | tf_op jit(solution)/shard_map/back/pallas_call | solution.py:627
  451.4 4.6 collective-permute-start.76
  463.3 17.6 %back.3 = (bf16[64,9216]{1,0:T(8,128)(2,1)}, bf16[64,9216]{1,0:T(8,128)(2,1)}, bf16[64,9216]{1,0:T(8,128)(2,1)}, bf16[64,9216]{1,0:T(8,128)(2,1)}) custom-call(s32[2]{0:T(128)} %pad_add_fusion.2.roles, bf16[512,256]{1,0:T(8,128)(2,1)} %get-tuple-element.555.refs_0_, bf16[512,256]{1,0:T(8,128)(2,1)} %get-tuple-element.536.refs_1_, ...), custom_call_target="tpu_custom_call" | custom-call | flops 1000 | bytes 1000 | tf_op jit(solution)/shard_map/back/pallas_call | solution.py:627
  481.0 7.1 %collective-permute-start.80 = (bf16[2304,256]{1,0:T(8,128)(2,1)S(1)}, bf16[2304,256]{1,0:T(8,128)(2,1)}, u32[]{:S(2)}, u32[]{:S(2)}) collective-permute-start(bf16[2304,256]{1,0:T(8,128)(2,1)S(1)} %copy-done.81), channel_id=1, source_target_pairs={{0,8},{4,12},{24,16},{28,20},{1,9},{5,13},{25,17},{29,21},{2,10},{... | collective-permute-start | bytes 3538952 | tf_op jit(solution)/shard_map/ppermute | solution.py:51
  501.5 9.9 %collective-permute-done.80 = bf16[2304,256]{1,0:T(8,128)(2,1)} collective-permute-done((bf16[2304,256]{1,0:T(8,128)(2,1)S(1)}, bf16[2304,256]{1,0:T(8,128)(2,1)}, u32[]{:S(2)}, u32[]{:S(2)}) %collective-permute-start.80) | collective-permute-done | bytes 1179680 | tf_op jit(solution)/shard_map/ppermute | solution.py:51
  511.4 4.7 collective-permute-start.83
  529.3 10.0 %collective-permute-done.83 = bf16[2304,256]{1,0:T(8,128)(2,1)S(1)} collective-permute-done((bf16[2304,256]{1,0:T(8,128)(2,1)S(1)}, bf16[2304,256]{1,0:T(8,128)(2,1)S(1)}, u32[]{:S(2)}, u32[]{:S(2)}) %collective-permute-start.83) | collective-permute-done | bytes 1179680 | tf_op jit(solution)/shard_map/ppermute | solution.py:51
  551.9 5.0 first_grad.2
  558.4 7.7 %collective-permute-done.84 = bf16[2304,256]{1,0:T(8,128)(2,1)} collective-permute-done((bf16[2304,256]{1,0:T(8,128)(2,1)}, bf16[2304,256]{1,0:T(8,128)(2,1)}, u32[]{:S(2)}, u32[]{:S(2)}) %collective-permute-start.84) | collective-permute-done | bytes 1179680 | tf_op jit(solution)/shard_map/ppermute | solution.py:51
  574.9 4.9 first_grad.3
  582.1 15.3 %unpool.2.refs_0_ = bf16[128,169,2,256]{3,2,1,0:T(2,128)(2,1)} custom-call(s32[128]{0:T(128)} %group.5, bf16[2,352,192]{2,1,0:T(8,128)(2,1)} %fusion.19.table, f32[4,256]{1,0:T(4,128)} %reshape.655.first, bf16[64,9216]{1,0:T(8,128)(2,1)} %get-tuple-element.615.keep.keep_in, bf16[64,9216]{1,0:T(8,128)(2,1)} %copy-done.60, bf16[64,9216]{1,0:T(8,128)(2,1)} %copy-done.56), custom_call_target="tpu_custom_call" | custom-call | flops 1000 | bytes 1000 | tf_op jit(solution)/shard_map/unpool/pallas_call | solution.py:252
  600.0 4.3 store.5.refs_0_
  614.6 15.2 %unpool.3 = bf16[128,169,2,256]{3,2,1,0:T(2,128)(2,1)} custom-call(s32[128]{0:T(128)} %group.5, bf16[2,352,192]{2,1,0:T(8,128)(2,1)} %fusion.19.table, f32[4,256]{1,0:T(4,128)} %reshape.655.first, bf16[64,9216]{1,0:T(8,128)(2,1)} %get-tuple-element.628.keep.keep_in, bf16[64,9216]{1,0:T(8,128)(2,1)} %copy-done.59, ...), custom_call_target="tpu_custom_call", output_to_operand_aliasing={{}: (6, {})} | custom-call | flops 1000 | bytes 1000 | tf_op jit(solution)/shard_map/unpool/pallas_call | solution.py:252
  (584 shorter events, 251.4 us)
Async XLA Ops:
  7.4 33.8 %collective-permute-start.1 = (bf16[1152,256]{1,0:T(8,128)(2,1)}, bf16[1152,256]{1,0:T(8,128)(2,1)}, u32[]{:S(2)}, u32[]{:S(2)}) collective-permute-start(bf16[1152,256]{1,0:T(8,128)(2,1)} %constant_dynamic-slice_fusion.9), channel_id=1, source_target_pairs={{0,4},{4,0},{8,12},{12,8},{16,20},{20,16},{24,28},{28,24},{1,5},{5... | collective-permute-start | bytes 1769480 | tf_op jit(solution)/shard_map/ppermute | solution.py:28
  12.0 62.5 %collective-permute-start.7 = (bf16[1152,512]{1,0:T(8,128)(2,1)}, bf16[1152,512]{1,0:T(8,128)(2,1)}, u32[]{:S(2)}, u32[]{:S(2)}) collective-permute-start(bf16[1152,512]{1,0:T(8,128)(2,1)} %constant_dynamic-slice_fusion.8), channel_id=1, source_target_pairs={{0,4},{4,0},{8,12},{12,8},{16,20},{20,16},{24,28},{28,24},{1,5},{5... | collective-permute-start | bytes 3538952 | tf_op jit(solution)/shard_map/ppermute | solution.py:28
  26.0 48.5 %collective-permute-start.6 = (bf16[512,1024]{1,0:T(8,128)(2,1)S(1)}, bf16[512,1024]{1,0:T(8,128)(2,1)S(1)}, u32[]{:S(2)}, u32[]{:S(2)}) collective-permute-start(bf16[512,1024]{1,0:T(8,128)(2,1)S(1)} %constant_dynamic-slice_fusion.7.refs_0_), channel_id=1, source_target_pairs={{0,2},{1,3},{2,0},{3,1},{4,6},{5,7},{6,4},{7,5},{8,10},{9,11},{10,... | collective-permute-start | bytes 3145736 | tf_op jit(solution)/shard_map/ppermute | solution.py:28
  41.3 35.0 %collective-permute-start.5 = (bf16[512,512]{1,0:T(8,128)(2,1)S(1)}, bf16[512,512]{1,0:T(8,128)(2,1)S(1)}, u32[]{:S(2)}, u32[]{:S(2)}) collective-permute-start(bf16[512,512]{1,0:T(8,128)(2,1)S(1)} %copy-done.95), channel_id=1, source_target_pairs={{0,4},{4,0},{8,12},{12,8},{16,20},{20,16},{24,28},{28,24},{1,5},{5... | collective-permute-start | bytes 1572872 | tf_op jit(solution)/shard_map/ppermute | solution.py:28
  51.3 33.0 %collective-permute-start.10 = (bf16[2304,256]{1,0:T(8,128)(2,1)S(1)}, bf16[2304,256]{1,0:T(8,128)(2,1)}, u32[]{:S(2)}, u32[]{:S(2)}) collective-permute-start(bf16[2304,256]{1,0:T(8,128)(2,1)S(1)} %maximum_select_fusion.1.refs_20_.refs_12_), channel_id=1, source_target_pairs={{8,16},{12,20},{16,8},{20,12},{9,17},{13,21},{17,9},{21,13},{10,18... | collective-permute-start | bytes 3538952 | tf_op jit(solution)/shard_map/ppermute | solution.py:51
  53.0 30.0 %collective-permute-start.11 = (bf16[2304,256]{1,0:T(8,128)(2,1)S(1)}, bf16[2304,256]{1,0:T(8,128)(2,1)S(1)}, u32[]{:S(2)}, u32[]{:S(2)}) collective-permute-start(bf16[2304,256]{1,0:T(8,128)(2,1)S(1)} %maximum_select_fusion.1.refs_20_.refs_12_), channel_id=1, source_target_pairs={{0,8},{4,12},{8,0},{12,4},{16,24},{20,28},{24,16},{28,20},{1,9},{5... | collective-permute-start | bytes 3538952 | tf_op jit(solution)/shard_map/ppermute | solution.py:51
  181.5 43.9 %collective-permute-start.32 = (bf16[2304,256]{1,0:T(8,128)(2,1)}, bf16[2304,256]{1,0:T(8,128)(2,1)}, u32[]{:S(2)}, u32[]{:S(2)}) collective-permute-start(bf16[2304,256]{1,0:T(8,128)(2,1)} %copy-done.22), channel_id=1, source_target_pairs={{8,16},{12,20},{16,8},{20,12},{9,17},{13,21},{17,9},{21,13},{10,18... | collective-permute-start | bytes 3538952 | tf_op jit(solution)/shard_map/ppermute | solution.py:51
  194.8 30.5 %collective-permute-start.34 = (bf16[2304,256]{1,0:T(8,128)(2,1)S(1)}, bf16[2304,256]{1,0:T(8,128)(2,1)}, u32[]{:S(2)}, u32[]{:S(2)}) collective-permute-start(bf16[2304,256]{1,0:T(8,128)(2,1)S(1)} %copy-done.31), channel_id=1, source_target_pairs={{0,1},{1,0},{2,3},{3,2},{4,5},{5,4},{6,7},{7,6},{8,9},{9,8},{10,11... | collective-permute-start | bytes 3538952 | tf_op jit(solution)/shard_map/ppermute | solution.py:28
  194.9 30.4 %collective-permute-start.35 = (bf16[2304,256]{1,0:T(8,128)(2,1)S(1)}, bf16[2304,256]{1,0:T(8,128)(2,1)}, u32[]{:S(2)}, u32[]{:S(2)}) collective-permute-start(bf16[2304,256]{1,0:T(8,128)(2,1)S(1)} %copy-done.15), channel_id=1, source_target_pairs={{0,1},{1,0},{2,3},{3,2},{4,5},{5,4},{6,7},{7,6},{8,9},{9,8},{10,11... | collective-permute-start | bytes 3538952 | tf_op jit(solution)/shard_map/ppermute | solution.py:28
  195.4 29.9 %collective-permute-start.36 = (bf16[2304,256]{1,0:T(8,128)(2,1)S(1)}, bf16[2304,256]{1,0:T(8,128)(2,1)}, u32[]{:S(2)}, u32[]{:S(2)}) collective-permute-start(bf16[2304,256]{1,0:T(8,128)(2,1)S(1)} %maximum_select_fusion.2.refs_20_.refs_16_), channel_id=1, source_target_pairs={{8,0},{12,4},{16,24},{20,28},{9,1},{13,5},{17,25},{21,29},{10,2},{... | collective-permute-start | bytes 3538952 | tf_op jit(solution)/shard_map/ppermute | solution.py:51
  254.5 35.6 %collective-permute-start.42 = (bf16[2304,256]{1,0:T(8,128)(2,1)}, bf16[2304,256]{1,0:T(8,128)(2,1)}, u32[]{:S(2)}, u32[]{:S(2)}) collective-permute-start(bf16[2304,256]{1,0:T(8,128)(2,1)} %broadcast_select_fusion.12.refs_14_), channel_id=1, source_target_pairs={{0,1},{1,0},{2,3},{3,2},{4,5},{5,4},{6,7},{7,6},{8,9},{9,8},{10,11... | collective-permute-start | bytes 3538952 | tf_op jit(solution)/shard_map/ppermute | solution.py:28
  255.0 35.1 %collective-permute-start.43 = (bf16[2304,256]{1,0:T(8,128)(2,1)}, bf16[2304,256]{1,0:T(8,128)(2,1)}, u32[]{:S(2)}, u32[]{:S(2)}) collective-permute-start(bf16[2304,256]{1,0:T(8,128)(2,1)} %broadcast_select_fusion.13.refs_10_), channel_id=1, source_target_pairs={{0,1},{1,0},{2,3},{3,2},{4,5},{5,4},{6,7},{7,6},{8,9},{9,8},{10,11... | collective-permute-start | bytes 3538952 | tf_op jit(solution)/shard_map/ppermute | solution.py:28
  255.1 35.0 %collective-permute-start.44 = (bf16[512,512]{1,0:T(8,128)(2,1)}, bf16[512,512]{1,0:T(8,128)(2,1)}, u32[]{:S(2)}, u32[]{:S(2)}) collective-permute-start(bf16[512,512]{1,0:T(8,128)(2,1)} %collective-permute-done.38.refs_1_), channel_id=1, source_target_pairs={{0,2},{1,3},{2,0},{3,1},{4,6},{5,7},{6,4},{7,5},{8,10},{9,11},{10,... | collective-permute-start | bytes 1572872 | tf_op jit(solution)/shard_map/ppermute | solution.py:28
  256.9 30.1 %collective-permute-start.45 = (bf16[2304,256]{1,0:T(8,128)(2,1)}, bf16[2304,256]{1,0:T(8,128)(2,1)}, u32[]{:S(2)}, u32[]{:S(2)}) collective-permute-start(bf16[2304,256]{1,0:T(8,128)(2,1)} %broadcast_select_fusion.10), channel_id=1, source_target_pairs={{0,8},{4,12},{8,0},{12,4},{16,24},{20,28},{24,16},{28,20},{1,9},{5... | collective-permute-start | bytes 3538952 | tf_op jit(solution)/shard_map/ppermute | solution.py:51
  290.1 32.5 %collective-permute-start.48 = (bf16[512,256]{1,0:T(8,128)(2,1)}, bf16[512,256]{1,0:T(8,128)(2,1)}, u32[]{:S(2)}, u32[]{:S(2)}) collective-permute-start(bf16[512,256]{1,0:T(8,128)(2,1)} %bitcast.25), channel_id=1, source_target_pairs={{0,4},{4,0},{8,12},{12,8},{16,20},{20,16},{24,28},{28,24},{1,5},{5... | collective-permute-start | bytes 786440 | tf_op jit(solution)/shard_map/ppermute | solution.py:28
  291.0 31.7 %collective-permute-start.47 = (bf16[1024,256]{1,0:T(8,128)(2,1)}, bf16[1024,256]{1,0:T(8,128)(2,1)}, u32[]{:S(2)}, u32[]{:S(2)}) collective-permute-start(bf16[1024,256]{1,0:T(8,128)(2,1)} %get-tuple-element.452), channel_id=1, source_target_pairs={{0,2},{1,3},{2,0},{3,1},{4,6},{5,7},{6,4},{7,5},{8,10},{9,11},{10,... | collective-permute-start | bytes 1572872 | tf_op jit(solution)/shard_map/ppermute | solution.py:28
  292.2 30.4 %collective-permute-start.50 = (bf16[2304,256]{1,0:T(8,128)(2,1)}, bf16[2304,256]{1,0:T(8,128)(2,1)}, u32[]{:S(2)}, u32[]{:S(2)}) collective-permute-start(bf16[2304,256]{1,0:T(8,128)(2,1)} %add_convert_fusion.13), channel_id=1, source_target_pairs={{8,16},{12,20},{16,8},{20,12},{9,17},{13,21},{17,9},{21,13},{10,18... | collective-permute-start | bytes 3538952 | tf_op jit(solution)/shard_map/ppermute | solution.py:51
  322.7 37.4 %collective-permute-start.52 = (bf16[1024,256]{1,0:T(8,128)(2,1)}, bf16[1024,256]{1,0:T(8,128)(2,1)}, u32[]{:S(2)}, u32[]{:S(2)}) collective-permute-start(bf16[1024,256]{1,0:T(8,128)(2,1)} %get-tuple-element.468), channel_id=1, source_target_pairs={{0,2},{1,3},{2,0},{3,1},{4,6},{5,7},{6,4},{7,5},{8,10},{9,11},{10,... | collective-permute-start | bytes 1572872 | tf_op jit(solution)/shard_map/ppermute | solution.py:28
  325.5 34.5 %collective-permute-start.54 = (bf16[2304,256]{1,0:T(8,128)(2,1)}, bf16[2304,256]{1,0:T(8,128)(2,1)}, u32[]{:S(2)}, u32[]{:S(2)}) collective-permute-start(bf16[2304,256]{1,0:T(8,128)(2,1)} %add_convert_fusion.12), channel_id=1, source_target_pairs={{8,16},{12,20},{16,8},{20,12},{9,17},{13,21},{17,9},{21,13},{10,18... | collective-permute-start | bytes 3538952 | tf_op jit(solution)/shard_map/ppermute | solution.py:51
  327.4 32.6 %collective-permute-start.56 = (bf16[2304,256]{1,0:T(8,128)(2,1)}, bf16[2304,256]{1,0:T(8,128)(2,1)}, u32[]{:S(2)}, u32[]{:S(2)}) collective-permute-start(bf16[2304,256]{1,0:T(8,128)(2,1)} %broadcast_select_fusion.6.refs_15_), channel_id=1, source_target_pairs={{0,1},{1,0},{2,3},{3,2},{4,5},{5,4},{6,7},{7,6},{8,9},{9,8},{10,11... | collective-permute-start | bytes 3538952 | tf_op jit(solution)/shard_map/ppermute | solution.py:28
  327.5 32.5 %collective-permute-start.55 = (bf16[2304,256]{1,0:T(8,128)(2,1)S(1)}, bf16[2304,256]{1,0:T(8,128)(2,1)}, u32[]{:S(2)}, u32[]{:S(2)}) collective-permute-start(bf16[2304,256]{1,0:T(8,128)(2,1)S(1)} %copy-done.2), channel_id=1, source_target_pairs={{0,1},{1,0},{2,3},{3,2},{4,5},{5,4},{6,7},{7,6},{8,9},{9,8},{10,11... | collective-permute-start | bytes 3538952 | tf_op jit(solution)/shard_map/ppermute | solution.py:28
  360.0 31.9 %collective-permute-start.57 = (bf16[2304,256]{1,0:T(8,128)(2,1)}, bf16[2304,256]{1,0:T(8,128)(2,1)}, u32[]{:S(2)}, u32[]{:S(2)}) collective-permute-start(bf16[2304,256]{1,0:T(8,128)(2,1)} %broadcast_select_fusion.2.refs_21_), channel_id=1, source_target_pairs={{0,1},{1,0},{2,3},{3,2},{4,5},{5,4},{6,7},{7,6},{8,9},{9,8},{10,11... | collective-permute-start | bytes 3538952 | tf_op jit(solution)/shard_map/ppermute | solution.py:28
  360.1 31.8 %collective-permute-start.58 = (bf16[2304,256]{1,0:T(8,128)(2,1)S(1)}, bf16[2304,256]{1,0:T(8,128)(2,1)}, u32[]{:S(2)}, u32[]{:S(2)}) collective-permute-start(bf16[2304,256]{1,0:T(8,128)(2,1)S(1)} %maximum_select_fusion.3.refs_20_), channel_id=1, source_target_pairs={{0,1},{1,0},{2,3},{3,2},{4,5},{5,4},{6,7},{7,6},{8,9},{9,8},{10,11... | collective-permute-start | bytes 3538952 | tf_op jit(solution)/shard_map/ppermute | solution.py:28
  360.6 31.3 %collective-permute-start.59 = (bf16[512,256]{1,0:T(8,128)(2,1)}, bf16[512,256]{1,0:T(8,128)(2,1)}, u32[]{:S(2)}, u32[]{:S(2)}) collective-permute-start(bf16[512,256]{1,0:T(8,128)(2,1)} %bitcast.31), channel_id=1, source_target_pairs={{0,4},{4,0},{8,12},{12,8},{16,20},{20,16},{24,28},{28,24},{1,5},{5... | collective-permute-start | bytes 786440 | tf_op jit(solution)/shard_map/ppermute | solution.py:28
  364.0 50.1 %collective-permute-start.64 = (bf16[2304,256]{1,0:T(8,128)(2,1)}, bf16[2304,256]{1,0:T(8,128)(2,1)}, u32[]{:S(2)}, u32[]{:S(2)}) collective-permute-start(bf16[2304,256]{1,0:T(8,128)(2,1)} %add_convert_fusion.11), channel_id=1, source_target_pairs={{8,16},{12,20},{16,8},{20,12},{9,17},{13,21},{17,9},{21,13},{10,18... | collective-permute-start | bytes 3538952 | tf_op jit(solution)/shard_map/ppermute | solution.py:51
  419.1 32.3 %collective-permute-start.74 = (bf16[2304,256]{1,0:T(8,128)(2,1)}, bf16[2304,256]{1,0:T(8,128)(2,1)}, u32[]{:S(2)}, u32[]{:S(2)}) collective-permute-start(bf16[2304,256]{1,0:T(8,128)(2,1)} %fusion.6), channel_id=1, source_target_pairs={{0,8},{4,12},{8,0},{12,4},{16,24},{20,28},{24,16},{28,20},{1,9},{5... | collective-permute-start | bytes 3538952 | tf_op jit(solution)/shard_map/ppermute | solution.py:51
  456.0 35.1 %collective-permute-start.75 = (bf16[64,9216]{1,0:T(8,128)(2,1)}, bf16[64,9216]{1,0:T(8,128)(2,1)S(1)}, u32[]{:S(2)}, u32[]{:S(2)}) collective-permute-start(bf16[64,9216]{1,0:T(8,128)(2,1)} %get-tuple-element.546), channel_id=1, source_target_pairs={{0,4},{4,0},{8,12},{12,8},{16,20},{20,16},{24,28},{28,24},{1,5},{5... | collective-permute-start | bytes 3538952 | tf_op jit(solution)/shard_map/ppermute | solution.py:28
  459.5 32.6 %collective-permute-start.78 = (bf16[2304,256]{1,0:T(8,128)(2,1)}, bf16[2304,256]{1,0:T(8,128)(2,1)}, u32[]{:S(2)}, u32[]{:S(2)}) collective-permute-start(bf16[2304,256]{1,0:T(8,128)(2,1)} %add_convert_fusion.7), channel_id=1, source_target_pairs={{8,16},{12,20},{16,8},{20,12},{9,17},{13,21},{17,9},{21,13},{10,18... | collective-permute-start | bytes 3538952 | tf_op jit(solution)/shard_map/ppermute | solution.py:51
  481.0 30.4 %collective-permute-start.80 = (bf16[2304,256]{1,0:T(8,128)(2,1)S(1)}, bf16[2304,256]{1,0:T(8,128)(2,1)}, u32[]{:S(2)}, u32[]{:S(2)}) collective-permute-start(bf16[2304,256]{1,0:T(8,128)(2,1)S(1)} %copy-done.81), channel_id=1, source_target_pairs={{0,8},{4,12},{24,16},{28,20},{1,9},{5,13},{25,17},{29,21},{2,10},{... | collective-permute-start | bytes 3538952 | tf_op jit(solution)/shard_map/ppermute | solution.py:51
  566.0 31.4 %collective-permute-start.91 = (bf16[2304,256]{1,0:T(8,128)(2,1)}, bf16[2304,256]{1,0:T(8,128)(2,1)}, u32[]{:S(2)}, u32[]{:S(2)}) collective-permute-start(bf16[2304,256]{1,0:T(8,128)(2,1)} %fusion.8), channel_id=1, source_target_pairs={{0,8},{4,12},{8,0},{12,4},{16,24},{20,28},{24,16},{28,20},{1,9},{5... | collective-permute-start | bytes 3538952 | tf_op jit(solution)/shard_map/ppermute | solution.py:51
  570.0 30.1 %collective-permute-start.93 = (bf16[1152,256]{1,0:T(8,128)(2,1)}, bf16[1152,256]{1,0:T(8,128)(2,1)}, u32[]{:S(2)}, u32[]{:S(2)}) collective-permute-start(bf16[1152,256]{1,0:T(8,128)(2,1)} %dynamic-slice_convert_fusion.2), channel_id=1, source_target_pairs={{0,4},{4,0},{8,12},{12,8},{16,20},{20,16},{24,28},{28,24},{1,5},{5... | collective-permute-start | bytes 1769480 | tf_op jit(solution)/shard_map/ppermute | solution.py:28
  573.9 32.1 %collective-permute-start.95 = (bf16[1152,256]{1,0:T(8,128)(2,1)S(1)}, bf16[1152,256]{1,0:T(8,128)(2,1)S(1)}, u32[]{:S(2)}, u32[]{:S(2)}) collective-permute-start(bf16[1152,256]{1,0:T(8,128)(2,1)S(1)} %dynamic-slice_convert_fusion.1), channel_id=1, source_target_pairs={{0,4},{4,0},{8,12},{12,8},{16,20},{20,16},{24,28},{28,24},{1,5},{5... | collective-permute-start | bytes 1769480 | tf_op jit(solution)/shard_map/ppermute | solution.py:28
  (198 other events, 3151.6 us)

commit v5 on v4

--- a/solution.py
+++ b/solution.py
@@ -16,6 +16,7 @@
 SMALL = pl.CostEstimate(flops=1000, bytes_accessed=1000, transcendentals=0)
 AHEAD = 2
 IMAGE_BLOCK = 16
+BLEND_STEPS = 4
 HALVES = 2
 
 
@@ -244,11 +245,11 @@
     lax.fori_loop(0, count, image, 0, unroll=2)
 
 
-def unpool(keep, came, other, group, table, first, places, at, count, before=()):
-    images, feats = keep.shape
+def unpool(keep, came, other, row, images, group, table, first, places, at, count, before=()):
+    feats = keep.shape[1]
     ch = first.shape[1]
     nb = IMAGE_BLOCK
-    rows = pl.BlockSpec((nb, feats), lambda i, g: (i, 0))
+    rows = pl.BlockSpec((nb, feats), lambda i, g: (row // nb + i, 0))
     return pl.pallas_call(
         functools.partial(unpool_kernel, at),
         grid_spec=pltpu.PrefetchScalarGridSpec(
@@ -341,6 +342,77 @@
         cost_estimate=SMALL,
         name="place_rows",
     )(places, *parts)
+
+
+def blend_kernel(counts, roles, *refs):
+    hold, in_sems, out_sems = refs[-3:]
+    blocks, outs = refs[: sum(counts)], refs[sum(counts) : -3]
+    rows = hold.shape[1] // BLEND_STEPS
+    outer = roles[0] == 1
+
+    def span(i):
+        return pl.ds(i * rows, rows)
+
+    def bring(block, k, i):
+        return pltpu.make_async_copy(block.at[span(i), :], hold.at[k, span(i), :], in_sems.at[k, i])
+
+    def leave(k, out, i):
+        return pltpu.make_async_copy(hold.at[k, span(i), :], out.at[span(i), :], out_sems.at[k, i])
+
+    groups, at = [], 0
+    for count in counts:
+        groups.append(blocks[at : at + count])
+        at += count
+    slots = [sum(max(count - 1, 1) for count in counts[:g]) for g in range(len(counts))]
+    for g, (first, *rest) in enumerate(groups):
+        for i in range(BLEND_STEPS):
+
+            @pl.when(outer)
+            def _(first=first, g=g, i=i):
+                bring(first, slots[g], i).start()
+
+            @pl.when(jnp.logical_not(outer))
+            def _(rest=rest, g=g, i=i):
+                for k, block in enumerate(rest):
+                    bring(block, slots[g] + k, i).start()
+
+    for g, (first, *rest) in enumerate(groups):
+        for i in range(BLEND_STEPS):
+            bring(first, slots[g], i).wait()
+            if len(rest) > 1:
+
+                @pl.when(jnp.logical_not(outer))
+                def _(rest=rest, g=g, i=i):
+                    for k in range(1, len(rest)):
+                        bring(rest[k], slots[g] + k, i).wait()
+                    total = sum(hold[slots[g] + k, span(i), :].astype(F32) for k in range(len(rest)))
+                    hold[slots[g], span(i), :] = total.astype(BF16)
+
+            leave(slots[g], outs[g], i).start()
+    for g in range(len(groups)):
+        for i in range(BLEND_STEPS):
+            leave(slots[g], outs[g], i).wait()
+
+
+def blend(roles, groups):
+    counts = [len(group) for group in groups]
+    shape = groups[0][0].shape
+    slots = sum(max(count - 1, 1) for count in counts)
+    anywhere = pl.BlockSpec(memory_space=pl.ANY)
+    return pl.pallas_call(
+        functools.partial(blend_kernel, counts),
+        in_specs=[pl.BlockSpec(memory_space=pltpu.SMEM)] + [anywhere] * sum(counts),
+        out_specs=[anywhere] * len(groups),
+        out_shape=[jax.ShapeDtypeStruct(shape, BF16)] * len(groups),
+        scratch_shapes=[
+            pltpu.VMEM((slots, *shape), BF16),
+            pltpu.SemaphoreType.DMA((slots, BLEND_STEPS)),
+            pltpu.SemaphoreType.DMA((slots, BLEND_STEPS)),
+        ],
+        compiler_params=params(),
+        cost_estimate=SMALL,
+        name="blend",
+    )(roles, *[block for group in groups for block in group])
 
 
 def tile_of(rows):
@@ -769,8 +841,8 @@
         own, other = ([parts[j] for j in range(self.chunks)] for parts in (self.stitched, self.crossed))
         return place_rows(self.places_of, [self.then(own[0])] + own[1:], other)
 
-    def unit_sums(self):
-        return jnp.concatenate([self.sums[j][:3] for j in range(self.chunks)], axis=1)
+    def unit_sums(self, *parts):
+        return jnp.concatenate([part[:3] for part in parts or self.sums.values()], axis=1)
 
     def small_grads(self, sums):
         mine, far = sums[:3], sums[3:6]
@@ -801,13 +873,16 @@
     def by_tower(self, partial):
         return either(self.y == 1, partial.reshape(2, 2, self.channels), 0)
 
-    def unpool(self, i, keep, came, other, before=()):
-        at = i * keep.shape[0]
+    def unpool(self, i, keep, came, other, before=(), part=0, parts=1):
+        images = keep.shape[0] // parts
+        at = i * keep.shape[0] + part * images
         return self.did(
             unpool(
                 self.then(keep),
                 came,
                 other,
+                part * images,
+                images,
                 self.group,
                 self.table,
                 self.first,
@@ -858,6 +933,12 @@
             p.is_outer, then(final[j]).astype(F32), into[j, 1].astype(F32) + middle[j].astype(F32)
         )
 
+    def blended(*groups):
+        (first, *rest), *others = groups
+        made = blend(p.roles, [(then(first), *rest)] + others)
+        did(made[0])
+        return made
+
     def pick(a, b):
         return did(jnp.where(p.is_outer, then(a), b))
 
@@ -878,6 +959,7 @@
     came_pair = p.swap_weight(2, 2)
     p.load_cotangents()
     p.keep_cross(cross_came)
+    p.table = did(then(p.table))
     came[0] = arrive(came[0])
     block(0)
     near[0] = ends(blocks[0])
@@ -938,7 +1020,6 @@
     for j in range(4):
         picked[j, 0] = blocks[j]
     picked[0, 1], picked[1, 1] = near[0], near[1]
-    picked[0, 2] = pick(first_out[0], inner[0])
     swapped[2] = last_out[0] = arrive(swapped[2])
     swapped[3] = last_out[1] = ends(value)
     inner[2] = arrive(inner[2])
@@ -949,15 +1030,15 @@
     c_y_b = p.send(c_swap, y_b)
     c_x_y_a = p.send(c_swap, x_y_a)
     c_x_y_b = p.send(c_swap, x_y_b)
-    picked[1, 2] = pick(first_out[1], inner[1])
     swapped[3] = last_out[1] = arrive(swapped[3])
     from_own[2] = send("outward", blocks[2])
+    p.vectors = did(then(p.vectors))
     c_y_b = arrive(c_y_b)
     c_x_y_a = arrive(c_x_y_a)
     c_x_y_b = arrive(c_x_y_b)
     core_swap(0, 0)
     core_swap(0, 1)
-    core_swap(1, 0)
+    cot_came = p.swap_cotangents([2, 3])
     feats = [
         [(kept_a, 0), (kept_b, 0)],
         [(y_a, 0), (y_b, 0)],
@@ -969,104 +1050,105 @@
         [(c_x_y_a, 0), (c_x_y_b, 0)],
     ]
     total[0] = p.chunk(0, feats, pieces(0))
+    outer[2] = arrive(outer[2])
     value = payload(part(0, 3), inner[2])
     from_own[2] = arrive(from_own[2])
     into[0, 3] = first_out[2] = ends(value)
-    for at in ((0, 0), (0, 1), (1, 0)):
-        core_came(*at)
-    outer[2] = arrive(outer[2])
+    core_came(0, 0)
+    core_came(0, 1)
+    cot_came = arrive(cot_came)
     inner[3] = send("middle", blocks[3])
-    cot_came = p.swap_cotangents([2, 3])
     act_came = p.send(y_swap, p.acts[0])
+    core_swap(1, 0)
     core_swap(1, 1)
     total[1] = p.chunk(1, feats, pieces(1))
     value = payload(part(0, 2), outer[2])
     into[0, 3] = first_out[2] = arrive(into[0, 3])
     into[0, 2] = last_out[2] = ends(value)
+    far0 = did(far_end(0))
     inner[3] = arrive(inner[3])
     outer[3] = send("middle", swapped[3])
-    value = payload(part(0, 1), blocks[3])
-    cot_came = arrive(cot_came)
+    cot_crossed = p.send(y_swap, cot_came)
     act_came = arrive(act_came)
+    core_came(1, 0)
     core_came(1, 1)
-    cot_crossed = p.send(y_swap, cot_came)
+    core_swap(2, 0)
+    core_swap(3, 0)
+    picked[0, 2], picked[1, 2], picked[0, 3], picked[1, 3], picked[2, 1], picked[2, 2], value = blended(
+        (first_out[0], inner[0]),
+        (first_out[1], inner[1]),
+        (last_out[0], outer[0]),
+        (last_out[1], outer[1]),
+        (from_own[2], swapped[2]),
+        (first_out[2], inner[2]),
+        (part(0, 1), blocks[3]),
+    )
+    act_mixes = [p.stitch(0, act_came)]
+    cot_crossed = arrive(cot_crossed)
+    into[0, 2] = last_out[2] = arrive(into[0, 2])
+    into[0, 1] = from_own[3] = ends(value)
+    p.cots[2] = p.cots[3] = (cot_came, cot_crossed)
+    core_came(2, 0)
+    core_came(3, 0)
+    act_came = p.send(y_swap, p.acts[1])
     core_swap(0, 2)
     core_swap(1, 2)
-    act_mix = p.stitch(0, act_came)
-    picked[0, 3] = pick(last_out[0], outer[0])
-    into[0, 2] = last_out[2] = arrive(into[0, 2])
-    into[0, 1] = from_own[3] = ends(value)
-    rest = did(far_end(0))
+    total[2] = p.chunk(2, feats, pieces(2))
     outer[3] = arrive(outer[3])
-    crossed[0] = send("middle", rest)
-    p.cots[2] = p.cots[3] = (cot_came, arrive(cot_crossed))
-    core_came(0, 2)
-    core_came(1, 2)
-    p.crossed[0] = p.send(x_swap, act_mix)
-    act_came = p.send(y_swap, p.acts[1])
-    core_swap(0, 3)
-    total[2] = p.chunk(2, feats, pieces(2))
-    value = payload(part(1, 3), inner[3])
+    [value] = blended((part(1, 3), inner[3]))
     into[0, 1] = from_own[3] = arrive(into[0, 1])
     into[1, 3] = first_out[3] = ends(value)
     rest = did(plus(0, 2, into[0, 2]))
-    picked[1, 3] = pick(last_out[1], outer[1])
+    crossed[0] = send("middle", far0)
+    act_came = arrive(act_came)
+    core_came(0, 2)
+    core_came(1, 2)
+    act_came2 = p.send(y_swap, p.acts[2])
+    core_swap(0, 3)
+    core_swap(1, 3)
+    value, picked[3, 1], picked[2, 3] = blended(
+        (part(1, 2), outer[3]), (from_own[3], swapped[3]), (last_out[2], outer[2])
+    )
+    act_mixes.append(p.stitch(1, act_came))
+    into[1, 3] = first_out[3] = arrive(into[1, 3])
+    into[1, 2] = last_out[3] = ends(value)
+    far1 = did(far_end(1))
     crossed[0] = arrive(crossed[0])
     middle[0] = send("middle", rest)
-    p.crossed[0] = arrive(p.crossed[0])
-    act_came = arrive(act_came)
+    act_came = arrive(act_came2)
     core_came(0, 3)
-    act_came2 = p.send(y_swap, p.acts[2])
-    core_swap(1, 3)
-    core_swap(2, 0)
-    value = payload(part(1, 2), outer[3])
-    act_mix = p.stitch(1, act_came)
-    picked[2, 1] = pick(from_own[2], swapped[2])
-    picked[2, 2] = pick(first_out[2], inner[2])
-    picked[3, 1] = pick(from_own[3], swapped[3])
-    into[1, 3] = first_out[3] = arrive(into[1, 3])
-    into[1, 2] = last_out[3] = ends(value)
-    rest = did(far_end(1))
-    value = payload(part(1, 1), plus(0, 1, crossed[0]))
-    picked[2, 3] = pick(last_out[2], outer[2])
-    middle[0] = arrive(middle[0])
-    crossed[1] = send("middle", rest)
-    act_came = arrive(act_came2)
     core_came(1, 3)
-    core_came(2, 0)
-    p.crossed[1] = p.send(x_swap, act_mix)
-    core_swap(3, 0)
+    core_swap(2, 1)
+    core_swap(2, 2)
     core_swap(3, 1)
-    act_mix = p.stitch(2, act_came)
-    picked[3, 2] = pick(first_out[3], inner[3])
+    value, picked[3, 2] = blended((part(1, 1), part(0, 1), crossed[0]), (first_out[3], inner[3]))
     far = did(jnp.concatenate([then(p.far_grads[0]), p.far_grads[1], p.far_grads[2]]))
+    act_mixes.append(p.stitch(2, act_came))
+    act_mixes = did(jnp.concatenate([then(act_mixes[0]), *act_mixes[1:]]))
     into[1, 2] = last_out[3] = arrive(into[1, 2])
     into[1, 1] = final[0] = ends(value)
-    p.crossed[1] = arrive(p.crossed[1])
-    core_came(3, 0)
-    core_came(3, 1)
-    p.crossed[2] = p.send(x_swap, act_mix)
-    core_swap(2, 1)
-    core_swap(2, 2)
-    total[3] = p.chunk(3, feats, pieces(3))
-    crossed[1] = arrive(crossed[1])
-    value = payload(part(2, 3), plus(1, 1, crossed[1]))
-    into[1, 1] = final[0] = arrive(into[1, 1])
-    into[2, 3] = final[1] = ends(value)
-    p.crossed[2] = arrive(p.crossed[2])
+    sums = did(p.unit_sums(then(p.sums[0]), p.sums[1], p.sums[2]))
     core_came(2, 1)
     core_came(2, 2)
+    core_came(3, 1)
     core_swap(2, 3)
     core_swap(3, 2)
+    mixes_came = p.send(x_swap, act_mixes)
+    total[3] = p.chunk(3, feats, pieces(3))
+    middle[0] = arrive(middle[0])
+    into[1, 1] = final[0] = arrive(into[1, 1])
+    into[2, 3] = inward(2, 3)
+    core_came(2, 3)
+    core_came(3, 2)
+    mixes_came = arrive(mixes_came)
     far = p.send(c_swap, far)
     came_last = p.send(c_swap, last_out[3])
-    middle[1] = send("middle", did(plus(1, 2, into[1, 2])))
-    core_came(2, 3)
     came_outer = p.send(c_swap, outer[3])
-    core_came(3, 2)
+    rows = {0: did(then(part(0, 0)) + edge(0))}
     far = arrive(far)
     far3 = p.send(c_swap, p.far_grads[3])
-    rows = {0: did(part(0, 0) + edge(0))}
+    crossed[1] = send("middle", far1)
+    rest = did(plus(1, 2, into[1, 2]))
     came_last = arrive(came_last)
     slab_came[0] = p.send(x_swap, p.leaving(rows[0]))
     came_outer = arrive(came_outer)
@@ -1081,79 +1163,84 @@
     )
     keep_far, leave_far = p.back(1, came_grads, own_pieces, far_pieces)
     came_far, came_x, own_y = {}, {}, {}
-    into[2, 3] = final[1] = arrive(into[2, 3])
+    into[2, 3] = arrive(into[2, 3])
+    into[2, 2] = inward(2, 2)
+    crossed[1] = arrive(crossed[1])
+    slab_came[0] = arrive(slab_came[0])
+    act_came = arrive(act_came)
+    middle[1] = send("middle", rest)
+    came_far[0] = p.send(x_swap, leave_far[0])
+    keep, leave = p.back(0, came_grads, own_pieces, far_pieces)
+    [far2] = blended((part(2, 3), part(2, 3), into[2, 3]))
+    into[2, 2] = arrive(into[2, 2])
     into[3, 3] = inward(3, 3)
-    slab_came[0] = arrive(slab_came[0])
-    came_far[0] = p.send(x_swap, leave_far[0])
-    act_came = arrive(act_came)
-    rest = did(far_end(2))
+    sums = did(jnp.concatenate([then(sums), p.unit_sums(p.sums[3])], axis=1))
     middle[1] = arrive(middle[1])
-    crossed[2] = send("middle", rest)
-    keep, leave = p.back(0, came_grads, own_pieces, far_pieces)
+    crossed[2] = send("middle", far2)
+    came_far[0] = arrive(came_far[0])
+    came_x[0] = p.send(x_swap, leave[0])
+    own_y[0] = p.send(y_swap, p.add(keep_far[0], came_far[0]))
+    value, own2 = blended((part(3, 2), part(1, 1), crossed[1]), (part(2, 2), part(2, 2), into[2, 2]))
+    act_mix = p.stitch(3, act_came)
+    p.store(0, rows[0], slab_came[0])
     into[3, 3] = arrive(into[3, 3])
-    into[2, 2] = inward(2, 2)
+    into[3, 2] = final[1] = ends(value)
     rest = did(far_end(3))
-    came_far[0] = arrive(came_far[0])
+    came_x[0] = arrive(came_x[0])
     came_far[1] = p.send(x_swap, leave_far[1])
     crossed[2] = arrive(crossed[2])
     crossed[3] = send("middle", rest)
-    own_y[0] = p.send(y_swap, p.add(keep_far[0], came_far[0]))
-    sums = did(then(p.unit_sums()))
-    act_mix = p.stitch(3, act_came)
-    p.store(0, rows[0], slab_came[0])
-    into[2, 2] = arrive(into[2, 2])
-    into[3, 2] = inward(3, 2)
-    rest = did(plus(2, 2, into[2, 2]))
+    own_y[0] = arrive(own_y[0])
+    p.crossed[3] = p.send(x_swap, act_mix)
+    [value] = blended((part(2, 1), part(2, 1), crossed[2]))
+    partial = p.first_grad(0, keep[0], came_x[0], own_y[0], pooled)
+    grad = (p.unpool(0, keep[0], came_x[0], own_y[0], (), 0, 2),)
+    into[3, 2] = final[1] = arrive(into[3, 2])
+    into[2, 1] = final[2] = ends(value)
+    last = did(plus(3, 2, into[3, 2]))
     came_far[1] = arrive(came_far[1])
-    came_x[0] = p.send(x_swap, leave[0])
+    came_x[1] = p.send(x_swap, leave[1])
     crossed[3] = arrive(crossed[3])
-    middle[2] = send("middle", rest)
-    own_y[0] = arrive(own_y[0])
+    middle[2] = send("middle", own2)
     own_y[1] = p.send(y_swap, p.add(keep_far[1], came_far[1]))
-    value = payload(part(2, 1), plus(2, 1, crossed[2]))
-    rows[1] = did(part(1, 0) + edge(1))
-    into[3, 2] = arrive(into[3, 2])
-    into[2, 1] = final[2] = ends(value)
-    rest = did(plus(3, 2, into[3, 2]))
-    came_x[0] = arrive(came_x[0])
-    came_x[1] = p.send(x_swap, leave[1])
-    middle[2] = arrive(middle[2])
-    middle[3] = send("middle", rest)
-    own_y[1] = arrive(own_y[1])
-    value = payload(part(3, 1), plus(3, 1, crossed[3]))
-    partial = p.first_grad(0, keep[0], came_x[0], own_y[0], pooled)
+    p.crossed[3] = arrive(p.crossed[3])
+    [value] = blended((part(3, 1), part(3, 1), crossed[3]))
+    grad = (p.unpool(0, keep[0], came_x[0], own_y[0], grad, 1, 2),)
+    rows[1] = did(then(part(1, 0)) + edge(1))
     into[2, 1] = final[2] = arrive(into[2, 1])
     into[3, 1] = final[3] = ends(value)
     came_x[1] = arrive(came_x[1])
     slab_came[1] = p.send(x_swap, p.leaving(rows[1]))
-    middle[3] = arrive(middle[3])
+    middle[2] = arrive(middle[2])
+    middle[3] = send("middle", last)
     rows[2] = did(part(2, 0) + edge(2))
     slab_came[2] = p.send(x_swap, p.leaving(rows[2]))
-    p.crossed[3] = p.send(x_swap, act_mix)
+    own_y[1] = arrive(own_y[1])
     partial = partial + p.first_grad(1, keep[1], came_x[1], own_y[1], pooled)
     partial = did(p.by_tower(partial).reshape(1, -1))
-    grad = (p.unpool(0, keep[0], came_x[0], own_y[0]),)
+    partial_came = p.send(c_swap, partial)
+    grad = p.unpool(1, keep[1], came_x[1], own_y[1], grad)
     into[3, 1] = final[3] = arrive(into[3, 1])
+    partial = did(partial + then(partial_came))
+    second_came = p.send(y_swap, jnp.concatenate([sums[2:], partial]))
+    slab_came[1] = arrive(slab_came[1])
+    middle[3] = arrive(middle[3])
     rows[3] = did(part(3, 0) + edge(3))
     slab_came[3] = p.send(x_swap, p.leaving(rows[3]))
-    partial_came = p.send(c_swap, partial)
-    slab_came[1] = arrive(slab_came[1])
     p.store(1, rows[1], slab_came[1])
-    partial = did(partial + then(partial_came))
-    second_came = p.send(y_swap, jnp.concatenate([sums[2:], partial]))
-    slab_came[2] = arrive(slab_came[2])
-    p.store(2, rows[2], slab_came[2])
     second_came = arrive(second_came)
     sums = did(jnp.concatenate([sums[:2], second_came[:1], partial + second_came[1:]]))
     sums_came = p.send(flipped, sums, "batch", 2)
-    grad = p.unpool(1, keep[1], came_x[1], own_y[1], grad)
+    slab_came[2] = arrive(slab_came[2])
+    p.store(2, rows[2], slab_came[2])
     sums = did(sums + then(sums_came))
     sums_came = p.send(flipped, sums, "batch", 4)
     slab_came[3] = arrive(slab_came[3])
     p.store(3, rows[3], slab_came[3])
     sums = did(sums + then(sums_came))
     sums_came = p.send(x_swap, sums)
-    p.crossed[3] = arrive(p.crossed[3])
+    for j in range(3):
+        p.crossed[j] = jnp.split(mixes_came, 3)[j]
     activations = did(p.activations())
     sums_came = then(sums_came)
     bias_grad, alpha2_grad = p.small_grads(jnp.concatenate([sums[:3], sums_came[:3]]))

time: 654 us -> 611 us (0.934)
  other arithmetic: 87.4 us -> 47.4 us
  waiting for transfers between devices: 185 us -> 149 us
  Pallas kernels: 194 us -> 227 us
    ppermute x35, waiting for transfers between devices: 128 us -> 74.3 us  [line(): return lax.ppermute(value, 'batch', pairs)]
    pallas_call x0 -> x8, Pallas kernels: none -> 29.6 us  [blend(): pl.pallas_call(functools.partial(blend_kernel, counts), in_specs=[pl.Bloc...]
    ppermute x65 -> x63, waiting for transfers between devices: 56.9 us -> 75 us  [flipped(): return lax.ppermute(value, axis, pairs)]
    select_n x9 -> x0, other arithmetic: 16.1 us -> none  [pick(): return did(jnp.where(p.is_outer, then(a), b))]
    select_n x11 -> x4, other arithmetic: 20.7 us -> 6.43 us  [payload(): return did(jnp.where(p.is_outer, then(inward), outward))]
    convert_element_type x8 -> x6, other arithmetic: 18 us -> 9.98 us  [plus(): return (part(j, s).astype(F32) + then(value).astype(F32)).astype(BF16)]
    ppermute x35, starting transfers between devices: 67.8 us -> 61 us  [line(): return lax.ppermute(value, 'batch', pairs)]
    pallas_call x2 -> x3, Pallas kernels: 30.4 us -> 34.6 us  [unpool(): pl.pallas_call(functools.partial(unpool_kernel, at), grid_spec=pltpu.Pref...]
  transfers between devices with their start and end apart: 100 -> 98, of which waited for: 25 -> 19; matrix products, arithmetic and copies ran while one was open for 20% -> 16% of each run, Pallas kernels for 30% -> 38%
where the time goes in v5:
time: 611 us; the launch traced here: 599 us
  Pallas kernels  227 us (37%)
  waiting for transfers between devices  149 us (24%)
  starting transfers between devices  112 us (18%)
  other arithmetic  47.4 us (8%)
  local copies, waits for them, and re-layouts  46.8 us (8%)
  matrix products  13.9 us (2%)
    pallas_call x4, Pallas kernels, chunk(): pl.pallas_call(functools.partial(chunk_kernel, [[len(p) for p in chunk] f...  85.3 us
    ppermute x63, waiting for transfers between devices, flipped(): return lax.ppermute(value, axis, pairs)  75 us
    ppermute x35, waiting for transfers between devices, line(): return lax.ppermute(value, 'batch', pairs)  74.3 us
    ppermute x35, starting transfers between devices, line(): return lax.ppermute(value, 'batch', pairs)  61 us
    ppermute x63, starting transfers between devices, flipped(): return lax.ppermute(value, axis, pairs)  51.1 us
    pallas_call x2, Pallas kernels, back(): pl.pallas_call(functools.partial(back_kernel, layout, [row for _, row in...  35.1 us
    pallas_call x3, Pallas kernels, unpool(): pl.pallas_call(functools.partial(unpool_kernel, at), grid_spec=pltpu.Pref...  34.6 us
    pallas_call x8, Pallas kernels, blend(): pl.pallas_call(functools.partial(blend_kernel, counts), in_specs=[pl.Bloc...  29.6 us
  transfers between devices with their start and end apart: 98, of which 19 were waited for; matrix products, arithmetic and copies ran while one was open for 16% of the time, Pallas kernels for 38%

profile of v5, /device:TPU:0, one launch (start us, length us, event | category | flops | bytes accessed | tf_op | source)
XLA Modules:
  0.0 599.3 jit_solution(1743917873633037071)
XLA Ops:
  24.5 4.4 collective-permute-start.4
  30.0 13.9 %fusion.2.summed = f32[128,2,36,256]{3,2,1,0:T(8,128)} fusion(bf16[128,2,169,256]{3,1,2,0:T(2,128)(2,1)} %param.8, bf16[36,169]{1,0:T(8,128)(2,1)S(1)} %and_convert_fusion), kind=kOutput, calls=%fused_computation.3 | convolution fusion | flops 797442048 | bytes 31600520 | tf_op jit(solution)/shard_map/pq,nsqc->nspc/dot_general | solution.py:780
  46.7 6.7 %collective-permute-done.4.refs_21_.refs_9_ = bf16[2304,256]{1,0:T(8,128)(2,1)S(1)} collective-permute-done((bf16[2304,256]{1,0:T(8,128)(2,1)S(1)}, bf16[2304,256]{1,0:T(8,128)(2,1)S(1)}, u32[]{:S(2)}, u32[]{:S(2)}) %collective-permute-start.4) | collective-permute-done | bytes 1179680 | tf_op jit(solution)/shard_map/ppermute | solution.py:52
  59.4 14.2 %mix.1 = (bf16[128,4608]{1,0:T(8,128)(2,1)}, bf16[128,4608]{1,0:T(8,128)(2,1)}, bf16[128,4608]{1,0:T(8,128)(2,1)}, bf16[128,4608]{1,0:T(8,128)(2,1)}, f32[2,128,9216]{2,1,0:T(8,128)}) custom-call(s32[128]{0:T(128)} %group.7, f32[2,36,256]{2,1,0:T(8,128)} %broadcast_in_dim.8.keep, f32[4,256]{1,0:T(4,128)} %reshape.655.first, f32[128,2,36,256]{3,2,1,0:T(8,128)} %fusion.2.summed), custom_call_target="tpu_custom_call" | custom-call | flops 1000 | bytes 1000 | tf_op jit(solution)/shard_map/mix/pallas_call | solution.py:149
  84.2 20.1 %collective-permute-done.8.refs_8_ = bf16[128,4608]{1,0:T(8,128)(2,1)} collective-permute-done((bf16[128,4608]{1,0:T(8,128)(2,1)S(1)}, bf16[128,4608]{1,0:T(8,128)(2,1)}, u32[]{:S(2)}, u32[]{:S(2)}) %collective-permute-start.8) | collective-permute-done | bytes 1179680 | tf_op jit(solution)/shard_map/ppermute | solution.py:29
  106.4 4.8 collective-permute-done.13.refs_22_.refs_0_
  114.3 17.0 %collective-permute-done.11.refs_9_ = bf16[128,4608]{1,0:T(8,128)(2,1)S(1)} collective-permute-done((bf16[128,4608]{1,0:T(8,128)(2,1)S(1)}, bf16[128,4608]{1,0:T(8,128)(2,1)S(1)}, u32[]{:S(2)}, u32[]{:S(2)}) %collective-permute-start.11) | collective-permute-done | bytes 1179680 | tf_op jit(solution)/shard_map/ppermute | solution.py:29
  134.9 4.9 collective-permute-done.22.refs_22_.refs_2_
  140.8 16.8 %collective-permute-done.20.refs_10_ = bf16[128,4608]{1,0:T(8,128)(2,1)} collective-permute-done((bf16[128,4608]{1,0:T(8,128)(2,1)}, bf16[128,4608]{1,0:T(8,128)(2,1)}, u32[]{:S(2)}, u32[]{:S(2)}) %collective-permute-start.20) | collective-permute-done | bytes 1179680 | tf_op jit(solution)/shard_map/ppermute | solution.py:29
  161.3 4.5 collective-permute-done.23.refs_24_.refs_4_.refs_9_.refs_22_
  165.8 17.3 %collective-permute-done.25.refs_11_ = bf16[128,4608]{1,0:T(8,128)(2,1)} collective-permute-done((bf16[128,4608]{1,0:T(8,128)(2,1)}, bf16[128,4608]{1,0:T(8,128)(2,1)}, u32[]{:S(2)}, u32[]{:S(2)}) %collective-permute-start.25) | collective-permute-done | bytes 1179680 | tf_op jit(solution)/shard_map/ppermute | solution.py:29
  194.7 21.2 %chunk.4 = (bf16[1024,256]{1,0:T(8,128)(2,1)}, bf16[512,256]{1,0:T(8,128)(2,1)}, bf16[512,256]{1,0:T(8,128)(2,1)}, f32[8,256]{1,0:T(8,128)}, f32[2304,256]{1,0:T...) custom-call(s32[2]{0:T(128)} %pad_add_fusion.2.roles, ...), custom_call_target="tpu_custom_call" | custom-call | flops 1000 | bytes 1000 | tf_op jit(solution)/shard_map/chunk/pallas_call | solution.py:589
  223.7 21.1 %chunk.5 = (bf16[1024,256]{1,0:T(8,128)(2,1)}, bf16[512,256]{1,0:T(8,128)(2,1)}, bf16[512,256]{1,0:T(8,128)(2,1)}, f32[8,256]{1,0:T(8,128)}, f32[2304,256]{1,0:T...) custom-call(s32[2]{0:T(128)} %pad_add_fusion.2.roles, ...), custom_call_target="tpu_custom_call" | custom-call | flops 1000 | bytes 1000 | tf_op jit(solution)/shard_map/chunk/pallas_call | solution.py:589
  254.7 7.5 %blend.8 = (bf16[2304,256]{1,0:T(8,128)(2,1)}, bf16[2304,256]{1,0:T(8,128)(2,1)}, bf16[2304,256]{1,0:T(8,128)(2,1)}, bf16[2304,256]{1,0:T(8,128)(2,1)}, bf16[230...) custom-call(s32[2]{0:T(128)} %pad_add_fusion.2.roles, bf16[2304,256]{1,0:T(8,128)(2,1)} %copy-done.45, ...), custom_call_target="tpu_custom_call" | custom-call | flops 1000 | bytes 1000 | tf_op jit(solution)/shard_map/blend/pallas_call | solution.py:402
  265.6 11.1 %collective-permute-done.44.refs_25_.refs_4_ = bf16[2304,256]{1,0:T(8,128)(2,1)} collective-permute-done((bf16[2304,256]{1,0:T(8,128)(2,1)}, bf16[2304,256]{1,0:T(8,128)(2,1)}, u32[]{:S(2)}, u32[]{:S(2)}) %collective-permute-start.44) | collective-permute-done | bytes 1179680 | tf_op jit(solution)/shard_map/ppermute | solution.py:52
  280.3 21.1 %chunk.6 = (bf16[1024,256]{1,0:T(8,128)(2,1)}, bf16[512,256]{1,0:T(8,128)(2,1)}, bf16[512,256]{1,0:T(8,128)(2,1)}, f32[8,256]{1,0:T(8,128)}, f32[2304,256]{1,0:T...) custom-call(s32[2]{0:T(128)} %pad_add_fusion.2.roles, ...), custom_call_target="tpu_custom_call" | custom-call | flops 1000 | bytes 1000 | tf_op jit(solution)/shard_map/chunk/pallas_call | solution.py:589
  312.2 3.9 blend.10
  319.4 13.5 %collective-permute-done.55.refs_3_.refs_23_ = bf16[2304,256]{1,0:T(8,128)(2,1)S(1)} collective-permute-done((bf16[2304,256]{1,0:T(8,128)(2,1)}, bf16[2304,256]{1,0:T(8,128)(2,1)S(1)}, u32[]{:S(2)}, u32[]{:S(2)}) %collective-permute-start.55) | collective-permute-done | bytes 1179680 | tf_op jit(solution)/shard_map/ppermute | solution.py:52
  346.6 13.2 %collective-permute-done.56.refs_25_.refs_23_ = bf16[2304,256]{1,0:T(8,128)(2,1)S(1)} collective-permute-done((bf16[2304,256]{1,0:T(8,128)(2,1)}, bf16[2304,256]{1,0:T(8,128)(2,1)S(1)}, u32[]{:S(2)}, u32[]{:S(2)}) %collective-permute-start.56) | collective-permute-done | bytes 1179680 | tf_op jit(solution)/shard_map/ppermute | solution.py:52
  361.4 21.9 %chunk.7 = (bf16[1024,256]{1,0:T(8,128)(2,1)}, bf16[512,256]{1,0:T(8,128)(2,1)}, bf16[512,256]{1,0:T(8,128)(2,1)}, f32[8,256]{1,0:T(8,128)}, f32[2304,256]{1,0:T...) custom-call(s32[2]{0:T(128)} %pad_add_fusion.2.roles, ...), custom_call_target="tpu_custom_call" | custom-call | flops 1000 | bytes 1000 | tf_op jit(solution)/shard_map/chunk/pallas_call | solution.py:589
  397.1 17.7 %back.2 = (bf16[64,9216]{1,0:T(8,128)(2,1)}, bf16[64,9216]{1,0:T(8,128)(2,1)}, bf16[64,9216]{1,0:T(8,128)(2,1)}, bf16[64,9216]{1,0:T(8,128)(2,1)}) custom-call(s32[2]{0:T(128)} %pad_add_fusion.2.roles, bf16[512,256]{1,0:T(8,128)(2,1)} %get-tuple-element.559.refs_0_, bf16[512,256]{1,0:T(8,128)(2,1)} %get-tuple-element.546.refs_1_, ...), custom_call_target="tpu_custom_call" | custom-call | flops 1000 | bytes 1000 | tf_op jit(solution)/shard_map/back/pallas_call | solution.py:699
  415.1 4.3 collective-permute-start.70
  421.6 17.4 %back.3 = (bf16[64,9216]{1,0:T(8,128)(2,1)}, bf16[64,9216]{1,0:T(8,128)(2,1)}, bf16[64,9216]{1,0:T(8,128)(2,1)}, bf16[64,9216]{1,0:T(8,128)(2,1)}) custom-call(s32[2]{0:T(128)} %pad_add_fusion.2.roles, bf16[512,256]{1,0:T(8,128)(2,1)} %get-tuple-element.559.refs_0_, bf16[512,256]{1,0:T(8,128)(2,1)} %get-tuple-element.546.refs_1_, ...), custom_call_target="tpu_custom_call" | custom-call | flops 1000 | bytes 1000 | tf_op jit(solution)/shard_map/back/pallas_call | solution.py:699
  444.4 5.7 collective-permute-start.77
  463.4 3.8 store.4.refs_0_
  467.2 6.4 %collective-permute-done.77 = bf16[2304,256]{1,0:T(8,128)(2,1)} collective-permute-done((bf16[2304,256]{1,0:T(8,128)(2,1)}, bf16[2304,256]{1,0:T(8,128)(2,1)}, u32[]{:S(2)}, u32[]{:S(2)}) %collective-permute-start.77) | collective-permute-done | bytes 1179680 | tf_op jit(solution)/shard_map/ppermute | solution.py:52
  487.0 5.0 first_grad.2
  493.5 9.5 %unpool.3.refs_0_ = bf16[128,169,2,256]{3,2,1,0:T(2,128)(2,1)} custom-call(s32[128]{0:T(128)} %group.7, bf16[2,352,192]{2,1,0:T(8,128)(2,1)} %fusion.15.table, f32[4,256]{1,0:T(4,128)} %reshape.655.first, bf16[64,9216]{1,0:T(8,128)(2,1)} %get-tuple-element.610.keep.keep_in, bf16[64,9216]{1,0:T(8,128)(2,1)} %copy-done.28, bf16[64,9216]{1,0:T(8,128)(2,1)} %copy-done.29), custom_call_target="tpu_custom_call" | custom-call | flops 1000 | bytes 1000 | tf_op jit(solution)/shard_map/unpool/pallas_call | solution.py:253
  518.3 9.8 %unpool.4.refs_0_ = bf16[128,169,2,256]{3,2,1,0:T(2,128)(2,1)} custom-call(s32[128]{0:T(128)} %group.7, bf16[2,352,192]{2,1,0:T(8,128)(2,1)} %fusion.15.table, f32[4,256]{1,0:T(4,128)} %reshape.655.first, bf16[64,9216]{1,0:T(8,128)(2,1)} %get-tuple-element.610.keep.keep_in, bf16[64,9216]{1,0:T(8,128)(2,1)} %copy-done.28, ...), custom_call_target="tpu_custom_call", output_to_operand_aliasing={{}: (6, {})} | custom-call | flops 1000 | bytes 1000 | tf_op jit(solution)/shard_map/unpool/pallas_call | solution.py:253
  543.6 5.0 first_grad.3
  550.4 15.3 %unpool.5 = bf16[128,169,2,256]{3,2,1,0:T(2,128)(2,1)} custom-call(s32[128]{0:T(128)} %group.7, bf16[2,352,192]{2,1,0:T(8,128)(2,1)} %fusion.15.table, f32[4,256]{1,0:T(4,128)} %reshape.655.first, bf16[64,9216]{1,0:T(8,128)(2,1)} %get-tuple-element.624.keep.keep_in, bf16[64,9216]{1,0:T(8,128)(2,1)} %copy-done.50, ...), custom_call_target="tpu_custom_call", output_to_operand_aliasing={{}: (6, {})} | custom-call | flops 1000 | bytes 1000 | tf_op jit(solution)/shard_map/unpool/pallas_call | solution.py:253
  586.2 3.8 store.7
  (515 shorter events, 233.8 us)
Async XLA Ops:
  7.4 36.4 %collective-permute-start.2 = (bf16[1152,256]{1,0:T(8,128)(2,1)}, bf16[1152,256]{1,0:T(8,128)(2,1)S(1)}, u32[]{:S(2)}, u32[]{:S(2)}) collective-permute-start(bf16[1152,256]{1,0:T(8,128)(2,1)} %constant_dynamic-slice_fusion.9), channel_id=1, source_target_pairs={{0,4},{4,0},{8,12},{12,8},{16,20},{20,16},{24,28},{28,24},{1,5},{5... | collective-permute-start | bytes 1769480 | tf_op jit(solution)/shard_map/ppermute | solution.py:29
  12.2 61.4 %collective-permute-start.7 = (bf16[1152,512]{1,0:T(8,128)(2,1)}, bf16[1152,512]{1,0:T(8,128)(2,1)}, u32[]{:S(2)}, u32[]{:S(2)}) collective-permute-start(bf16[1152,512]{1,0:T(8,128)(2,1)} %constant_dynamic-slice_fusion.8), channel_id=1, source_target_pairs={{0,4},{4,0},{8,12},{12,8},{16,20},{20,16},{24,28},{28,24},{1,5},{5... | collective-permute-start | bytes 3538952 | tf_op jit(solution)/shard_map/ppermute | solution.py:29
  23.7 29.7 %collective-permute-start.3 = (bf16[2304,256]{1,0:T(8,128)(2,1)S(1)}, bf16[2304,256]{1,0:T(8,128)(2,1)S(1)}, u32[]{:S(2)}, u32[]{:S(2)}) collective-permute-start(bf16[2304,256]{1,0:T(8,128)(2,1)S(1)} %maximum_select_fusion.refs_20_.refs_8_), channel_id=1, source_target_pairs={{8,16},{12,20},{16,8},{20,12},{9,17},{13,21},{17,9},{21,13},{10,18... | collective-permute-start | bytes 3538952 | tf_op jit(solution)/shard_map/ppermute | solution.py:52
  24.5 29.0 %collective-permute-start.4 = (bf16[2304,256]{1,0:T(8,128)(2,1)S(1)}, bf16[2304,256]{1,0:T(8,128)(2,1)S(1)}, u32[]{:S(2)}, u32[]{:S(2)}) collective-permute-start(bf16[2304,256]{1,0:T(8,128)(2,1)S(1)} %maximum_select_fusion.refs_20_.refs_8_), channel_id=1, source_target_pairs={{0,8},{4,12},{8,0},{12,4},{16,24},{20,28},{24,16},{28,20},{1,9},{5... | collective-permute-start | bytes 3538952 | tf_op jit(solution)/shard_map/ppermute | solution.py:52
  28.9 44.8 %collective-permute-start.6 = (bf16[512,1024]{1,0:T(8,128)(2,1)S(1)}, bf16[512,1024]{1,0:T(8,128)(2,1)S(1)}, u32[]{:S(2)}, u32[]{:S(2)}) collective-permute-start(bf16[512,1024]{1,0:T(8,128)(2,1)S(1)} %constant_dynamic-slice_fusion.7.refs_0_), channel_id=1, source_target_pairs={{0,2},{1,3},{2,0},{3,1},{4,6},{5,7},{6,4},{7,5},{8,10},{9,11},{10,... | collective-permute-start | bytes 3145736 | tf_op jit(solution)/shard_map/ppermute | solution.py:29
  43.8 31.6 %collective-permute-start.5 = (bf16[512,512]{1,0:T(8,128)(2,1)}, bf16[512,512]{1,0:T(8,128)(2,1)S(1)}, u32[]{:S(2)}, u32[]{:S(2)}) collective-permute-start(bf16[512,512]{1,0:T(8,128)(2,1)} %get-tuple-element.342), channel_id=1, source_target_pairs={{0,4},{4,0},{8,12},{12,8},{16,20},{20,16},{24,28},{28,24},{1,5},{5... | collective-permute-start | bytes 1572872 | tf_op jit(solution)/shard_map/ppermute | solution.py:29
  54.5 29.0 %collective-permute-start.9 = (bf16[2304,256]{1,0:T(8,128)(2,1)S(1)}, bf16[2304,256]{1,0:T(8,128)(2,1)}, u32[]{:S(2)}, u32[]{:S(2)}) collective-permute-start(bf16[2304,256]{1,0:T(8,128)(2,1)S(1)} %maximum_select_fusion.1.refs_20_.refs_12_), channel_id=1, source_target_pairs={{8,16},{12,20},{16,8},{20,12},{9,17},{13,21},{17,9},{21,13},{10,18... | collective-permute-start | bytes 3538952 | tf_op jit(solution)/shard_map/ppermute | solution.py:52
  75.6 30.8 %collective-permute-start.14 = (bf16[128,4608]{1,0:T(8,128)(2,1)S(1)}, bf16[128,4608]{1,0:T(8,128)(2,1)S(1)}, u32[]{:S(2)}, u32[]{:S(2)}) collective-permute-start(bf16[128,4608]{1,0:T(8,128)(2,1)S(1)} %copy-done.4), channel_id=1, source_target_pairs={{0,1},{1,0},{2,3},{3,2},{4,5},{5,4},{6,7},{7,6},{8,9},{9,8},{10,11... | collective-permute-start | bytes 3538952 | tf_op jit(solution)/shard_map/ppermute | solution.py:29
  76.0 29.5 %collective-permute-start.15 = (bf16[128,4608]{1,0:T(8,128)(2,1)S(1)}, bf16[128,4608]{1,0:T(8,128)(2,1)}, u32[]{:S(2)}, u32[]{:S(2)}) collective-permute-start(bf16[128,4608]{1,0:T(8,128)(2,1)S(1)} %copy-done.99), channel_id=1, source_target_pairs={{0,2},{1,3},{2,0},{3,1},{4,6},{5,7},{6,4},{7,5},{8,10},{9,11},{10,... | collective-permute-start | bytes 3538952 | tf_op jit(solution)/shard_map/ppermute | solution.py:29
  82.2 29.1 %collective-permute-start.13 = (bf16[2304,256]{1,0:T(8,128)(2,1)S(1)}, bf16[2304,256]{1,0:T(8,128)(2,1)S(1)}, u32[]{:S(2)}, u32[]{:S(2)}) collective-permute-start(bf16[2304,256]{1,0:T(8,128)(2,1)S(1)} %copy-done.40), channel_id=1, source_target_pairs={{8,0},{12,4},{16,24},{20,28},{9,1},{13,5},{17,25},{21,29},{10,2},{... | collective-permute-start | bytes 3538952 | tf_op jit(solution)/shard_map/ppermute | solution.py:52
  83.5 29.1 %collective-permute-start.12 = (bf16[2304,256]{1,0:T(8,128)(2,1)S(1)}, bf16[2304,256]{1,0:T(8,128)(2,1)S(1)}, u32[]{:S(2)}, u32[]{:S(2)}) collective-permute-start(bf16[2304,256]{1,0:T(8,128)(2,1)S(1)} %collective-permute-done.4.refs_21_.refs_9_), channel_id=1, source_target_pairs={{8,16},{12,20},{16,8},{20,12},{9,17},{13,21},{17,9},{21,13},{10,18... | collective-permute-start | bytes 3538952 | tf_op jit(solution)/shard_map/ppermute | solution.py:52
  185.7 30.3 %collective-permute-start.35 = (bf16[2304,256]{1,0:T(8,128)(2,1)}, bf16[2304,256]{1,0:T(8,128)(2,1)}, u32[]{:S(2)}, u32[]{:S(2)}) collective-permute-start(bf16[2304,256]{1,0:T(8,128)(2,1)} %collective-permute-done.23.refs_24_.refs_4_.refs_9_.refs_22_), channel_id=1, source_target_pairs={{8,16},{12,20},{16,8},{20,12},{9,17},{13,21},{17,9},{21,13},{10,18... | collective-permute-start | bytes 3538952 | tf_op jit(solution)/shard_map/ppermute | solution.py:52
  220.8 31.1 %collective-permute-start.37 = (bf16[1024,256]{1,0:T(8,128)(2,1)}, bf16[1024,256]{1,0:T(8,128)(2,1)}, u32[]{:S(2)}, u32[]{:S(2)}) collective-permute-start(bf16[1024,256]{1,0:T(8,128)(2,1)} %get-tuple-element.426), channel_id=1, source_target_pairs={{0,2},{1,3},{2,0},{3,1},{4,6},{5,7},{6,4},{7,5},{8,10},{9,11},{10,... | collective-permute-start | bytes 1572872 | tf_op jit(solution)/shard_map/ppermute | solution.py:29
  222.4 29.5 %collective-permute-start.41 = (bf16[2304,256]{1,0:T(8,128)(2,1)S(1)}, bf16[2304,256]{1,0:T(8,128)(2,1)S(1)}, u32[]{:S(2)}, u32[]{:S(2)}) collective-permute-start(bf16[2304,256]{1,0:T(8,128)(2,1)S(1)} %copy-done.15), channel_id=1, source_target_pairs={{0,1},{1,0},{2,3},{3,2},{4,5},{5,4},{6,7},{7,6},{8,9},{9,8},{10,11... | collective-permute-start | bytes 3538952 | tf_op jit(solution)/shard_map/ppermute | solution.py:29
  247.4 29.2 %collective-permute-start.44 = (bf16[2304,256]{1,0:T(8,128)(2,1)}, bf16[2304,256]{1,0:T(8,128)(2,1)}, u32[]{:S(2)}, u32[]{:S(2)}) collective-permute-start(bf16[2304,256]{1,0:T(8,128)(2,1)} %broadcast_select_fusion), channel_id=1, source_target_pairs={{0,8},{4,12},{8,0},{12,4},{16,24},{20,28},{24,16},{28,20},{1,9},{5... | collective-permute-start | bytes 3538952 | tf_op jit(solution)/shard_map/ppermute | solution.py:52
  253.5 47.9 %collective-permute-start.49 = (bf16[2304,256]{1,0:T(8,128)(2,1)}, bf16[2304,256]{1,0:T(8,128)(2,1)S(1)}, u32[]{:S(2)}, u32[]{:S(2)}) collective-permute-start(bf16[2304,256]{1,0:T(8,128)(2,1)} %collective-permute-done.24.refs_24_.refs_6_.refs_3_.refs_22_), channel_id=1, source_target_pairs={{8,16},{12,20},{16,8},{20,12},{9,17},{13,21},{17,9},{21,13},{10,18... | collective-permute-start | bytes 3538952 | tf_op jit(solution)/shard_map/ppermute | solution.py:52
  278.4 31.9 %collective-permute-start.47 = (bf16[2304,256]{1,0:T(8,128)(2,1)S(1)}, bf16[2304,256]{1,0:T(8,128)(2,1)S(1)}, u32[]{:S(2)}, u32[]{:S(2)}) collective-permute-start(bf16[2304,256]{1,0:T(8,128)(2,1)S(1)} %copy-done.41), channel_id=1, source_target_pairs={{0,1},{1,0},{2,3},{3,2},{4,5},{5,4},{6,7},{7,6},{8,9},{9,8},{10,11... | collective-permute-start | bytes 3538952 | tf_op jit(solution)/shard_map/ppermute | solution.py:29
  278.5 31.8 %collective-permute-start.46 = (bf16[2304,256]{1,0:T(8,128)(2,1)}, bf16[2304,256]{1,0:T(8,128)(2,1)S(1)}, u32[]{:S(2)}, u32[]{:S(2)}) collective-permute-start(bf16[2304,256]{1,0:T(8,128)(2,1)} %get-tuple-element.462.refs_14_), channel_id=1, source_target_pairs={{0,1},{1,0},{2,3},{3,2},{4,5},{5,4},{6,7},{7,6},{8,9},{9,8},{10,11... | collective-permute-start | bytes 3538952 | tf_op jit(solution)/shard_map/ppermute | solution.py:29
  279.8 30.5 %collective-permute-start.48 = (bf16[1024,256]{1,0:T(8,128)(2,1)}, bf16[1024,256]{1,0:T(8,128)(2,1)}, u32[]{:S(2)}, u32[]{:S(2)}) collective-permute-start(bf16[1024,256]{1,0:T(8,128)(2,1)} %get-tuple-element.460), channel_id=1, source_target_pairs={{0,2},{1,3},{2,0},{3,1},{4,6},{5,7},{6,4},{7,5},{8,10},{9,11},{10,... | collective-permute-start | bytes 1572872 | tf_op jit(solution)/shard_map/ppermute | solution.py:29
  334.5 48.8 %collective-permute-start.61 = (bf16[2304,256]{1,0:T(8,128)(2,1)}, bf16[2304,256]{1,0:T(8,128)(2,1)}, u32[]{:S(2)}, u32[]{:S(2)}) collective-permute-start(bf16[2304,256]{1,0:T(8,128)(2,1)} %add_convert_fusion.6), channel_id=1, source_target_pairs={{8,16},{12,20},{16,8},{20,12},{9,17},{13,21},{17,9},{21,13},{10,18... | collective-permute-start | bytes 3538952 | tf_op jit(solution)/shard_map/ppermute | solution.py:52
  415.1 29.3 %collective-permute-start.70 = (bf16[2304,256]{1,0:T(8,128)(2,1)S(1)}, bf16[2304,256]{1,0:T(8,128)(2,1)S(1)}, u32[]{:S(2)}, u32[]{:S(2)}) collective-permute-start(bf16[2304,256]{1,0:T(8,128)(2,1)S(1)} %copy-done.52), channel_id=1, source_target_pairs={{0,8},{4,12},{24,16},{28,20},{1,9},{5,13},{25,17},{29,21},{2,10},{... | collective-permute-start | bytes 3538952 | tf_op jit(solution)/shard_map/ppermute | solution.py:52
  419.5 30.6 %collective-permute-start.75 = (bf16[2304,256]{1,0:T(8,128)(2,1)S(1)}, bf16[2304,256]{1,0:T(8,128)(2,1)S(1)}, u32[]{:S(2)}, u32[]{:S(2)}) collective-permute-start(bf16[2304,256]{1,0:T(8,128)(2,1)S(1)} %add_convert_fusion.4), channel_id=1, source_target_pairs={{8,16},{12,20},{16,8},{20,12},{9,17},{13,21},{17,9},{21,13},{10,18... | collective-permute-start | bytes 3538952 | tf_op jit(solution)/shard_map/ppermute | solution.py:52
  420.2 29.9 %collective-permute-start.74 = (bf16[64,9216]{1,0:T(8,128)(2,1)}, bf16[64,9216]{1,0:T(8,128)(2,1)S(1)}, u32[]{:S(2)}, u32[]{:S(2)}) collective-permute-start(bf16[64,9216]{1,0:T(8,128)(2,1)} %get-tuple-element.558), channel_id=1, source_target_pairs={{0,4},{4,0},{8,12},{12,8},{16,20},{20,16},{24,28},{28,24},{1,5},{5... | collective-permute-start | bytes 3538952 | tf_op jit(solution)/shard_map/ppermute | solution.py:29
  444.4 29.2 %collective-permute-start.77 = (bf16[2304,256]{1,0:T(8,128)(2,1)}, bf16[2304,256]{1,0:T(8,128)(2,1)}, u32[]{:S(2)}, u32[]{:S(2)}) collective-permute-start(bf16[2304,256]{1,0:T(8,128)(2,1)} %get-tuple-element.564), channel_id=1, source_target_pairs={{0,8},{4,12},{24,16},{28,20},{1,9},{5,13},{25,17},{29,21},{2,10},{... | collective-permute-start | bytes 3538952 | tf_op jit(solution)/shard_map/ppermute | solution.py:52
  473.6 29.4 %collective-permute-start.81 = (bf16[2304,256]{1,0:T(8,128)(2,1)}, bf16[2304,256]{1,0:T(8,128)(2,1)S(1)}, u32[]{:S(2)}, u32[]{:S(2)}) collective-permute-start(bf16[2304,256]{1,0:T(8,128)(2,1)} %get-tuple-element.581), channel_id=1, source_target_pairs={{0,8},{4,12},{8,0},{12,4},{16,24},{20,28},{24,16},{28,20},{1,9},{5... | collective-permute-start | bytes 3538952 | tf_op jit(solution)/shard_map/ppermute | solution.py:52
  483.6 31.8 %collective-permute-start.85 = (bf16[512,256]{1,0:T(8,128)(2,1)}, bf16[512,256]{1,0:T(8,128)(2,1)}, u32[]{:S(2)}, u32[]{:S(2)}) collective-permute-start(bf16[512,256]{1,0:T(8,128)(2,1)} %bitcast.41), channel_id=1, source_target_pairs={{0,4},{4,0},{8,12},{12,8},{16,20},{20,16},{24,28},{28,24},{1,5},{5... | collective-permute-start | bytes 786440 | tf_op jit(solution)/shard_map/ppermute | solution.py:29
  507.9 29.2 %collective-permute-start.86 = (bf16[2304,256]{1,0:T(8,128)(2,1)}, bf16[2304,256]{1,0:T(8,128)(2,1)}, u32[]{:S(2)}, u32[]{:S(2)}) collective-permute-start(bf16[2304,256]{1,0:T(8,128)(2,1)} %get-tuple-element.603), channel_id=1, source_target_pairs={{8,16},{12,20},{16,8},{20,12},{9,17},{13,21},{17,9},{21,13},{10,18... | collective-permute-start | bytes 3538952 | tf_op jit(solution)/shard_map/ppermute | solution.py:52
  513.4 29.1 %collective-permute-start.83 = (bf16[64,9216]{1,0:T(8,128)(2,1)}, bf16[64,9216]{1,0:T(8,128)(2,1)S(1)}, u32[]{:S(2)}, u32[]{:S(2)}) collective-permute-start(bf16[64,9216]{1,0:T(8,128)(2,1)} %add_convert_fusion), channel_id=1, source_target_pairs={{0,2},{1,3},{2,0},{3,1},{4,6},{5,7},{6,4},{7,5},{8,10},{9,11},{10,... | collective-permute-start | bytes 3538952 | tf_op jit(solution)/shard_map/ppermute | solution.py:29
  531.3 34.3 %collective-permute-start.89 = (bf16[2304,256]{1,0:T(8,128)(2,1)}, bf16[2304,256]{1,0:T(8,128)(2,1)}, u32[]{:S(2)}, u32[]{:S(2)}) collective-permute-start(bf16[2304,256]{1,0:T(8,128)(2,1)} %blend.15), channel_id=1, source_target_pairs={{0,8},{4,12},{8,0},{12,4},{16,24},{20,28},{24,16},{28,20},{1,9},{5... | collective-permute-start | bytes 3538952 | tf_op jit(solution)/shard_map/ppermute | solution.py:52
  535.8 31.9 %collective-permute-start.92 = (bf16[1152,256]{1,0:T(8,128)(2,1)}, bf16[1152,256]{1,0:T(8,128)(2,1)}, u32[]{:S(2)}, u32[]{:S(2)}) collective-permute-start(bf16[1152,256]{1,0:T(8,128)(2,1)} %dynamic-slice_convert_fusion.2), channel_id=1, source_target_pairs={{0,4},{4,0},{8,12},{12,8},{16,20},{20,16},{24,28},{28,24},{1,5},{5... | collective-permute-start | bytes 1769480 | tf_op jit(solution)/shard_map/ppermute | solution.py:29
  537.1 30.5 %collective-permute-start.91 = (bf16[2304,256]{1,0:T(8,128)(2,1)}, bf16[2304,256]{1,0:T(8,128)(2,1)}, u32[]{:S(2)}, u32[]{:S(2)}) collective-permute-start(bf16[2304,256]{1,0:T(8,128)(2,1)} %add_convert_fusion.1), channel_id=1, source_target_pairs={{8,16},{12,20},{16,8},{20,12},{9,17},{13,21},{17,9},{21,13},{10,18... | collective-permute-start | bytes 3538952 | tf_op jit(solution)/shard_map/ppermute | solution.py:52
  549.6 29.5 %collective-permute-start.94 = (bf16[1152,256]{1,0:T(8,128)(2,1)S(1)}, bf16[1152,256]{1,0:T(8,128)(2,1)S(1)}, u32[]{:S(2)}, u32[]{:S(2)}) collective-permute-start(bf16[1152,256]{1,0:T(8,128)(2,1)S(1)} %copy-done.78), channel_id=1, source_target_pairs={{0,4},{4,0},{8,12},{12,8},{16,20},{20,16},{24,28},{28,24},{1,5},{5... | collective-permute-start | bytes 1769480 | tf_op jit(solution)/shard_map/ppermute | solution.py:29
  (167 other events, 2809.4 us)

commit v6 on v5

--- a/solution.py
+++ b/solution.py
@@ -168,47 +168,8 @@
     )(group, keep, first, summed)
 
 
-def first_grad_kernel(pooled, keep, came, other, out):
-    ch = out.shape[2]
-
-    @pl.when(pl.program_id(0) == 0)
-    def _():
-        out[...] = jnp.zeros_like(out)
-
-    for a in range(2):
-        sums = [0.0, 0.0]
-        for p in range(POOLED):
-            lanes = slice(p * ch, (p + 1) * ch)
-            if a == 0:
-                grad = keep[:, lanes].astype(F32) + came[:, lanes].astype(F32)
-            else:
-                grad = other[:, lanes].astype(F32)
-            for s in range(2):
-                sums[s] = sums[s] + grad * pooled[s, :, lanes]
-        for s in range(2):
-            out[2 * a + s] += sums[s]
-
-
-def first_grad(pooled, keep, came, other, at):
-    images, feats = keep.shape
-    ch = feats // POOLED
-    nb = IMAGE_BLOCK
-    rows = pl.BlockSpec((nb, feats), lambda i: (i, 0))
-    sums = pl.pallas_call(
-        first_grad_kernel,
-        grid=(images // nb,),
-        in_specs=[pl.BlockSpec((2, nb, feats), lambda i: (0, at // nb + i, 0)), rows, rows, rows],
-        out_specs=pl.BlockSpec((4, nb, ch), lambda i: (0, 0, 0)),
-        out_shape=jax.ShapeDtypeStruct((4, nb, ch), F32),
-        compiler_params=params(),
-        cost_estimate=SMALL,
-        name="first_grad",
-    )(pooled, keep, came, other)
-    return jnp.sum(sums, axis=1)
-
-
-def unpool_kernel(start, group, table, first, keep_in, came_in, other_in, *refs):
-    out, own, other = refs[-3:]
+def unpool_kernel(start, group, table, first, keep_in, came_in, other_in, pooled, *refs):
+    out, sums, own, other = refs[-4:]
     count = out.shape[0]
     base = start + pl.program_id(0) * count
     ch = out.shape[3]
@@ -218,13 +179,23 @@
     def _():
         own[...] = jnp.zeros_like(own)
         other[...] = jnp.zeros_like(other)
-
-    for p in range(POOLED):
-        for h in range(ch // LANES):
+        sums[...] = jnp.zeros_like(sums)
+
+    for h in range(ch // LANES):
+        totals = [0.0] * 4
+        for p in range(POOLED):
             lanes = slice(p * ch + h * LANES, p * ch + (h + 1) * LANES)
             rows = pl.ds(p, count, stride=PITCH)
-            own[h, rows, :] = keep_in[:, lanes].astype(F32) + came_in[:, lanes].astype(F32)
-            other[h, rows, :] = other_in[:, lanes].astype(F32)
+            g0 = keep_in[:, lanes].astype(F32) + came_in[:, lanes].astype(F32)
+            g1 = other_in[:, lanes].astype(F32)
+            own[h, rows, :] = g0
+            other[h, rows, :] = g1
+            for s in range(2):
+                value = pooled[s, :, lanes]
+                totals[s] = totals[s] + g0 * value
+                totals[2 + s] = totals[2 + s] + g1 * value
+        for k in range(4):
+            sums[k, :, h * LANES : (h + 1) * LANES] += totals[k]
 
     def image(n, carry):
         window = table[group[base + n]]
@@ -245,12 +216,12 @@
     lax.fori_loop(0, count, image, 0, unroll=2)
 
 
-def unpool(keep, came, other, row, images, group, table, first, places, at, count, before=()):
+def unpool(keep, came, other, pooled, row, images, group, table, first, places, at, count, before=()):
     feats = keep.shape[1]
     ch = first.shape[1]
     nb = IMAGE_BLOCK
     rows = pl.BlockSpec((nb, feats), lambda i, g: (row // nb + i, 0))
-    return pl.pallas_call(
+    grad, sums = pl.pallas_call(
         functools.partial(unpool_kernel, at),
         grid_spec=pltpu.PrefetchScalarGridSpec(
             num_scalar_prefetch=1,
@@ -261,17 +232,22 @@
                 rows,
                 rows,
                 rows,
+                pl.BlockSpec((2, nb, feats), lambda i, g: (0, at // nb + i, 0)),
             ]
             + [pl.BlockSpec(memory_space=pl.ANY)] * len(before),
-            out_specs=pl.BlockSpec((nb, places, 2, ch), lambda i, g: (at // nb + i, 0, 0, 0)),
+            out_specs=[
+                pl.BlockSpec((nb, places, 2, ch), lambda i, g: (at // nb + i, 0, 0, 0)),
+                pl.BlockSpec((4, nb, ch), lambda i, g: (0, 0, 0)),
+            ],
             scratch_shapes=[pltpu.VMEM((ch // LANES, nb * PITCH, LANES), F32)] * 2,
         ),
-        out_shape=jax.ShapeDtypeStruct((count, places, 2, ch), BF16),
-        input_output_aliases={6: 0} if before else {},
+        out_shape=[jax.ShapeDtypeStruct((count, places, 2, ch), BF16), jax.ShapeDtypeStruct((4, nb, ch), F32)],
+        input_output_aliases={7: 0} if before else {},
         compiler_params=params(),
         cost_estimate=SMALL,
         name="unpool",
-    )(group, table, first, keep, came, other, *before)
+    )(group, table, first, keep, came, other, pooled, *before)
+    return grad, sums
 
 
 def store_kernel(chunk, chunks, x, own, came, *refs):
@@ -867,31 +843,27 @@
     def add(self, keep, came):
         return self.did((keep.astype(F32) + self.then(came).astype(F32)).astype(BF16))
 
-    def first_grad(self, i, keep, came, other, pooled):
-        return self.did(first_grad(pooled, self.then(keep), came, other, i * keep.shape[0]))
-
     def by_tower(self, partial):
         return either(self.y == 1, partial.reshape(2, 2, self.channels), 0)
 
-    def unpool(self, i, keep, came, other, before=(), part=0, parts=1):
+    def unpool(self, i, keep, came, other, pooled, before=(), part=0, parts=1):
         images = keep.shape[0] // parts
-        at = i * keep.shape[0] + part * images
-        return self.did(
-            unpool(
-                self.then(keep),
-                came,
-                other,
-                part * images,
-                images,
-                self.group,
-                self.table,
-                self.first,
-                self.places,
-                at,
-                self.count,
-                before,
-            )
+        grad, sums = unpool(
+            self.then(keep),
+            came,
+            other,
+            pooled,
+            part * images,
+            images,
+            self.group,
+            self.table,
+            self.first,
+            self.places,
+            i * keep.shape[0] + part * images,
+            self.count,
+            before,
         )
+        return (self.did(grad),), sums
 
 
 def line_program(p):
@@ -956,7 +928,6 @@
     came[0] = p.swap_weight(0)
     came[1] = p.swap_weight(1)
     cross_came = p.send(y_swap, p.cross)
-    came_pair = p.swap_weight(2, 2)
     p.load_cotangents()
     p.keep_cross(cross_came)
     p.table = did(then(p.table))
@@ -964,6 +935,7 @@
     block(0)
     near[0] = ends(blocks[0])
     inner[0] = send("middle", blocks[0])
+    came_pair = p.swap_weight(2, 2)
     p.cot_across = p.send(y_swap, p.cot_mine)
     p.pool_table = then(p.pool_table)
     summed = did(p.pool())
@@ -984,7 +956,6 @@
     c_kept_a = p.send(c_swap, kept_a)
     came[2], came[3] = came_pair[:, : p.n], came_pair[:, p.n :]
     block(2)
-    block(3)
     near[1] = arrive(near[1])
     first_out[0] = send("outward", inner[0])
     inner[1] = arrive(inner[1])
@@ -995,6 +966,7 @@
     y_b = p.send(y_swap, sent_b)
     c_kept_a = arrive(c_kept_a)
     c_kept_b = p.send(c_swap, kept_b)
+    block(3)
     first_out[0] = arrive(first_out[0])
     first_out[1] = send("outward", inner[1])
     outer[0] = arrive(outer[0])
@@ -1090,9 +1062,9 @@
     p.cots[2] = p.cots[3] = (cot_came, cot_crossed)
     core_came(2, 0)
     core_came(3, 0)
-    act_came = p.send(y_swap, p.acts[1])
     core_swap(0, 2)
     core_swap(1, 2)
+    core_swap(2, 1)
     total[2] = p.chunk(2, feats, pieces(2))
     outer[3] = arrive(outer[3])
     [value] = blended((part(1, 3), inner[3]))
@@ -1100,58 +1072,55 @@
     into[1, 3] = first_out[3] = ends(value)
     rest = did(plus(0, 2, into[0, 2]))
     crossed[0] = send("middle", far0)
-    act_came = arrive(act_came)
     core_came(0, 2)
     core_came(1, 2)
-    act_came2 = p.send(y_swap, p.acts[2])
+    core_came(2, 1)
+    acts_came = p.send(y_swap, jnp.concatenate([then(p.acts[1]), p.acts[2]], axis=1))
     core_swap(0, 3)
     core_swap(1, 3)
     value, picked[3, 1], picked[2, 3] = blended(
         (part(1, 2), outer[3]), (from_own[3], swapped[3]), (last_out[2], outer[2])
     )
-    act_mixes.append(p.stitch(1, act_came))
     into[1, 3] = first_out[3] = arrive(into[1, 3])
     into[1, 2] = last_out[3] = ends(value)
     far1 = did(far_end(1))
     crossed[0] = arrive(crossed[0])
     middle[0] = send("middle", rest)
-    act_came = arrive(act_came2)
+    acts_came = arrive(acts_came)
     core_came(0, 3)
     core_came(1, 3)
-    core_swap(2, 1)
     core_swap(2, 2)
     core_swap(3, 1)
+    core_swap(2, 3)
     value, picked[3, 2] = blended((part(1, 1), part(0, 1), crossed[0]), (first_out[3], inner[3]))
     far = did(jnp.concatenate([then(p.far_grads[0]), p.far_grads[1], p.far_grads[2]]))
-    act_mixes.append(p.stitch(2, act_came))
+    for j in (1, 2):
+        act_mixes.append(p.stitch(j, acts_came[:, (j - 1) * p.n : j * p.n]))
     act_mixes = did(jnp.concatenate([then(act_mixes[0]), *act_mixes[1:]]))
     into[1, 2] = last_out[3] = arrive(into[1, 2])
     into[1, 1] = final[0] = ends(value)
     sums = did(p.unit_sums(then(p.sums[0]), p.sums[1], p.sums[2]))
-    core_came(2, 1)
     core_came(2, 2)
     core_came(3, 1)
-    core_swap(2, 3)
+    core_came(2, 3)
     core_swap(3, 2)
+    came_outer = p.send(c_swap, outer[3])
     mixes_came = p.send(x_swap, act_mixes)
     total[3] = p.chunk(3, feats, pieces(3))
     middle[0] = arrive(middle[0])
     into[1, 1] = final[0] = arrive(into[1, 1])
     into[2, 3] = inward(2, 3)
-    core_came(2, 3)
     core_came(3, 2)
+    came_outer = arrive(came_outer)
     mixes_came = arrive(mixes_came)
     far = p.send(c_swap, far)
     came_last = p.send(c_swap, last_out[3])
-    came_outer = p.send(c_swap, outer[3])
+    far3 = p.send(c_swap, p.far_grads[3])
+    crossed[1] = send("middle", far1)
     rows = {0: did(then(part(0, 0)) + edge(0))}
     far = arrive(far)
-    far3 = p.send(c_swap, p.far_grads[3])
-    crossed[1] = send("middle", far1)
-    rest = did(plus(1, 2, into[1, 2]))
+    slab_came[0] = p.send(x_swap, p.leaving(rows[0]))
     came_last = arrive(came_last)
-    slab_came[0] = p.send(x_swap, p.leaving(rows[0]))
-    came_outer = arrive(came_outer)
     far3 = arrive(far3)
     act_came = p.send(y_swap, p.acts[3])
     third = far.shape[0] // 3
@@ -1165,23 +1134,26 @@
     came_far, came_x, own_y = {}, {}, {}
     into[2, 3] = arrive(into[2, 3])
     into[2, 2] = inward(2, 2)
+    [rest] = blended((part(1, 2), part(1, 2), into[1, 2]))
     crossed[1] = arrive(crossed[1])
     slab_came[0] = arrive(slab_came[0])
     act_came = arrive(act_came)
     middle[1] = send("middle", rest)
     came_far[0] = p.send(x_swap, leave_far[0])
     keep, leave = p.back(0, came_grads, own_pieces, far_pieces)
-    [far2] = blended((part(2, 3), part(2, 3), into[2, 3]))
     into[2, 2] = arrive(into[2, 2])
     into[3, 3] = inward(3, 3)
-    sums = did(jnp.concatenate([then(sums), p.unit_sums(p.sums[3])], axis=1))
+    [far2] = blended((part(2, 3), part(2, 3), into[2, 3]))
     middle[1] = arrive(middle[1])
     crossed[2] = send("middle", far2)
     came_far[0] = arrive(came_far[0])
     came_x[0] = p.send(x_swap, leave[0])
     own_y[0] = p.send(y_swap, p.add(keep_far[0], came_far[0]))
     value, own2 = blended((part(3, 2), part(1, 1), crossed[1]), (part(2, 2), part(2, 2), into[2, 2]))
+    sums = jnp.concatenate([sums, p.unit_sums(p.sums[3])], axis=1)
     act_mix = p.stitch(3, act_came)
+    for j in range(3):
+        p.crossed[j] = did(then(mixes_came)[j * p.n * 2 : (j + 1) * p.n * 2])
     p.store(0, rows[0], slab_came[0])
     into[3, 3] = arrive(into[3, 3])
     into[3, 2] = final[1] = ends(value)
@@ -1191,10 +1163,8 @@
     crossed[2] = arrive(crossed[2])
     crossed[3] = send("middle", rest)
     own_y[0] = arrive(own_y[0])
-    p.crossed[3] = p.send(x_swap, act_mix)
     [value] = blended((part(2, 1), part(2, 1), crossed[2]))
-    partial = p.first_grad(0, keep[0], came_x[0], own_y[0], pooled)
-    grad = (p.unpool(0, keep[0], came_x[0], own_y[0], (), 0, 2),)
+    grad, partial_a = p.unpool(0, keep[0], came_x[0], own_y[0], pooled, (), 0, 2)
     into[3, 2] = final[1] = arrive(into[3, 2])
     into[2, 1] = final[2] = ends(value)
     last = did(plus(3, 2, into[3, 2]))
@@ -1203,30 +1173,31 @@
     crossed[3] = arrive(crossed[3])
     middle[2] = send("middle", own2)
     own_y[1] = p.send(y_swap, p.add(keep_far[1], came_far[1]))
-    p.crossed[3] = arrive(p.crossed[3])
+    p.crossed[3] = p.send(x_swap, act_mix)
     [value] = blended((part(3, 1), part(3, 1), crossed[3]))
-    grad = (p.unpool(0, keep[0], came_x[0], own_y[0], grad, 1, 2),)
-    rows[1] = did(then(part(1, 0)) + edge(1))
+    grad, partial_b = p.unpool(0, keep[0], came_x[0], own_y[0], pooled, grad, 1, 2)
     into[2, 1] = final[2] = arrive(into[2, 1])
     into[3, 1] = final[3] = ends(value)
     came_x[1] = arrive(came_x[1])
-    slab_came[1] = p.send(x_swap, p.leaving(rows[1]))
     middle[2] = arrive(middle[2])
     middle[3] = send("middle", last)
+    rows[1] = did(then(part(1, 0)) + edge(1))
+    slab_came[1] = p.send(x_swap, p.leaving(rows[1]))
+    own_y[1] = arrive(own_y[1])
+    p.crossed[3] = arrive(p.crossed[3])
     rows[2] = did(part(2, 0) + edge(2))
     slab_came[2] = p.send(x_swap, p.leaving(rows[2]))
-    own_y[1] = arrive(own_y[1])
-    partial = partial + p.first_grad(1, keep[1], came_x[1], own_y[1], pooled)
+    [grad], partial = p.unpool(1, keep[1], came_x[1], own_y[1], pooled, grad)
+    into[3, 1] = final[3] = arrive(into[3, 1])
+    middle[3] = arrive(middle[3])
+    partial = jnp.sum(then(partial_a) + partial_b + partial, axis=1)
     partial = did(p.by_tower(partial).reshape(1, -1))
     partial_came = p.send(c_swap, partial)
-    grad = p.unpool(1, keep[1], came_x[1], own_y[1], grad)
-    into[3, 1] = final[3] = arrive(into[3, 1])
+    slab_came[1] = arrive(slab_came[1])
+    rows[3] = did(part(3, 0) + edge(3))
+    slab_came[3] = p.send(x_swap, p.leaving(rows[3]))
     partial = did(partial + then(partial_came))
     second_came = p.send(y_swap, jnp.concatenate([sums[2:], partial]))
-    slab_came[1] = arrive(slab_came[1])
-    middle[3] = arrive(middle[3])
-    rows[3] = did(part(3, 0) + edge(3))
-    slab_came[3] = p.send(x_swap, p.leaving(rows[3]))
     p.store(1, rows[1], slab_came[1])
     second_came = arrive(second_came)
     sums = did(jnp.concatenate([sums[:2], second_came[:1], partial + second_came[1:]]))
@@ -1235,13 +1206,11 @@
     p.store(2, rows[2], slab_came[2])
     sums = did(sums + then(sums_came))
     sums_came = p.send(flipped, sums, "batch", 4)
+    activations = did(p.activations())
+    sums = did(sums + then(sums_came))
+    sums_came = p.send(x_swap, sums)
     slab_came[3] = arrive(slab_came[3])
     p.store(3, rows[3], slab_came[3])
-    sums = did(sums + then(sums_came))
-    sums_came = p.send(x_swap, sums)
-    for j in range(3):
-        p.crossed[j] = jnp.split(mixes_came, 3)[j]
-    activations = did(p.activations())
     sums_came = then(sums_came)
     bias_grad, alpha2_grad = p.small_grads(jnp.concatenate([sums[:3], sums_came[:3]]))
     alpha1_grad = (sums[3] + sums_came[3]).reshape(2, 2, p.channels)
@@ -1285,8 +1254,8 @@
     for i in range(2):
         other = y_swap(p.add(keep_far[i], x_swap(leave_far[i])))
         came = x_swap(leave[i])
-        partial = partial + p.first_grad(i, keep[i], came, other, pooled)
-        grad = (p.unpool(i, keep[i], came, other, grad),)
+        grad, sums = p.unpool(i, keep[i], came, other, pooled, grad)
+        partial = partial + jnp.sum(sums, axis=1)
     alpha1_grad = lax.psum(p.by_tower(partial), ("batch", "tower"))
     input_grad = jnp.swapaxes(grad[0], 1, 2)
     return (p.activations(), input_grad, p.weight_grad[0], bias_grad, alpha1_grad, alpha2_grad)

time: 611 us -> 600 us (0.982)
    ppermute x63 -> x62, waiting for transfers between devices: 75 us -> 63.9 us  [flipped(): return lax.ppermute(value, axis, pairs)]
    pallas_call x2 -> x0, Pallas kernels: 9.99 us -> none  [first_grad(): pl.pallas_call(first_grad_kernel, grid=(images // nb,), in_specs=[pl.Bloc...]
    ppermute x35, waiting for transfers between devices: 74.3 us -> 83.9 us  [line(): return lax.ppermute(value, 'batch', pairs)]
    slice x0 -> x5, local copies, waits for them, and re-layouts: none -> 7.7 us  [the longest x3 5.01 us: line_program(): p.crossed[j] = did(then(mixes_came)[j * p.n * 2:(j + 1) * p.n * 2])]
    ppermute x63 -> x62, starting transfers between devices: 51.1 us -> 47.9 us  [flipped(): return lax.ppermute(value, axis, pairs)]
    pallas_call x8 -> x9, Pallas kernels: 29.6 us -> 32.2 us  [blend(): pl.pallas_call(functools.partial(blend_kernel, counts), in_specs=[pl.Bloc...]
  transfers between devices with their start and end apart: 98 -> 97, of which waited for: 19 -> 24; matrix products, arithmetic and copies ran while one was open for 16% -> 17% of each run, Pallas kernels for 38% -> 38%
where the time goes in v6:
time: 600 us; the launch traced here: 589 us
  Pallas kernels  221 us (37%)
  waiting for transfers between devices  148 us (25%)
  starting transfers between devices  109 us (18%)
  local copies, waits for them, and re-layouts  47.8 us (8%)
  other arithmetic  46.4 us (8%)
  matrix products  13.9 us (2%)
    pallas_call x4, Pallas kernels, chunk(): pl.pallas_call(functools.partial(chunk_kernel, [[len(p) for p in chunk] f...  85.3 us
    ppermute x35, waiting for transfers between devices, line(): return lax.ppermute(value, 'batch', pairs)  83.9 us
    ppermute x62, waiting for transfers between devices, flipped(): return lax.ppermute(value, axis, pairs)  63.9 us
    ppermute x35, starting transfers between devices, line(): return lax.ppermute(value, 'batch', pairs)  61.2 us
    ppermute x62, starting transfers between devices, flipped(): return lax.ppermute(value, axis, pairs)  47.9 us
    pallas_call x3, Pallas kernels, unpool(): pl.pallas_call(functools.partial(unpool_kernel, at), grid_spec=pltpu.Pref...  36 us
    pallas_call x2, Pallas kernels, back(): pl.pallas_call(functools.partial(back_kernel, layout, [row for _, row in...  35 us
    pallas_call x9, Pallas kernels, blend(): pl.pallas_call(functools.partial(blend_kernel, counts), in_specs=[pl.Bloc...  32.2 us
  transfers between devices with their start and end apart: 97, of which 24 were waited for; matrix products, arithmetic and copies ran while one was open for 17% of the time, Pallas kernels for 38%

profile of v6, /device:TPU:0, one launch (start us, length us, event | category | flops | bytes accessed | tf_op | source)
XLA Modules:
  0.0 588.9 jit_solution(16250108520201793379)
XLA Ops:
  32.0 13.9 %fusion.2.summed = f32[128,2,36,256]{3,2,1,0:T(8,128)} fusion(bf16[128,2,169,256]{3,1,2,0:T(2,128)(2,1)} %param.8, bf16[36,169]{1,0:T(8,128)(2,1)S(1)} %and_convert_fusion), kind=kOutput, calls=%fused_computation.3 | convolution fusion | flops 797442048 | bytes 31600520 | tf_op jit(solution)/shard_map/pq,nsqc->nspc/dot_general | solution.py:756
  56.6 14.2 %mix.1 = (bf16[128,4608]{1,0:T(8,128)(2,1)}, bf16[128,4608]{1,0:T(8,128)(2,1)}, bf16[128,4608]{1,0:T(8,128)(2,1)}, bf16[128,4608]{1,0:T(8,128)(2,1)}, f32[2,128,9216]{2,1,0:T(8,128)}) custom-call(s32[128]{0:T(128)} %group.7, f32[2,36,256]{2,1,0:T(8,128)} %broadcast_in_dim.8.keep, f32[4,256]{1,0:T(4,128)} %reshape.654.first, f32[128,2,36,256]{3,2,1,0:T(8,128)} %fusion.2.summed), custom_call_target="tpu_custom_call" | custom-call | flops 1000 | bytes 1000 | tf_op jit(solution)/shard_map/mix/pallas_call | solution.py:149
  79.7 17.4 %collective-permute-done.10.refs_8_ = bf16[128,4608]{1,0:T(8,128)(2,1)} collective-permute-done((bf16[128,4608]{1,0:T(8,128)(2,1)}, bf16[128,4608]{1,0:T(8,128)(2,1)}, u32[]{:S(2)}, u32[]{:S(2)}) %collective-permute-start.10) | collective-permute-done | bytes 1179680 | tf_op jit(solution)/shard_map/ppermute | solution.py:29
  101.7 5.7 collective-permute-done.15.refs_22_.refs_0_
  110.4 12.6 %collective-permute-done.13.refs_9_ = bf16[128,4608]{1,0:T(8,128)(2,1)} collective-permute-done((bf16[128,4608]{1,0:T(8,128)(2,1)S(1)}, bf16[128,4608]{1,0:T(8,128)(2,1)}, u32[]{:S(2)}, u32[]{:S(2)}) %collective-permute-start.13) | collective-permute-done | bytes 1179680 | tf_op jit(solution)/shard_map/ppermute | solution.py:29
  125.4 11.8 %collective-permute-done.22.refs_22_.refs_2_ = bf16[2304,256]{1,0:T(8,128)(2,1)} collective-permute-done((bf16[2304,256]{1,0:T(8,128)(2,1)}, bf16[2304,256]{1,0:T(8,128)(2,1)}, u32[]{:S(2)}, u32[]{:S(2)}) %collective-permute-start.22) | collective-permute-done | bytes 1179680 | tf_op jit(solution)/shard_map/ppermute | solution.py:52
  138.0 11.1 %collective-permute-done.20.refs_10_ = bf16[128,4608]{1,0:T(8,128)(2,1)} collective-permute-done((bf16[128,4608]{1,0:T(8,128)(2,1)}, bf16[128,4608]{1,0:T(8,128)(2,1)}, u32[]{:S(2)}, u32[]{:S(2)}) %collective-permute-start.20) | collective-permute-done | bytes 1179680 | tf_op jit(solution)/shard_map/ppermute | solution.py:29
  152.6 11.6 %collective-permute-done.23.refs_24_.refs_4_.refs_9_.refs_22_ = bf16[2304,256]{1,0:T(8,128)(2,1)} collective-permute-done((bf16[2304,256]{1,0:T(8,128)(2,1)S(1)}, bf16[2304,256]{1,0:T(8,128)(2,1)}, u32[]{:S(2)}, u32[]{:S(2)}) %collective-permute-start.23) | collective-permute-done | bytes 1179680 | tf_op jit(solution)/shard_map/ppermute | solution.py:52
  164.4 6.9 %collective-permute-done.25.refs_11_ = bf16[128,4608]{1,0:T(8,128)(2,1)} collective-permute-done((bf16[128,4608]{1,0:T(8,128)(2,1)}, bf16[128,4608]{1,0:T(8,128)(2,1)}, u32[]{:S(2)}, u32[]{:S(2)}) %collective-permute-start.25) | collective-permute-done | bytes 1179680 | tf_op jit(solution)/shard_map/ppermute | solution.py:29
  174.4 15.9 %collective-permute-done.24.refs_24_.refs_6_.refs_3_.refs_22_ = bf16[2304,256]{1,0:T(8,128)(2,1)} collective-permute-done((bf16[2304,256]{1,0:T(8,128)(2,1)}, bf16[2304,256]{1,0:T(8,128)(2,1)}, u32[]{:S(2)}, u32[]{:S(2)}) %collective-permute-start.24) | collective-permute-done | bytes 1179680 | tf_op jit(solution)/shard_map/ppermute | solution.py:52
  193.3 21.2 %chunk.4 = (bf16[1024,256]{1,0:T(8,128)(2,1)}, bf16[512,256]{1,0:T(8,128)(2,1)}, bf16[512,256]{1,0:T(8,128)(2,1)}, f32[8,256]{1,0:T(8,128)}, f32[2304,256]{1,0:T...) custom-call(s32[2]{0:T(128)} %pad_add_fusion.2.roles, ...), custom_call_target="tpu_custom_call" | custom-call | flops 1000 | bytes 1000 | tf_op jit(solution)/shard_map/chunk/pallas_call | solution.py:565
  222.6 21.1 %chunk.5 = (bf16[1024,256]{1,0:T(8,128)(2,1)}, bf16[512,256]{1,0:T(8,128)(2,1)}, bf16[512,256]{1,0:T(8,128)(2,1)}, f32[8,256]{1,0:T(8,128)}, f32[2304,256]{1,0:T...) custom-call(s32[2]{0:T(128)} %pad_add_fusion.2.roles, ...), custom_call_target="tpu_custom_call" | custom-call | flops 1000 | bytes 1000 | tf_op jit(solution)/shard_map/chunk/pallas_call | solution.py:565
  253.0 7.5 %blend.9 = (bf16[2304,256]{1,0:T(8,128)(2,1)}, bf16[2304,256]{1,0:T(8,128)(2,1)}, bf16[2304,256]{1,0:T(8,128)(2,1)}, bf16[2304,256]{1,0:T(8,128)(2,1)}, bf16[230...) custom-call(s32[2]{0:T(128)} %pad_add_fusion.2.roles, ...), custom_call_target="tpu_custom_call" | custom-call | flops 1000 | bytes 1000 | tf_op jit(solution)/shard_map/blend/pallas_call | solution.py:378
  264.7 9.8 %collective-permute-done.44.refs_25_.refs_4_ = bf16[2304,256]{1,0:T(8,128)(2,1)} collective-permute-done((bf16[2304,256]{1,0:T(8,128)(2,1)}, bf16[2304,256]{1,0:T(8,128)(2,1)}, u32[]{:S(2)}, u32[]{:S(2)}) %collective-permute-start.44) | collective-permute-done | bytes 1179680 | tf_op jit(solution)/shard_map/ppermute | solution.py:52
  276.4 21.1 %chunk.6 = (bf16[1024,256]{1,0:T(8,128)(2,1)}, bf16[512,256]{1,0:T(8,128)(2,1)}, bf16[512,256]{1,0:T(8,128)(2,1)}, f32[8,256]{1,0:T(8,128)}, f32[2304,256]{1,0:T...) custom-call(s32[2]{0:T(128)} %pad_add_fusion.2.roles, ...), custom_call_target="tpu_custom_call" | custom-call | flops 1000 | bytes 1000 | tf_op jit(solution)/shard_map/chunk/pallas_call | solution.py:565
  310.9 3.9 blend.11
  314.8 14.2 %collective-permute-done.55.refs_3_.refs_23_ = bf16[2304,256]{1,0:T(8,128)(2,1)S(1)} collective-permute-done((bf16[2304,256]{1,0:T(8,128)(2,1)}, bf16[2304,256]{1,0:T(8,128)(2,1)S(1)}, u32[]{:S(2)}, u32[]{:S(2)}) %collective-permute-start.55) | collective-permute-done | bytes 1179680 | tf_op jit(solution)/shard_map/ppermute | solution.py:52
  349.9 5.6 collective-permute-done.56.refs_25_.refs_23_.refs_2_
  358.0 21.9 %chunk.7 = (bf16[1024,256]{1,0:T(8,128)(2,1)}, bf16[512,256]{1,0:T(8,128)(2,1)}, bf16[512,256]{1,0:T(8,128)(2,1)}, f32[8,256]{1,0:T(8,128)}, f32[2304,256]{1,0:T...) custom-call(s32[2]{0:T(128)} %pad_add_fusion.2.roles, ...), custom_call_target="tpu_custom_call" | custom-call | flops 1000 | bytes 1000 | tf_op jit(solution)/shard_map/chunk/pallas_call | solution.py:565
  382.5 4.6 collective-permute-start.68
  393.8 17.5 %back.2 = (bf16[64,9216]{1,0:T(8,128)(2,1)}, bf16[64,9216]{1,0:T(8,128)(2,1)}, bf16[64,9216]{1,0:T(8,128)(2,1)}, bf16[64,9216]{1,0:T(8,128)(2,1)}) custom-call(s32[2]{0:T(128)} %pad_add_fusion.2.roles, bf16[512,256]{1,0:T(8,128)(2,1)} %get-tuple-element.562.refs_0_, bf16[512,256]{1,0:T(8,128)(2,1)} %get-tuple-element.547.refs_1_, ...), custom_call_target="tpu_custom_call" | custom-call | flops 1000 | bytes 1000 | tf_op jit(solution)/shard_map/back/pallas_call | solution.py:675
  412.0 4.6 collective-permute-start.73
  421.8 17.4 %back.3 = (bf16[64,9216]{1,0:T(8,128)(2,1)}, bf16[64,9216]{1,0:T(8,128)(2,1)}, bf16[64,9216]{1,0:T(8,128)(2,1)}, bf16[64,9216]{1,0:T(8,128)(2,1)}) custom-call(s32[2]{0:T(128)} %pad_add_fusion.2.roles, bf16[512,256]{1,0:T(8,128)(2,1)} %get-tuple-element.562.refs_0_, bf16[512,256]{1,0:T(8,128)(2,1)} %get-tuple-element.547.refs_1_, ...), custom_call_target="tpu_custom_call" | custom-call | flops 1000 | bytes 1000 | tf_op jit(solution)/shard_map/back/pallas_call | solution.py:675
  441.5 5.7 collective-permute-start.76
  466.7 3.9 store.4.refs_0_
  484.1 10.0 %unpool.3 = (bf16[128,169,2,256]{3,2,1,0:T(2,128)(2,1)}, f32[4,16,256]{2,1,0:T(8,128)}) custom-call(s32[128]{0:T(128)} %group.7, bf16[2,352,192]{2,1,0:T(8,128)(2,1)} %fusion.15.table, f32[4,256]{1,0:T(4,128)} %reshape.654.first, bf16[64,9216]{1,0:T(8,128)(2,1)} %get-tuple-element.612.keep_in, bf16[64,9216]{1,0:T(8,128)(2,1)} %copy-done.35, ...), custom_call_target="tpu_custom_call" | custom-call | flops 1000 | bytes 1000 | tf_op jit(solution)/shard_map/unpool/pallas_call | solution.py:224
  513.0 10.0 %unpool.4 = (bf16[128,169,2,256]{3,2,1,0:T(2,128)(2,1)}, f32[4,16,256]{2,1,0:T(8,128)}) custom-call(s32[128]{0:T(128)} %group.7, bf16[2,352,192]{2,1,0:T(8,128)(2,1)} %fusion.15.table, f32[4,256]{1,0:T(4,128)} %reshape.654.first, bf16[64,9216]{1,0:T(8,128)(2,1)} %get-tuple-element.612.keep_in, ...), custom_call_target="tpu_custom_call", output_to_operand_aliasing={{0}: (7, {})} | custom-call | flops 1000 | bytes 1000 | tf_op jit(solution)/shard_map/unpool/pallas_call | solution.py:224
  526.2 5.1 collective-permute-done.83.came_in
  541.3 16.0 %unpool.5 = (bf16[128,169,2,256]{3,2,1,0:T(2,128)(2,1)}, f32[4,16,256]{2,1,0:T(8,128)}) custom-call(s32[128]{0:T(128)} %group.7, bf16[2,352,192]{2,1,0:T(8,128)(2,1)} %fusion.15.table, f32[4,256]{1,0:T(4,128)} %reshape.654.first, bf16[64,9216]{1,0:T(8,128)(2,1)} %get-tuple-element.629.keep_in, ...), custom_call_target="tpu_custom_call", output_to_operand_aliasing={{0}: (7, {})} | custom-call | flops 1000 | bytes 1000 | tf_op jit(solution)/shard_map/unpool/pallas_call | solution.py:224
  564.1 3.8 store.5.refs_0_
  571.8 3.8 store.6.refs_0_
  582.4 3.8 store.7
  (484 shorter events, 232.5 us)
Async XLA Ops:
  7.4 38.4 %collective-permute-start.2 = (bf16[1152,256]{1,0:T(8,128)(2,1)}, bf16[1152,256]{1,0:T(8,128)(2,1)}, u32[]{:S(2)}, u32[]{:S(2)}) collective-permute-start(bf16[1152,256]{1,0:T(8,128)(2,1)} %constant_dynamic-slice_fusion.9), channel_id=1, source_target_pairs={{0,4},{4,0},{8,12},{12,8},{16,20},{20,16},{24,28},{28,24},{1,5},{5... | collective-permute-start | bytes 1769480 | tf_op jit(solution)/shard_map/ppermute | solution.py:29
  24.9 29.3 %collective-permute-start.3 = (bf16[2304,256]{1,0:T(8,128)(2,1)S(1)}, bf16[2304,256]{1,0:T(8,128)(2,1)}, u32[]{:S(2)}, u32[]{:S(2)}) collective-permute-start(bf16[2304,256]{1,0:T(8,128)(2,1)S(1)} %maximum_select_fusion.refs_20_.refs_8_), channel_id=1, source_target_pairs={{8,16},{12,20},{16,8},{20,12},{9,17},{13,21},{17,9},{21,13},{10,18... | collective-permute-start | bytes 3538952 | tf_op jit(solution)/shard_map/ppermute | solution.py:52
  29.0 41.9 %collective-permute-start.7 = (bf16[1152,512]{1,0:T(8,128)(2,1)}, bf16[1152,512]{1,0:T(8,128)(2,1)}, u32[]{:S(2)}, u32[]{:S(2)}) collective-permute-start(bf16[1152,512]{1,0:T(8,128)(2,1)} %constant_dynamic-slice_fusion.5), channel_id=1, source_target_pairs={{0,4},{4,0},{8,12},{12,8},{16,20},{20,16},{24,28},{28,24},{1,5},{5... | collective-permute-start | bytes 3538952 | tf_op jit(solution)/shard_map/ppermute | solution.py:29
  30.5 40.4 %collective-permute-start.6 = (bf16[512,1024]{1,0:T(8,128)(2,1)S(1)}, bf16[512,1024]{1,0:T(8,128)(2,1)S(1)}, u32[]{:S(2)}, u32[]{:S(2)}) collective-permute-start(bf16[512,1024]{1,0:T(8,128)(2,1)S(1)} %constant_dynamic-slice_fusion.8.refs_0_), channel_id=1, source_target_pairs={{0,2},{1,3},{2,0},{3,1},{4,6},{5,7},{6,4},{7,5},{8,10},{9,11},{10,... | collective-permute-start | bytes 3145736 | tf_op jit(solution)/shard_map/ppermute | solution.py:29
  76.5 30.9 %collective-permute-start.15 = (bf16[2304,256]{1,0:T(8,128)(2,1)}, bf16[2304,256]{1,0:T(8,128)(2,1)}, u32[]{:S(2)}, u32[]{:S(2)}) collective-permute-start(bf16[2304,256]{1,0:T(8,128)(2,1)} %collective-permute-done.3.refs_23_.refs_1_), channel_id=1, source_target_pairs={{8,0},{12,4},{16,24},{20,28},{9,1},{13,5},{17,25},{21,29},{10,2},{... | collective-permute-start | bytes 3538952 | tf_op jit(solution)/shard_map/ppermute | solution.py:52
  78.0 30.7 %collective-permute-start.14 = (bf16[2304,256]{1,0:T(8,128)(2,1)}, bf16[2304,256]{1,0:T(8,128)(2,1)}, u32[]{:S(2)}, u32[]{:S(2)}) collective-permute-start(bf16[2304,256]{1,0:T(8,128)(2,1)} %collective-permute-done.4.refs_21_.refs_9_), channel_id=1, source_target_pairs={{8,16},{12,20},{16,8},{20,12},{9,17},{13,21},{17,9},{21,13},{10,18... | collective-permute-start | bytes 3538952 | tf_op jit(solution)/shard_map/ppermute | solution.py:52
  107.4 29.9 %collective-permute-start.22 = (bf16[2304,256]{1,0:T(8,128)(2,1)}, bf16[2304,256]{1,0:T(8,128)(2,1)}, u32[]{:S(2)}, u32[]{:S(2)}) collective-permute-start(bf16[2304,256]{1,0:T(8,128)(2,1)} %collective-permute-done.11.refs_23_.refs_3_), channel_id=1, source_target_pairs={{8,0},{12,4},{16,24},{20,28},{9,1},{13,5},{17,25},{21,29},{10,2},{... | collective-permute-start | bytes 3538952 | tf_op jit(solution)/shard_map/ppermute | solution.py:52
  108.7 28.6 %collective-permute-start.21 = (bf16[2304,256]{1,0:T(8,128)(2,1)}, bf16[2304,256]{1,0:T(8,128)(2,1)}, u32[]{:S(2)}, u32[]{:S(2)}) collective-permute-start(bf16[2304,256]{1,0:T(8,128)(2,1)} %collective-permute-done.12.refs_21_.refs_13_), channel_id=1, source_target_pairs={{8,16},{12,20},{16,8},{20,12},{9,17},{13,21},{17,9},{21,13},{10,18... | collective-permute-start | bytes 3538952 | tf_op jit(solution)/shard_map/ppermute | solution.py:52
  172.0 42.4 %collective-permute-start.35 = (bf16[2304,256]{1,0:T(8,128)(2,1)}, bf16[2304,256]{1,0:T(8,128)(2,1)}, u32[]{:S(2)}, u32[]{:S(2)}) collective-permute-start(bf16[2304,256]{1,0:T(8,128)(2,1)} %collective-permute-done.23.refs_24_.refs_4_.refs_9_.refs_22_), channel_id=1, source_target_pairs={{8,16},{12,20},{16,8},{20,12},{9,17},{13,21},{17,9},{21,13},{10,18... | collective-permute-start | bytes 3538952 | tf_op jit(solution)/shard_map/ppermute | solution.py:52
  217.3 29.0 %collective-permute-start.39 = (bf16[2304,256]{1,0:T(8,128)(2,1)}, bf16[2304,256]{1,0:T(8,128)(2,1)S(1)}, u32[]{:S(2)}, u32[]{:S(2)}) collective-permute-start(bf16[2304,256]{1,0:T(8,128)(2,1)} %broadcast_select_fusion.1), channel_id=1, source_target_pairs={{0,8},{4,12},{8,0},{12,4},{16,24},{20,28},{24,16},{28,20},{1,9},{5... | collective-permute-start | bytes 3538952 | tf_op jit(solution)/shard_map/ppermute | solution.py:52
  219.3 29.5 %collective-permute-start.38 = (bf16[2304,256]{1,0:T(8,128)(2,1)S(1)}, bf16[2304,256]{1,0:T(8,128)(2,1)S(1)}, u32[]{:S(2)}, u32[]{:S(2)}) collective-permute-start(bf16[2304,256]{1,0:T(8,128)(2,1)S(1)} %maximum_select_fusion.3.refs_13_.refs_20_), channel_id=1, source_target_pairs={{8,16},{12,20},{16,8},{20,12},{9,17},{13,21},{17,9},{21,13},{10,18... | collective-permute-start | bytes 3538952 | tf_op jit(solution)/shard_map/ppermute | solution.py:52
  220.1 30.5 %collective-permute-start.37 = (bf16[1024,256]{1,0:T(8,128)(2,1)}, bf16[1024,256]{1,0:T(8,128)(2,1)}, u32[]{:S(2)}, u32[]{:S(2)}) collective-permute-start(bf16[1024,256]{1,0:T(8,128)(2,1)} %get-tuple-element.431), channel_id=1, source_target_pairs={{0,2},{1,3},{2,0},{3,1},{4,6},{5,7},{6,4},{7,5},{8,10},{9,11},{10,... | collective-permute-start | bytes 1572872 | tf_op jit(solution)/shard_map/ppermute | solution.py:29
  222.1 28.5 %collective-permute-start.41 = (bf16[2304,256]{1,0:T(8,128)(2,1)}, bf16[2304,256]{1,0:T(8,128)(2,1)S(1)}, u32[]{:S(2)}, u32[]{:S(2)}) collective-permute-start(bf16[2304,256]{1,0:T(8,128)(2,1)} %maximum_select_fusion.1.refs_20_.refs_12_), channel_id=1, source_target_pairs={{0,1},{1,0},{2,3},{3,2},{4,5},{5,4},{6,7},{7,6},{8,9},{9,8},{10,11... | collective-permute-start | bytes 3538952 | tf_op jit(solution)/shard_map/ppermute | solution.py:29
  222.1 28.5 %collective-permute-start.40 = (bf16[2304,256]{1,0:T(8,128)(2,1)}, bf16[2304,256]{1,0:T(8,128)(2,1)}, u32[]{:S(2)}, u32[]{:S(2)}) collective-permute-start(bf16[2304,256]{1,0:T(8,128)(2,1)} %collective-permute-done.12.refs_21_.refs_13_), channel_id=1, source_target_pairs={{0,1},{1,0},{2,3},{3,2},{4,5},{5,4},{6,7},{7,6},{8,9},{9,8},{10,11... | collective-permute-start | bytes 3538952 | tf_op jit(solution)/shard_map/ppermute | solution.py:29
  246.3 28.2 %collective-permute-start.44 = (bf16[2304,256]{1,0:T(8,128)(2,1)}, bf16[2304,256]{1,0:T(8,128)(2,1)}, u32[]{:S(2)}, u32[]{:S(2)}) collective-permute-start(bf16[2304,256]{1,0:T(8,128)(2,1)} %broadcast_select_fusion), channel_id=1, source_target_pairs={{0,8},{4,12},{8,0},{12,4},{16,24},{20,28},{24,16},{28,20},{1,9},{5... | collective-permute-start | bytes 3538952 | tf_op jit(solution)/shard_map/ppermute | solution.py:52
  252.2 45.3 %collective-permute-start.49 = (bf16[2304,256]{1,0:T(8,128)(2,1)}, bf16[2304,256]{1,0:T(8,128)(2,1)S(1)}, u32[]{:S(2)}, u32[]{:S(2)}) collective-permute-start(bf16[2304,256]{1,0:T(8,128)(2,1)} %collective-permute-done.24.refs_24_.refs_6_.refs_3_.refs_22_), channel_id=1, source_target_pairs={{8,16},{12,20},{16,8},{20,12},{9,17},{13,21},{17,9},{21,13},{10,18... | collective-permute-start | bytes 3538952 | tf_op jit(solution)/shard_map/ppermute | solution.py:52
  275.7 32.0 %collective-permute-start.48 = (bf16[2304,256]{1,0:T(8,128)(2,1)S(1)}, bf16[2304,256]{1,0:T(8,128)(2,1)S(1)}, u32[]{:S(2)}, u32[]{:S(2)}) collective-permute-start(bf16[2304,256]{1,0:T(8,128)(2,1)S(1)} %copy-done.27), channel_id=1, source_target_pairs={{0,1},{1,0},{2,3},{3,2},{4,5},{5,4},{6,7},{7,6},{8,9},{9,8},{10,11... | collective-permute-start | bytes 3538952 | tf_op jit(solution)/shard_map/ppermute | solution.py:29
  275.8 32.0 %collective-permute-start.47 = (bf16[2304,256]{1,0:T(8,128)(2,1)}, bf16[2304,256]{1,0:T(8,128)(2,1)S(1)}, u32[]{:S(2)}, u32[]{:S(2)}) collective-permute-start(bf16[2304,256]{1,0:T(8,128)(2,1)} %get-tuple-element.467.refs_14_), channel_id=1, source_target_pairs={{0,1},{1,0},{2,3},{3,2},{4,5},{5,4},{6,7},{7,6},{8,9},{9,8},{10,11... | collective-permute-start | bytes 3538952 | tf_op jit(solution)/shard_map/ppermute | solution.py:29
  276.3 31.5 %collective-permute-start.46 = (bf16[2304,256]{1,0:T(8,128)(2,1)}, bf16[2304,256]{1,0:T(8,128)(2,1)}, u32[]{:S(2)}, u32[]{:S(2)}) collective-permute-start(bf16[2304,256]{1,0:T(8,128)(2,1)} %get-tuple-element.468.refs_17_), channel_id=1, source_target_pairs={{0,1},{1,0},{2,3},{3,2},{4,5},{5,4},{6,7},{7,6},{8,9},{9,8},{10,11... | collective-permute-start | bytes 3538952 | tf_op jit(solution)/shard_map/ppermute | solution.py:29
  309.8 27.8 %collective-permute-start.51 = (bf16[2304,256]{1,0:T(8,128)(2,1)S(1)}, bf16[2304,256]{1,0:T(8,128)(2,1)S(1)}, u32[]{:S(2)}, u32[]{:S(2)}) collective-permute-start(bf16[2304,256]{1,0:T(8,128)(2,1)S(1)} %copy-done.29), channel_id=1, source_target_pairs={{0,1},{1,0},{2,3},{3,2},{4,5},{5,4},{6,7},{7,6},{8,9},{9,8},{10,11... | collective-permute-start | bytes 3538952 | tf_op jit(solution)/shard_map/ppermute | solution.py:29
  331.2 48.7 %collective-permute-start.64 = (bf16[2304,256]{1,0:T(8,128)(2,1)}, bf16[2304,256]{1,0:T(8,128)(2,1)}, u32[]{:S(2)}, u32[]{:S(2)}) collective-permute-start(bf16[2304,256]{1,0:T(8,128)(2,1)} %add_convert_fusion.5), channel_id=1, source_target_pairs={{8,16},{12,20},{16,8},{20,12},{9,17},{13,21},{17,9},{21,13},{10,18... | collective-permute-start | bytes 3538952 | tf_op jit(solution)/shard_map/ppermute | solution.py:52
  382.5 29.5 %collective-permute-start.68 = (bf16[2304,256]{1,0:T(8,128)(2,1)S(1)}, bf16[2304,256]{1,0:T(8,128)(2,1)}, u32[]{:S(2)}, u32[]{:S(2)}) collective-permute-start(bf16[2304,256]{1,0:T(8,128)(2,1)S(1)} %copy-done.39), channel_id=1, source_target_pairs={{0,8},{4,12},{24,16},{28,20},{1,9},{5,13},{25,17},{29,21},{2,10},{... | collective-permute-start | bytes 3538952 | tf_op jit(solution)/shard_map/ppermute | solution.py:52
  387.1 32.2 %collective-permute-start.71 = (bf16[2304,256]{1,0:T(8,128)(2,1)}, bf16[2304,256]{1,0:T(8,128)(2,1)S(1)}, u32[]{:S(2)}, u32[]{:S(2)}) collective-permute-start(bf16[2304,256]{1,0:T(8,128)(2,1)} %add_convert_fusion.4), channel_id=1, source_target_pairs={{8,16},{12,20},{16,8},{20,12},{9,17},{13,21},{17,9},{21,13},{10,18... | collective-permute-start | bytes 3538952 | tf_op jit(solution)/shard_map/ppermute | solution.py:52
  391.7 27.7 %collective-permute-start.70 = (bf16[1152,256]{1,0:T(8,128)(2,1)}, bf16[1152,256]{1,0:T(8,128)(2,1)}, u32[]{:S(2)}, u32[]{:S(2)}) collective-permute-start(bf16[1152,256]{1,0:T(8,128)(2,1)} %dynamic-slice_convert_fusion.3), channel_id=1, source_target_pairs={{0,4},{4,0},{8,12},{12,8},{16,20},{20,16},{24,28},{28,24},{1,5},{5... | collective-permute-start | bytes 1769480 | tf_op jit(solution)/shard_map/ppermute | solution.py:29
  412.0 29.5 %collective-permute-start.73 = (bf16[2304,256]{1,0:T(8,128)(2,1)S(1)}, bf16[2304,256]{1,0:T(8,128)(2,1)S(1)}, u32[]{:S(2)}, u32[]{:S(2)}) collective-permute-start(bf16[2304,256]{1,0:T(8,128)(2,1)S(1)} %copy-done.38), channel_id=1, source_target_pairs={{0,8},{4,12},{24,16},{28,20},{1,9},{5,13},{25,17},{29,21},{2,10},{... | collective-permute-start | bytes 3538952 | tf_op jit(solution)/shard_map/ppermute | solution.py:52
  419.4 30.6 %collective-permute-start.74 = (bf16[2304,256]{1,0:T(8,128)(2,1)}, bf16[2304,256]{1,0:T(8,128)(2,1)S(1)}, u32[]{:S(2)}, u32[]{:S(2)}) collective-permute-start(bf16[2304,256]{1,0:T(8,128)(2,1)} %blend.13), channel_id=1, source_target_pairs={{8,16},{12,20},{16,8},{20,12},{9,17},{13,21},{17,9},{21,13},{10,18... | collective-permute-start | bytes 3538952 | tf_op jit(solution)/shard_map/ppermute | solution.py:52
  420.1 29.8 %collective-permute-start.72 = (bf16[64,9216]{1,0:T(8,128)(2,1)}, bf16[64,9216]{1,0:T(8,128)(2,1)S(1)}, u32[]{:S(2)}, u32[]{:S(2)}) collective-permute-start(bf16[64,9216]{1,0:T(8,128)(2,1)} %get-tuple-element.561), channel_id=1, source_target_pairs={{0,4},{4,0},{8,12},{12,8},{16,20},{20,16},{24,28},{28,24},{1,5},{5... | collective-permute-start | bytes 3538952 | tf_op jit(solution)/shard_map/ppermute | solution.py:29
  441.5 29.1 %collective-permute-start.76 = (bf16[2304,256]{1,0:T(8,128)(2,1)}, bf16[2304,256]{1,0:T(8,128)(2,1)}, u32[]{:S(2)}, u32[]{:S(2)}) collective-permute-start(bf16[2304,256]{1,0:T(8,128)(2,1)} %get-tuple-element.568), channel_id=1, source_target_pairs={{0,8},{4,12},{24,16},{28,20},{1,9},{5,13},{25,17},{29,21},{2,10},{... | collective-permute-start | bytes 3538952 | tf_op jit(solution)/shard_map/ppermute | solution.py:52
  507.7 29.5 %collective-permute-start.88 = (bf16[64,9216]{1,0:T(8,128)(2,1)}, bf16[64,9216]{1,0:T(8,128)(2,1)S(1)}, u32[]{:S(2)}, u32[]{:S(2)}) collective-permute-start(bf16[64,9216]{1,0:T(8,128)(2,1)} %add_convert_fusion), channel_id=1, source_target_pairs={{0,2},{1,3},{2,0},{3,1},{4,6},{5,7},{6,4},{7,5},{8,10},{9,11},{10,... | collective-permute-start | bytes 3538952 | tf_op jit(solution)/shard_map/ppermute | solution.py:29
  508.6 28.7 %collective-permute-start.87 = (bf16[512,256]{1,0:T(8,128)(2,1)}, bf16[512,256]{1,0:T(8,128)(2,1)}, u32[]{:S(2)}, u32[]{:S(2)}) collective-permute-start(bf16[512,256]{1,0:T(8,128)(2,1)} %bitcast.41), channel_id=1, source_target_pairs={{0,4},{4,0},{8,12},{12,8},{16,20},{20,16},{24,28},{28,24},{1,5},{5... | collective-permute-start | bytes 786440 | tf_op jit(solution)/shard_map/ppermute | solution.py:29
  523.0 34.3 %collective-permute-start.86 = (bf16[2304,256]{1,0:T(8,128)(2,1)}, bf16[2304,256]{1,0:T(8,128)(2,1)}, u32[]{:S(2)}, u32[]{:S(2)}) collective-permute-start(bf16[2304,256]{1,0:T(8,128)(2,1)} %blend.17), channel_id=1, source_target_pairs={{0,8},{4,12},{8,0},{12,4},{16,24},{20,28},{24,16},{28,20},{1,9},{5... | collective-permute-start | bytes 3538952 | tf_op jit(solution)/shard_map/ppermute | solution.py:52
  540.3 30.7 %collective-permute-start.93 = (bf16[1152,256]{1,0:T(8,128)(2,1)}, bf16[1152,256]{1,0:T(8,128)(2,1)S(1)}, u32[]{:S(2)}, u32[]{:S(2)}) collective-permute-start(bf16[1152,256]{1,0:T(8,128)(2,1)} %dynamic-slice_convert_fusion.1), channel_id=1, source_target_pairs={{0,4},{4,0},{8,12},{12,8},{16,20},{20,16},{24,28},{28,24},{1,5},{5... | collective-permute-start | bytes 1769480 | tf_op jit(solution)/shard_map/ppermute | solution.py:29
  (152 other events, 2468.1 us)

commit v7 on v6

--- a/solution.py
+++ b/solution.py
@@ -1134,12 +1134,12 @@
     came_far, came_x, own_y = {}, {}, {}
     into[2, 3] = arrive(into[2, 3])
     into[2, 2] = inward(2, 2)
-    [rest] = blended((part(1, 2), part(1, 2), into[1, 2]))
     crossed[1] = arrive(crossed[1])
     slab_came[0] = arrive(slab_came[0])
     act_came = arrive(act_came)
+    came_far[0] = p.send(x_swap, leave_far[0])
+    [rest] = blended((part(1, 2), part(1, 2), into[1, 2]))
     middle[1] = send("middle", rest)
-    came_far[0] = p.send(x_swap, leave_far[0])
     keep, leave = p.back(0, came_grads, own_pieces, far_pieces)
     into[2, 2] = arrive(into[2, 2])
     into[3, 3] = inward(3, 3)

time: 600 us -> 600 us (level)
  no operation moved by 1% of the time
where the time goes in v7:
time: 600 us; the launch traced here: 589 us
  Pallas kernels  221 us (37%)
  waiting for transfers between devices  148 us (25%)
  starting transfers between devices  109 us (18%)
  local copies, waits for them, and re-layouts  48 us (8%)
  other arithmetic  46.4 us (8%)
  matrix products  13.9 us (2%)
    pallas_call x4, Pallas kernels, chunk(): pl.pallas_call(functools.partial(chunk_kernel, [[len(p) for p in chunk] f...  85.3 us
    ppermute x35, waiting for transfers between devices, line(): return lax.ppermute(value, 'batch', pairs)  83.9 us
    ppermute x62, waiting for transfers between devices, flipped(): return lax.ppermute(value, axis, pairs)  63.8 us
    ppermute x35, starting transfers between devices, line(): return lax.ppermute(value, 'batch', pairs)  61.4 us
    ppermute x62, starting transfers between devices, flipped(): return lax.ppermute(value, axis, pairs)  47.8 us
    pallas_call x3, Pallas kernels, unpool(): pl.pallas_call(functools.partial(unpool_kernel, at), grid_spec=pltpu.Pref...  36.1 us
    pallas_call x2, Pallas kernels, back(): pl.pallas_call(functools.partial(back_kernel, layout, [row for _, row in...  35 us
    pallas_call x9, Pallas kernels, blend(): pl.pallas_call(functools.partial(blend_kernel, counts), in_specs=[pl.Bloc...  32.2 us
  transfers between devices with their start and end apart: 97, of which 24 were waited for; matrix products, arithmetic and copies ran while one was open for 17% of the time, Pallas kernels for 38%

profile of v7, /device:TPU:0, one launch (start us, length us, event | category | flops | bytes accessed | tf_op | source)
XLA Modules:
  0.0 589.0 jit_solution(3247076088579403164)
XLA Ops:
  32.0 13.9 %fusion.2.summed = f32[128,2,36,256]{3,2,1,0:T(8,128)} fusion(bf16[128,2,169,256]{3,1,2,0:T(2,128)(2,1)} %param.8, bf16[36,169]{1,0:T(8,128)(2,1)S(1)} %and_convert_fusion), kind=kOutput, calls=%fused_computation.3 | convolution fusion | flops 797442048 | bytes 31600520 | tf_op jit(solution)/shard_map/pq,nsqc->nspc/dot_general | solution.py:756
  56.6 14.2 %mix.1 = (bf16[128,4608]{1,0:T(8,128)(2,1)}, bf16[128,4608]{1,0:T(8,128)(2,1)}, bf16[128,4608]{1,0:T(8,128)(2,1)}, bf16[128,4608]{1,0:T(8,128)(2,1)}, f32[2,128,9216]{2,1,0:T(8,128)}) custom-call(s32[128]{0:T(128)} %group.7, f32[2,36,256]{2,1,0:T(8,128)} %broadcast_in_dim.8.keep, f32[4,256]{1,0:T(4,128)} %reshape.654.first, f32[128,2,36,256]{3,2,1,0:T(8,128)} %fusion.2.summed), custom_call_target="tpu_custom_call" | custom-call | flops 1000 | bytes 1000 | tf_op jit(solution)/shard_map/mix/pallas_call | solution.py:149
  79.7 17.4 %collective-permute-done.10.refs_8_ = bf16[128,4608]{1,0:T(8,128)(2,1)} collective-permute-done((bf16[128,4608]{1,0:T(8,128)(2,1)}, bf16[128,4608]{1,0:T(8,128)(2,1)}, u32[]{:S(2)}, u32[]{:S(2)}) %collective-permute-start.10) | collective-permute-done | bytes 1179680 | tf_op jit(solution)/shard_map/ppermute | solution.py:29
  101.8 5.7 collective-permute-done.15.refs_22_.refs_0_
  110.4 12.6 %collective-permute-done.13.refs_9_ = bf16[128,4608]{1,0:T(8,128)(2,1)} collective-permute-done((bf16[128,4608]{1,0:T(8,128)(2,1)S(1)}, bf16[128,4608]{1,0:T(8,128)(2,1)}, u32[]{:S(2)}, u32[]{:S(2)}) %collective-permute-start.13) | collective-permute-done | bytes 1179680 | tf_op jit(solution)/shard_map/ppermute | solution.py:29
  125.4 11.8 %collective-permute-done.22.refs_22_.refs_2_ = bf16[2304,256]{1,0:T(8,128)(2,1)} collective-permute-done((bf16[2304,256]{1,0:T(8,128)(2,1)}, bf16[2304,256]{1,0:T(8,128)(2,1)}, u32[]{:S(2)}, u32[]{:S(2)}) %collective-permute-start.22) | collective-permute-done | bytes 1179680 | tf_op jit(solution)/shard_map/ppermute | solution.py:52
  138.0 11.1 %collective-permute-done.20.refs_10_ = bf16[128,4608]{1,0:T(8,128)(2,1)} collective-permute-done((bf16[128,4608]{1,0:T(8,128)(2,1)}, bf16[128,4608]{1,0:T(8,128)(2,1)}, u32[]{:S(2)}, u32[]{:S(2)}) %collective-permute-start.20) | collective-permute-done | bytes 1179680 | tf_op jit(solution)/shard_map/ppermute | solution.py:29
  152.6 11.6 %collective-permute-done.23.refs_24_.refs_4_.refs_9_.refs_22_ = bf16[2304,256]{1,0:T(8,128)(2,1)} collective-permute-done((bf16[2304,256]{1,0:T(8,128)(2,1)S(1)}, bf16[2304,256]{1,0:T(8,128)(2,1)}, u32[]{:S(2)}, u32[]{:S(2)}) %collective-permute-start.23) | collective-permute-done | bytes 1179680 | tf_op jit(solution)/shard_map/ppermute | solution.py:52
  164.5 6.9 %collective-permute-done.25.refs_11_ = bf16[128,4608]{1,0:T(8,128)(2,1)} collective-permute-done((bf16[128,4608]{1,0:T(8,128)(2,1)}, bf16[128,4608]{1,0:T(8,128)(2,1)}, u32[]{:S(2)}, u32[]{:S(2)}) %collective-permute-start.25) | collective-permute-done | bytes 1179680 | tf_op jit(solution)/shard_map/ppermute | solution.py:29
  174.4 15.9 %collective-permute-done.24.refs_24_.refs_6_.refs_3_.refs_22_ = bf16[2304,256]{1,0:T(8,128)(2,1)} collective-permute-done((bf16[2304,256]{1,0:T(8,128)(2,1)}, bf16[2304,256]{1,0:T(8,128)(2,1)}, u32[]{:S(2)}, u32[]{:S(2)}) %collective-permute-start.24) | collective-permute-done | bytes 1179680 | tf_op jit(solution)/shard_map/ppermute | solution.py:52
  193.3 21.2 %chunk.4 = (bf16[1024,256]{1,0:T(8,128)(2,1)}, bf16[512,256]{1,0:T(8,128)(2,1)}, bf16[512,256]{1,0:T(8,128)(2,1)}, f32[8,256]{1,0:T(8,128)}, f32[2304,256]{1,0:T...) custom-call(s32[2]{0:T(128)} %pad_add_fusion.2.roles, ...), custom_call_target="tpu_custom_call" | custom-call | flops 1000 | bytes 1000 | tf_op jit(solution)/shard_map/chunk/pallas_call | solution.py:565
  222.6 21.1 %chunk.5 = (bf16[1024,256]{1,0:T(8,128)(2,1)}, bf16[512,256]{1,0:T(8,128)(2,1)}, bf16[512,256]{1,0:T(8,128)(2,1)}, f32[8,256]{1,0:T(8,128)}, f32[2304,256]{1,0:T...) custom-call(s32[2]{0:T(128)} %pad_add_fusion.2.roles, ...), custom_call_target="tpu_custom_call" | custom-call | flops 1000 | bytes 1000 | tf_op jit(solution)/shard_map/chunk/pallas_call | solution.py:565
  253.0 7.5 %blend.9 = (bf16[2304,256]{1,0:T(8,128)(2,1)}, bf16[2304,256]{1,0:T(8,128)(2,1)}, bf16[2304,256]{1,0:T(8,128)(2,1)}, bf16[2304,256]{1,0:T(8,128)(2,1)}, bf16[230...) custom-call(s32[2]{0:T(128)} %pad_add_fusion.2.roles, ...), custom_call_target="tpu_custom_call" | custom-call | flops 1000 | bytes 1000 | tf_op jit(solution)/shard_map/blend/pallas_call | solution.py:378
  264.6 9.9 %collective-permute-done.44.refs_25_.refs_4_ = bf16[2304,256]{1,0:T(8,128)(2,1)} collective-permute-done((bf16[2304,256]{1,0:T(8,128)(2,1)}, bf16[2304,256]{1,0:T(8,128)(2,1)}, u32[]{:S(2)}, u32[]{:S(2)}) %collective-permute-start.44) | collective-permute-done | bytes 1179680 | tf_op jit(solution)/shard_map/ppermute | solution.py:52
  276.4 21.1 %chunk.6 = (bf16[1024,256]{1,0:T(8,128)(2,1)}, bf16[512,256]{1,0:T(8,128)(2,1)}, bf16[512,256]{1,0:T(8,128)(2,1)}, f32[8,256]{1,0:T(8,128)}, f32[2304,256]{1,0:T...) custom-call(s32[2]{0:T(128)} %pad_add_fusion.2.roles, ...), custom_call_target="tpu_custom_call" | custom-call | flops 1000 | bytes 1000 | tf_op jit(solution)/shard_map/chunk/pallas_call | solution.py:565
  310.9 3.9 blend.11
  314.8 14.2 %collective-permute-done.55.refs_3_.refs_23_ = bf16[2304,256]{1,0:T(8,128)(2,1)S(1)} collective-permute-done((bf16[2304,256]{1,0:T(8,128)(2,1)}, bf16[2304,256]{1,0:T(8,128)(2,1)S(1)}, u32[]{:S(2)}, u32[]{:S(2)}) %collective-permute-start.55) | collective-permute-done | bytes 1179680 | tf_op jit(solution)/shard_map/ppermute | solution.py:52
  349.9 5.6 collective-permute-done.56.refs_25_.refs_23_.refs_2_
  358.0 21.9 %chunk.7 = (bf16[1024,256]{1,0:T(8,128)(2,1)}, bf16[512,256]{1,0:T(8,128)(2,1)}, bf16[512,256]{1,0:T(8,128)(2,1)}, f32[8,256]{1,0:T(8,128)}, f32[2304,256]{1,0:T...) custom-call(s32[2]{0:T(128)} %pad_add_fusion.2.roles, ...), custom_call_target="tpu_custom_call" | custom-call | flops 1000 | bytes 1000 | tf_op jit(solution)/shard_map/chunk/pallas_call | solution.py:565
  382.5 4.7 collective-permute-start.71
  393.9 17.5 %back.2 = (bf16[64,9216]{1,0:T(8,128)(2,1)}, bf16[64,9216]{1,0:T(8,128)(2,1)}, bf16[64,9216]{1,0:T(8,128)(2,1)}, bf16[64,9216]{1,0:T(8,128)(2,1)}) custom-call(s32[2]{0:T(128)} %pad_add_fusion.2.roles, bf16[512,256]{1,0:T(8,128)(2,1)} %get-tuple-element.560.refs_0_, bf16[512,256]{1,0:T(8,128)(2,1)} %get-tuple-element.546.refs_1_, ...), custom_call_target="tpu_custom_call" | custom-call | flops 1000 | bytes 1000 | tf_op jit(solution)/shard_map/back/pallas_call | solution.py:675
  412.0 4.6 collective-permute-start.73
  421.8 17.5 %back.3 = (bf16[64,9216]{1,0:T(8,128)(2,1)}, bf16[64,9216]{1,0:T(8,128)(2,1)}, bf16[64,9216]{1,0:T(8,128)(2,1)}, bf16[64,9216]{1,0:T(8,128)(2,1)}) custom-call(s32[2]{0:T(128)} %pad_add_fusion.2.roles, bf16[512,256]{1,0:T(8,128)(2,1)} %get-tuple-element.560.refs_0_, bf16[512,256]{1,0:T(8,128)(2,1)} %get-tuple-element.546.refs_1_, ...), custom_call_target="tpu_custom_call" | custom-call | flops 1000 | bytes 1000 | tf_op jit(solution)/shard_map/back/pallas_call | solution.py:675
  441.5 5.7 collective-permute-start.76
  466.7 3.9 store.4.refs_0_
  484.1 10.0 %unpool.3 = (bf16[128,169,2,256]{3,2,1,0:T(2,128)(2,1)}, f32[4,16,256]{2,1,0:T(8,128)}) custom-call(s32[128]{0:T(128)} %group.7, bf16[2,352,192]{2,1,0:T(8,128)(2,1)} %fusion.15.table, f32[4,256]{1,0:T(4,128)} %reshape.654.first, bf16[64,9216]{1,0:T(8,128)(2,1)} %get-tuple-element.610.keep_in, bf16[64,9216]{1,0:T(8,128)(2,1)} %copy-done.35, ...), custom_call_target="tpu_custom_call" | custom-call | flops 1000 | bytes 1000 | tf_op jit(solution)/shard_map/unpool/pallas_call | solution.py:224
  512.9 10.0 %unpool.4 = (bf16[128,169,2,256]{3,2,1,0:T(2,128)(2,1)}, f32[4,16,256]{2,1,0:T(8,128)}) custom-call(s32[128]{0:T(128)} %group.7, bf16[2,352,192]{2,1,0:T(8,128)(2,1)} %fusion.15.table, f32[4,256]{1,0:T(4,128)} %reshape.654.first, bf16[64,9216]{1,0:T(8,128)(2,1)} %get-tuple-element.610.keep_in, ...), custom_call_target="tpu_custom_call", output_to_operand_aliasing={{0}: (7, {})} | custom-call | flops 1000 | bytes 1000 | tf_op jit(solution)/shard_map/unpool/pallas_call | solution.py:224
  526.4 4.9 collective-permute-done.83.came_in
  541.3 16.0 %unpool.5 = (bf16[128,169,2,256]{3,2,1,0:T(2,128)(2,1)}, f32[4,16,256]{2,1,0:T(8,128)}) custom-call(s32[128]{0:T(128)} %group.7, bf16[2,352,192]{2,1,0:T(8,128)(2,1)} %fusion.15.table, f32[4,256]{1,0:T(4,128)} %reshape.654.first, bf16[64,9216]{1,0:T(8,128)(2,1)} %get-tuple-element.627.keep_in, ...), custom_call_target="tpu_custom_call", output_to_operand_aliasing={{0}: (7, {})} | custom-call | flops 1000 | bytes 1000 | tf_op jit(solution)/shard_map/unpool/pallas_call | solution.py:224
  564.0 3.8 store.5.refs_0_
  571.9 3.8 store.6.refs_0_
  582.5 3.8 store.7
  (484 shorter events, 232.6 us)
Async XLA Ops:
  7.4 38.4 %collective-permute-start.2 = (bf16[1152,256]{1,0:T(8,128)(2,1)}, bf16[1152,256]{1,0:T(8,128)(2,1)}, u32[]{:S(2)}, u32[]{:S(2)}) collective-permute-start(bf16[1152,256]{1,0:T(8,128)(2,1)} %constant_dynamic-slice_fusion.9), channel_id=1, source_target_pairs={{0,4},{4,0},{8,12},{12,8},{16,20},{20,16},{24,28},{28,24},{1,5},{5... | collective-permute-start | bytes 1769480 | tf_op jit(solution)/shard_map/ppermute | solution.py:29
  24.9 29.3 %collective-permute-start.3 = (bf16[2304,256]{1,0:T(8,128)(2,1)S(1)}, bf16[2304,256]{1,0:T(8,128)(2,1)}, u32[]{:S(2)}, u32[]{:S(2)}) collective-permute-start(bf16[2304,256]{1,0:T(8,128)(2,1)S(1)} %maximum_select_fusion.refs_20_.refs_8_), channel_id=1, source_target_pairs={{8,16},{12,20},{16,8},{20,12},{9,17},{13,21},{17,9},{21,13},{10,18... | collective-permute-start | bytes 3538952 | tf_op jit(solution)/shard_map/ppermute | solution.py:52
  29.0 41.9 %collective-permute-start.7 = (bf16[1152,512]{1,0:T(8,128)(2,1)}, bf16[1152,512]{1,0:T(8,128)(2,1)}, u32[]{:S(2)}, u32[]{:S(2)}) collective-permute-start(bf16[1152,512]{1,0:T(8,128)(2,1)} %constant_dynamic-slice_fusion.5), channel_id=1, source_target_pairs={{0,4},{4,0},{8,12},{12,8},{16,20},{20,16},{24,28},{28,24},{1,5},{5... | collective-permute-start | bytes 3538952 | tf_op jit(solution)/shard_map/ppermute | solution.py:29
  30.5 40.4 %collective-permute-start.6 = (bf16[512,1024]{1,0:T(8,128)(2,1)S(1)}, bf16[512,1024]{1,0:T(8,128)(2,1)S(1)}, u32[]{:S(2)}, u32[]{:S(2)}) collective-permute-start(bf16[512,1024]{1,0:T(8,128)(2,1)S(1)} %constant_dynamic-slice_fusion.8.refs_0_), channel_id=1, source_target_pairs={{0,2},{1,3},{2,0},{3,1},{4,6},{5,7},{6,4},{7,5},{8,10},{9,11},{10,... | collective-permute-start | bytes 3145736 | tf_op jit(solution)/shard_map/ppermute | solution.py:29
  76.6 30.9 %collective-permute-start.15 = (bf16[2304,256]{1,0:T(8,128)(2,1)}, bf16[2304,256]{1,0:T(8,128)(2,1)}, u32[]{:S(2)}, u32[]{:S(2)}) collective-permute-start(bf16[2304,256]{1,0:T(8,128)(2,1)} %collective-permute-done.3.refs_23_.refs_1_), channel_id=1, source_target_pairs={{8,0},{12,4},{16,24},{20,28},{9,1},{13,5},{17,25},{21,29},{10,2},{... | collective-permute-start | bytes 3538952 | tf_op jit(solution)/shard_map/ppermute | solution.py:52
  78.0 30.7 %collective-permute-start.14 = (bf16[2304,256]{1,0:T(8,128)(2,1)}, bf16[2304,256]{1,0:T(8,128)(2,1)}, u32[]{:S(2)}, u32[]{:S(2)}) collective-permute-start(bf16[2304,256]{1,0:T(8,128)(2,1)} %collective-permute-done.4.refs_21_.refs_9_), channel_id=1, source_target_pairs={{8,16},{12,20},{16,8},{20,12},{9,17},{13,21},{17,9},{21,13},{10,18... | collective-permute-start | bytes 3538952 | tf_op jit(solution)/shard_map/ppermute | solution.py:52
  107.4 29.9 %collective-permute-start.22 = (bf16[2304,256]{1,0:T(8,128)(2,1)}, bf16[2304,256]{1,0:T(8,128)(2,1)}, u32[]{:S(2)}, u32[]{:S(2)}) collective-permute-start(bf16[2304,256]{1,0:T(8,128)(2,1)} %collective-permute-done.11.refs_23_.refs_3_), channel_id=1, source_target_pairs={{8,0},{12,4},{16,24},{20,28},{9,1},{13,5},{17,25},{21,29},{10,2},{... | collective-permute-start | bytes 3538952 | tf_op jit(solution)/shard_map/ppermute | solution.py:52
  108.7 28.6 %collective-permute-start.21 = (bf16[2304,256]{1,0:T(8,128)(2,1)}, bf16[2304,256]{1,0:T(8,128)(2,1)}, u32[]{:S(2)}, u32[]{:S(2)}) collective-permute-start(bf16[2304,256]{1,0:T(8,128)(2,1)} %collective-permute-done.12.refs_21_.refs_13_), channel_id=1, source_target_pairs={{8,16},{12,20},{16,8},{20,12},{9,17},{13,21},{17,9},{21,13},{10,18... | collective-permute-start | bytes 3538952 | tf_op jit(solution)/shard_map/ppermute | solution.py:52
  172.0 42.5 %collective-permute-start.35 = (bf16[2304,256]{1,0:T(8,128)(2,1)}, bf16[2304,256]{1,0:T(8,128)(2,1)}, u32[]{:S(2)}, u32[]{:S(2)}) collective-permute-start(bf16[2304,256]{1,0:T(8,128)(2,1)} %collective-permute-done.23.refs_24_.refs_4_.refs_9_.refs_22_), channel_id=1, source_target_pairs={{8,16},{12,20},{16,8},{20,12},{9,17},{13,21},{17,9},{21,13},{10,18... | collective-permute-start | bytes 3538952 | tf_op jit(solution)/shard_map/ppermute | solution.py:52
  217.3 29.1 %collective-permute-start.39 = (bf16[2304,256]{1,0:T(8,128)(2,1)}, bf16[2304,256]{1,0:T(8,128)(2,1)S(1)}, u32[]{:S(2)}, u32[]{:S(2)}) collective-permute-start(bf16[2304,256]{1,0:T(8,128)(2,1)} %broadcast_select_fusion.1), channel_id=1, source_target_pairs={{0,8},{4,12},{8,0},{12,4},{16,24},{20,28},{24,16},{28,20},{1,9},{5... | collective-permute-start | bytes 3538952 | tf_op jit(solution)/shard_map/ppermute | solution.py:52
  219.4 29.5 %collective-permute-start.38 = (bf16[2304,256]{1,0:T(8,128)(2,1)S(1)}, bf16[2304,256]{1,0:T(8,128)(2,1)S(1)}, u32[]{:S(2)}, u32[]{:S(2)}) collective-permute-start(bf16[2304,256]{1,0:T(8,128)(2,1)S(1)} %maximum_select_fusion.3.refs_13_.refs_20_), channel_id=1, source_target_pairs={{8,16},{12,20},{16,8},{20,12},{9,17},{13,21},{17,9},{21,13},{10,18... | collective-permute-start | bytes 3538952 | tf_op jit(solution)/shard_map/ppermute | solution.py:52
  220.1 30.5 %collective-permute-start.37 = (bf16[1024,256]{1,0:T(8,128)(2,1)}, bf16[1024,256]{1,0:T(8,128)(2,1)}, u32[]{:S(2)}, u32[]{:S(2)}) collective-permute-start(bf16[1024,256]{1,0:T(8,128)(2,1)} %get-tuple-element.430), channel_id=1, source_target_pairs={{0,2},{1,3},{2,0},{3,1},{4,6},{5,7},{6,4},{7,5},{8,10},{9,11},{10,... | collective-permute-start | bytes 1572872 | tf_op jit(solution)/shard_map/ppermute | solution.py:29
  222.1 28.5 %collective-permute-start.41 = (bf16[2304,256]{1,0:T(8,128)(2,1)}, bf16[2304,256]{1,0:T(8,128)(2,1)S(1)}, u32[]{:S(2)}, u32[]{:S(2)}) collective-permute-start(bf16[2304,256]{1,0:T(8,128)(2,1)} %maximum_select_fusion.1.refs_20_.refs_12_), channel_id=1, source_target_pairs={{0,1},{1,0},{2,3},{3,2},{4,5},{5,4},{6,7},{7,6},{8,9},{9,8},{10,11... | collective-permute-start | bytes 3538952 | tf_op jit(solution)/shard_map/ppermute | solution.py:29
  222.1 28.5 %collective-permute-start.40 = (bf16[2304,256]{1,0:T(8,128)(2,1)}, bf16[2304,256]{1,0:T(8,128)(2,1)}, u32[]{:S(2)}, u32[]{:S(2)}) collective-permute-start(bf16[2304,256]{1,0:T(8,128)(2,1)} %collective-permute-done.12.refs_21_.refs_13_), channel_id=1, source_target_pairs={{0,1},{1,0},{2,3},{3,2},{4,5},{5,4},{6,7},{7,6},{8,9},{9,8},{10,11... | collective-permute-start | bytes 3538952 | tf_op jit(solution)/shard_map/ppermute | solution.py:29
  246.3 28.2 %collective-permute-start.44 = (bf16[2304,256]{1,0:T(8,128)(2,1)}, bf16[2304,256]{1,0:T(8,128)(2,1)}, u32[]{:S(2)}, u32[]{:S(2)}) collective-permute-start(bf16[2304,256]{1,0:T(8,128)(2,1)} %broadcast_select_fusion), channel_id=1, source_target_pairs={{0,8},{4,12},{8,0},{12,4},{16,24},{20,28},{24,16},{28,20},{1,9},{5... | collective-permute-start | bytes 3538952 | tf_op jit(solution)/shard_map/ppermute | solution.py:52
  252.2 45.3 %collective-permute-start.49 = (bf16[2304,256]{1,0:T(8,128)(2,1)}, bf16[2304,256]{1,0:T(8,128)(2,1)S(1)}, u32[]{:S(2)}, u32[]{:S(2)}) collective-permute-start(bf16[2304,256]{1,0:T(8,128)(2,1)} %collective-permute-done.24.refs_24_.refs_6_.refs_3_.refs_22_), channel_id=1, source_target_pairs={{8,16},{12,20},{16,8},{20,12},{9,17},{13,21},{17,9},{21,13},{10,18... | collective-permute-start | bytes 3538952 | tf_op jit(solution)/shard_map/ppermute | solution.py:52
  275.7 32.0 %collective-permute-start.48 = (bf16[2304,256]{1,0:T(8,128)(2,1)S(1)}, bf16[2304,256]{1,0:T(8,128)(2,1)S(1)}, u32[]{:S(2)}, u32[]{:S(2)}) collective-permute-start(bf16[2304,256]{1,0:T(8,128)(2,1)S(1)} %copy-done.27), channel_id=1, source_target_pairs={{0,1},{1,0},{2,3},{3,2},{4,5},{5,4},{6,7},{7,6},{8,9},{9,8},{10,11... | collective-permute-start | bytes 3538952 | tf_op jit(solution)/shard_map/ppermute | solution.py:29
  275.8 32.0 %collective-permute-start.47 = (bf16[2304,256]{1,0:T(8,128)(2,1)}, bf16[2304,256]{1,0:T(8,128)(2,1)S(1)}, u32[]{:S(2)}, u32[]{:S(2)}) collective-permute-start(bf16[2304,256]{1,0:T(8,128)(2,1)} %get-tuple-element.466.refs_14_), channel_id=1, source_target_pairs={{0,1},{1,0},{2,3},{3,2},{4,5},{5,4},{6,7},{7,6},{8,9},{9,8},{10,11... | collective-permute-start | bytes 3538952 | tf_op jit(solution)/shard_map/ppermute | solution.py:29
  276.3 31.5 %collective-permute-start.46 = (bf16[2304,256]{1,0:T(8,128)(2,1)}, bf16[2304,256]{1,0:T(8,128)(2,1)}, u32[]{:S(2)}, u32[]{:S(2)}) collective-permute-start(bf16[2304,256]{1,0:T(8,128)(2,1)} %get-tuple-element.467.refs_17_), channel_id=1, source_target_pairs={{0,1},{1,0},{2,3},{3,2},{4,5},{5,4},{6,7},{7,6},{8,9},{9,8},{10,11... | collective-permute-start | bytes 3538952 | tf_op jit(solution)/shard_map/ppermute | solution.py:29
  309.9 27.8 %collective-permute-start.51 = (bf16[2304,256]{1,0:T(8,128)(2,1)S(1)}, bf16[2304,256]{1,0:T(8,128)(2,1)S(1)}, u32[]{:S(2)}, u32[]{:S(2)}) collective-permute-start(bf16[2304,256]{1,0:T(8,128)(2,1)S(1)} %copy-done.29), channel_id=1, source_target_pairs={{0,1},{1,0},{2,3},{3,2},{4,5},{5,4},{6,7},{7,6},{8,9},{9,8},{10,11... | collective-permute-start | bytes 3538952 | tf_op jit(solution)/shard_map/ppermute | solution.py:29
  331.2 48.7 %collective-permute-start.64 = (bf16[2304,256]{1,0:T(8,128)(2,1)}, bf16[2304,256]{1,0:T(8,128)(2,1)}, u32[]{:S(2)}, u32[]{:S(2)}) collective-permute-start(bf16[2304,256]{1,0:T(8,128)(2,1)} %add_convert_fusion.5), channel_id=1, source_target_pairs={{8,16},{12,20},{16,8},{20,12},{9,17},{13,21},{17,9},{21,13},{10,18... | collective-permute-start | bytes 3538952 | tf_op jit(solution)/shard_map/ppermute | solution.py:52
  382.5 29.5 %collective-permute-start.71 = (bf16[2304,256]{1,0:T(8,128)(2,1)S(1)}, bf16[2304,256]{1,0:T(8,128)(2,1)}, u32[]{:S(2)}, u32[]{:S(2)}) collective-permute-start(bf16[2304,256]{1,0:T(8,128)(2,1)S(1)} %copy-done.39), channel_id=1, source_target_pairs={{0,8},{4,12},{24,16},{28,20},{1,9},{5,13},{25,17},{29,21},{2,10},{... | collective-permute-start | bytes 3538952 | tf_op jit(solution)/shard_map/ppermute | solution.py:52
  387.2 29.4 %collective-permute-start.70 = (bf16[2304,256]{1,0:T(8,128)(2,1)}, bf16[2304,256]{1,0:T(8,128)(2,1)S(1)}, u32[]{:S(2)}, u32[]{:S(2)}) collective-permute-start(bf16[2304,256]{1,0:T(8,128)(2,1)} %add_convert_fusion.4), channel_id=1, source_target_pairs={{8,16},{12,20},{16,8},{20,12},{9,17},{13,21},{17,9},{21,13},{10,18... | collective-permute-start | bytes 3538952 | tf_op jit(solution)/shard_map/ppermute | solution.py:52
  412.0 29.5 %collective-permute-start.73 = (bf16[2304,256]{1,0:T(8,128)(2,1)S(1)}, bf16[2304,256]{1,0:T(8,128)(2,1)S(1)}, u32[]{:S(2)}, u32[]{:S(2)}) collective-permute-start(bf16[2304,256]{1,0:T(8,128)(2,1)S(1)} %copy-done.38), channel_id=1, source_target_pairs={{0,8},{4,12},{24,16},{28,20},{1,9},{5,13},{25,17},{29,21},{2,10},{... | collective-permute-start | bytes 3538952 | tf_op jit(solution)/shard_map/ppermute | solution.py:52
  419.4 30.6 %collective-permute-start.74 = (bf16[2304,256]{1,0:T(8,128)(2,1)}, bf16[2304,256]{1,0:T(8,128)(2,1)S(1)}, u32[]{:S(2)}, u32[]{:S(2)}) collective-permute-start(bf16[2304,256]{1,0:T(8,128)(2,1)} %blend.13), channel_id=1, source_target_pairs={{8,16},{12,20},{16,8},{20,12},{9,17},{13,21},{17,9},{21,13},{10,18... | collective-permute-start | bytes 3538952 | tf_op jit(solution)/shard_map/ppermute | solution.py:52
  420.1 29.9 %collective-permute-start.72 = (bf16[64,9216]{1,0:T(8,128)(2,1)}, bf16[64,9216]{1,0:T(8,128)(2,1)S(1)}, u32[]{:S(2)}, u32[]{:S(2)}) collective-permute-start(bf16[64,9216]{1,0:T(8,128)(2,1)} %get-tuple-element.558), channel_id=1, source_target_pairs={{0,4},{4,0},{8,12},{12,8},{16,20},{20,16},{24,28},{28,24},{1,5},{5... | collective-permute-start | bytes 3538952 | tf_op jit(solution)/shard_map/ppermute | solution.py:29
  441.5 29.2 %collective-permute-start.76 = (bf16[2304,256]{1,0:T(8,128)(2,1)}, bf16[2304,256]{1,0:T(8,128)(2,1)}, u32[]{:S(2)}, u32[]{:S(2)}) collective-permute-start(bf16[2304,256]{1,0:T(8,128)(2,1)} %get-tuple-element.566), channel_id=1, source_target_pairs={{0,8},{4,12},{24,16},{28,20},{1,9},{5,13},{25,17},{29,21},{2,10},{... | collective-permute-start | bytes 3538952 | tf_op jit(solution)/shard_map/ppermute | solution.py:52
  503.7 27.6 %collective-permute-start.83 = (bf16[64,9216]{1,0:T(8,128)(2,1)}, bf16[64,9216]{1,0:T(8,128)(2,1)S(1)}, u32[]{:S(2)}, u32[]{:S(2)}) collective-permute-start(bf16[64,9216]{1,0:T(8,128)(2,1)} %get-tuple-element.602), channel_id=1, source_target_pairs={{0,4},{4,0},{8,12},{12,8},{16,20},{20,16},{24,28},{28,24},{1,5},{5... | collective-permute-start | bytes 3538952 | tf_op jit(solution)/shard_map/ppermute | solution.py:29
  507.8 29.4 %collective-permute-start.88 = (bf16[64,9216]{1,0:T(8,128)(2,1)}, bf16[64,9216]{1,0:T(8,128)(2,1)S(1)}, u32[]{:S(2)}, u32[]{:S(2)}) collective-permute-start(bf16[64,9216]{1,0:T(8,128)(2,1)} %add_convert_fusion), channel_id=1, source_target_pairs={{0,2},{1,3},{2,0},{3,1},{4,6},{5,7},{6,4},{7,5},{8,10},{9,11},{10,... | collective-permute-start | bytes 3538952 | tf_op jit(solution)/shard_map/ppermute | solution.py:29
  508.6 28.6 %collective-permute-start.87 = (bf16[512,256]{1,0:T(8,128)(2,1)}, bf16[512,256]{1,0:T(8,128)(2,1)}, u32[]{:S(2)}, u32[]{:S(2)}) collective-permute-start(bf16[512,256]{1,0:T(8,128)(2,1)} %bitcast.41), channel_id=1, source_target_pairs={{0,4},{4,0},{8,12},{12,8},{16,20},{20,16},{24,28},{28,24},{1,5},{5... | collective-permute-start | bytes 786440 | tf_op jit(solution)/shard_map/ppermute | solution.py:29
  523.0 34.4 %collective-permute-start.86 = (bf16[2304,256]{1,0:T(8,128)(2,1)}, bf16[2304,256]{1,0:T(8,128)(2,1)}, u32[]{:S(2)}, u32[]{:S(2)}) collective-permute-start(bf16[2304,256]{1,0:T(8,128)(2,1)} %blend.17), channel_id=1, source_target_pairs={{0,8},{4,12},{8,0},{12,4},{16,24},{20,28},{24,16},{28,20},{1,9},{5... | collective-permute-start | bytes 3538952 | tf_op jit(solution)/shard_map/ppermute | solution.py:52
  540.3 30.8 %collective-permute-start.93 = (bf16[1152,256]{1,0:T(8,128)(2,1)}, bf16[1152,256]{1,0:T(8,128)(2,1)S(1)}, u32[]{:S(2)}, u32[]{:S(2)}) collective-permute-start(bf16[1152,256]{1,0:T(8,128)(2,1)} %dynamic-slice_convert_fusion.1), channel_id=1, source_target_pairs={{0,4},{4,0},{8,12},{12,8},{16,20},{20,16},{24,28},{28,24},{1,5},{5... | collective-permute-start | bytes 1769480 | tf_op jit(solution)/shard_map/ppermute | solution.py:29
  (152 other events, 2445.8 us)
